TPU v7x, 256 devices: a whole 4x4x8 slice. The times are simulated.
256 devices in a mesh: shot: 16 (over x_hi, z), gx: 8 (over y, core), gy: 2 (over x_lo).
Axes of the slice: x: 4 (x_hi: 2, x_lo: 2; x = x_hi * 2 + x_lo), y: 4, z: 8, core: 2. Of those that a mesh axis runs over, the one named last changes fastest.
Arguments:
- older_field: float32 [16, 64, 64, 256], P('shot', None, 'gx', 'gy'), may hold values from -6 to 6
- newer_field: float32 [16, 64, 64, 256], P('shot', None, 'gx', 'gy'), may hold values from -6 to 6
- velocity: float32 [64, 64, 256], P(None, 'gx', 'gy'), may hold values from 0.03 to 0.1
- preconditioner: float32 [64, 64, 256], P('shot', 'gx', 'gy'), may hold values from 0.2 to 2
- traces: float32 [16, 4, 2048], P('shot'), may hold values from -6 to 6
- receiver_z: int32 [16, 2048], P('shot'), may hold values from 0 to 63
- receiver_x: int32 [16, 2048], P('shot'), may hold values from 0 to 63
- receiver_y: int32 [16, 2048], P('shot'), may hold values from 0 to 255
- aperture_x: int32 [16], P('shot'), may hold values from 0 to 16
- aperture_y: int32 [16], P('shot'), may hold values from 0 to 64
Outputs:
- image_step: float32 [64, 64, 256], P('shot', 'gx', 'gy')
- new_residual: float32 [16, 4, 2048], P('shot')
All inputs are finite; a program needn't handle non-finite values.
Results may differ from a plain program's by a relative error of at most 0.023.
Values sent between devices are 32-bit elements; how exact they have to be, the bound alone decides.
No kernel may reach another device: no remote copies, remote signals or barrier semaphores. Data moves between devices by JAX's collectives and lax.ppermute only.
A program may use at most 64 MiB of HBM per device.

v0:
```python
import jax
import jax.numpy as jnp
from jax import lax
from jax.sharding import PartitionSpec as P

STEPS = 4


stencil_weights = (-205.0 / 72.0, 8.0 / 5.0, -1.0 / 5.0, 8.0 / 315.0, -1.0 / 560.0)


def padded_2(cells, sides, width):
    for axis, dim in sides:
        count = lax.axis_size(axis)
        ends = count - 1
        head = lax.slice_in_dim(cells, 0, width, axis=dim)
        tail = lax.slice_in_dim(cells, cells.shape[dim] - width, cells.shape[dim], axis=dim)
        cells = jnp.concatenate(
            [
                lax.ppermute(tail, axis, [(i, (i + 1) % count) for i in range(ends)]),
                cells,
                lax.ppermute(head, axis, [((i + 1) % count, i) for i in range(ends)]),
            ],
            axis=dim,
        )
    return cells


def lap_core(padded):
    extended = jnp.pad(padded, ((4, 4), (0, 0), (0, 0)))
    full_z, full_x, full_y = extended.shape

    def window(shift_z, shift_x, shift_y):
        return extended[
            4 + shift_z : full_z - 4 + shift_z,
            4 + shift_x : full_x - 4 + shift_x,
            4 + shift_y : full_y - 4 + shift_y,
        ]

    result = 3.0 * stencil_weights[0] * window(0, 0, 0)
    for reach in range(1, 5):
        pairs = (
            window(reach, 0, 0)
            + window(-reach, 0, 0)
            + (window(0, reach, 0) + window(0, -reach, 0))
            + (window(0, 0, reach) + window(0, 0, -reach))
        )
        result = result + stencil_weights[reach] * pairs
    return result


def lap_local(field):
    return lap_core(padded_2(field, (("gx", 1), ("gy", 2)), 4))


def background(older, newer, velocity):
    accels = []
    for moment in range(STEPS):
        accel = velocity * lap_local(newer)
        nxt = 2.0 * newer - older + accel
        accels.append(accel)
        older, newer = (newer, nxt)
    return accels


def on_device(
    older_field,
    newer_field,
    velocity,
    preconditioner,
    traces,
    receiver_z,
    receiver_x,
    receiver_y,
    aperture_x,
    aperture_y,
):
    older = older_field[0]
    newer = newer_field[0]
    shot_traces = traces[0]
    depth, span_x, span_y = velocity.shape
    anchor_x = lax.axis_index("gx") * span_x
    anchor_y = lax.axis_index("gy") * span_y
    width_x = span_x * lax.axis_size("gx") * 3 // 4
    width_y = span_y * lax.axis_size("gy") * 3 // 4
    cells_x = anchor_x + jnp.arange(span_x, dtype=jnp.int32)
    cells_y = anchor_y + jnp.arange(span_y, dtype=jnp.int32)
    inside_x = (cells_x >= aperture_x[0]) & (cells_x < aperture_x[0] + width_x)
    inside_y = (cells_y >= aperture_y[0]) & (cells_y < aperture_y[0] + width_y)
    window_mask = (inside_x[:, None] & inside_y[None, :]).astype(jnp.float32)[None]
    lat_x = receiver_x[0] - anchor_x
    lat_y = receiver_y[0] - anchor_y
    present = (lat_x >= 0) & (lat_x < span_x) & (lat_y >= 0) & (lat_y < span_y)
    flat_index = (
        receiver_z[0] * (span_x * span_y)
        + jnp.clip(lat_x, 0, span_x - 1) * span_y
        + jnp.clip(lat_y, 0, span_y - 1)
    )
    cell_count = depth * span_x * span_y

    def inject(values):
        spread = (
            jnp.zeros((cell_count,), jnp.float32)
            .at[flat_index]
            .add(jnp.where(present, values, 0.0))
        )
        return spread.reshape(depth, span_x, span_y)

    def sample(field):
        return jnp.where(present, field.reshape(-1)[flat_index], 0.0)

    accels = background(older, newer, velocity)
    latest = jnp.zeros_like(older)
    later = inject(shot_traces[STEPS - 1])
    grad = accels[STEPS - 1] * later
    for moment in range(STEPS - 2, -1, -1):
        adjoint = 2.0 * later - latest + lap_local(velocity * later) + inject(shot_traces[moment])
        grad = grad + accels[moment] * adjoint
        latest, later = (later, adjoint)
    owned = lax.psum_scatter(window_mask * grad, "shot", scatter_dimension=0, tiled=True)
    scaled = preconditioner * owned
    descent_dot = lax.psum(jnp.sum(owned * scaled), ("shot", "gx", "gy"))
    scaled_full = lax.all_gather(scaled, "shot", axis=0, tiled=True)
    source = window_mask * scaled_full
    before = jnp.zeros_like(older)
    current = source * accels[0]
    samples = [sample(current)]
    for moment in range(1, STEPS):
        nxt = 2.0 * current - before + velocity * lap_local(current) + source * accels[moment]
        samples.append(sample(nxt))
        before, current = (current, nxt)
    predicted = lax.psum(jnp.stack(samples), ("gx", "gy"))
    trace_energy = lax.psum(jnp.sum(predicted * predicted), "shot")
    step_length = descent_dot / (trace_energy + 1e-06)
    return (step_length * scaled, (shot_traces - step_length * predicted)[None])


def solution(mesh):
    return jax.shard_map(
        on_device,
        mesh=mesh,
        in_specs=(
            P("shot", None, "gx", "gy"),
            P("shot", None, "gx", "gy"),
            P(None, "gx", "gy"),
            P("shot", "gx", "gy"),
            P("shot", None, None),
            P("shot", None),
            P("shot", None),
            P("shot", None),
            P("shot"),
            P("shot"),
        ),
        out_specs=(P("shot", "gx", "gy"), P("shot", None, None)),
        check_vma=False,
    )
```

profile of v0, /device:TPU:32, one launch (start us, length us, event | category | flops | bytes accessed | tf_op | source)
XLA Modules:
  0.0 729.9 jit_solution(9629425863661775656)
XLA Ops:
  8.3 1.7 collective-permute-start
  13.9 11.3 %scatter_custom_fusion = f32[65536]{0:T(1024)S(1)} fusion(s32[2048]{0:T(1024)S(1)} %bitcast.68, f32[2048]{0:T(1024)S(1)} %get-tuple-element.89, f32[]{:T(128)} %constant.7.clone.1), kind=kCustom, calls=%fused_computation.601 | custom fusion | flops 2048 | bytes 262148 | tf_op jit(solution)/shard_map/scatter-add | solution.py:105
  25.3 4.4 collective-permute-start.16
  31.1 11.3 %scatter_custom_fusion.1 = f32[65536]{0:T(1024)S(1)} fusion(s32[2048]{0:T(1024)S(1)} %bitcast.69, f32[2048]{0:T(1024)S(1)} %get-tuple-element.88, f32[]{:T(128)} %constant.7.clone.1), kind=kCustom, calls=%fused_computation.599 | custom fusion | flops 2048 | bytes 262148 | tf_op jit(solution)/shard_map/scatter-add | solution.py:105
  42.4 11.3 %scatter_custom_fusion.2 = f32[65536]{0:T(1024)S(1)} fusion(s32[2048]{0:T(1024)S(1)} %bitcast.70, f32[2048]{0:T(1024)S(1)} %get-tuple-element.87, f32[]{:T(128)} %constant.7.clone.1), kind=kCustom, calls=%fused_computation.597 | custom fusion | flops 2048 | bytes 262148 | tf_op jit(solution)/shard_map/scatter-add | solution.py:105
  53.7 11.3 %scatter_custom_fusion.3 = f32[65536]{0:T(1024)S(1)} fusion(s32[2048]{0:T(1024)S(1)} %bitcast.71, f32[2048]{0:T(1024)S(1)} %get-tuple-element.86, f32[]{:T(128)} %constant.7.clone.1), kind=kCustom, calls=%fused_computation.595 | custom fusion | flops 2048 | bytes 262148 | tf_op jit(solution)/shard_map/scatter-add | solution.py:105
  66.8 3.4 collective-permute-start.2
  71.8 4.6 collective-permute-start.18
  77.7 3.3 collective-permute-done.2
  81.0 4.7 collective-permute-done.3
  88.6 4.3 collective-permute-start.4
  92.9 1.8 collective-permute-start.5
  94.6 2.4 collective-permute-done.19
  99.7 3.1 collective-permute-start.20
  104.4 1.5 collective-permute-start.6
  108.5 3.6 collective-permute-start.22
  113.5 2.2 collective-permute-done.6
  115.7 4.7 collective-permute-done.7
  123.0 6.5 collective-permute-start.8
  134.3 4.6 collective-permute-start.24
  143.3 1.5 collective-permute-done.25
  145.1 3.1 collective-permute-start.26
  149.7 1.5 collective-permute-done.10
  151.2 4.7 collective-permute-done.11
  158.5 7.5 %collective-permute-start.12 = (f32[64,4,128]{2,1,0:T(4,128)S(1)}, f32[64,4,128]{2,1,0:T(4,128)S(1)}, u32[]{:S(2)}, u32[]{:S(2)}) collective-permute-start(f32[64,4,128]{2,1,0:T(4,128)S(1)} %get-tuple-element.64), channel_id=1, source_target_pairs={{0,2},{2,4},{4,6},{6,8},{8,10},{10,12},{12,14},{1,3},{3,5},{5,7},{... | collective-permute-start | bytes 393224 | tf_op jit(solution)/shard_map/ppermute | solution.py:20
  168.1 3.4 collective-permute-done.13
  175.4 7.4 %collective-permute-done.14 = f32[64,16,4]{2,1,0:T(8,128)S(1)} collective-permute-done((f32[64,16,4]{2,1,0:T(8,128)S(1)}, f32[64,16,4]{2,1,0:T(8,128)S(1)}, u32[]{:S(2)}, u32[]{:S(2)}) %collective-permute-start.14) | collective-permute-done | bytes 16416 | tf_op jit(solution)/shard_map/ppermute | solution.py:20
  182.9 4.7 collective-permute-done.15
  189.1 3.0 fusion.88
  192.2 200.6 %reduce-scatter.2.cloned.1.call-done = f32[4,8,128]{2,1,0:T(8,128)} async-done(((f32[64,8,128]{2,1,0:T(8,128)}), f32[4,8,128]{2,1,0:T(8,128)}) %reduce-scatter.2.cloned.1.call-update) | async-done | bytes 16400 | tf_op jit(solution)/shard_map/reduce_scatter | solution.py:120
  394.1 38.3 %all_gather.3 = f32[64,8,128]{2,1,0:T(8,128)S(1)} all-gather(f32[4,8,128]{2,1,0:T(8,128)S(1)} %get-tuple-element.3), channel_id=1, replica_groups=mesh['shot'=16,'gx'=8,'gy'=2] {'shot'}, dimensions={0}, use_global_device_ids=true | all-gather | bytes 278528 | tf_op jit(solution)/shard_map/all_gather | solution.py:123
  435.0 3.7 collective-permute-done.29
  439.0 2.5 collective-permute-start.30
  442.8 8.3 %collective-permute-done.30 = f32[64,16,4]{2,1,0:T(8,128)S(1)} collective-permute-done((f32[64,16,4]{2,1,0:T(8,128)S(1)}, f32[64,16,4]{2,1,0:T(8,128)S(1)}, u32[]{:S(2)}, u32[]{:S(2)}) %collective-permute-start.30) | collective-permute-done | bytes 16416 | tf_op jit(solution)/shard_map/ppermute | solution.py:20
  451.1 4.7 collective-permute-done.31
  458.5 4.1 collective-permute-start.32
  463.9 4.6 collective-permute-done.33
  471.8 8.0 %collective-permute-done.34 = f32[64,16,4]{2,1,0:T(8,128)S(1)} collective-permute-done((f32[64,16,4]{2,1,0:T(8,128)S(1)}, f32[64,16,4]{2,1,0:T(8,128)S(1)}, u32[]{:S(2)}, u32[]{:S(2)}) %collective-permute-start.34) | collective-permute-done | bytes 16416 | tf_op jit(solution)/shard_map/ppermute | solution.py:20
  479.8 4.7 collective-permute-done.35
  487.2 4.2 collective-permute-start.36
  492.7 4.2 collective-permute-done.37
  500.8 11.8 %gather_fusion = f32[2048]{0:T(1024)S(1)} fusion(f32[65536]{0:T(1024)S(1)} %bitcast.60, s32[2048]{0:T(1024)S(1)} %broadcast_clamp_fusion), kind=kCustom, calls=%fused_computation | custom fusion | bytes 24576 | tf_op jit(solution)/shard_map/gather | solution.py:110
  512.6 11.8 %gather_fusion.1 = f32[2048]{0:T(1024)S(1)} fusion(f32[65536]{0:T(1024)S(1)} %bitcast.61, s32[2048]{0:T(1024)S(1)} %broadcast_clamp_fusion), kind=kCustom, calls=%fused_computation.1 | custom fusion | bytes 24576 | tf_op jit(solution)/shard_map/gather | solution.py:110
  524.4 11.8 %gather_fusion.2 = f32[2048]{0:T(1024)S(1)} fusion(f32[65536]{0:T(1024)S(1)} %bitcast.62, s32[2048]{0:T(1024)S(1)} %broadcast_clamp_fusion), kind=kCustom, calls=%fused_computation.2 | custom fusion | bytes 24576 | tf_op jit(solution)/shard_map/gather | solution.py:110
  538.9 11.8 %gather_fusion.3 = f32[2048]{0:T(1024)S(1)} fusion(f32[65536]{0:T(1024)S(1)} %fusion.11, s32[2048]{0:T(1024)S(1)} %broadcast_clamp_fusion), kind=kCustom, calls=%fused_computation.3 | custom fusion | bytes 24576 | tf_op jit(solution)/shard_map/gather | solution.py:110
  550.8 56.7 %psum.22 = f32[4,2048]{1,0:T(4,128)S(1)} all-reduce(f32[4,2048]{1,0:T(4,128)S(1)} %pad_maximum_fusion.40), channel_id=1, replica_groups=mesh['shot'=16,'gx'=8,'gy'=2] {'gx','gy'}, use_global_device_ids=true, to_apply=%region_7.8 | all-reduce | flops 8192 | bytes 65536 | tf_op jit(solution)/shard_map/psum | solution.py:132
  608.1 75.0 %psum.21 = f32[]{:T(128)} all-reduce(f32[]{:T(128)} %get-tuple-element.2), channel_id=1, replica_groups=mesh['shot'=16,'gx'=8,'gy'=2] {'shot','gx','gy'}, use_global_device_ids=true, to_apply=%region_6.7 | all-reduce | flops 1 | bytes 8 | tf_op jit(solution)/shard_map/psum | solution.py:122
  683.0 37.2 %psum.23 = f32[]{:T(128)} all-reduce(f32[]{:T(128)} %multiply_reduce_fusion), channel_id=1, replica_groups=mesh['shot'=16,'gx'=8,'gy'=2] {'shot'}, use_global_device_ids=true, to_apply=%region_9.10 | all-reduce | flops 1 | bytes 8 | tf_op jit(solution)/shard_map/psum | solution.py:133
  (132 shorter events, 69.0 us)
Async XLA Ops:
  7.2 18.1 %copy-start = (f32[64,8,128]{2,1,0:T(8,128)S(1)}, f32[64,8,128]{2,1,0:T(8,128)}, u32[]{:S(2)}) copy-start(f32[64,8,128]{2,1,0:T(8,128)} %param.12) | copy-start | bytes 786436
  7.2 385.6 %reduce-scatter.2.cloned.1.call-start = ((), (), s32[]{:S(2)}) async-start(), calls=%async_computation.1 | async-start | bytes 278528 | tf_op jit(solution)/shard_map/reduce_scatter | solution.py:120
  8.3 58.1 %collective-permute-start = (f32[64,4,128]{2,1,0:T(4,128)S(1)}, f32[64,4,128]{2,1,0:T(4,128)S(1)}, u32[]{:S(2)}, u32[]{:S(2)}) collective-permute-start(f32[64,4,128]{2,1,0:T(4,128)S(1)} %get-tuple-element.76), channel_id=1, source_target_pairs={{0,2},{2,4},{4,6},{6,8},{8,10},{10,12},{12,14},{1,3},{3,5},{5,7},{... | collective-permute-start | bytes 393224 | tf_op jit(solution)/shard_map/ppermute | solution.py:20
  10.1 56.4 %collective-permute-start.1 = (f32[64,4,128]{2,1,0:T(4,128)S(1)}, f32[64,4,128]{2,1,0:T(4,128)S(1)}, u32[]{:S(2)}, u32[]{:S(2)}) collective-permute-start(f32[64,4,128]{2,1,0:T(4,128)S(1)} %get-tuple-element.77), channel_id=1, source_target_pairs={{2,0},{4,2},{6,4},{8,6},{10,8},{12,10},{14,12},{3,1},{5,3},{7,5},{... | collective-permute-start | bytes 393224 | tf_op jit(solution)/shard_map/ppermute | solution.py:22
  13.9 52.5 %copy-start.1 = (f32[1,64,8,128]{3,2,1,0:T(8,128)S(1)}, f32[1,64,8,128]{3,2,1,0:T(8,128)}, u32[]{:S(2)}) copy-start(f32[1,64,8,128]{3,2,1,0:T(8,128)} %param.11) | copy-start | bytes 786436
  25.3 46.1 %collective-permute-start.16 = (f32[64,4,128]{2,1,0:T(4,128)S(1)}, f32[64,4,128]{2,1,0:T(4,128)S(1)}, u32[]{:S(2)}, u32[]{:S(2)}) collective-permute-start(f32[64,4,128]{2,1,0:T(4,128)S(1)} %get-tuple-element.74), channel_id=1, source_target_pairs={{0,2},{2,4},{4,6},{6,8},{8,10},{10,12},{12,14},{1,3},{3,5},{5,7},{... | collective-permute-start | bytes 393224 | tf_op jit(solution)/shard_map/ppermute | solution.py:20
  29.8 41.8 %collective-permute-start.17 = (f32[64,4,128]{2,1,0:T(4,128)S(1)}, f32[64,4,128]{2,1,0:T(4,128)S(1)}, u32[]{:S(2)}, u32[]{:S(2)}) collective-permute-start(f32[64,4,128]{2,1,0:T(4,128)S(1)} %get-tuple-element.75), channel_id=1, source_target_pairs={{2,0},{4,2},{6,4},{8,6},{10,8},{12,10},{14,12},{3,1},{5,3},{7,5},{... | collective-permute-start | bytes 393224 | tf_op jit(solution)/shard_map/ppermute | solution.py:22
  66.8 14.3 %collective-permute-start.2 = (f32[64,16,4]{2,1,0:T(8,128)S(1)}, f32[64,16,4]{2,1,0:T(8,128)S(1)}, u32[]{:S(2)}, u32[]{:S(2)}) collective-permute-start(f32[64,16,4]{2,1,0:T(8,128)S(1)} %get-tuple-element.57), channel_id=1, source_target_pairs={{0,1},{2,3},{4,5},{6,7},{8,9},{10,11},{12,13},{14,15},{16,17},{18,... | collective-permute-start | bytes 49160 | tf_op jit(solution)/shard_map/ppermute | solution.py:20
  70.2 15.6 %collective-permute-start.3 = (f32[64,16,4]{2,1,0:T(8,128)S(1)}, f32[64,16,4]{2,1,0:T(8,128)S(1)}, u32[]{:S(2)}, u32[]{:S(2)}) collective-permute-start(f32[64,16,4]{2,1,0:T(8,128)S(1)} %get-tuple-element.56), channel_id=1, source_target_pairs={{1,0},{3,2},{5,4},{7,6},{9,8},{11,10},{13,12},{15,14},{17,16},{19,... | collective-permute-start | bytes 49160 | tf_op jit(solution)/shard_map/ppermute | solution.py:22
  71.8 22.8 %collective-permute-start.18 = (f32[64,16,4]{2,1,0:T(8,128)S(1)}, f32[64,16,4]{2,1,0:T(8,128)S(1)}, u32[]{:S(2)}, u32[]{:S(2)}) collective-permute-start(f32[64,16,4]{2,1,0:T(8,128)S(1)} %get-tuple-element.53), channel_id=1, source_target_pairs={{0,1},{2,3},{4,5},{6,7},{8,9},{10,11},{12,13},{14,15},{16,17},{18,... | collective-permute-start | bytes 49160 | tf_op jit(solution)/shard_map/ppermute | solution.py:20
  76.4 20.6 %collective-permute-start.19 = (f32[64,16,4]{2,1,0:T(8,128)S(1)}, f32[64,16,4]{2,1,0:T(8,128)S(1)}, u32[]{:S(2)}, u32[]{:S(2)}) collective-permute-start(f32[64,16,4]{2,1,0:T(8,128)S(1)} %get-tuple-element.52), channel_id=1, source_target_pairs={{1,0},{3,2},{5,4},{7,6},{9,8},{11,10},{13,12},{15,14},{17,16},{19,... | collective-permute-start | bytes 49160 | tf_op jit(solution)/shard_map/ppermute | solution.py:22
  86.5 1.0 copy-start.2
  88.6 15.5 %collective-permute-start.4 = (f32[64,4,128]{2,1,0:T(4,128)S(1)}, f32[64,4,128]{2,1,0:T(4,128)S(1)}, u32[]{:S(2)}, u32[]{:S(2)}) collective-permute-start(f32[64,4,128]{2,1,0:T(4,128)S(1)} %get-tuple-element.68), channel_id=1, source_target_pairs={{0,2},{2,4},{4,6},{6,8},{8,10},{10,12},{12,14},{1,3},{3,5},{5,7},{... | collective-permute-start | bytes 393224 | tf_op jit(solution)/shard_map/ppermute | solution.py:20
  92.9 11.2 %collective-permute-start.5 = (f32[64,4,128]{2,1,0:T(4,128)S(1)}, f32[64,4,128]{2,1,0:T(4,128)S(1)}, u32[]{:S(2)}, u32[]{:S(2)}) collective-permute-start(f32[64,4,128]{2,1,0:T(4,128)S(1)} %get-tuple-element.69), channel_id=1, source_target_pairs={{2,0},{4,2},{6,4},{8,6},{10,8},{12,10},{14,12},{3,1},{5,3},{7,5},{... | collective-permute-start | bytes 393224 | tf_op jit(solution)/shard_map/ppermute | solution.py:22
  99.7 7.6 %collective-permute-start.20 = (f32[64,4,128]{2,1,0:T(4,128)S(1)}, f32[64,4,128]{2,1,0:T(4,128)S(1)}, u32[]{:S(2)}, u32[]{:S(2)}) collective-permute-start(f32[64,4,128]{2,1,0:T(4,128)S(1)} %get-tuple-element.72), channel_id=1, source_target_pairs={{0,2},{2,4},{4,6},{6,8},{8,10},{10,12},{12,14},{1,3},{3,5},{5,7},{... | collective-permute-start | bytes 393224 | tf_op jit(solution)/shard_map/ppermute | solution.py:20
  102.8 5.5 collective-permute-start.21
  104.4 11.3 %collective-permute-start.6 = (f32[64,16,4]{2,1,0:T(8,128)S(1)}, f32[64,16,4]{2,1,0:T(8,128)S(1)}, u32[]{:S(2)}, u32[]{:S(2)}) collective-permute-start(f32[64,16,4]{2,1,0:T(8,128)S(1)} %get-tuple-element.41), channel_id=1, source_target_pairs={{0,1},{2,3},{4,5},{6,7},{8,9},{10,11},{12,13},{14,15},{16,17},{18,... | collective-permute-start | bytes 49160 | tf_op jit(solution)/shard_map/ppermute | solution.py:20
  105.9 14.4 %collective-permute-start.7 = (f32[64,16,4]{2,1,0:T(8,128)S(1)}, f32[64,16,4]{2,1,0:T(8,128)S(1)}, u32[]{:S(2)}, u32[]{:S(2)}) collective-permute-start(f32[64,16,4]{2,1,0:T(8,128)S(1)} %get-tuple-element.40), channel_id=1, source_target_pairs={{1,0},{3,2},{5,4},{7,6},{9,8},{11,10},{13,12},{15,14},{17,16},{19,... | collective-permute-start | bytes 49160 | tf_op jit(solution)/shard_map/ppermute | solution.py:22
  108.5 22.3 %collective-permute-start.22 = (f32[64,16,4]{2,1,0:T(8,128)S(1)}, f32[64,16,4]{2,1,0:T(8,128)S(1)}, u32[]{:S(2)}, u32[]{:S(2)}) collective-permute-start(f32[64,16,4]{2,1,0:T(8,128)S(1)} %get-tuple-element.49), channel_id=1, source_target_pairs={{0,1},{2,3},{4,5},{6,7},{8,9},{10,11},{12,13},{14,15},{16,17},{18,... | collective-permute-start | bytes 49160 | tf_op jit(solution)/shard_map/ppermute | solution.py:20
  112.2 19.4 %collective-permute-start.23 = (f32[64,16,4]{2,1,0:T(8,128)S(1)}, f32[64,16,4]{2,1,0:T(8,128)S(1)}, u32[]{:S(2)}, u32[]{:S(2)}) collective-permute-start(f32[64,16,4]{2,1,0:T(8,128)S(1)} %get-tuple-element.48), channel_id=1, source_target_pairs={{1,0},{3,2},{5,4},{7,6},{9,8},{11,10},{13,12},{15,14},{17,16},{19,... | collective-permute-start | bytes 49160 | tf_op jit(solution)/shard_map/ppermute | solution.py:22
  123.0 17.1 %collective-permute-start.8 = (f32[64,4,128]{2,1,0:T(4,128)S(1)}, f32[64,4,128]{2,1,0:T(4,128)S(1)}, u32[]{:S(2)}, u32[]{:S(2)}) collective-permute-start(f32[64,4,128]{2,1,0:T(4,128)S(1)} %get-tuple-element.66), channel_id=1, source_target_pairs={{0,2},{2,4},{4,6},{6,8},{8,10},{10,12},{12,14},{1,3},{3,5},{5,7},{... | collective-permute-start | bytes 393224 | tf_op jit(solution)/shard_map/ppermute | solution.py:20
  129.6 10.6 %collective-permute-start.9 = (f32[64,4,128]{2,1,0:T(4,128)S(1)}, f32[64,4,128]{2,1,0:T(4,128)S(1)}, u32[]{:S(2)}, u32[]{:S(2)}) collective-permute-start(f32[64,4,128]{2,1,0:T(4,128)S(1)} %get-tuple-element.67), channel_id=1, source_target_pairs={{2,0},{4,2},{6,4},{8,6},{10,8},{12,10},{14,12},{3,1},{5,3},{7,5},{... | collective-permute-start | bytes 393224 | tf_op jit(solution)/shard_map/ppermute | solution.py:22
  134.3 9.0 %collective-permute-start.24 = (f32[64,4,128]{2,1,0:T(4,128)S(1)}, f32[64,4,128]{2,1,0:T(4,128)S(1)}, u32[]{:S(2)}, u32[]{:S(2)}) collective-permute-start(f32[64,4,128]{2,1,0:T(4,128)S(1)} %get-tuple-element.71), channel_id=1, source_target_pairs={{0,2},{2,4},{4,6},{6,8},{8,10},{10,12},{12,14},{1,3},{3,5},{5,7},{... | collective-permute-start | bytes 393224 | tf_op jit(solution)/shard_map/ppermute | solution.py:20
  138.8 5.9 collective-permute-start.25
  140.5 10.7 %collective-permute-start.10 = (f32[64,16,4]{2,1,0:T(8,128)S(1)}, f32[64,16,4]{2,1,0:T(8,128)S(1)}, u32[]{:S(2)}, u32[]{:S(2)}) collective-permute-start(f32[64,16,4]{2,1,0:T(8,128)S(1)} %get-tuple-element.37), channel_id=1, source_target_pairs={{0,1},{2,3},{4,5},{6,7},{8,9},{10,11},{12,13},{14,15},{16,17},{18,... | collective-permute-start | bytes 49160 | tf_op jit(solution)/shard_map/ppermute | solution.py:20
  141.9 13.9 %collective-permute-start.11 = (f32[64,16,4]{2,1,0:T(8,128)S(1)}, f32[64,16,4]{2,1,0:T(8,128)S(1)}, u32[]{:S(2)}, u32[]{:S(2)}) collective-permute-start(f32[64,16,4]{2,1,0:T(8,128)S(1)} %get-tuple-element.36), channel_id=1, source_target_pairs={{1,0},{3,2},{5,4},{7,6},{9,8},{11,10},{13,12},{15,14},{17,16},{19,... | collective-permute-start | bytes 49160 | tf_op jit(solution)/shard_map/ppermute | solution.py:22
  145.1 22.3 %collective-permute-start.26 = (f32[64,16,4]{2,1,0:T(8,128)S(1)}, f32[64,16,4]{2,1,0:T(8,128)S(1)}, u32[]{:S(2)}, u32[]{:S(2)}) collective-permute-start(f32[64,16,4]{2,1,0:T(8,128)S(1)} %get-tuple-element.45), channel_id=1, source_target_pairs={{0,1},{2,3},{4,5},{6,7},{8,9},{10,11},{12,13},{14,15},{16,17},{18,... | collective-permute-start | bytes 49160 | tf_op jit(solution)/shard_map/ppermute | solution.py:20
  148.2 19.2 %collective-permute-start.27 = (f32[64,16,4]{2,1,0:T(8,128)S(1)}, f32[64,16,4]{2,1,0:T(8,128)S(1)}, u32[]{:S(2)}, u32[]{:S(2)}) collective-permute-start(f32[64,16,4]{2,1,0:T(8,128)S(1)} %get-tuple-element.44), channel_id=1, source_target_pairs={{1,0},{3,2},{5,4},{7,6},{9,8},{11,10},{13,12},{15,14},{17,16},{19,... | collective-permute-start | bytes 49160 | tf_op jit(solution)/shard_map/ppermute | solution.py:22
  158.5 9.6 %collective-permute-start.12 = (f32[64,4,128]{2,1,0:T(4,128)S(1)}, f32[64,4,128]{2,1,0:T(4,128)S(1)}, u32[]{:S(2)}, u32[]{:S(2)}) collective-permute-start(f32[64,4,128]{2,1,0:T(4,128)S(1)} %get-tuple-element.64), channel_id=1, source_target_pairs={{0,2},{2,4},{4,6},{6,8},{8,10},{10,12},{12,14},{1,3},{3,5},{5,7},{... | collective-permute-start | bytes 393224 | tf_op jit(solution)/shard_map/ppermute | solution.py:20
  166.1 5.5 collective-permute-start.13
  171.9 11.0 %collective-permute-start.14 = (f32[64,16,4]{2,1,0:T(8,128)S(1)}, f32[64,16,4]{2,1,0:T(8,128)S(1)}, u32[]{:S(2)}, u32[]{:S(2)}) collective-permute-start(f32[64,16,4]{2,1,0:T(8,128)S(1)} %get-tuple-element.33), channel_id=1, source_target_pairs={{0,1},{2,3},{4,5},{6,7},{8,9},{10,11},{12,13},{14,15},{16,17},{18,... | collective-permute-start | bytes 49160 | tf_op jit(solution)/shard_map/ppermute | solution.py:20
  173.4 14.2 %collective-permute-start.15 = (f32[64,16,4]{2,1,0:T(8,128)S(1)}, f32[64,16,4]{2,1,0:T(8,128)S(1)}, u32[]{:S(2)}, u32[]{:S(2)}) collective-permute-start(f32[64,16,4]{2,1,0:T(8,128)S(1)} %get-tuple-element.32), channel_id=1, source_target_pairs={{1,0},{3,2},{5,4},{7,6},{9,8},{11,10},{13,12},{15,14},{17,16},{19,... | collective-permute-start | bytes 49160 | tf_op jit(solution)/shard_map/ppermute | solution.py:22
  189.1 203.7 %copy-start.4 = (f32[4,8,128]{2,1,0:T(8,128)S(1)}, f32[4,8,128]{2,1,0:T(8,128)}, u32[]{:S(2)}) copy-start(f32[4,8,128]{2,1,0:T(8,128)} %param.13) | copy-start | bytes 49156
  432.4 2.6 collective-permute-start.28
  433.7 5.0 collective-permute-start.29
  439.0 12.1 %collective-permute-start.30 = (f32[64,16,4]{2,1,0:T(8,128)S(1)}, f32[64,16,4]{2,1,0:T(8,128)S(1)}, u32[]{:S(2)}, u32[]{:S(2)}) collective-permute-start(f32[64,16,4]{2,1,0:T(8,128)S(1)} %get-tuple-element.29), channel_id=1, source_target_pairs={{0,1},{2,3},{4,5},{6,7},{8,9},{10,11},{12,13},{14,15},{16,17},{18,... | collective-permute-start | bytes 49160 | tf_op jit(solution)/shard_map/ppermute | solution.py:20
  441.5 14.3 %collective-permute-start.31 = (f32[64,16,4]{2,1,0:T(8,128)S(1)}, f32[64,16,4]{2,1,0:T(8,128)S(1)}, u32[]{:S(2)}, u32[]{:S(2)}) collective-permute-start(f32[64,16,4]{2,1,0:T(8,128)S(1)} %get-tuple-element.28), channel_id=1, source_target_pairs={{1,0},{3,2},{5,4},{7,6},{9,8},{11,10},{13,12},{15,14},{17,16},{19,... | collective-permute-start | bytes 49160 | tf_op jit(solution)/shard_map/ppermute | solution.py:22
  458.5 5.4 collective-permute-start.32
  462.6 5.9 collective-permute-start.33
  468.8 11.0 %collective-permute-start.34 = (f32[64,16,4]{2,1,0:T(8,128)S(1)}, f32[64,16,4]{2,1,0:T(8,128)S(1)}, u32[]{:S(2)}, u32[]{:S(2)}) collective-permute-start(f32[64,16,4]{2,1,0:T(8,128)S(1)} %get-tuple-element.25), channel_id=1, source_target_pairs={{0,1},{2,3},{4,5},{6,7},{8,9},{10,11},{12,13},{14,15},{16,17},{18,... | collective-permute-start | bytes 49160 | tf_op jit(solution)/shard_map/ppermute | solution.py:20
  470.3 14.2 %collective-permute-start.35 = (f32[64,16,4]{2,1,0:T(8,128)S(1)}, f32[64,16,4]{2,1,0:T(8,128)S(1)}, u32[]{:S(2)}, u32[]{:S(2)}) collective-permute-start(f32[64,16,4]{2,1,0:T(8,128)S(1)} %get-tuple-element.24), channel_id=1, source_target_pairs={{1,0},{3,2},{5,4},{7,6},{9,8},{11,10},{13,12},{15,14},{17,16},{19,... | collective-permute-start | bytes 49160 | tf_op jit(solution)/shard_map/ppermute | solution.py:22
  487.2 5.5 collective-permute-start.36
  491.4 5.5 collective-permute-start.37
  498.1 38.2 %collective-permute-start.38 = (f32[64,16,4]{2,1,0:T(8,128)}, f32[64,16,4]{2,1,0:T(8,128)S(1)}, u32[]{:S(2)}, u32[]{:S(2)}) collective-permute-start(f32[64,16,4]{2,1,0:T(8,128)} %get-tuple-element.21), channel_id=1, source_target_pairs={{0,1},{2,3},{4,5},{6,7},{8,9},{10,11},{12,13},{14,15},{16,17},{18,... | collective-permute-start | bytes 49160 | tf_op jit(solution)/shard_map/ppermute | solution.py:20
  499.5 36.7 %collective-permute-start.39 = (f32[64,16,4]{2,1,0:T(8,128)S(1)}, f32[64,16,4]{2,1,0:T(8,128)S(1)}, u32[]{:S(2)}, u32[]{:S(2)}) collective-permute-start(f32[64,16,4]{2,1,0:T(8,128)S(1)} %get-tuple-element.20), channel_id=1, source_target_pairs={{1,0},{3,2},{5,4},{7,6},{9,8},{11,10},{13,12},{15,14},{17,16},{19,... | collective-permute-start | bytes 49160 | tf_op jit(solution)/shard_map/ppermute | solution.py:22
  538.9 182.7 %copy-start.3 = (f32[1,4,2048]{2,1,0:T(4,128)S(1)}, f32[1,4,2048]{2,1,0:T(4,128)}, u32[]{:S(2)}) copy-start(f32[1,4,2048]{2,1,0:T(4,128)} %param.14) | copy-start | bytes 98308
Sparse Core Ops, SparseCore 0:
  192.3 200.4 reduce-scatter.1
where the time goes:
time: 741 us; the launch traced here: 730 us
  waiting for transfers between devices  281 us (38%)
  blocking collectives  207 us (28%)
  starting transfers between devices  93.1 us (13%)
  other arithmetic  77.9 us (11%)
  local copies, waits for them, and re-layouts  52.6 us (7%)
  between operations  17.9 us (2%)
    reduce_scatter x1, waiting for transfers between devices, on_device(): lax.psum_scatter(window_mask * grad, 'shot', scatter_dimension=0, tiled=T...  201 us
    psum x1, blocking collectives, on_device(): descent_dot = lax.psum(jnp.sum(owned * scaled), ('shot', 'gx', 'gy'))  75 us
    ppermute x20, starting transfers between devices, padded_2(): lax.ppermute(tail, axis, [(i, (i + 1) % count) for i in range(ends)])  66.4 us
    psum x1, blocking collectives, on_device(): predicted = lax.psum(jnp.stack(samples), ('gx', 'gy'))  56.7 us
    ppermute x20, waiting for transfers between devices, padded_2(): lax.ppermute(head, axis, [((i + 1) % count, i) for i in range(ends)])  49.8 us
    gather x4, local copies, waits for them, and re-layouts, sample(): return jnp.where(present, field.reshape(-1)[flat_index], 0.0)  47.1 us
    scatter-add x4, other arithmetic, inject(): spread = jnp.zeros((cell_count,), jnp.float32).at[flat_index].add(jnp.whe...  45.3 us
    all_gather x1, blocking collectives, on_device(): scaled_full = lax.all_gather(scaled, 'shot', axis=0, tiled=True)  38.3 us
  transfers between devices with their start and end apart: 41, of which 21 were waited for; matrix products, arithmetic and copies ran while one was open for 14% of the time, Pallas kernels for 0%

commit v1 on v0

v1 whole, which is shorter than its diff:
```python
import jax
import jax.numpy as jnp
from jax import lax
from jax.experimental import pallas as pl
from jax.experimental.pallas import tpu as pltpu
from jax.sharding import PartitionSpec as P

STEPS = 4
NZ, BX, BY = 64, 8, 128
NREC = 2048
F32, BF16, I32 = jnp.float32, jnp.bfloat16, jnp.int32
weights = (-205.0 / 72.0, 8.0 / 5.0, -1.0 / 5.0, 8.0 / 315.0, -1.0 / 560.0)


def call(kernel, outs, scratch=(), limit=24, flops=10_000_000):
    def run(*args, smem=0):
        specs = [
            pl.BlockSpec(memory_space=pltpu.SMEM if i < smem else pltpu.VMEM)
            for i in range(len(args))
        ]
        return pl.pallas_call(
            kernel,
            out_shape=[jax.ShapeDtypeStruct(s, d) for s, d in outs],
            in_specs=specs,
            out_specs=[pl.BlockSpec(memory_space=pltpu.VMEM) for _ in outs],
            scratch_shapes=list(scratch),
            compiler_params=pltpu.CompilerParams(vmem_limit_bytes=limit * 1024 * 1024),
            cost_estimate=pl.CostEstimate(
                flops=flops, bytes_accessed=2_000_000, transcendentals=0
            ),
        )(*args)

    return run


def lanes(rows):
    return lax.broadcasted_iota(I32, (rows, BY), 1)


def near_edge(gy, lane):
    return ((gy == 0) & (lane >= BY - 4)) | ((gy == 1) & (lane < 4))


def far_edge(gy, lane):
    return ((gy == 0) & (lane < 4)) | ((gy == 1) & (lane >= BY - 4))


def send_edges(load, outer_ref, inner_ref, strip_ref, slot, scal):
    core, gy = scal[0], scal[1]
    keep = near_edge(gy, lanes(8))
    for i in range(4):
        outer_ref[slot, i] = load(4 * core + i)
        inner_ref[slot, i] = load(4 * (1 - core) + i)
    for half in range(2):
        packed = jnp.zeros((8, BY), F32)
        for j in range(32):
            index = half * 32 + j
            plane = load(index // 8)[8 * (index % 8) : 8 * (index % 8) + 8]
            packed = packed + pltpu.roll(jnp.where(keep, plane, 0.0), 4 * j, 1)
        strip_ref[slot, 8 * half : 8 * half + 8] = packed


def fill(padded, side, load, outer_ref, inner_ref, strip_ref, slot, scal):
    core, gy = scal[0], scal[1]
    keep = far_edge(gy, lanes(8))
    zero = jnp.zeros((8, BY), F32)
    for x in range(BX):
        padded[4 + x, 0:8] = zero
        padded[4 + x, 72:80] = zero
        padded[4 + x, 8:72] = load(x)
    for i in range(4):
        padded[12 * core + i, 8:72] = outer_ref[slot, i]
        padded[12 * (1 - core) + i, 8:72] = inner_ref[slot, i]
    for half in range(2):
        packed = strip_ref[slot, 8 * half : 8 * half + 8]
        for j in range(32):
            index = half * 32 + j
            turned = pltpu.roll(packed, (BY - 4 * j) % BY, 1)
            side[index // 8, 8 * (index % 8) : 8 * (index % 8) + 8] = jnp.where(keep, turned, 0.0)


def lap(padded, side, x):
    lane = lanes(NZ)
    centre = padded[4 + x, 8:72]
    other = side[x]
    result = (3.0 * weights[0]) * centre
    for k in range(1, 5):
        along_z = padded[4 + x, 8 + k : 72 + k] + padded[4 + x, 8 - k : 72 - k]
        along_x = padded[4 + x + k, 8:72] + padded[4 + x - k, 8:72]
        right = pltpu.roll(jnp.where(lane < k, other, centre), BY - k, 1)
        left = pltpu.roll(jnp.where(lane >= BY - k, other, centre), k, 1)
        result = result + weights[k] * ((along_z + along_x) + (right + left))
    return result


FIELD = ((BX, NZ, BY), F32)
PADDED = pltpu.VMEM((16, 80, BY), F32)
SIDE = pltpu.VMEM((BX, NZ, BY), F32)


def edges(count):
    return [((count, 4, NZ, BY), F32), ((count, 4, NZ, BY), F32), ((count, 16, BY), F32)]


def first_kernel(scal, newer, older, newer_out, older_out, outer, inner, strip):
    for x in range(BX):
        newer_out[x] = newer[pl.ds(x, NZ, stride=8), :]
        older_out[x] = older[pl.ds(x, NZ, stride=8), :]
    send_edges(lambda x: newer_out[x], outer, inner, strip, 0, scal)


def two_pieces(values):
    high = values.astype(BF16)
    return high, (values - high.astype(F32)).astype(BF16)


def prepare_kernel(scal, vel, traces, rz, rx, ry, vel_out, inj, pick_cell, pick_y, spread):
    for x in range(BX):
        vel_out[x] = vel[pl.ds(x, NZ, stride=8), :]
    lat_x = rx[...] - scal[2]
    lat_y = ry[...] - scal[3]
    present = (lat_x >= 0) & (lat_x < BX) & (lat_y >= 0) & (lat_y < BY)
    row = jnp.where(present, lat_x * NZ + rz[...], -1)
    col = jnp.where(present, lat_y, -1)

    def rows(i, carry):
        number = lax.broadcasted_iota(I32, (16, NREC), 0) + 16 * i
        pick_cell[pl.ds(pl.multiple_of(16 * i, 16), 16), :] = jnp.where(number == row, 1.0, 0.0).astype(BF16)
        return carry

    lax.fori_loop(0, 32, rows, 0)
    for n in range(STEPS):
        value = traces[n : n + 1, :]
        high, low = two_pieces(value)
        high, low = high.astype(F32), low.astype(F32)

        def columns(i, carry):
            number = lax.broadcasted_iota(I32, (16, NREC), 0) + 16 * i
            hit = number == col
            at = pl.multiple_of(16 * i, 16)
            if n == 0:
                pick_y[pl.ds(at, 16), :] = jnp.where(hit, 1.0, 0.0).astype(BF16)
            spread[pl.ds(at, 16), :] = jnp.where(hit, high, 0.0).astype(BF16)
            spread[pl.ds(pl.multiple_of(BY + at, 16), 16), :] = jnp.where(hit, low, 0.0).astype(BF16)
            return carry

        lax.fori_loop(0, 8, columns, 0)
        both = lax.dot_general(
            pick_cell[...], spread[...], (((1,), (1,)), ((), ())), preferred_element_type=F32
        )
        for x in range(BX):
            part = both[NZ * x : NZ * x + NZ]
            inj[n, x] = part[:, :BY] + part[:, BY:]


def forward1_kernel(scal, newer, older, vel, inj, outer, inner, strip, acc, nxt, q, outer_o, inner_o, strip_o, padded, side):
    fill(padded, side, lambda x: newer[x], outer, inner, strip, 0, scal)
    for x in range(BX):
        a = vel[x] * lap(padded, side, x)
        acc[x] = a
        nxt[x] = (2.0 * newer[x] - older[x]) + a
        q[x] = vel[x] * inj[3, x]
    send_edges(lambda x: nxt[x], outer_o, inner_o, strip_o, 0, scal)
    send_edges(lambda x: q[x], outer_o, inner_o, strip_o, 1, scal)


def make_forward(moment):
    def kernel(scal, newer, older, vel, inj, q_in, latest, later, outer, inner, strip,
               acc, nxt, p, q, outer_o, inner_o, strip_o, padded, side):
        fill(padded, side, lambda x: newer[x], outer, inner, strip, 0, scal)
        for x in range(BX):
            a = vel[x] * lap(padded, side, x)
            acc[x] = a
            nxt[x] = (2.0 * newer[x] - older[x]) + a
        send_edges(lambda x: nxt[x], outer_o, inner_o, strip_o, 0, scal)
        fill(padded, side, lambda x: q_in[x], outer, inner, strip, 1, scal)
        for x in range(BX):
            before = 2.0 * inj[3, x] if moment == 1 else 2.0 * later[x] - latest[x]
            value = (before + lap(padded, side, x)) + inj[3 - moment, x]
            p[x] = value
            q[x] = vel[x] * value
        send_edges(lambda x: q[x], outer_o, inner_o, strip_o, 1, scal)

    return kernel


def window(scal, x):
    column = lanes(NZ) + scal[3]
    at_x = scal[2] + x
    inside_x = (at_x >= scal[4]) & (at_x < scal[4] + 48)
    return (column >= scal[5]) & (column < scal[5] + 192) & inside_x


def last_kernel(scal, newer, vel, inj, q_in, latest, later, acc0, acc1, acc2, outer, inner, strip, acc3, grad, padded, side, padded2, side2):
    fill(padded, side, lambda x: newer[x], outer, inner, strip, 0, scal)
    fill(padded2, side2, lambda x: q_in[x], outer, inner, strip, 1, scal)
    for x in range(BX):
        a = vel[x] * lap(padded, side, x)
        acc3[x] = a
        p0 = ((2.0 * later[x] - latest[x]) + lap(padded2, side2, x)) + inj[0, x]
        total = ((a * inj[3, x] + acc2[x] * latest[x]) + acc1[x] * later[x]) + acc0[x] * p0
        grad[pl.ds(x, NZ, stride=8), :] = jnp.where(window(scal, x), total, 0.0)


def gradient_kernel(parts, pre, scaled, copies, dot):
    total = parts[0:32]
    for s in range(1, 16):
        total = total + parts[32 * s : 32 * s + 32]
    value = pre[...] * total
    scaled[...] = value
    for s in range(16):
        copies[32 * s : 32 * s + 32] = value
    product = total * value
    dot[...] = (product[0:8] + product[8:16]) + (product[16:24] + product[24:32])


def born1_kernel(scal, full, acc0, source, d, outer_o, inner_o, strip_o):
    for x in range(BX):
        s = jnp.where(window(scal, x), full[pl.ds(x, NZ, stride=8), :], 0.0)
        source[x] = s
        d[x] = s * acc0[x]
    send_edges(lambda x: d[x], outer_o, inner_o, strip_o, 0, scal)


def make_born(moment, last):
    def kernel(scal, now, before, source, acc, vel, outer, inner, strip, *rest):
        if last:
            pick_cell, pick_y, s1, s2, s3, dot, payload, padded, side, d, pieces, block = rest
        else:
            d, outer_o, inner_o, strip_o, padded, side = rest
        fill(padded, side, lambda x: now[x], outer, inner, strip, 0, scal)
        for x in range(BX):
            base = 2.0 * now[x]
            if moment > 1:
                base = base - before[x]
            d[x] = (base + vel[x] * lap(padded, side, x)) + source[x] * acc[x]
        if not last:
            send_edges(lambda x: d[x], outer_o, inner_o, strip_o, 0, scal)
            return
        s4 = sampled(d, pieces, pick_cell, pick_y)
        energy = jnp.zeros((1, BY), F32)
        for n, values in enumerate((s1[...], s2[...], s3[...], s4)):
            for j in range(16):
                piece = values[:, BY * j : BY * j + BY]
                block[16 * n + j : 16 * n + j + 1, :] = piece
                energy = energy + piece * piece
        block[64:72, :] = jnp.zeros((8, BY), F32)
        block[64:65, :] = energy
        block[65:66, :] = jnp.sum(dot[...], axis=0, keepdims=True)
        for i in range(16):
            payload[i] = block[...]

    return kernel


def sampled(field, pieces, pick_cell, pick_y):
    for x in range(BX):
        high, low = two_pieces(field[x])
        pieces[NZ * x : NZ * x + NZ, :BY] = high
        pieces[NZ * x : NZ * x + NZ, BY:] = low
    at_cell = lax.dot_general(
        pieces[...], pick_cell[...], (((0,), (0,)), ((), ())), preferred_element_type=F32
    )
    chosen = (at_cell[:BY] + at_cell[BY:]) * pick_y[...].astype(F32)
    return jnp.sum(chosen, axis=0, keepdims=True)


def sample_kernel(field, pick_cell, pick_y, out, pieces):
    out[...] = sampled(field, pieces, pick_cell, pick_y)


def exchange(outer, inner, strip):
    chips = [(2 * i + 1, 2 * i + 2) for i in range(3)]
    across = chips + [(b, a) for a, b in chips]
    swap = [(i, i ^ 1) for i in range(8)]
    return (
        lax.ppermute(outer, "gx", across),
        lax.ppermute(inner, "gx", swap),
        lax.ppermute(strip, "gy", [(0, 1), (1, 0)]),
    )


def on_device(older_field, newer_field, velocity, preconditioner, traces,
              receiver_z, receiver_x, receiver_y, aperture_x, aperture_y):
    flat = (NZ * BX, BY)
    gx, gy = lax.axis_index("gx"), lax.axis_index("gy")
    scal = jnp.stack([gx % 2, gy, gx * BX, gy * BY, aperture_x[0], aperture_y[0]]).astype(I32)
    newer, older, *e = call(first_kernel, [FIELD, FIELD] + edges(1))(
        scal, newer_field.reshape(flat), older_field.reshape(flat), smem=1)
    e = exchange(*e)
    vel, inj, pick_cell, pick_y = call(
        prepare_kernel,
        [FIELD, ((4, BX, NZ, BY), F32), ((512, NREC), BF16), ((BY, NREC), BF16)],
        [pltpu.VMEM((2 * BY, NREC), BF16)], limit=40,
    )(scal, velocity.reshape(flat), traces[0], receiver_z, receiver_x, receiver_y, smem=1)
    acc0, u1, q, *e = call(forward1_kernel, [FIELD] * 3 + edges(2), [PADDED, SIDE])(
        scal, newer, older, vel, inj, *e, smem=1)
    e = exchange(*e)
    acc1, u2, p2, q, *e = call(make_forward(1), [FIELD] * 4 + edges(2), [PADDED, SIDE])(
        scal, u1, newer, vel, inj, q, q, q, *e, smem=1)
    e = exchange(*e)
    acc2, u3, p1, q, *e = call(
        make_forward_later, [FIELD] * 4 + edges(2), [PADDED, SIDE])(
        scal, u2, u1, vel, inj, q, p2, *e, smem=1)
    e = exchange(*e)
    acc3, grad = call(last_kernel, [FIELD, (flat, F32)], [PADDED, SIDE, PADDED, SIDE])(
        scal, u3, vel, inj, q, p2, p1, acc0, acc1, acc2, *e, smem=1)
    parts = lax.all_to_all(grad.reshape(16, 4, BX, BY), "shot", 0, 0, tiled=True)
    scaled, copies, dot = call(
        gradient_kernel, [((32, BY), F32), (flat, F32), ((8, BY), F32)])(
        parts.reshape(flat), preconditioner.reshape(32, BY))
    full = lax.all_to_all(copies.reshape(16, 4, BX, BY), "shot", 0, 0, tiled=True)
    source, d1, *e = call(born1_kernel, [FIELD, FIELD] + edges(1))(
        scal, full.reshape(flat), acc0, smem=1)
    e = exchange(*e)
    sample = call(sample_kernel, [((1, NREC), F32)], [pltpu.VMEM((512, 2 * BY), BF16)], flops=600_000_000)
    s1, = sample(d1, pick_cell, pick_y)
    d2, *e = call(make_born(1, False), [FIELD] + edges(1), [PADDED, SIDE])(
        scal, d1, d1, source, acc1, vel, *e, smem=1)
    e = exchange(*e)
    s2, = sample(d2, pick_cell, pick_y)
    d3, *e = call(make_born(2, False), [FIELD] + edges(1), [PADDED, SIDE])(
        scal, d2, d1, source, acc2, vel, *e, smem=1)
    e = exchange(*e)
    s3, = sample(d3, pick_cell, pick_y)
    payload, = call(
        make_born(3, True), [((16, 72, BY), F32)],
        [PADDED, SIDE, pltpu.VMEM((BX, NZ, BY), F32), pltpu.VMEM((512, 2 * BY), BF16), pltpu.VMEM((72, BY), F32)],
    )(scal, d3, d2, source, acc3, vel, *e, pick_cell, pick_y, s1, s2, s3, dot, smem=1)
    arrived = lax.all_to_all(payload, ("gx", "gy"), 0, 0, tiled=True)
    summed = jnp.sum(arrived, axis=0)
    stats = lax.all_to_all(jnp.broadcast_to(summed[None, 64:72], (16, 8, BY)), "shot", 0, 0, tiled=True)
    trace_energy = jnp.sum(stats[:, 0])
    descent_dot = jnp.sum(stats[:, 1])
    step_length = descent_dot / (trace_energy + 1e-6)
    predicted = summed[:64].reshape(4, NREC)
    return (step_length * scaled.reshape(4, BX, BY), (traces[0] - step_length * predicted)[None])


def make_forward_later(scal, newer, older, vel, inj, q_in, later, outer, inner, strip,
                       acc, nxt, p, q, outer_o, inner_o, strip_o, padded, side):
    fill(padded, side, lambda x: newer[x], outer, inner, strip, 0, scal)
    for x in range(BX):
        a = vel[x] * lap(padded, side, x)
        acc[x] = a
        nxt[x] = (2.0 * newer[x] - older[x]) + a
    send_edges(lambda x: nxt[x], outer_o, inner_o, strip_o, 0, scal)
    fill(padded, side, lambda x: q_in[x], outer, inner, strip, 1, scal)
    for x in range(BX):
        value = ((2.0 * later[x] - inj[3, x]) + lap(padded, side, x)) + inj[1, x]
        p[x] = value
        q[x] = vel[x] * value
    send_edges(lambda x: q[x], outer_o, inner_o, strip_o, 1, scal)


def solution(mesh):
    return jax.shard_map(
        on_device,
        mesh=mesh,
        in_specs=(
            P("shot", None, "gx", "gy"),
            P("shot", None, "gx", "gy"),
            P(None, "gx", "gy"),
            P("shot", "gx", "gy"),
            P("shot", None, None),
            P("shot", None),
            P("shot", None),
            P("shot", None),
            P("shot"),
            P("shot"),
        ),
        out_specs=(P("shot", "gx", "gy"), P("shot", None, None)),
        check_vma=False,
    )
```

time: 741 us -> 152 us (0.21); the launches traced: 730 us -> 150 us
  waiting for transfers between devices: 281 us -> 19.2 us
  blocking collectives: 207 us -> 66 us
  other arithmetic: 77.9 us -> 2.48 us
  starting transfers between devices: 93.1 us -> 29 us
  local copies, waits for them, and re-layouts: 52.6 us -> 5.83 us
  Pallas kernels: 0 us -> 24.4 us
  between operations: 17.9 us -> 3.45 us
    reduce_scatter x1 -> x0, waiting for transfers between devices: 201 us -> none  [on_device(): lax.psum_scatter(window_mask * grad, 'shot', scatter_dimension=0, tiled=T...]
    psum x3 -> x0, blocking collectives: 169 us -> none  [the longest x1 75 us: on_device(): descent_dot = lax.psum(jnp.sum(owned * scaled), ('shot', 'gx', 'gy'))]
    all_to_all x0 -> x4, blocking collectives: none -> 66 us  [the longest x1 22.5 us: on_device(): lax.all_to_all(grad.reshape(16, 4, BX, BY), 'shot', 0, 0, tiled=True)]
    ppermute x40 -> x21, starting transfers between devices: 93.1 us -> 29 us  [the longest x7 20.4 us: exchange(): lax.ppermute(inner, 'gx', swap)]
    ppermute x40 -> x21, waiting for transfers between devices: 80.6 us -> 19.2 us  [the longest x7 19.1 us: exchange(): lax.ppermute(strip, 'gy', [(0, 1), (1, 0)])]
    gather x4 -> x0, local copies, waits for them, and re-layouts: 47.1 us -> none  [sample(): return jnp.where(present, field.reshape(-1)[flat_index], 0.0)]
    scatter-add x4 -> x0, other arithmetic: 45.3 us -> none  [inject(): spread = jnp.zeros((cell_count,), jnp.float32).at[flat_index].add(jnp.whe...]
    all_gather x1 -> x0, blocking collectives: 38.3 us -> none  [on_device(): scaled_full = lax.all_gather(scaled, 'shot', axis=0, tiled=True)]
  transfers between devices with their start and end apart: 41 -> 21, of which waited for: 21 -> 6; matrix products, arithmetic and copies ran while one was open for 14% -> 0% of each run, Pallas kernels for 0% -> 6%
where the time goes in v1:
time: 152 us; the launch traced here: 150 us
  blocking collectives  66 us (43%)
  starting transfers between devices  29 us (19%)
  Pallas kernels  24.4 us (16%)
  waiting for transfers between devices  19.2 us (13%)
  local copies, waits for them, and re-layouts  5.83 us (4%)
  between operations  3.45 us (2%)
  other arithmetic  2.48 us (2%)
    pallas_call x14, Pallas kernels, run(): pl.pallas_call(kernel, out_shape=[jax.ShapeDtypeStruct(s, d) for s, d in...  24.4 us
    all_to_all x1, blocking collectives, on_device(): lax.all_to_all(grad.reshape(16, 4, BX, BY), 'shot', 0, 0, tiled=True)  22.5 us
    ppermute x7, starting transfers between devices, exchange(): lax.ppermute(inner, 'gx', swap)  20.4 us
    ppermute x7, waiting for transfers between devices, exchange(): lax.ppermute(strip, 'gy', [(0, 1), (1, 0)])  19.1 us
    all_to_all x1, blocking collectives, on_device(): lax.all_to_all(copies.reshape(16, 4, BX, BY), 'shot', 0, 0, tiled=True)  15.8 us
    all_to_all x1, blocking collectives, on_device(): arrived = lax.all_to_all(payload, ('gx', 'gy'), 0, 0, tiled=True)  14.2 us
    all_to_all x1, blocking collectives, on_device(): lax.all_to_all(jnp.broadcast_to(summed[None, 64:72], (16, 8, BY)), 'shot'...  13.5 us
    unnamed x18, local copies, waits for them, and re-layouts  5.71 us
  transfers between devices with their start and end apart: 21, of which 6 were waited for; matrix products, arithmetic and copies ran while one was open for 0% of the time, Pallas kernels for 6%

profile of v1, /device:TPU:32, one launch (start us, length us, event | category | flops | bytes accessed | tf_op | source)
XLA Modules:
  0.0 150.2 jit_solution(6697129128405345990)
XLA Ops:
  2.0 1.0 copy-done
  3.0 0.9 copy-done.1
  3.9 0.7 shard_map.113
  4.6 0.7 collective-permute-start
  5.3 3.0 %collective-permute-start.1 = (f32[1,4,64,128]{3,2,1,0:T(8,128)S(1)}, f32[1,4,64,128]{3,2,1,0:T(8,128)S(1)}, u32[]{:S(2)}, u32[]{:S(2)}) collective-permute-start(f32[1,4,64,128]{3,2,1,0:T(8,128)S(1)} %get-tuple-element.54), channel_id=1, source_target_pairs={{0,2},{2,0},{4,6},{6,4},{8,10},{10,8},{12,14},{14,12},{1,3},{3,1},... | collective-permute-start | bytes 393224 | tf_op jit(solution)/shard_map/ppermute | solution.py:278
  8.3 1.5 collective-permute-start.2
  9.8 0.9 copy-done.2
  10.8 0.8 copy-done.3
  11.5 0.7 copy-done.6
  12.2 0.7 copy-done.7
  12.9 0.7 copy-done.8
  13.6 7.3 %shard_map.114 = (f32[8,64,128]{2,1,0:T(8,128)S(1)}, f32[4,8,64,128]{3,2,1,0:T(8,128)S(1)}, bf16[512,2048]{1,0:T(8,128)(2,1)S(1)}, bf16[128,2048]{1,0:T(8,128)(2,1)S(1)}) custom-call(s32[6]{0:T(128)S(1)} %stack.19.scal, f32[512,128]{1,0:T(8,128)S(1)} %bitcast.21, f32[4,2048]{1,0:T(4,128)S(1)} %bitcast.24, s32[1,2048]{1,0:T(1,128)S(1)} %copy-done.6, ...), custom_call_target="tpu_custom_call" | custom-call | flops 10000000 | bytes 2000000 | tf_op jit(solution)/shard_map/pallas_call | solution.py:21
  20.9 1.5 %shard_map.115 = (f32[8,64,128]{2,1,0:T(8,128)S(1)}, f32[8,64,128]{2,1,0:T(8,128)S(1)}, f32[8,64,128]{2,1,0:T(8,128)S(1)}, f32[2,4,64,128]{3,2,1,0:T(8,128)S(1)}...) custom-call(s32[6]{0:T(128)S(1)} %stack.19.scal, f32[8,64,128]{2,1,0:T(8,128)S(1)} %get-tuple-element.49.newer.older, ...), custom_call_target="tpu_custom_call" | custom-call | flops 10000000 | bytes 2000000 | tf_op jit(solution)/shard_map/pallas_call | solution.py:21
  22.4 0.7 collective-permute-start.3
  23.1 3.0 %collective-permute-start.4 = (f32[2,4,64,128]{3,2,1,0:T(8,128)S(1)}, f32[2,4,64,128]{3,2,1,0:T(8,128)S(1)}, u32[]{:S(2)}, u32[]{:S(2)}) collective-permute-start(f32[2,4,64,128]{3,2,1,0:T(8,128)S(1)} %get-tuple-element.59), channel_id=1, source_target_pairs={{0,2},{2,0},{4,6},{6,4},{8,10},{10,8},{12,14},{14,12},{1,3},{3,1},... | collective-permute-start | bytes 786440 | tf_op jit(solution)/shard_map/ppermute | solution.py:278
  26.7 3.2 %collective-permute-done.5.strip = f32[2,16,128]{2,1,0:T(8,128)S(1)} collective-permute-done((f32[2,16,128]{2,1,0:T(8,128)S(1)}, f32[2,16,128]{2,1,0:T(8,128)S(1)}, u32[]{:S(2)}, u32[]{:S(2)}) %collective-permute-start.5) | collective-permute-done | bytes 16416 | tf_op jit(solution)/shard_map/ppermute | solution.py:279
  29.9 2.2 %shard_map.116 = (f32[8,64,128]{2,1,0:T(8,128)S(1)}, f32[8,64,128]{2,1,0:T(8,128)S(1)}, f32[8,64,128]{2,1,0:T(8,128)S(1)}, f32[8,64,128]{2,1,0:T(8,128)S(1)}, f3...) custom-call(s32[6]{0:T(128)S(1)} %stack.19.scal, ...), custom_call_target="tpu_custom_call" | custom-call | flops 10000000 | bytes 2000000 | tf_op jit(solution)/shard_map/pallas_call | solution.py:21
  32.1 0.7 collective-permute-start.6
  32.8 3.3 %collective-permute-start.7 = (f32[2,4,64,128]{3,2,1,0:T(8,128)S(1)}, f32[2,4,64,128]{3,2,1,0:T(8,128)S(1)}, u32[]{:S(2)}, u32[]{:S(2)}) collective-permute-start(f32[2,4,64,128]{3,2,1,0:T(8,128)S(1)} %get-tuple-element.65), channel_id=1, source_target_pairs={{0,2},{2,0},{4,6},{6,4},{8,10},{10,8},{12,14},{14,12},{1,3},{3,1},... | collective-permute-start | bytes 786440 | tf_op jit(solution)/shard_map/ppermute | solution.py:278
  36.6 3.2 %collective-permute-done.8.strip = f32[2,16,128]{2,1,0:T(8,128)S(1)} collective-permute-done((f32[2,16,128]{2,1,0:T(8,128)S(1)}, f32[2,16,128]{2,1,0:T(8,128)S(1)}, u32[]{:S(2)}, u32[]{:S(2)}) %collective-permute-start.8) | collective-permute-done | bytes 16416 | tf_op jit(solution)/shard_map/ppermute | solution.py:279
  39.8 2.3 %shard_map.117 = (f32[8,64,128]{2,1,0:T(8,128)S(1)}, f32[8,64,128]{2,1,0:T(8,128)S(1)}, f32[8,64,128]{2,1,0:T(8,128)S(1)}, f32[8,64,128]{2,1,0:T(8,128)S(1)}, f3...) custom-call(s32[6]{0:T(128)S(1)} %stack.19.scal, ...), custom_call_target="tpu_custom_call" | custom-call | flops 10000000 | bytes 2000000 | tf_op jit(solution)/shard_map/pallas_call | solution.py:21
  42.1 0.7 collective-permute-start.9
  42.8 3.3 %collective-permute-start.10 = (f32[2,4,64,128]{3,2,1,0:T(8,128)S(1)}, f32[2,4,64,128]{3,2,1,0:T(8,128)S(1)}, u32[]{:S(2)}, u32[]{:S(2)}) collective-permute-start(f32[2,4,64,128]{3,2,1,0:T(8,128)S(1)} %get-tuple-element.74), channel_id=1, source_target_pairs={{0,2},{2,0},{4,6},{6,4},{8,10},{10,8},{12,14},{14,12},{1,3},{3,1},... | collective-permute-start | bytes 786440 | tf_op jit(solution)/shard_map/ppermute | solution.py:278
  46.6 3.2 %collective-permute-done.11.strip = f32[2,16,128]{2,1,0:T(8,128)S(1)} collective-permute-done((f32[2,16,128]{2,1,0:T(8,128)S(1)}, f32[2,16,128]{2,1,0:T(8,128)S(1)}, u32[]{:S(2)}, u32[]{:S(2)}) %collective-permute-start.11) | collective-permute-done | bytes 16416 | tf_op jit(solution)/shard_map/ppermute | solution.py:279
  49.8 2.1 %shard_map.118 = (f32[8,64,128]{2,1,0:T(8,128)S(1)}, f32[512,128]{1,0:T(8,128)S(1)}) custom-call(s32[6]{0:T(128)S(1)} %stack.19.scal, f32[8,64,128]{2,1,0:T(8,128)S(1)} %get-tuple-element.67.newer, f32[8,64,128]{2,1,0:T(8,128)S(1)} %get-tuple-element.51.vel, f32[4,8,64,128]{3,2,1,0:T(8,128)S(1)} %get-tuple-element.52.inj, ...), custom_call_target="tpu_custom_call" | custom-call | flops 10000000 | bytes 2000000 | tf_op jit(solution)/shard_map/pallas_call | solution.py:21
  51.9 22.5 %all_to_all.20 = f32[16,4,8,128]{3,2,1,0:T(8,128)S(1)} all-to-all(f32[16,4,8,128]{3,2,1,0:T(8,128)S(1)} %bitcast.22), channel_id=1, replica_groups=mesh['shot'=16,'gx'=8,'gy'=2] {'shot'}, dimensions={0} | all-to-all | bytes 524288 | tf_op jit(solution)/shard_map/all_to_all | solution.py:308
  74.5 15.8 %all_to_all.21 = f32[16,4,8,128]{3,2,1,0:T(8,128)S(1)} all-to-all(f32[16,4,8,128]{3,2,1,0:T(8,128)S(1)} %bitcast.23), channel_id=1, replica_groups=mesh['shot'=16,'gx'=8,'gy'=2] {'shot'}, dimensions={0} | all-to-all | bytes 524288 | tf_op jit(solution)/shard_map/all_to_all | solution.py:312
  90.3 0.7 shard_map.120
  91.0 0.7 collective-permute-start.12
  91.7 3.2 %collective-permute-start.13 = (f32[1,4,64,128]{3,2,1,0:T(8,128)S(1)}, f32[1,4,64,128]{3,2,1,0:T(8,128)S(1)}, u32[]{:S(2)}, u32[]{:S(2)}) collective-permute-start(f32[1,4,64,128]{3,2,1,0:T(8,128)S(1)} %get-tuple-element.81), channel_id=1, source_target_pairs={{0,2},{2,0},{4,6},{6,4},{8,10},{10,8},{12,14},{14,12},{1,3},{3,1},... | collective-permute-start | bytes 393224 | tf_op jit(solution)/shard_map/ppermute | solution.py:278
  95.1 3.4 %collective-permute-done.14.strip = f32[1,16,128]{2,1,0:T(8,128)S(1)} collective-permute-done((f32[1,16,128]{2,1,0:T(8,128)S(1)}, f32[1,16,128]{2,1,0:T(8,128)S(1)}, u32[]{:S(2)}, u32[]{:S(2)}) %collective-permute-start.14) | collective-permute-done | bytes 8224 | tf_op jit(solution)/shard_map/ppermute | solution.py:279
  98.5 1.4 shard_map.121
  99.9 0.7 collective-permute-start.15
  100.6 2.7 %collective-permute-start.16 = (f32[1,4,64,128]{3,2,1,0:T(8,128)S(1)}, f32[1,4,64,128]{3,2,1,0:T(8,128)S(1)}, u32[]{:S(2)}, u32[]{:S(2)}) collective-permute-start(f32[1,4,64,128]{3,2,1,0:T(8,128)S(1)} %get-tuple-element.85), channel_id=1, source_target_pairs={{0,2},{2,0},{4,6},{6,4},{8,10},{10,8},{12,14},{14,12},{1,3},{3,1},... | collective-permute-start | bytes 393224 | tf_op jit(solution)/shard_map/ppermute | solution.py:278
  103.5 3.4 %collective-permute-done.17.strip = f32[1,16,128]{2,1,0:T(8,128)S(1)} collective-permute-done((f32[1,16,128]{2,1,0:T(8,128)S(1)}, f32[1,16,128]{2,1,0:T(8,128)S(1)}, u32[]{:S(2)}, u32[]{:S(2)}) %collective-permute-start.17) | collective-permute-done | bytes 8224 | tf_op jit(solution)/shard_map/ppermute | solution.py:279
  107.0 1.5 shard_map.122
  108.4 0.7 collective-permute-start.18
  109.1 2.0 %collective-permute-start.19 = (f32[1,4,64,128]{3,2,1,0:T(8,128)S(1)}, f32[1,4,64,128]{3,2,1,0:T(8,128)S(1)}, u32[]{:S(2)}, u32[]{:S(2)}) collective-permute-start(f32[1,4,64,128]{3,2,1,0:T(8,128)S(1)} %get-tuple-element.90), channel_id=1, source_target_pairs={{0,2},{2,0},{4,6},{6,4},{8,10},{10,8},{12,14},{14,12},{1,3},{3,1},... | collective-permute-start | bytes 393224 | tf_op jit(solution)/shard_map/ppermute | solution.py:278
  111.1 0.8 shard_map.123.rest_2_
  111.9 0.8 shard_map.124.rest_3_
  113.0 0.8 shard_map.125.rest_4_
  113.7 2.6 %collective-permute-done.20.strip = f32[1,16,128]{2,1,0:T(8,128)S(1)} collective-permute-done((f32[1,16,128]{2,1,0:T(8,128)S(1)}, f32[1,16,128]{2,1,0:T(8,128)S(1)}, u32[]{:S(2)}, u32[]{:S(2)}) %collective-permute-start.20) | collective-permute-done | bytes 8224 | tf_op jit(solution)/shard_map/ppermute | solution.py:279
  116.4 2.3 %shard_map.126 = f32[16,72,128]{2,1,0:T(8,128)S(1)} custom-call(s32[6]{0:T(128)S(1)} %stack.19.scal, f32[8,64,128]{2,1,0:T(8,128)S(1)} %get-tuple-element.87.field.now, f32[8,64,128]{2,1,0:T(8,128)S(1)} %get-tuple-element.83.now.field.before, f32[8,64,128]{2,1,0:T(8,128)S(1)} %get-tuple-element.79.source, f32[8,64,128]{2,1,0:T(8,128)S(1)} %get-tuple-element.88.acc, ...), custom_call_target="tpu_custom_call" | custom-call | flops 10000000 | bytes 2000000 | tf_op jit(solution)/shard_map/pallas_call | solution.py:21
  118.7 14.2 %all_to_all.22 = f32[16,72,128]{2,1,0:T(8,128)S(1)} all-to-all(f32[16,72,128]{2,1,0:T(8,128)S(1)} %shard_map.126), channel_id=1, replica_groups=mesh['shot'=16,'gx'=8,'gy'=2] {'gx','gy'}, dimensions={0} | all-to-all | bytes 1179648 | tf_op jit(solution)/shard_map/all_to_all | solution.py:330
  133.0 13.5 %all_to_all.23 = f32[16,8,128]{2,1,0:T(8,128)S(1)} all-to-all(f32[16,8,128]{2,1,0:T(8,128)S(1)} %broadcast_in_dim.2), channel_id=1, replica_groups=mesh['shot'=16,'gx'=8,'gy'=2] {'shot'}, dimensions={0} | all-to-all | bytes 131072 | tf_op jit(solution)/shard_map/all_to_all | solution.py:332
  146.5 0.6 reduce_sum.29
  149.0 0.6 multiply_bitcast_fusion
  149.6 0.6 sub.4
  (41 shorter events, 3.2 us)
Async XLA Ops:
  2.0 1.0 copy-start
  3.0 0.9 copy-start.1
  4.6 16.3 %collective-permute-start = (f32[1,4,64,128]{3,2,1,0:T(8,128)S(1)}, f32[1,4,64,128]{3,2,1,0:T(8,128)S(1)}, u32[]{:S(2)}, u32[]{:S(2)}) collective-permute-start(f32[1,4,64,128]{3,2,1,0:T(8,128)S(1)} %get-tuple-element.53), channel_id=1, source_target_pairs={{2,4},{6,8},{10,12},{4,2},{8,6},{12,10},{3,5},{7,9},{11,13},{5,3},... | collective-permute-start | bytes 393224 | tf_op jit(solution)/shard_map/ppermute | solution.py:277
  5.3 15.6 %collective-permute-start.1 = (f32[1,4,64,128]{3,2,1,0:T(8,128)S(1)}, f32[1,4,64,128]{3,2,1,0:T(8,128)S(1)}, u32[]{:S(2)}, u32[]{:S(2)}) collective-permute-start(f32[1,4,64,128]{3,2,1,0:T(8,128)S(1)} %get-tuple-element.54), channel_id=1, source_target_pairs={{0,2},{2,0},{4,6},{6,4},{8,10},{10,8},{12,14},{14,12},{1,3},{3,1},... | collective-permute-start | bytes 393224 | tf_op jit(solution)/shard_map/ppermute | solution.py:278
  8.3 12.6 %collective-permute-start.2 = (f32[1,16,128]{2,1,0:T(8,128)S(1)}, f32[1,16,128]{2,1,0:T(8,128)S(1)}, u32[]{:S(2)}, u32[]{:S(2)}) collective-permute-start(f32[1,16,128]{2,1,0:T(8,128)S(1)} %get-tuple-element.55), channel_id=1, source_target_pairs={{0,1},{1,0},{2,3},{3,2},{4,5},{5,4},{6,7},{7,6},{8,9},{9,8},{10,11... | collective-permute-start | bytes 24584 | tf_op jit(solution)/shard_map/ppermute | solution.py:279
  9.8 0.9 copy-start.2
  10.8 0.8 copy-start.3
  11.5 0.7 copy-start.6
  12.2 0.7 copy-start.7
  12.9 0.7 copy-start.8
  22.4 7.4 %collective-permute-start.3 = (f32[2,4,64,128]{3,2,1,0:T(8,128)S(1)}, f32[2,4,64,128]{3,2,1,0:T(8,128)S(1)}, u32[]{:S(2)}, u32[]{:S(2)}) collective-permute-start(f32[2,4,64,128]{3,2,1,0:T(8,128)S(1)} %get-tuple-element.58), channel_id=1, source_target_pairs={{2,4},{6,8},{10,12},{4,2},{8,6},{12,10},{3,5},{7,9},{11,13},{5,3},... | collective-permute-start | bytes 786440 | tf_op jit(solution)/shard_map/ppermute | solution.py:277
  23.1 6.8 %collective-permute-start.4 = (f32[2,4,64,128]{3,2,1,0:T(8,128)S(1)}, f32[2,4,64,128]{3,2,1,0:T(8,128)S(1)}, u32[]{:S(2)}, u32[]{:S(2)}) collective-permute-start(f32[2,4,64,128]{3,2,1,0:T(8,128)S(1)} %get-tuple-element.59), channel_id=1, source_target_pairs={{0,2},{2,0},{4,6},{6,4},{8,10},{10,8},{12,14},{14,12},{1,3},{3,1},... | collective-permute-start | bytes 786440 | tf_op jit(solution)/shard_map/ppermute | solution.py:278
  26.1 3.7 %collective-permute-start.5 = (f32[2,16,128]{2,1,0:T(8,128)S(1)}, f32[2,16,128]{2,1,0:T(8,128)S(1)}, u32[]{:S(2)}, u32[]{:S(2)}) collective-permute-start(f32[2,16,128]{2,1,0:T(8,128)S(1)} %get-tuple-element.60), channel_id=1, source_target_pairs={{0,1},{1,0},{2,3},{3,2},{4,5},{5,4},{6,7},{7,6},{8,9},{9,8},{10,11... | collective-permute-start | bytes 49160 | tf_op jit(solution)/shard_map/ppermute | solution.py:279
  32.1 7.7 %collective-permute-start.6 = (f32[2,4,64,128]{3,2,1,0:T(8,128)S(1)}, f32[2,4,64,128]{3,2,1,0:T(8,128)S(1)}, u32[]{:S(2)}, u32[]{:S(2)}) collective-permute-start(f32[2,4,64,128]{3,2,1,0:T(8,128)S(1)} %get-tuple-element.64), channel_id=1, source_target_pairs={{2,4},{6,8},{10,12},{4,2},{8,6},{12,10},{3,5},{7,9},{11,13},{5,3},... | collective-permute-start | bytes 786440 | tf_op jit(solution)/shard_map/ppermute | solution.py:277
  32.8 7.0 %collective-permute-start.7 = (f32[2,4,64,128]{3,2,1,0:T(8,128)S(1)}, f32[2,4,64,128]{3,2,1,0:T(8,128)S(1)}, u32[]{:S(2)}, u32[]{:S(2)}) collective-permute-start(f32[2,4,64,128]{3,2,1,0:T(8,128)S(1)} %get-tuple-element.65), channel_id=1, source_target_pairs={{0,2},{2,0},{4,6},{6,4},{8,10},{10,8},{12,14},{14,12},{1,3},{3,1},... | collective-permute-start | bytes 786440 | tf_op jit(solution)/shard_map/ppermute | solution.py:278
  36.1 3.7 %collective-permute-start.8 = (f32[2,16,128]{2,1,0:T(8,128)S(1)}, f32[2,16,128]{2,1,0:T(8,128)S(1)}, u32[]{:S(2)}, u32[]{:S(2)}) collective-permute-start(f32[2,16,128]{2,1,0:T(8,128)S(1)} %get-tuple-element.66), channel_id=1, source_target_pairs={{0,1},{1,0},{2,3},{3,2},{4,5},{5,4},{6,7},{7,6},{8,9},{9,8},{10,11... | collective-permute-start | bytes 49160 | tf_op jit(solution)/shard_map/ppermute | solution.py:279
  42.1 7.7 %collective-permute-start.9 = (f32[2,4,64,128]{3,2,1,0:T(8,128)S(1)}, f32[2,4,64,128]{3,2,1,0:T(8,128)S(1)}, u32[]{:S(2)}, u32[]{:S(2)}) collective-permute-start(f32[2,4,64,128]{3,2,1,0:T(8,128)S(1)} %get-tuple-element.73), channel_id=1, source_target_pairs={{2,4},{6,8},{10,12},{4,2},{8,6},{12,10},{3,5},{7,9},{11,13},{5,3},... | collective-permute-start | bytes 786440 | tf_op jit(solution)/shard_map/ppermute | solution.py:277
  42.8 7.0 %collective-permute-start.10 = (f32[2,4,64,128]{3,2,1,0:T(8,128)S(1)}, f32[2,4,64,128]{3,2,1,0:T(8,128)S(1)}, u32[]{:S(2)}, u32[]{:S(2)}) collective-permute-start(f32[2,4,64,128]{3,2,1,0:T(8,128)S(1)} %get-tuple-element.74), channel_id=1, source_target_pairs={{0,2},{2,0},{4,6},{6,4},{8,10},{10,8},{12,14},{14,12},{1,3},{3,1},... | collective-permute-start | bytes 786440 | tf_op jit(solution)/shard_map/ppermute | solution.py:278
  46.0 3.7 %collective-permute-start.11 = (f32[2,16,128]{2,1,0:T(8,128)S(1)}, f32[2,16,128]{2,1,0:T(8,128)S(1)}, u32[]{:S(2)}, u32[]{:S(2)}) collective-permute-start(f32[2,16,128]{2,1,0:T(8,128)S(1)} %get-tuple-element.75), channel_id=1, source_target_pairs={{0,1},{1,0},{2,3},{3,2},{4,5},{5,4},{6,7},{7,6},{8,9},{9,8},{10,11... | collective-permute-start | bytes 49160 | tf_op jit(solution)/shard_map/ppermute | solution.py:279
  49.8 24.7 %copy-start.5 = (f32[4,8,128]{2,1,0:T(8,128)S(1)}, f32[4,8,128]{2,1,0:T(8,128)}, u32[]{:S(2)}) copy-start(f32[4,8,128]{2,1,0:T(8,128)} %param.13) | copy-start | bytes 49156
  91.0 7.5 %collective-permute-start.12 = (f32[1,4,64,128]{3,2,1,0:T(8,128)S(1)}, f32[1,4,64,128]{3,2,1,0:T(8,128)S(1)}, u32[]{:S(2)}, u32[]{:S(2)}) collective-permute-start(f32[1,4,64,128]{3,2,1,0:T(8,128)S(1)} %get-tuple-element.80), channel_id=1, source_target_pairs={{2,4},{6,8},{10,12},{4,2},{8,6},{12,10},{3,5},{7,9},{11,13},{5,3},... | collective-permute-start | bytes 393224 | tf_op jit(solution)/shard_map/ppermute | solution.py:277
  91.7 6.8 %collective-permute-start.13 = (f32[1,4,64,128]{3,2,1,0:T(8,128)S(1)}, f32[1,4,64,128]{3,2,1,0:T(8,128)S(1)}, u32[]{:S(2)}, u32[]{:S(2)}) collective-permute-start(f32[1,4,64,128]{3,2,1,0:T(8,128)S(1)} %get-tuple-element.81), channel_id=1, source_target_pairs={{0,2},{2,0},{4,6},{6,4},{8,10},{10,8},{12,14},{14,12},{1,3},{3,1},... | collective-permute-start | bytes 393224 | tf_op jit(solution)/shard_map/ppermute | solution.py:278
  94.8 3.7 %collective-permute-start.14 = (f32[1,16,128]{2,1,0:T(8,128)S(1)}, f32[1,16,128]{2,1,0:T(8,128)S(1)}, u32[]{:S(2)}, u32[]{:S(2)}) collective-permute-start(f32[1,16,128]{2,1,0:T(8,128)S(1)} %get-tuple-element.82), channel_id=1, source_target_pairs={{0,1},{1,0},{2,3},{3,2},{4,5},{5,4},{6,7},{7,6},{8,9},{9,8},{10,11... | collective-permute-start | bytes 24584 | tf_op jit(solution)/shard_map/ppermute | solution.py:279
  99.9 7.1 %collective-permute-start.15 = (f32[1,4,64,128]{3,2,1,0:T(8,128)S(1)}, f32[1,4,64,128]{3,2,1,0:T(8,128)S(1)}, u32[]{:S(2)}, u32[]{:S(2)}) collective-permute-start(f32[1,4,64,128]{3,2,1,0:T(8,128)S(1)} %get-tuple-element.84), channel_id=1, source_target_pairs={{2,4},{6,8},{10,12},{4,2},{8,6},{12,10},{3,5},{7,9},{11,13},{5,3},... | collective-permute-start | bytes 393224 | tf_op jit(solution)/shard_map/ppermute | solution.py:277
  100.6 6.4 %collective-permute-start.16 = (f32[1,4,64,128]{3,2,1,0:T(8,128)S(1)}, f32[1,4,64,128]{3,2,1,0:T(8,128)S(1)}, u32[]{:S(2)}, u32[]{:S(2)}) collective-permute-start(f32[1,4,64,128]{3,2,1,0:T(8,128)S(1)} %get-tuple-element.85), channel_id=1, source_target_pairs={{0,2},{2,0},{4,6},{6,4},{8,10},{10,8},{12,14},{14,12},{1,3},{3,1},... | collective-permute-start | bytes 393224 | tf_op jit(solution)/shard_map/ppermute | solution.py:278
  103.3 3.7 %collective-permute-start.17 = (f32[1,16,128]{2,1,0:T(8,128)S(1)}, f32[1,16,128]{2,1,0:T(8,128)S(1)}, u32[]{:S(2)}, u32[]{:S(2)}) collective-permute-start(f32[1,16,128]{2,1,0:T(8,128)S(1)} %get-tuple-element.86), channel_id=1, source_target_pairs={{0,1},{1,0},{2,3},{3,2},{4,5},{5,4},{6,7},{7,6},{8,9},{9,8},{10,11... | collective-permute-start | bytes 24584 | tf_op jit(solution)/shard_map/ppermute | solution.py:279
  108.4 7.9 %collective-permute-start.18 = (f32[1,4,64,128]{3,2,1,0:T(8,128)S(1)}, f32[1,4,64,128]{3,2,1,0:T(8,128)S(1)}, u32[]{:S(2)}, u32[]{:S(2)}) collective-permute-start(f32[1,4,64,128]{3,2,1,0:T(8,128)S(1)} %get-tuple-element.89), channel_id=1, source_target_pairs={{2,4},{6,8},{10,12},{4,2},{8,6},{12,10},{3,5},{7,9},{11,13},{5,3},... | collective-permute-start | bytes 393224 | tf_op jit(solution)/shard_map/ppermute | solution.py:277
  109.1 7.3 %collective-permute-start.19 = (f32[1,4,64,128]{3,2,1,0:T(8,128)S(1)}, f32[1,4,64,128]{3,2,1,0:T(8,128)S(1)}, u32[]{:S(2)}, u32[]{:S(2)}) collective-permute-start(f32[1,4,64,128]{3,2,1,0:T(8,128)S(1)} %get-tuple-element.90), channel_id=1, source_target_pairs={{0,2},{2,0},{4,6},{6,4},{8,10},{10,8},{12,14},{14,12},{1,3},{3,1},... | collective-permute-start | bytes 393224 | tf_op jit(solution)/shard_map/ppermute | solution.py:278
  112.6 3.7 %collective-permute-start.20 = (f32[1,16,128]{2,1,0:T(8,128)S(1)}, f32[1,16,128]{2,1,0:T(8,128)S(1)}, u32[]{:S(2)}, u32[]{:S(2)}) collective-permute-start(f32[1,16,128]{2,1,0:T(8,128)S(1)} %get-tuple-element.91), channel_id=1, source_target_pairs={{0,1},{1,0},{2,3},{3,2},{4,5},{5,4},{6,7},{7,6},{8,9},{9,8},{10,11... | collective-permute-start | bytes 24584 | tf_op jit(solution)/shard_map/ppermute | solution.py:279
  118.6 31.0 %copy-start.4 = (f32[1,4,2048]{2,1,0:T(4,128)S(1)}, f32[1,4,2048]{2,1,0:T(4,128)}, u32[]{:S(2)}) copy-start(f32[1,4,2048]{2,1,0:T(4,128)} %param.14) | copy-start | bytes 98308

commit v2 on v1

--- a/solution.py
+++ b/solution.py
@@ -13,11 +13,10 @@
 
 
 def call(kernel, outs, scratch=(), limit=24, flops=10_000_000):
-    def run(*args, smem=0):
-        specs = [
-            pl.BlockSpec(memory_space=pltpu.SMEM if i < smem else pltpu.VMEM)
-            for i in range(len(args))
-        ]
+    def run(*args, smem=0, hbm=0):
+        spaces = [pltpu.SMEM] * smem + [pltpu.HBM] * hbm
+        spaces = spaces + [pltpu.VMEM] * (len(args) - smem - hbm)
+        specs = [pl.BlockSpec(memory_space=space) for space in spaces]
         return pl.pallas_call(
             kernel,
             out_shape=[jax.ShapeDtypeStruct(s, d) for s, d in outs],
@@ -68,8 +67,9 @@
         padded[4 + x, 0:8] = zero
         padded[4 + x, 72:80] = zero
         padded[4 + x, 8:72] = load(x)
+    inside = ((scal[2] > 0) | (core == 1)) & ((scal[2] < 7 * BX) | (core == 0))
     for i in range(4):
-        padded[12 * core + i, 8:72] = outer_ref[slot, i]
+        padded[12 * core + i, 8:72] = jnp.where(inside, outer_ref[slot, i], 0.0)
         padded[12 * (1 - core) + i, 8:72] = inner_ref[slot, i]
     for half in range(2):
         packed = strip_ref[slot, 8 * half : 8 * half + 8]
@@ -102,10 +102,17 @@
     return [((count, 4, NZ, BY), F32), ((count, 4, NZ, BY), F32), ((count, 16, BY), F32)]
 
 
-def first_kernel(scal, newer, older, newer_out, older_out, outer, inner, strip):
-    for x in range(BX):
-        newer_out[x] = newer[pl.ds(x, NZ, stride=8), :]
-        older_out[x] = older[pl.ds(x, NZ, stride=8), :]
+def first_kernel(scal, newer, newer_out, outer, inner, strip, raw, sem):
+    copies = [
+        pltpu.make_async_copy(newer.at[pl.ds(128 * i, 128)], raw.at[pl.ds(128 * i, 128)], sem.at[i])
+        for i in range(4)
+    ]
+    for copy in copies:
+        copy.start()
+    for copy in copies:
+        copy.wait()
+    for x in range(BX):
+        newer_out[x] = raw[pl.ds(x, NZ, stride=8), :]
     send_edges(lambda x: newer_out[x], outer, inner, strip, 0, scal)
 
 
@@ -114,43 +121,77 @@
     return high, (values - high.astype(F32)).astype(BF16)
 
 
-def prepare_kernel(scal, vel, traces, rz, rx, ry, vel_out, inj, pick_cell, pick_y, spread):
-    for x in range(BX):
-        vel_out[x] = vel[pl.ds(x, NZ, stride=8), :]
+def prepare_kernel(scal, rz_in, rx_in, ry_in, traces_in, vel_in, older_in,
+                   vel_out, older_out, inj, pick_cell, pick_y,
+                   rz, rx, ry, traces, vel, older, at_depth, spread, sem):
+    copies = [
+        pltpu.make_async_copy(source, target, sem.at[i])
+        for i, (source, target) in enumerate(
+            ((rz_in, rz), (rx_in, rx), (ry_in, ry), (traces_in, traces), (vel_in, vel), (older_in, older))
+        )
+    ]
+    for copy in copies:
+        copy.start()
+    for copy in copies[:4]:
+        copy.wait()
     lat_x = rx[...] - scal[2]
     lat_y = ry[...] - scal[3]
     present = (lat_x >= 0) & (lat_x < BX) & (lat_y >= 0) & (lat_y < BY)
-    row = jnp.where(present, lat_x * NZ + rz[...], -1)
+    depth = jnp.where(present, rz[...], -1)
     col = jnp.where(present, lat_y, -1)
 
-    def rows(i, carry):
+    def block(i):
+        return pl.ds(pl.multiple_of(16 * i, 16), 16)
+
+    def wide(row):
+        return jnp.broadcast_to(row, (16, NREC)).astype(BF16)
+
+    def hits(i, wanted):
         number = lax.broadcasted_iota(I32, (16, NREC), 0) + 16 * i
-        pick_cell[pl.ds(pl.multiple_of(16 * i, 16), 16), :] = jnp.where(number == row, 1.0, 0.0).astype(BF16)
+        return jnp.where(number == wanted, 1.0, 0.0).astype(BF16)
+
+    def depths(i, carry):
+        at_depth[block(i), :] = hits(i, depth)
         return carry
 
-    lax.fori_loop(0, 32, rows, 0)
+    lax.fori_loop(0, 4, depths, 0)
+
+    def planes(x, carry):
+        here = wide(jnp.where(lat_x == x, 1.0, 0.0))
+        for i in range(4):
+            pick_cell[block(4 * x + i), :] = at_depth[16 * i : 16 * i + 16] * here
+        return carry
+
+    lax.fori_loop(0, BX, planes, 0)
+
+    def columns(i, carry):
+        pick_y[block(i), :] = hits(i, col)
+        return carry
+
+    lax.fori_loop(0, 8, columns, 0)
     for n in range(STEPS):
         value = traces[n : n + 1, :]
-        high, low = two_pieces(value)
-        high, low = high.astype(F32), low.astype(F32)
-
-        def columns(i, carry):
-            number = lax.broadcasted_iota(I32, (16, NREC), 0) + 16 * i
-            hit = number == col
-            at = pl.multiple_of(16 * i, 16)
-            if n == 0:
-                pick_y[pl.ds(at, 16), :] = jnp.where(hit, 1.0, 0.0).astype(BF16)
-            spread[pl.ds(at, 16), :] = jnp.where(hit, high, 0.0).astype(BF16)
-            spread[pl.ds(pl.multiple_of(BY + at, 16), 16), :] = jnp.where(hit, low, 0.0).astype(BF16)
+        coarse = value.astype(BF16).astype(F32)
+        high, low = wide(coarse), wide(value - coarse)
+
+        def weigh(i, carry):
+            picked = pick_y[block(i), :]
+            spread[block(i), :] = picked * high
+            spread[block(8 + i), :] = picked * low
             return carry
 
-        lax.fori_loop(0, 8, columns, 0)
+        lax.fori_loop(0, 8, weigh, 0)
         both = lax.dot_general(
             pick_cell[...], spread[...], (((1,), (1,)), ((), ())), preferred_element_type=F32
         )
         for x in range(BX):
             part = both[NZ * x : NZ * x + NZ]
             inj[n, x] = part[:, :BY] + part[:, BY:]
+    for copy in copies[4:]:
+        copy.wait()
+    for x in range(BX):
+        vel_out[x] = vel[pl.ds(x, NZ, stride=8), :]
+        older_out[x] = older[pl.ds(x, NZ, stride=8), :]
 
 
 def forward1_kernel(scal, newer, older, vel, inj, outer, inner, strip, acc, nxt, q, outer_o, inner_o, strip_o, padded, side):
@@ -225,7 +266,7 @@
 def make_born(moment, last):
     def kernel(scal, now, before, source, acc, vel, outer, inner, strip, *rest):
         if last:
-            pick_cell, pick_y, s1, s2, s3, dot, payload, padded, side, d, pieces, block = rest
+            pick_cell, pick_y, s1, s2, s3, dot, block, padded, side, d, pieces = rest
         else:
             d, outer_o, inner_o, strip_o, padded, side = rest
         fill(padded, side, lambda x: now[x], outer, inner, strip, 0, scal)
@@ -247,8 +288,6 @@
         block[64:72, :] = jnp.zeros((8, BY), F32)
         block[64:65, :] = energy
         block[65:66, :] = jnp.sum(dot[...], axis=0, keepdims=True)
-        for i in range(16):
-            payload[i] = block[...]
 
     return kernel
 
@@ -269,8 +308,38 @@
     out[...] = sampled(field, pieces, pick_cell, pick_y)
 
 
+def pair_kernel(mine, theirs, copies):
+    total = mine[...] + theirs[...]
+    for i in range(8):
+        copies[i] = total
+
+
+def collect_kernel(arrived, predicted, copies):
+    total = arrived[0]
+    for i in range(1, 8):
+        total = total + arrived[i]
+    predicted[...] = total[0:64]
+    for i in range(16):
+        copies[i] = total[64:72]
+
+
+def finish_kernel(stats, predicted, scaled, traces, image, residual):
+    total = stats[0]
+    for i in range(1, 16):
+        total = total + stats[i]
+    energy = jnp.sum(total[0:1], axis=1, keepdims=True)
+    dot = jnp.sum(total[1:2], axis=1, keepdims=True)
+    step = dot / (energy + 1e-6)
+    image[...] = step * scaled[...]
+    for n in range(STEPS):
+        for j in range(16):
+            at = pl.ds(BY * j, BY)
+            row = predicted[16 * n + j : 16 * n + j + 1, :]
+            residual[n : n + 1, at] = traces[n : n + 1, at] - step * row
+
+
 def exchange(outer, inner, strip):
-    chips = [(2 * i + 1, 2 * i + 2) for i in range(3)]
+    chips = [(2 * i + 1, (2 * i + 2) % 8) for i in range(4)]
     across = chips + [(b, a) for a, b in chips]
     swap = [(i, i ^ 1) for i in range(8)]
     return (
@@ -285,14 +354,25 @@
     flat = (NZ * BX, BY)
     gx, gy = lax.axis_index("gx"), lax.axis_index("gy")
     scal = jnp.stack([gx % 2, gy, gx * BX, gy * BY, aperture_x[0], aperture_y[0]]).astype(I32)
-    newer, older, *e = call(first_kernel, [FIELD, FIELD] + edges(1))(
-        scal, newer_field.reshape(flat), older_field.reshape(flat), smem=1)
-    e = exchange(*e)
-    vel, inj, pick_cell, pick_y = call(
+    newer, *e = call(
+        first_kernel, [FIELD] + edges(1), [pltpu.VMEM(flat, F32), pltpu.SemaphoreType.DMA((4,))]
+    )(scal, newer_field.reshape(flat), smem=1, hbm=1)
+    e = exchange(*e)
+    vel, older, inj, pick_cell, pick_y = call(
         prepare_kernel,
-        [FIELD, ((4, BX, NZ, BY), F32), ((512, NREC), BF16), ((BY, NREC), BF16)],
-        [pltpu.VMEM((2 * BY, NREC), BF16)], limit=40,
-    )(scal, velocity.reshape(flat), traces[0], receiver_z, receiver_x, receiver_y, smem=1)
+        [FIELD, FIELD, ((4, BX, NZ, BY), F32), ((512, NREC), BF16), ((BY, NREC), BF16)],
+        [pltpu.VMEM((1, NREC), I32)] * 3
+        + [
+            pltpu.VMEM((4, NREC), F32),
+            pltpu.VMEM(flat, F32),
+            pltpu.VMEM(flat, F32),
+            pltpu.VMEM((NZ, NREC), BF16),
+            pltpu.VMEM((2 * BY, NREC), BF16),
+            pltpu.SemaphoreType.DMA((6,)),
+        ],
+        limit=40,
+    )(scal, receiver_z, receiver_x, receiver_y, traces[0], velocity.reshape(flat),
+      older_field.reshape(flat), smem=1, hbm=6)
     acc0, u1, q, *e = call(forward1_kernel, [FIELD] * 3 + edges(2), [PADDED, SIDE])(
         scal, newer, older, vel, inj, *e, smem=1)
     e = exchange(*e)
@@ -300,7 +380,7 @@
         scal, u1, newer, vel, inj, q, q, q, *e, smem=1)
     e = exchange(*e)
     acc2, u3, p1, q, *e = call(
-        make_forward_later, [FIELD] * 4 + edges(2), [PADDED, SIDE])(
+        forward2_kernel, [FIELD] * 4 + edges(2), [PADDED, SIDE])(
         scal, u2, u1, vel, inj, q, p2, *e, smem=1)
     e = exchange(*e)
     acc3, grad = call(last_kernel, [FIELD, (flat, F32)], [PADDED, SIDE, PADDED, SIDE])(
@@ -323,21 +403,22 @@
         scal, d2, d1, source, acc2, vel, *e, smem=1)
     e = exchange(*e)
     s3, = sample(d3, pick_cell, pick_y)
-    payload, = call(
-        make_born(3, True), [((16, 72, BY), F32)],
-        [PADDED, SIDE, pltpu.VMEM((BX, NZ, BY), F32), pltpu.VMEM((512, 2 * BY), BF16), pltpu.VMEM((72, BY), F32)],
+    block, = call(
+        make_born(3, True), [((72, BY), F32)],
+        [PADDED, SIDE, pltpu.VMEM((BX, NZ, BY), F32), pltpu.VMEM((512, 2 * BY), BF16)],
     )(scal, d3, d2, source, acc3, vel, *e, pick_cell, pick_y, s1, s2, s3, dot, smem=1)
-    arrived = lax.all_to_all(payload, ("gx", "gy"), 0, 0, tiled=True)
-    summed = jnp.sum(arrived, axis=0)
-    stats = lax.all_to_all(jnp.broadcast_to(summed[None, 64:72], (16, 8, BY)), "shot", 0, 0, tiled=True)
-    trace_energy = jnp.sum(stats[:, 0])
-    descent_dot = jnp.sum(stats[:, 1])
-    step_length = descent_dot / (trace_energy + 1e-6)
-    predicted = summed[:64].reshape(4, NREC)
-    return (step_length * scaled.reshape(4, BX, BY), (traces[0] - step_length * predicted)[None])
-
-
-def make_forward_later(scal, newer, older, vel, inj, q_in, later, outer, inner, strip,
+    theirs = lax.ppermute(block, "gx", [(i, i ^ 1) for i in range(8)])
+    payload, = call(pair_kernel, [((8, 72, BY), F32)])(block, theirs)
+    same_core = [[2 * (2 * c + k) + g for c in range(4) for g in range(2)] for k in range(2)]
+    arrived = lax.all_to_all(payload, ("gx", "gy"), 0, 0, axis_index_groups=same_core, tiled=True)
+    predicted, stats = call(collect_kernel, [((64, BY), F32), ((16, 8, BY), F32)])(arrived)
+    stats = lax.all_to_all(stats, "shot", 0, 0, tiled=True)
+    image, residual = call(finish_kernel, [((32, BY), F32), ((4, NREC), F32)])(
+        stats, predicted, scaled, traces[0])
+    return image.reshape(4, BX, BY), residual[None]
+
+
+def forward2_kernel(scal, newer, older, vel, inj, q_in, later, outer, inner, strip,
                        acc, nxt, p, q, outer_o, inner_o, strip_o, padded, side):
     fill(padded, side, lambda x: newer[x], outer, inner, strip, 0, scal)
     for x in range(BX):

time: 152 us -> 137 us (0.901); the launches traced: 150 us -> 137 us
  starting transfers between devices: 29 us -> 13.4 us
  waiting for transfers between devices: 19.2 us -> 29.2 us
  blocking collectives: 66 us -> 61.4 us
  other arithmetic: 2.48 us -> 0 us
    ppermute x7, starting transfers between devices: 20.4 us -> 0.55 us  [exchange(): lax.ppermute(inner, 'gx', swap)]
    ppermute x7, waiting for transfers between devices: 0.02 us -> 8.89 us  [exchange(): lax.ppermute(outer, 'gx', across)]
    ppermute x7, starting transfers between devices: 4.7 us -> 8.87 us  [exchange(): lax.ppermute(outer, 'gx', across)]
    all_to_all x2, blocking collectives: 27.7 us -> 25.7 us  [the longest x1 14.7 us: on_device(): stats = lax.all_to_all(stats, 'shot', 0, 0, tiled=True)]
    pallas_call x14 -> x17, Pallas kernels: 24.4 us -> 25.1 us  [run(): pl.pallas_call(kernel, out_shape=[jax.ShapeDtypeStruct(s, d) for s, d in...]
    unnamed x18 -> x16, local copies, waits for them, and re-layouts: 5.71 us -> 5.7 us
  transfers between devices with their start and end apart: 21 -> 22, of which waited for: 6 -> 12; matrix products, arithmetic and copies ran while one was open for 0% -> 0% of each run, Pallas kernels for 6% -> 7%
where the time goes in v2:
time: 137 us
  blocking collectives  61.4 us (45%)
  waiting for transfers between devices  29.2 us (21%)
  Pallas kernels  25.1 us (18%)
  starting transfers between devices  13.4 us (10%)
  local copies, waits for them, and re-layouts  5.79 us (4%)
  between operations  2.07 us (2%)
    pallas_call x17, Pallas kernels, run(): pl.pallas_call(kernel, out_shape=[jax.ShapeDtypeStruct(s, d) for s, d in...  25.1 us
    all_to_all x1, blocking collectives, on_device(): lax.all_to_all(grad.reshape(16, 4, BX, BY), 'shot', 0, 0, tiled=True)  21.1 us
    ppermute x7, waiting for transfers between devices, exchange(): lax.ppermute(strip, 'gy', [(0, 1), (1, 0)])  19.1 us
    all_to_all x1, blocking collectives, on_device(): stats = lax.all_to_all(stats, 'shot', 0, 0, tiled=True)  14.7 us
    all_to_all x1, blocking collectives, on_device(): lax.all_to_all(copies.reshape(16, 4, BX, BY), 'shot', 0, 0, tiled=True)  14.5 us
    all_to_all x1, blocking collectives, on_device(): lax.all_to_all(payload, ('gx', 'gy'), 0, 0, axis_index_groups=same_core,...  11 us
    ppermute x7, waiting for transfers between devices, exchange(): lax.ppermute(outer, 'gx', across)  8.89 us
    ppermute x7, starting transfers between devices, exchange(): lax.ppermute(outer, 'gx', across)  8.87 us
  transfers between devices with their start and end apart: 22, of which 12 were waited for; matrix products, arithmetic and copies ran while one was open for 0% of the time, Pallas kernels for 7%

profile of v2, /device:TPU:32, one launch (start us, length us, event | category | flops | bytes accessed | tf_op | source)
XLA Modules:
  0.0 136.9 jit_solution(324020266938484992)
XLA Ops:
  2.0 1.0 copy-done
  3.0 1.1 shard_map.113
  4.1 2.5 %collective-permute-start = (f32[1,4,64,128]{3,2,1,0:T(8,128)S(1)}, f32[1,4,64,128]{3,2,1,0:T(8,128)S(1)}, u32[]{:S(2)}, u32[]{:S(2)}) collective-permute-start(f32[1,4,64,128]{3,2,1,0:T(8,128)S(1)} %get-tuple-element.57), channel_id=1, source_target_pairs={{2,4},{6,8},{10,12},{14,0},{4,2},{8,6},{12,10},{0,14},{3,5},{7,9},... | collective-permute-start | bytes 393224 | tf_op jit(solution)/shard_map/ppermute | solution.py:346
  6.6 1.5 %collective-permute-start.2 = (f32[1,16,128]{2,1,0:T(8,128)S(1)}, f32[1,16,128]{2,1,0:T(8,128)S(1)}, u32[]{:S(2)}, u32[]{:S(2)}) collective-permute-start(f32[1,16,128]{2,1,0:T(8,128)S(1)} %get-tuple-element.59), channel_id=1, source_target_pairs={{0,1},{1,0},{2,3},{3,2},{4,5},{5,4},{6,7},{7,6},{8,9},{9,8},{10,11... | collective-permute-start | bytes 24584 | tf_op jit(solution)/shard_map/ppermute | solution.py:348
  8.1 0.9 copy-done.1
  9.1 0.9 copy-done.2
  10.0 0.8 copy-done.3
  10.8 0.7 copy-done.5
  11.5 0.7 copy-done.6
  12.2 0.7 copy-done.7
  12.9 6.8 %shard_map.114 = (f32[8,64,128]{2,1,0:T(8,128)S(1)}, f32[8,64,128]{2,1,0:T(8,128)S(1)}, f32[4,8,64,128]{3,2,1,0:T(8,128)S(1)}, bf16[512,2048]{1,0:T(8,128)(2,1)S(1)}, bf16[128,2048]{1,0:T(8,128)(2,1)S(1)}) custom-call(s32[6]{0:T(128)S(1)} %stack.19.scal, s32[1,2048]{1,0:T(1,128)S(1)} %copy-done.5, s32[1,2048]{1,0:T(1,128)S(1)} %copy-done.6, ...), custom_call_target="tpu_custom_call" | custom-call | flops 10000000 | bytes 2000000 | tf_op jit(solution)/shard_map/pallas_call | solution.py:20
  19.7 1.5 %shard_map.115 = (f32[8,64,128]{2,1,0:T(8,128)S(1)}, f32[8,64,128]{2,1,0:T(8,128)S(1)}, f32[8,64,128]{2,1,0:T(8,128)S(1)}, f32[2,4,64,128]{3,2,1,0:T(8,128)S(1)}...) custom-call(s32[6]{0:T(128)S(1)} %stack.19.scal, f32[8,64,128]{2,1,0:T(8,128)S(1)} %get-tuple-element.53.newer.older, ...), custom_call_target="tpu_custom_call" | custom-call | flops 10000000 | bytes 2000000 | tf_op jit(solution)/shard_map/pallas_call | solution.py:20
  21.2 0.7 collective-permute-start.3
  22.3 0.5 collective-permute-start.5
  22.8 3.2 %collective-permute-done.5.strip = f32[2,16,128]{2,1,0:T(8,128)S(1)} collective-permute-done((f32[2,16,128]{2,1,0:T(8,128)S(1)}, f32[2,16,128]{2,1,0:T(8,128)S(1)}, u32[]{:S(2)}, u32[]{:S(2)}) %collective-permute-start.5) | collective-permute-done | bytes 16416 | tf_op jit(solution)/shard_map/ppermute | solution.py:348
  26.0 2.3 %collective-permute-done.3.outer = f32[2,4,64,128]{3,2,1,0:T(8,128)S(1)} collective-permute-done((f32[2,4,64,128]{3,2,1,0:T(8,128)S(1)}, f32[2,4,64,128]{3,2,1,0:T(8,128)S(1)}, u32[]{:S(2)}, u32[]{:S(2)}) %collective-permute-start.3) | collective-permute-done | bytes 262176 | tf_op jit(solution)/shard_map/ppermute | solution.py:346
  28.3 2.2 %shard_map.116 = (f32[8,64,128]{2,1,0:T(8,128)S(1)}, f32[8,64,128]{2,1,0:T(8,128)S(1)}, f32[8,64,128]{2,1,0:T(8,128)S(1)}, f32[8,64,128]{2,1,0:T(8,128)S(1)}, f3...) custom-call(s32[6]{0:T(128)S(1)} %stack.19.scal, ...), custom_call_target="tpu_custom_call" | custom-call | flops 10000000 | bytes 2000000 | tf_op jit(solution)/shard_map/pallas_call | solution.py:20
  30.6 0.7 collective-permute-start.6
  31.2 0.5 collective-permute-start.8
  31.8 3.2 %collective-permute-done.8.strip = f32[2,16,128]{2,1,0:T(8,128)S(1)} collective-permute-done((f32[2,16,128]{2,1,0:T(8,128)S(1)}, f32[2,16,128]{2,1,0:T(8,128)S(1)}, u32[]{:S(2)}, u32[]{:S(2)}) %collective-permute-start.8) | collective-permute-done | bytes 16416 | tf_op jit(solution)/shard_map/ppermute | solution.py:348
  35.0 2.7 %collective-permute-done.6.outer = f32[2,4,64,128]{3,2,1,0:T(8,128)S(1)} collective-permute-done((f32[2,4,64,128]{3,2,1,0:T(8,128)S(1)}, f32[2,4,64,128]{3,2,1,0:T(8,128)S(1)}, u32[]{:S(2)}, u32[]{:S(2)}) %collective-permute-start.6) | collective-permute-done | bytes 262176 | tf_op jit(solution)/shard_map/ppermute | solution.py:346
  37.7 2.3 %shard_map.117 = (f32[8,64,128]{2,1,0:T(8,128)S(1)}, f32[8,64,128]{2,1,0:T(8,128)S(1)}, f32[8,64,128]{2,1,0:T(8,128)S(1)}, f32[8,64,128]{2,1,0:T(8,128)S(1)}, f3...) custom-call(s32[6]{0:T(128)S(1)} %stack.19.scal, ...), custom_call_target="tpu_custom_call" | custom-call | flops 10000000 | bytes 2000000 | tf_op jit(solution)/shard_map/pallas_call | solution.py:20
  39.9 0.7 collective-permute-start.9
  40.6 0.5 collective-permute-start.11
  41.1 3.2 %collective-permute-done.11.strip = f32[2,16,128]{2,1,0:T(8,128)S(1)} collective-permute-done((f32[2,16,128]{2,1,0:T(8,128)S(1)}, f32[2,16,128]{2,1,0:T(8,128)S(1)}, u32[]{:S(2)}, u32[]{:S(2)}) %collective-permute-start.11) | collective-permute-done | bytes 16416 | tf_op jit(solution)/shard_map/ppermute | solution.py:348
  44.3 2.7 %collective-permute-done.9.outer = f32[2,4,64,128]{3,2,1,0:T(8,128)S(1)} collective-permute-done((f32[2,4,64,128]{3,2,1,0:T(8,128)S(1)}, f32[2,4,64,128]{3,2,1,0:T(8,128)S(1)}, u32[]{:S(2)}, u32[]{:S(2)}) %collective-permute-start.9) | collective-permute-done | bytes 262176 | tf_op jit(solution)/shard_map/ppermute | solution.py:346
  47.0 2.1 %shard_map.118 = (f32[8,64,128]{2,1,0:T(8,128)S(1)}, f32[512,128]{1,0:T(8,128)S(1)}) custom-call(s32[6]{0:T(128)S(1)} %stack.19.scal, f32[8,64,128]{2,1,0:T(8,128)S(1)} %get-tuple-element.71.newer, f32[8,64,128]{2,1,0:T(8,128)S(1)} %get-tuple-element.55.vel, f32[4,8,64,128]{3,2,1,0:T(8,128)S(1)} %get-tuple-element.56.inj, ...), custom_call_target="tpu_custom_call" | custom-call | flops 10000000 | bytes 2000000 | tf_op jit(solution)/shard_map/pallas_call | solution.py:20
  49.2 21.1 %all_to_all.20 = f32[16,4,8,128]{3,2,1,0:T(8,128)S(1)} all-to-all(f32[16,4,8,128]{3,2,1,0:T(8,128)S(1)} %bitcast.18), channel_id=1, replica_groups=mesh['shot'=16,'gx'=8,'gy'=2] {'shot'}, dimensions={0} | all-to-all | bytes 524288 | tf_op jit(solution)/shard_map/all_to_all | solution.py:388
  70.3 14.5 %all_to_all.21 = f32[16,4,8,128]{3,2,1,0:T(8,128)S(1)} all-to-all(f32[16,4,8,128]{3,2,1,0:T(8,128)S(1)} %bitcast.19), channel_id=1, replica_groups=mesh['shot'=16,'gx'=8,'gy'=2] {'shot'}, dimensions={0} | all-to-all | bytes 524288 | tf_op jit(solution)/shard_map/all_to_all | solution.py:392
  84.8 0.7 shard_map.120
  85.5 1.4 %collective-permute-start.12 = (f32[1,4,64,128]{3,2,1,0:T(8,128)S(1)}, f32[1,4,64,128]{3,2,1,0:T(8,128)S(1)}, u32[]{:S(2)}, u32[]{:S(2)}) collective-permute-start(f32[1,4,64,128]{3,2,1,0:T(8,128)S(1)} %get-tuple-element.84), channel_id=1, source_target_pairs={{2,4},{6,8},{10,12},{14,0},{4,2},{8,6},{12,10},{0,14},{3,5},{7,9},... | collective-permute-start | bytes 393224 | tf_op jit(solution)/shard_map/ppermute | solution.py:346
  87.2 3.4 %collective-permute-done.14.strip = f32[1,16,128]{2,1,0:T(8,128)S(1)} collective-permute-done((f32[1,16,128]{2,1,0:T(8,128)S(1)}, f32[1,16,128]{2,1,0:T(8,128)S(1)}, u32[]{:S(2)}, u32[]{:S(2)}) %collective-permute-start.14) | collective-permute-done | bytes 8224 | tf_op jit(solution)/shard_map/ppermute | solution.py:348
  90.6 0.6 collective-permute-done.12.outer
  91.2 1.4 %shard_map.121 = (f32[8,64,128]{2,1,0:T(8,128)S(1)}, f32[1,4,64,128]{3,2,1,0:T(8,128)S(1)}, f32[1,4,64,128]{3,2,1,0:T(8,128)S(1)}, f32[1,16,128]{2,1,0:T(8,128)S(1)}) custom-call(s32[6]{0:T(128)S(1)} %stack.19.scal, f32[8,64,128]{2,1,0:T(8,128)S(1)} %get-tuple-element.82.now.before.field, f32[8,64,128]{2,1,0:T(8,128)S(1)} %get-tuple-element.82.now.before.field, ...), custom_call_target="tpu_custom_call" | custom-call | flops 10000000 | bytes 2000000 | tf_op jit(solution)/shard_map/pallas_call | solution.py:20
  92.7 1.5 %collective-permute-start.15 = (f32[1,4,64,128]{3,2,1,0:T(8,128)S(1)}, f32[1,4,64,128]{3,2,1,0:T(8,128)S(1)}, u32[]{:S(2)}, u32[]{:S(2)}) collective-permute-start(f32[1,4,64,128]{3,2,1,0:T(8,128)S(1)} %get-tuple-element.88), channel_id=1, source_target_pairs={{2,4},{6,8},{10,12},{14,0},{4,2},{8,6},{12,10},{0,14},{3,5},{7,9},... | collective-permute-start | bytes 393224 | tf_op jit(solution)/shard_map/ppermute | solution.py:346
  94.3 3.4 %collective-permute-done.17.strip = f32[1,16,128]{2,1,0:T(8,128)S(1)} collective-permute-done((f32[1,16,128]{2,1,0:T(8,128)S(1)}, f32[1,16,128]{2,1,0:T(8,128)S(1)}, u32[]{:S(2)}, u32[]{:S(2)}) %collective-permute-start.17) | collective-permute-done | bytes 8224 | tf_op jit(solution)/shard_map/ppermute | solution.py:348
  97.8 0.6 collective-permute-done.15.outer
  98.4 1.5 %shard_map.122 = (f32[8,64,128]{2,1,0:T(8,128)S(1)}, f32[1,4,64,128]{3,2,1,0:T(8,128)S(1)}, f32[1,4,64,128]{3,2,1,0:T(8,128)S(1)}, f32[1,16,128]{2,1,0:T(8,128)S(1)}) custom-call(s32[6]{0:T(128)S(1)} %stack.19.scal, f32[8,64,128]{2,1,0:T(8,128)S(1)} %get-tuple-element.87.now.field.before, f32[8,64,128]{2,1,0:T(8,128)S(1)} %get-tuple-element.82.now.before.field, ...), custom_call_target="tpu_custom_call" | custom-call | flops 10000000 | bytes 2000000 | tf_op jit(solution)/shard_map/pallas_call | solution.py:20
  99.8 1.5 %collective-permute-start.18 = (f32[1,4,64,128]{3,2,1,0:T(8,128)S(1)}, f32[1,4,64,128]{3,2,1,0:T(8,128)S(1)}, u32[]{:S(2)}, u32[]{:S(2)}) collective-permute-start(f32[1,4,64,128]{3,2,1,0:T(8,128)S(1)} %get-tuple-element.93), channel_id=1, source_target_pairs={{2,4},{6,8},{10,12},{14,0},{4,2},{8,6},{12,10},{0,14},{3,5},{7,9},... | collective-permute-start | bytes 393224 | tf_op jit(solution)/shard_map/ppermute | solution.py:346
  101.4 0.8 shard_map.123.rest_2_
  102.2 0.8 shard_map.124.rest_3_
  103.3 0.8 shard_map.125.rest_4_
  104.1 2.6 %collective-permute-done.20.strip = f32[1,16,128]{2,1,0:T(8,128)S(1)} collective-permute-done((f32[1,16,128]{2,1,0:T(8,128)S(1)}, f32[1,16,128]{2,1,0:T(8,128)S(1)}, u32[]{:S(2)}, u32[]{:S(2)}) %collective-permute-start.20) | collective-permute-done | bytes 8224 | tf_op jit(solution)/shard_map/ppermute | solution.py:348
  106.8 2.2 %shard_map.126.mine = f32[72,128]{1,0:T(8,128)S(1)} custom-call(s32[6]{0:T(128)S(1)} %stack.19.scal, f32[8,64,128]{2,1,0:T(8,128)S(1)} %get-tuple-element.91.field.now, f32[8,64,128]{2,1,0:T(8,128)S(1)} %get-tuple-element.87.now.field.before, f32[8,64,128]{2,1,0:T(8,128)S(1)} %get-tuple-element.83.source, f32[8,64,128]{2,1,0:T(8,128)S(1)} %get-tuple-element.92.acc, ...), custom_call_target="tpu_custom_call" | custom-call | flops 10000000 | bytes 2000000 | tf_op jit(solution)/shard_map/pallas_call | solution.py:20
  109.1 1.2 collective-permute-done.21.theirs
  110.3 11.0 %all_to_all.22.arrived = f32[8,72,128]{2,1,0:T(8,128)S(1)} all-to-all(f32[8,72,128]{2,1,0:T(8,128)S(1)} %shard_map.127), channel_id=1, replica_groups={{0,1,4,5,8,9,12,13},{2,3,6,7,10,11,14,15},{16,17,20,21,24,25,28,29},{18..., dimensions={0} | all-to-all | bytes 589824 | tf_op jit(solution)/shard_map/all_to_all | solution.py:413
  121.4 14.7 %all_to_all.23.stats = f32[16,8,128]{2,1,0:T(8,128)S(1)} all-to-all(f32[16,8,128]{2,1,0:T(8,128)S(1)} %get-tuple-element.99), channel_id=1, replica_groups=mesh['shot'=16,'gx'=8,'gy'=2] {'shot'}, dimensions={0} | all-to-all | bytes 131072 | tf_op jit(solution)/shard_map/all_to_all | solution.py:415
  136.1 0.8 shard_map.129
  (34 shorter events, 1.6 us)
Async XLA Ops:
  2.0 1.0 copy-start
  4.1 15.6 %collective-permute-start = (f32[1,4,64,128]{3,2,1,0:T(8,128)S(1)}, f32[1,4,64,128]{3,2,1,0:T(8,128)S(1)}, u32[]{:S(2)}, u32[]{:S(2)}) collective-permute-start(f32[1,4,64,128]{3,2,1,0:T(8,128)S(1)} %get-tuple-element.57), channel_id=1, source_target_pairs={{2,4},{6,8},{10,12},{14,0},{4,2},{8,6},{12,10},{0,14},{3,5},{7,9},... | collective-permute-start | bytes 393224 | tf_op jit(solution)/shard_map/ppermute | solution.py:346
  6.6 13.1 %collective-permute-start.1 = (f32[1,4,64,128]{3,2,1,0:T(8,128)S(1)}, f32[1,4,64,128]{3,2,1,0:T(8,128)S(1)}, u32[]{:S(2)}, u32[]{:S(2)}) collective-permute-start(f32[1,4,64,128]{3,2,1,0:T(8,128)S(1)} %get-tuple-element.58), channel_id=1, source_target_pairs={{0,2},{2,0},{4,6},{6,4},{8,10},{10,8},{12,14},{14,12},{1,3},{3,1},... | collective-permute-start | bytes 393224 | tf_op jit(solution)/shard_map/ppermute | solution.py:347
  6.6 13.0 %collective-permute-start.2 = (f32[1,16,128]{2,1,0:T(8,128)S(1)}, f32[1,16,128]{2,1,0:T(8,128)S(1)}, u32[]{:S(2)}, u32[]{:S(2)}) collective-permute-start(f32[1,16,128]{2,1,0:T(8,128)S(1)} %get-tuple-element.59), channel_id=1, source_target_pairs={{0,1},{1,0},{2,3},{3,2},{4,5},{5,4},{6,7},{7,6},{8,9},{9,8},{10,11... | collective-permute-start | bytes 24584 | tf_op jit(solution)/shard_map/ppermute | solution.py:348
  8.1 0.9 copy-start.1
  9.1 0.9 copy-start.2
  10.0 0.8 copy-start.3
  10.8 0.7 copy-start.5
  11.5 0.7 copy-start.6
  12.2 0.7 copy-start.7
  21.2 7.1 %collective-permute-start.3 = (f32[2,4,64,128]{3,2,1,0:T(8,128)S(1)}, f32[2,4,64,128]{3,2,1,0:T(8,128)S(1)}, u32[]{:S(2)}, u32[]{:S(2)}) collective-permute-start(f32[2,4,64,128]{3,2,1,0:T(8,128)S(1)} %get-tuple-element.62), channel_id=1, source_target_pairs={{2,4},{6,8},{10,12},{14,0},{4,2},{8,6},{12,10},{0,14},{3,5},{7,9},... | collective-permute-start | bytes 786440 | tf_op jit(solution)/shard_map/ppermute | solution.py:346
  21.9 6.4 %collective-permute-start.4 = (f32[2,4,64,128]{3,2,1,0:T(8,128)S(1)}, f32[2,4,64,128]{3,2,1,0:T(8,128)S(1)}, u32[]{:S(2)}, u32[]{:S(2)}) collective-permute-start(f32[2,4,64,128]{3,2,1,0:T(8,128)S(1)} %get-tuple-element.63), channel_id=1, source_target_pairs={{0,2},{2,0},{4,6},{6,4},{8,10},{10,8},{12,14},{14,12},{1,3},{3,1},... | collective-permute-start | bytes 786440 | tf_op jit(solution)/shard_map/ppermute | solution.py:347
  22.3 3.7 %collective-permute-start.5 = (f32[2,16,128]{2,1,0:T(8,128)S(1)}, f32[2,16,128]{2,1,0:T(8,128)S(1)}, u32[]{:S(2)}, u32[]{:S(2)}) collective-permute-start(f32[2,16,128]{2,1,0:T(8,128)S(1)} %get-tuple-element.64), channel_id=1, source_target_pairs={{0,1},{1,0},{2,3},{3,2},{4,5},{5,4},{6,7},{7,6},{8,9},{9,8},{10,11... | collective-permute-start | bytes 49160 | tf_op jit(solution)/shard_map/ppermute | solution.py:348
  30.6 7.1 %collective-permute-start.6 = (f32[2,4,64,128]{3,2,1,0:T(8,128)S(1)}, f32[2,4,64,128]{3,2,1,0:T(8,128)S(1)}, u32[]{:S(2)}, u32[]{:S(2)}) collective-permute-start(f32[2,4,64,128]{3,2,1,0:T(8,128)S(1)} %get-tuple-element.68), channel_id=1, source_target_pairs={{2,4},{6,8},{10,12},{14,0},{4,2},{8,6},{12,10},{0,14},{3,5},{7,9},... | collective-permute-start | bytes 786440 | tf_op jit(solution)/shard_map/ppermute | solution.py:346
  31.2 6.4 %collective-permute-start.7 = (f32[2,4,64,128]{3,2,1,0:T(8,128)S(1)}, f32[2,4,64,128]{3,2,1,0:T(8,128)S(1)}, u32[]{:S(2)}, u32[]{:S(2)}) collective-permute-start(f32[2,4,64,128]{3,2,1,0:T(8,128)S(1)} %get-tuple-element.69), channel_id=1, source_target_pairs={{0,2},{2,0},{4,6},{6,4},{8,10},{10,8},{12,14},{14,12},{1,3},{3,1},... | collective-permute-start | bytes 786440 | tf_op jit(solution)/shard_map/ppermute | solution.py:347
  31.2 3.7 %collective-permute-start.8 = (f32[2,16,128]{2,1,0:T(8,128)S(1)}, f32[2,16,128]{2,1,0:T(8,128)S(1)}, u32[]{:S(2)}, u32[]{:S(2)}) collective-permute-start(f32[2,16,128]{2,1,0:T(8,128)S(1)} %get-tuple-element.70), channel_id=1, source_target_pairs={{0,1},{1,0},{2,3},{3,2},{4,5},{5,4},{6,7},{7,6},{8,9},{9,8},{10,11... | collective-permute-start | bytes 49160 | tf_op jit(solution)/shard_map/ppermute | solution.py:348
  39.9 7.1 %collective-permute-start.9 = (f32[2,4,64,128]{3,2,1,0:T(8,128)S(1)}, f32[2,4,64,128]{3,2,1,0:T(8,128)S(1)}, u32[]{:S(2)}, u32[]{:S(2)}) collective-permute-start(f32[2,4,64,128]{3,2,1,0:T(8,128)S(1)} %get-tuple-element.77), channel_id=1, source_target_pairs={{2,4},{6,8},{10,12},{14,0},{4,2},{8,6},{12,10},{0,14},{3,5},{7,9},... | collective-permute-start | bytes 786440 | tf_op jit(solution)/shard_map/ppermute | solution.py:346
  40.6 6.4 %collective-permute-start.10 = (f32[2,4,64,128]{3,2,1,0:T(8,128)S(1)}, f32[2,4,64,128]{3,2,1,0:T(8,128)S(1)}, u32[]{:S(2)}, u32[]{:S(2)}) collective-permute-start(f32[2,4,64,128]{3,2,1,0:T(8,128)S(1)} %get-tuple-element.78), channel_id=1, source_target_pairs={{0,2},{2,0},{4,6},{6,4},{8,10},{10,8},{12,14},{14,12},{1,3},{3,1},... | collective-permute-start | bytes 786440 | tf_op jit(solution)/shard_map/ppermute | solution.py:347
  40.6 3.7 %collective-permute-start.11 = (f32[2,16,128]{2,1,0:T(8,128)S(1)}, f32[2,16,128]{2,1,0:T(8,128)S(1)}, u32[]{:S(2)}, u32[]{:S(2)}) collective-permute-start(f32[2,16,128]{2,1,0:T(8,128)S(1)} %get-tuple-element.79), channel_id=1, source_target_pairs={{0,1},{1,0},{2,3},{3,2},{4,5},{5,4},{6,7},{7,6},{8,9},{9,8},{10,11... | collective-permute-start | bytes 49160 | tf_op jit(solution)/shard_map/ppermute | solution.py:348
  47.0 23.2 %copy-start.4 = (f32[4,8,128]{2,1,0:T(8,128)S(1)}, f32[4,8,128]{2,1,0:T(8,128)}, u32[]{:S(2)}) copy-start(f32[4,8,128]{2,1,0:T(8,128)} %param.13) | copy-start | bytes 49156
  85.5 5.7 %collective-permute-start.12 = (f32[1,4,64,128]{3,2,1,0:T(8,128)S(1)}, f32[1,4,64,128]{3,2,1,0:T(8,128)S(1)}, u32[]{:S(2)}, u32[]{:S(2)}) collective-permute-start(f32[1,4,64,128]{3,2,1,0:T(8,128)S(1)} %get-tuple-element.84), channel_id=1, source_target_pairs={{2,4},{6,8},{10,12},{14,0},{4,2},{8,6},{12,10},{0,14},{3,5},{7,9},... | collective-permute-start | bytes 393224 | tf_op jit(solution)/shard_map/ppermute | solution.py:346
  87.0 4.2 %collective-permute-start.13 = (f32[1,4,64,128]{3,2,1,0:T(8,128)S(1)}, f32[1,4,64,128]{3,2,1,0:T(8,128)S(1)}, u32[]{:S(2)}, u32[]{:S(2)}) collective-permute-start(f32[1,4,64,128]{3,2,1,0:T(8,128)S(1)} %get-tuple-element.85), channel_id=1, source_target_pairs={{0,2},{2,0},{4,6},{6,4},{8,10},{10,8},{12,14},{14,12},{1,3},{3,1},... | collective-permute-start | bytes 393224 | tf_op jit(solution)/shard_map/ppermute | solution.py:347
  87.0 3.7 %collective-permute-start.14 = (f32[1,16,128]{2,1,0:T(8,128)S(1)}, f32[1,16,128]{2,1,0:T(8,128)S(1)}, u32[]{:S(2)}, u32[]{:S(2)}) collective-permute-start(f32[1,16,128]{2,1,0:T(8,128)S(1)} %get-tuple-element.86), channel_id=1, source_target_pairs={{0,1},{1,0},{2,3},{3,2},{4,5},{5,4},{6,7},{7,6},{8,9},{9,8},{10,11... | collective-permute-start | bytes 24584 | tf_op jit(solution)/shard_map/ppermute | solution.py:348
  92.7 5.7 %collective-permute-start.15 = (f32[1,4,64,128]{3,2,1,0:T(8,128)S(1)}, f32[1,4,64,128]{3,2,1,0:T(8,128)S(1)}, u32[]{:S(2)}, u32[]{:S(2)}) collective-permute-start(f32[1,4,64,128]{3,2,1,0:T(8,128)S(1)} %get-tuple-element.88), channel_id=1, source_target_pairs={{2,4},{6,8},{10,12},{14,0},{4,2},{8,6},{12,10},{0,14},{3,5},{7,9},... | collective-permute-start | bytes 393224 | tf_op jit(solution)/shard_map/ppermute | solution.py:346
  94.1 4.2 %collective-permute-start.16 = (f32[1,4,64,128]{3,2,1,0:T(8,128)S(1)}, f32[1,4,64,128]{3,2,1,0:T(8,128)S(1)}, u32[]{:S(2)}, u32[]{:S(2)}) collective-permute-start(f32[1,4,64,128]{3,2,1,0:T(8,128)S(1)} %get-tuple-element.89), channel_id=1, source_target_pairs={{0,2},{2,0},{4,6},{6,4},{8,10},{10,8},{12,14},{14,12},{1,3},{3,1},... | collective-permute-start | bytes 393224 | tf_op jit(solution)/shard_map/ppermute | solution.py:347
  94.1 3.7 %collective-permute-start.17 = (f32[1,16,128]{2,1,0:T(8,128)S(1)}, f32[1,16,128]{2,1,0:T(8,128)S(1)}, u32[]{:S(2)}, u32[]{:S(2)}) collective-permute-start(f32[1,16,128]{2,1,0:T(8,128)S(1)} %get-tuple-element.90), channel_id=1, source_target_pairs={{0,1},{1,0},{2,3},{3,2},{4,5},{5,4},{6,7},{7,6},{8,9},{9,8},{10,11... | collective-permute-start | bytes 24584 | tf_op jit(solution)/shard_map/ppermute | solution.py:348
  99.8 6.9 %collective-permute-start.18 = (f32[1,4,64,128]{3,2,1,0:T(8,128)S(1)}, f32[1,4,64,128]{3,2,1,0:T(8,128)S(1)}, u32[]{:S(2)}, u32[]{:S(2)}) collective-permute-start(f32[1,4,64,128]{3,2,1,0:T(8,128)S(1)} %get-tuple-element.93), channel_id=1, source_target_pairs={{2,4},{6,8},{10,12},{14,0},{4,2},{8,6},{12,10},{0,14},{3,5},{7,9},... | collective-permute-start | bytes 393224 | tf_op jit(solution)/shard_map/ppermute | solution.py:346
  101.3 5.5 %collective-permute-start.19 = (f32[1,4,64,128]{3,2,1,0:T(8,128)S(1)}, f32[1,4,64,128]{3,2,1,0:T(8,128)S(1)}, u32[]{:S(2)}, u32[]{:S(2)}) collective-permute-start(f32[1,4,64,128]{3,2,1,0:T(8,128)S(1)} %get-tuple-element.94), channel_id=1, source_target_pairs={{0,2},{2,0},{4,6},{6,4},{8,10},{10,8},{12,14},{14,12},{1,3},{3,1},... | collective-permute-start | bytes 393224 | tf_op jit(solution)/shard_map/ppermute | solution.py:347
  103.0 3.7 %collective-permute-start.20 = (f32[1,16,128]{2,1,0:T(8,128)S(1)}, f32[1,16,128]{2,1,0:T(8,128)S(1)}, u32[]{:S(2)}, u32[]{:S(2)}) collective-permute-start(f32[1,16,128]{2,1,0:T(8,128)S(1)} %get-tuple-element.95), channel_id=1, source_target_pairs={{0,1},{1,0},{2,3},{3,2},{4,5},{5,4},{6,7},{7,6},{8,9},{9,8},{10,11... | collective-permute-start | bytes 24584 | tf_op jit(solution)/shard_map/ppermute | solution.py:348
  109.0 1.3 collective-permute-start.21

commit v3 on v2

--- a/solution.py
+++ b/solution.py
@@ -102,17 +102,9 @@
     return [((count, 4, NZ, BY), F32), ((count, 4, NZ, BY), F32), ((count, 16, BY), F32)]
 
 
-def first_kernel(scal, newer, newer_out, outer, inner, strip, raw, sem):
-    copies = [
-        pltpu.make_async_copy(newer.at[pl.ds(128 * i, 128)], raw.at[pl.ds(128 * i, 128)], sem.at[i])
-        for i in range(4)
-    ]
-    for copy in copies:
-        copy.start()
-    for copy in copies:
-        copy.wait()
-    for x in range(BX):
-        newer_out[x] = raw[pl.ds(x, NZ, stride=8), :]
+def first_kernel(scal, newer, newer_out, outer, inner, strip):
+    for x in range(BX):
+        newer_out[x] = newer[pl.ds(x, NZ, stride=8), :]
     send_edges(lambda x: newer_out[x], outer, inner, strip, 0, scal)
 
 
@@ -121,30 +113,46 @@
     return high, (values - high.astype(F32)).astype(BF16)
 
 
-def prepare_kernel(scal, rz_in, rx_in, ry_in, traces_in, vel_in, older_in,
-                   vel_out, older_out, inj, pick_cell, pick_y,
-                   rz, rx, ry, traces, vel, older, at_depth, spread, sem):
-    copies = [
-        pltpu.make_async_copy(source, target, sem.at[i])
-        for i, (source, target) in enumerate(
-            ((rz_in, rz), (rx_in, rx), (ry_in, ry), (traces_in, traces), (vel_in, vel), (older_in, older))
-        )
-    ]
-    for copy in copies:
-        copy.start()
-    for copy in copies[:4]:
-        copy.wait()
-    lat_x = rx[...] - scal[2]
-    lat_y = ry[...] - scal[3]
+def block(i):
+    return pl.ds(pl.multiple_of(16 * i, 16), 16)
+
+
+def wide(row):
+    return jnp.broadcast_to(row, (16, NREC)).astype(BF16)
+
+
+def inject(n, traces, pick_cell, pick_y, spread, inj, slot=0):
+    value = traces[n : n + 1, :]
+    coarse = value.astype(BF16).astype(F32)
+    high, low = wide(coarse), wide(value - coarse)
+
+    def weigh(i, carry):
+        picked = pick_y[block(i), :]
+        spread[block(i), :] = picked * high
+        spread[block(8 + i), :] = picked * low
+        return carry
+
+    lax.fori_loop(0, 8, weigh, 0)
+    both = lax.dot_general(
+        pick_cell[...], spread[...], (((1,), (1,)), ((), ())), preferred_element_type=F32
+    )
+    for x in range(BX):
+        part = both[NZ * x : NZ * x + NZ]
+        inj[slot, x] = part[:, :BY] + part[:, BY:]
+
+
+def inject_kernel(shot, pick_cell, pick_y, inj, spread):
+    for n in range(3):
+        inject(n, shot, pick_cell, pick_y, spread, inj, n)
+
+
+def prepare_kernel(scal, shot, inj, pick_cell, pick_y, at_depth, spread):
+    code = shot[4:5, :].astype(I32)
+    lat_x = ((code >> 6) & 63) - scal[2]
+    lat_y = (code >> 12) - scal[3]
     present = (lat_x >= 0) & (lat_x < BX) & (lat_y >= 0) & (lat_y < BY)
-    depth = jnp.where(present, rz[...], -1)
+    depth = jnp.where(present, code & 63, -1)
     col = jnp.where(present, lat_y, -1)
-
-    def block(i):
-        return pl.ds(pl.multiple_of(16 * i, 16), 16)
-
-    def wide(row):
-        return jnp.broadcast_to(row, (16, NREC)).astype(BF16)
 
     def hits(i, wanted):
         number = lax.broadcasted_iota(I32, (16, NREC), 0) + 16 * i
@@ -169,45 +177,31 @@
         return carry
 
     lax.fori_loop(0, 8, columns, 0)
-    for n in range(STEPS):
-        value = traces[n : n + 1, :]
-        coarse = value.astype(BF16).astype(F32)
-        high, low = wide(coarse), wide(value - coarse)
-
-        def weigh(i, carry):
-            picked = pick_y[block(i), :]
-            spread[block(i), :] = picked * high
-            spread[block(8 + i), :] = picked * low
-            return carry
-
-        lax.fori_loop(0, 8, weigh, 0)
-        both = lax.dot_general(
-            pick_cell[...], spread[...], (((1,), (1,)), ((), ())), preferred_element_type=F32
-        )
-        for x in range(BX):
-            part = both[NZ * x : NZ * x + NZ]
-            inj[n, x] = part[:, :BY] + part[:, BY:]
-    for copy in copies[4:]:
-        copy.wait()
-    for x in range(BX):
-        vel_out[x] = vel[pl.ds(x, NZ, stride=8), :]
-        older_out[x] = older[pl.ds(x, NZ, stride=8), :]
-
-
-def forward1_kernel(scal, newer, older, vel, inj, outer, inner, strip, acc, nxt, q, outer_o, inner_o, strip_o, padded, side):
+    inject(3, shot, pick_cell, pick_y, spread, inj)
+
+
+def planes_kernel(older_in, vel_in, older, vel):
+    for x in range(BX):
+        older[x] = older_in[pl.ds(x, NZ, stride=8), :]
+        vel[x] = vel_in[pl.ds(x, NZ, stride=8), :]
+
+
+def forward1_kernel(scal, newer, older, vel, inj3, outer, inner, strip, acc, nxt, q, outer_o, inner_o, strip_o, padded, side):
     fill(padded, side, lambda x: newer[x], outer, inner, strip, 0, scal)
     for x in range(BX):
         a = vel[x] * lap(padded, side, x)
         acc[x] = a
         nxt[x] = (2.0 * newer[x] - older[x]) + a
-        q[x] = vel[x] * inj[3, x]
+        q[x] = vel[x] * inj3[0, x]
     send_edges(lambda x: nxt[x], outer_o, inner_o, strip_o, 0, scal)
     send_edges(lambda x: q[x], outer_o, inner_o, strip_o, 1, scal)
 
 
 def make_forward(moment):
-    def kernel(scal, newer, older, vel, inj, q_in, latest, later, outer, inner, strip,
-               acc, nxt, p, q, outer_o, inner_o, strip_o, padded, side):
+    def kernel(scal, newer, older, vel, inj, inj3, q_in, *rest):
+        if moment == 2:
+            later, rest = rest[0], rest[1:]
+        outer, inner, strip, acc, nxt, p, q, outer_o, inner_o, strip_o, padded, side = rest
         fill(padded, side, lambda x: newer[x], outer, inner, strip, 0, scal)
         for x in range(BX):
             a = vel[x] * lap(padded, side, x)
@@ -216,7 +210,7 @@
         send_edges(lambda x: nxt[x], outer_o, inner_o, strip_o, 0, scal)
         fill(padded, side, lambda x: q_in[x], outer, inner, strip, 1, scal)
         for x in range(BX):
-            before = 2.0 * inj[3, x] if moment == 1 else 2.0 * later[x] - latest[x]
+            before = 2.0 * inj3[0, x] if moment == 1 else 2.0 * later[x] - inj3[0, x]
             value = (before + lap(padded, side, x)) + inj[3 - moment, x]
             p[x] = value
             q[x] = vel[x] * value
@@ -232,14 +226,14 @@
     return (column >= scal[5]) & (column < scal[5] + 192) & inside_x
 
 
-def last_kernel(scal, newer, vel, inj, q_in, latest, later, acc0, acc1, acc2, outer, inner, strip, acc3, grad, padded, side, padded2, side2):
+def last_kernel(scal, newer, vel, inj, inj3, q_in, latest, later, acc0, acc1, acc2, outer, inner, strip, acc3, grad, padded, side, padded2, side2):
     fill(padded, side, lambda x: newer[x], outer, inner, strip, 0, scal)
     fill(padded2, side2, lambda x: q_in[x], outer, inner, strip, 1, scal)
     for x in range(BX):
         a = vel[x] * lap(padded, side, x)
         acc3[x] = a
         p0 = ((2.0 * later[x] - latest[x]) + lap(padded2, side2, x)) + inj[0, x]
-        total = ((a * inj[3, x] + acc2[x] * latest[x]) + acc1[x] * later[x]) + acc0[x] * p0
+        total = ((a * inj3[0, x] + acc2[x] * latest[x]) + acc1[x] * later[x]) + acc0[x] * p0
         grad[pl.ds(x, NZ, stride=8), :] = jnp.where(window(scal, x), total, 0.0)
 
 
@@ -354,37 +348,30 @@
     flat = (NZ * BX, BY)
     gx, gy = lax.axis_index("gx"), lax.axis_index("gy")
     scal = jnp.stack([gx % 2, gy, gx * BX, gy * BY, aperture_x[0], aperture_y[0]]).astype(I32)
-    newer, *e = call(
-        first_kernel, [FIELD] + edges(1), [pltpu.VMEM(flat, F32), pltpu.SemaphoreType.DMA((4,))]
-    )(scal, newer_field.reshape(flat), smem=1, hbm=1)
-    e = exchange(*e)
-    vel, older, inj, pick_cell, pick_y = call(
+    newer, *e = call(first_kernel, [FIELD] + edges(1))(scal, newer_field.reshape(flat), smem=1)
+    e = exchange(*e)
+    code = receiver_z | (receiver_x << 6) | (receiver_y << 12)
+    shot = jnp.concatenate([traces[0], code.astype(F32)], axis=0)
+    inj3, pick_cell, pick_y = call(
         prepare_kernel,
-        [FIELD, FIELD, ((4, BX, NZ, BY), F32), ((512, NREC), BF16), ((BY, NREC), BF16)],
-        [pltpu.VMEM((1, NREC), I32)] * 3
-        + [
-            pltpu.VMEM((4, NREC), F32),
-            pltpu.VMEM(flat, F32),
-            pltpu.VMEM(flat, F32),
-            pltpu.VMEM((NZ, NREC), BF16),
-            pltpu.VMEM((2 * BY, NREC), BF16),
-            pltpu.SemaphoreType.DMA((6,)),
-        ],
-        limit=40,
-    )(scal, receiver_z, receiver_x, receiver_y, traces[0], velocity.reshape(flat),
-      older_field.reshape(flat), smem=1, hbm=6)
+        [((1, BX, NZ, BY), F32), ((512, NREC), BF16), ((BY, NREC), BF16)],
+        [pltpu.VMEM((NZ, NREC), BF16), pltpu.VMEM((2 * BY, NREC), BF16)],
+    )(scal, shot, smem=1)
+    older, vel = call(planes_kernel, [FIELD, FIELD])(older_field.reshape(flat), velocity.reshape(flat))
     acc0, u1, q, *e = call(forward1_kernel, [FIELD] * 3 + edges(2), [PADDED, SIDE])(
-        scal, newer, older, vel, inj, *e, smem=1)
-    e = exchange(*e)
+        scal, newer, older, vel, inj3, *e, smem=1)
+    e = exchange(*e)
+    inj, = call(inject_kernel, [((3, BX, NZ, BY), F32)], [pltpu.VMEM((2 * BY, NREC), BF16)], flops=2_000_000_000)(
+        shot, pick_cell, pick_y)
     acc1, u2, p2, q, *e = call(make_forward(1), [FIELD] * 4 + edges(2), [PADDED, SIDE])(
-        scal, u1, newer, vel, inj, q, q, q, *e, smem=1)
+        scal, u1, newer, vel, inj, inj3, q, *e, smem=1)
     e = exchange(*e)
     acc2, u3, p1, q, *e = call(
-        forward2_kernel, [FIELD] * 4 + edges(2), [PADDED, SIDE])(
-        scal, u2, u1, vel, inj, q, p2, *e, smem=1)
+        make_forward(2), [FIELD] * 4 + edges(2), [PADDED, SIDE])(
+        scal, u2, u1, vel, inj, inj3, q, p2, *e, smem=1)
     e = exchange(*e)
     acc3, grad = call(last_kernel, [FIELD, (flat, F32)], [PADDED, SIDE, PADDED, SIDE])(
-        scal, u3, vel, inj, q, p2, p1, acc0, acc1, acc2, *e, smem=1)
+        scal, u3, vel, inj, inj3, q, p2, p1, acc0, acc1, acc2, *e, smem=1)
     parts = lax.all_to_all(grad.reshape(16, 4, BX, BY), "shot", 0, 0, tiled=True)
     scaled, copies, dot = call(
         gradient_kernel, [((32, BY), F32), (flat, F32), ((8, BY), F32)])(
@@ -416,22 +403,6 @@
     image, residual = call(finish_kernel, [((32, BY), F32), ((4, NREC), F32)])(
         stats, predicted, scaled, traces[0])
     return image.reshape(4, BX, BY), residual[None]
-
-
-def forward2_kernel(scal, newer, older, vel, inj, q_in, later, outer, inner, strip,
-                       acc, nxt, p, q, outer_o, inner_o, strip_o, padded, side):
-    fill(padded, side, lambda x: newer[x], outer, inner, strip, 0, scal)
-    for x in range(BX):
-        a = vel[x] * lap(padded, side, x)
-        acc[x] = a
-        nxt[x] = (2.0 * newer[x] - older[x]) + a
-    send_edges(lambda x: nxt[x], outer_o, inner_o, strip_o, 0, scal)
-    fill(padded, side, lambda x: q_in[x], outer, inner, strip, 1, scal)
-    for x in range(BX):
-        value = ((2.0 * later[x] - inj[3, x]) + lap(padded, side, x)) + inj[1, x]
-        p[x] = value
-        q[x] = vel[x] * value
-    send_edges(lambda x: q[x], outer_o, inner_o, strip_o, 1, scal)
 
 
 def solution(mesh):

time: 137 us -> 131 us (0.956)
  waiting for transfers between devices: 29.2 us -> 23.4 us
  starting transfers between devices: 13.4 us -> 16.4 us
  local copies, waits for them, and re-layouts: 5.79 us -> 2.94 us
  Pallas kernels: 25.1 us -> 23.5 us
  other arithmetic: 0 us -> 1.53 us
    ppermute x7, waiting for transfers between devices: 19.1 us -> 15.9 us  [exchange(): lax.ppermute(strip, 'gy', [(0, 1), (1, 0)])]
    ppermute x7, starting transfers between devices: 8.87 us -> 11.9 us  [exchange(): lax.ppermute(outer, 'gx', across)]
    unnamed x16 -> x10, local copies, waits for them, and re-layouts: 5.7 us -> 2.85 us
    ppermute x7, waiting for transfers between devices: 8.89 us -> 6.25 us  [exchange(): lax.ppermute(outer, 'gx', across)]
    pallas_call x17 -> x19, Pallas kernels: 25.1 us -> 23.5 us  [run(): pl.pallas_call(kernel, out_shape=[jax.ShapeDtypeStruct(s, d) for s, d in...]
  transfers between devices with their start and end apart: 22 -> 22, of which waited for: 12 -> 9; matrix products, arithmetic and copies ran while one was open for 0% -> 1% of each run, Pallas kernels for 7% -> 6%
where the time goes in v3:
time: 131 us
  blocking collectives  61.1 us (47%)
  Pallas kernels  23.5 us (18%)
  waiting for transfers between devices  23.4 us (18%)
  starting transfers between devices  16.4 us (13%)
  local copies, waits for them, and re-layouts  2.94 us (2%)
  between operations  2.09 us (2%)
  other arithmetic  1.53 us (1%)
    pallas_call x19, Pallas kernels, run(): pl.pallas_call(kernel, out_shape=[jax.ShapeDtypeStruct(s, d) for s, d in...  23.5 us
    all_to_all x1, blocking collectives, on_device(): lax.all_to_all(grad.reshape(16, 4, BX, BY), 'shot', 0, 0, tiled=True)  21.1 us
    ppermute x7, waiting for transfers between devices, exchange(): lax.ppermute(strip, 'gy', [(0, 1), (1, 0)])  15.9 us
    all_to_all x1, blocking collectives, on_device(): stats = lax.all_to_all(stats, 'shot', 0, 0, tiled=True)  14.7 us
    all_to_all x1, blocking collectives, on_device(): lax.all_to_all(copies.reshape(16, 4, BX, BY), 'shot', 0, 0, tiled=True)  14.5 us
    ppermute x7, starting transfers between devices, exchange(): lax.ppermute(outer, 'gx', across)  11.9 us
    all_to_all x1, blocking collectives, on_device(): lax.all_to_all(payload, ('gx', 'gy'), 0, 0, axis_index_groups=same_core,...  10.8 us
    ppermute x7, waiting for transfers between devices, exchange(): lax.ppermute(outer, 'gx', across)  6.25 us
  transfers between devices with their start and end apart: 22, of which 9 were waited for; matrix products, arithmetic and copies ran while one was open for 1% of the time, Pallas kernels for 6%

profile of v3, /device:TPU:32, one launch (start us, length us, event | category | flops | bytes accessed | tf_op | source)
XLA Modules:
  0.0 130.9 jit_solution(5333861979791390525)
XLA Ops:
  2.0 1.0 copy-done
  3.0 0.7 shard_map.113
  3.7 1.6 %collective-permute-start.2 = (f32[1,16,128]{2,1,0:T(8,128)S(1)}, f32[1,16,128]{2,1,0:T(8,128)S(1)}, u32[]{:S(2)}, u32[]{:S(2)}) collective-permute-start(f32[1,16,128]{2,1,0:T(8,128)S(1)} %get-tuple-element.59), channel_id=1, source_target_pairs={{0,1},{1,0},{2,3},{3,2},{4,5},{5,4},{6,7},{7,6},{8,9},{9,8},{10,11... | collective-permute-start | bytes 24584 | tf_op jit(solution)/shard_map/ppermute | solution.py:342
  5.2 2.2 %collective-permute-start = (f32[1,4,64,128]{3,2,1,0:T(8,128)S(1)}, f32[1,4,64,128]{3,2,1,0:T(8,128)S(1)}, u32[]{:S(2)}, u32[]{:S(2)}) collective-permute-start(f32[1,4,64,128]{3,2,1,0:T(8,128)S(1)} %get-tuple-element.57), channel_id=1, source_target_pairs={{2,4},{6,8},{10,12},{14,0},{4,2},{8,6},{12,10},{0,14},{3,5},{7,9},... | collective-permute-start | bytes 393224 | tf_op jit(solution)/shard_map/ppermute | solution.py:340
  7.4 0.7 or_convert_fusion
  8.2 0.8 pad_maximum_fusion.shot
  8.9 1.9 %shard_map.115 = (f32[1,8,64,128]{3,2,1,0:T(8,128)S(1)}, bf16[512,2048]{1,0:T(8,128)(2,1)S(1)}, bf16[128,2048]{1,0:T(8,128)(2,1)S(1)}) custom-call(s32[6]{0:T(128)S(1)} %stack.19.scal, f32[5,2048]{1,0:T(8,128)S(1)} %pad_maximum_fusion.shot), custom_call_target="tpu_custom_call" | custom-call | flops 10000000 | bytes 2000000 | tf_op jit(solution)/shard_map/pallas_call | solution.py:20
  10.8 0.9 copy-done.1
  11.8 0.9 copy-done.2
  12.8 1.5 %shard_map.116 = (f32[8,64,128]{2,1,0:T(8,128)S(1)}, f32[8,64,128]{2,1,0:T(8,128)S(1)}, f32[8,64,128]{2,1,0:T(8,128)S(1)}, f32[2,4,64,128]{3,2,1,0:T(8,128)S(1)}...) custom-call(s32[6]{0:T(128)S(1)} %stack.19.scal, f32[8,64,128]{2,1,0:T(8,128)S(1)} %get-tuple-element.53.newer.older, ...), custom_call_target="tpu_custom_call" | custom-call | flops 10000000 | bytes 2000000 | tf_op jit(solution)/shard_map/pallas_call | solution.py:20
  14.4 1.0 collective-permute-start.3
  15.4 0.3 collective-permute-start.4
  15.7 0.5 collective-permute-start.5
  16.2 3.6 %shard_map.117.inj = f32[3,8,64,128]{3,2,1,0:T(8,128)S(1)} custom-call(f32[5,2048]{1,0:T(8,128)S(1)} %pad_maximum_fusion.shot, bf16[512,2048]{1,0:T(8,128)(2,1)S(1)} %get-tuple-element.61.pick_cell.rest_0_, bf16[128,2048]{1,0:T(8,128)(2,1)S(1)} %get-tuple-element.62.pick_y.rest_1_), custom_call_target="tpu_custom_call" | custom-call | flops 2000000000 | bytes 2000000 | tf_op jit(solution)/shard_map/pallas_call | solution.py:20
  19.9 1.6 %collective-permute-done.3.rest_0_ = f32[2,4,64,128]{3,2,1,0:T(8,128)S(1)} collective-permute-done((f32[2,4,64,128]{3,2,1,0:T(8,128)S(1)}, f32[2,4,64,128]{3,2,1,0:T(8,128)S(1)}, u32[]{:S(2)}, u32[]{:S(2)}) %collective-permute-start.3) | collective-permute-done | bytes 262176 | tf_op jit(solution)/shard_map/ppermute | solution.py:340
  21.5 2.2 %shard_map.118 = (f32[8,64,128]{2,1,0:T(8,128)S(1)}, f32[8,64,128]{2,1,0:T(8,128)S(1)}, f32[8,64,128]{2,1,0:T(8,128)S(1)}, f32[8,64,128]{2,1,0:T(8,128)S(1)}, f3...) custom-call(s32[6]{0:T(128)S(1)} %stack.19.scal, ...), custom_call_target="tpu_custom_call" | custom-call | flops 10000000 | bytes 2000000 | tf_op jit(solution)/shard_map/pallas_call | solution.py:20
  23.7 1.0 collective-permute-start.6
  24.7 0.5 collective-permute-start.8
  25.3 3.2 %collective-permute-done.8.rest_3_ = f32[2,16,128]{2,1,0:T(8,128)S(1)} collective-permute-done((f32[2,16,128]{2,1,0:T(8,128)S(1)}, f32[2,16,128]{2,1,0:T(8,128)S(1)}, u32[]{:S(2)}, u32[]{:S(2)}) %collective-permute-start.8) | collective-permute-done | bytes 16416 | tf_op jit(solution)/shard_map/ppermute | solution.py:342
  28.5 2.3 %collective-permute-done.6.rest_1_ = f32[2,4,64,128]{3,2,1,0:T(8,128)S(1)} collective-permute-done((f32[2,4,64,128]{3,2,1,0:T(8,128)S(1)}, f32[2,4,64,128]{3,2,1,0:T(8,128)S(1)}, u32[]{:S(2)}, u32[]{:S(2)}) %collective-permute-start.6) | collective-permute-done | bytes 262176 | tf_op jit(solution)/shard_map/ppermute | solution.py:340
  30.8 2.3 %shard_map.119 = (f32[8,64,128]{2,1,0:T(8,128)S(1)}, f32[8,64,128]{2,1,0:T(8,128)S(1)}, f32[8,64,128]{2,1,0:T(8,128)S(1)}, f32[8,64,128]{2,1,0:T(8,128)S(1)}, f3...) custom-call(s32[6]{0:T(128)S(1)} %stack.19.scal, ...), custom_call_target="tpu_custom_call" | custom-call | flops 10000000 | bytes 2000000 | tf_op jit(solution)/shard_map/pallas_call | solution.py:20
  33.0 1.2 collective-permute-start.9
  34.3 0.5 collective-permute-start.11
  34.8 3.2 %collective-permute-done.11.strip = f32[2,16,128]{2,1,0:T(8,128)S(1)} collective-permute-done((f32[2,16,128]{2,1,0:T(8,128)S(1)}, f32[2,16,128]{2,1,0:T(8,128)S(1)}, u32[]{:S(2)}, u32[]{:S(2)}) %collective-permute-start.11) | collective-permute-done | bytes 16416 | tf_op jit(solution)/shard_map/ppermute | solution.py:342
  38.0 2.3 %collective-permute-done.9.outer = f32[2,4,64,128]{3,2,1,0:T(8,128)S(1)} collective-permute-done((f32[2,4,64,128]{3,2,1,0:T(8,128)S(1)}, f32[2,4,64,128]{3,2,1,0:T(8,128)S(1)}, u32[]{:S(2)}, u32[]{:S(2)}) %collective-permute-start.9) | collective-permute-done | bytes 262176 | tf_op jit(solution)/shard_map/ppermute | solution.py:340
  40.3 2.1 %shard_map.120 = (f32[8,64,128]{2,1,0:T(8,128)S(1)}, f32[512,128]{1,0:T(8,128)S(1)}) custom-call(s32[6]{0:T(128)S(1)} %stack.19.scal, f32[8,64,128]{2,1,0:T(8,128)S(1)} %get-tuple-element.73.newer, f32[8,64,128]{2,1,0:T(8,128)S(1)} %get-tuple-element.55.vel, f32[3,8,64,128]{3,2,1,0:T(8,128)S(1)} %shard_map.117.inj, ...), custom_call_target="tpu_custom_call" | custom-call | flops 10000000 | bytes 2000000 | tf_op jit(solution)/shard_map/pallas_call | solution.py:20
  42.5 21.1 %all_to_all.20 = f32[16,4,8,128]{3,2,1,0:T(8,128)S(1)} all-to-all(f32[16,4,8,128]{3,2,1,0:T(8,128)S(1)} %bitcast.20), channel_id=1, replica_groups=mesh['shot'=16,'gx'=8,'gy'=2] {'shot'}, dimensions={0} | all-to-all | bytes 524288 | tf_op jit(solution)/shard_map/all_to_all | solution.py:375
  63.6 14.5 %all_to_all.21 = f32[16,4,8,128]{3,2,1,0:T(8,128)S(1)} all-to-all(f32[16,4,8,128]{3,2,1,0:T(8,128)S(1)} %bitcast.21), channel_id=1, replica_groups=mesh['shot'=16,'gx'=8,'gy'=2] {'shot'}, dimensions={0} | all-to-all | bytes 524288 | tf_op jit(solution)/shard_map/all_to_all | solution.py:379
  78.2 0.7 shard_map.122
  78.9 2.4 %collective-permute-start.12 = (f32[1,4,64,128]{3,2,1,0:T(8,128)S(1)}, f32[1,4,64,128]{3,2,1,0:T(8,128)S(1)}, u32[]{:S(2)}, u32[]{:S(2)}) collective-permute-start(f32[1,4,64,128]{3,2,1,0:T(8,128)S(1)} %get-tuple-element.86), channel_id=1, source_target_pairs={{2,4},{6,8},{10,12},{14,0},{4,2},{8,6},{12,10},{0,14},{3,5},{7,9},... | collective-permute-start | bytes 393224 | tf_op jit(solution)/shard_map/ppermute | solution.py:340
  81.2 0.2 collective-permute-start.14
  81.4 3.4 %collective-permute-done.14.strip = f32[1,16,128]{2,1,0:T(8,128)S(1)} collective-permute-done((f32[1,16,128]{2,1,0:T(8,128)S(1)}, f32[1,16,128]{2,1,0:T(8,128)S(1)}, u32[]{:S(2)}, u32[]{:S(2)}) %collective-permute-start.14) | collective-permute-done | bytes 8224 | tf_op jit(solution)/shard_map/ppermute | solution.py:342
  84.9 1.4 %shard_map.123 = (f32[8,64,128]{2,1,0:T(8,128)S(1)}, f32[1,4,64,128]{3,2,1,0:T(8,128)S(1)}, f32[1,4,64,128]{3,2,1,0:T(8,128)S(1)}, f32[1,16,128]{2,1,0:T(8,128)S(1)}) custom-call(s32[6]{0:T(128)S(1)} %stack.19.scal, f32[8,64,128]{2,1,0:T(8,128)S(1)} %get-tuple-element.84.now.before.field, f32[8,64,128]{2,1,0:T(8,128)S(1)} %get-tuple-element.84.now.before.field, ...), custom_call_target="tpu_custom_call" | custom-call | flops 10000000 | bytes 2000000 | tf_op jit(solution)/shard_map/pallas_call | solution.py:20
  86.3 2.0 %collective-permute-start.15 = (f32[1,4,64,128]{3,2,1,0:T(8,128)S(1)}, f32[1,4,64,128]{3,2,1,0:T(8,128)S(1)}, u32[]{:S(2)}, u32[]{:S(2)}) collective-permute-start(f32[1,4,64,128]{3,2,1,0:T(8,128)S(1)} %get-tuple-element.90), channel_id=1, source_target_pairs={{2,4},{6,8},{10,12},{14,0},{4,2},{8,6},{12,10},{0,14},{3,5},{7,9},... | collective-permute-start | bytes 393224 | tf_op jit(solution)/shard_map/ppermute | solution.py:340
  88.3 0.2 collective-permute-start.17
  88.6 3.4 %collective-permute-done.17.strip = f32[1,16,128]{2,1,0:T(8,128)S(1)} collective-permute-done((f32[1,16,128]{2,1,0:T(8,128)S(1)}, f32[1,16,128]{2,1,0:T(8,128)S(1)}, u32[]{:S(2)}, u32[]{:S(2)}) %collective-permute-start.17) | collective-permute-done | bytes 8224 | tf_op jit(solution)/shard_map/ppermute | solution.py:342
  92.0 1.4 %shard_map.124 = (f32[8,64,128]{2,1,0:T(8,128)S(1)}, f32[1,4,64,128]{3,2,1,0:T(8,128)S(1)}, f32[1,4,64,128]{3,2,1,0:T(8,128)S(1)}, f32[1,16,128]{2,1,0:T(8,128)S(1)}) custom-call(s32[6]{0:T(128)S(1)} %stack.19.scal, f32[8,64,128]{2,1,0:T(8,128)S(1)} %get-tuple-element.89.now.field.before, f32[8,64,128]{2,1,0:T(8,128)S(1)} %get-tuple-element.84.now.before.field, ...), custom_call_target="tpu_custom_call" | custom-call | flops 10000000 | bytes 2000000 | tf_op jit(solution)/shard_map/pallas_call | solution.py:20
  93.4 2.0 %collective-permute-start.18 = (f32[1,4,64,128]{3,2,1,0:T(8,128)S(1)}, f32[1,4,64,128]{3,2,1,0:T(8,128)S(1)}, u32[]{:S(2)}, u32[]{:S(2)}) collective-permute-start(f32[1,4,64,128]{3,2,1,0:T(8,128)S(1)} %get-tuple-element.95), channel_id=1, source_target_pairs={{2,4},{6,8},{10,12},{14,0},{4,2},{8,6},{12,10},{0,14},{3,5},{7,9},... | collective-permute-start | bytes 393224 | tf_op jit(solution)/shard_map/ppermute | solution.py:340
  95.5 0.8 shard_map.125.rest_2_
  96.3 0.8 shard_map.126.rest_3_
  97.0 0.5 collective-permute-start.20
  97.6 0.8 shard_map.127.rest_4_
  98.4 2.6 %collective-permute-done.20.strip = f32[1,16,128]{2,1,0:T(8,128)S(1)} collective-permute-done((f32[1,16,128]{2,1,0:T(8,128)S(1)}, f32[1,16,128]{2,1,0:T(8,128)S(1)}, u32[]{:S(2)}, u32[]{:S(2)}) %collective-permute-start.20) | collective-permute-done | bytes 8224 | tf_op jit(solution)/shard_map/ppermute | solution.py:342
  101.0 2.2 %shard_map.128.mine = f32[72,128]{1,0:T(8,128)S(1)} custom-call(s32[6]{0:T(128)S(1)} %stack.19.scal, f32[8,64,128]{2,1,0:T(8,128)S(1)} %get-tuple-element.93.field.now, f32[8,64,128]{2,1,0:T(8,128)S(1)} %get-tuple-element.89.now.field.before, f32[8,64,128]{2,1,0:T(8,128)S(1)} %get-tuple-element.85.source, f32[8,64,128]{2,1,0:T(8,128)S(1)} %get-tuple-element.94.acc, ...), custom_call_target="tpu_custom_call" | custom-call | flops 10000000 | bytes 2000000 | tf_op jit(solution)/shard_map/pallas_call | solution.py:20
  103.4 1.2 collective-permute-done.21.theirs
  104.6 10.8 %all_to_all.22.arrived = f32[8,72,128]{2,1,0:T(8,128)S(1)} all-to-all(f32[8,72,128]{2,1,0:T(8,128)S(1)} %shard_map.129), channel_id=1, replica_groups={{0,1,4,5,8,9,12,13},{2,3,6,7,10,11,14,15},{16,17,20,21,24,25,28,29},{18..., dimensions={0} | all-to-all | bytes 589824 | tf_op jit(solution)/shard_map/all_to_all | solution.py:400
  115.4 14.7 %all_to_all.23.stats = f32[16,8,128]{2,1,0:T(8,128)S(1)} all-to-all(f32[16,8,128]{2,1,0:T(8,128)S(1)} %get-tuple-element.99), channel_id=1, replica_groups=mesh['shot'=16,'gx'=8,'gy'=2] {'shot'}, dimensions={0} | all-to-all | bytes 131072 | tf_op jit(solution)/shard_map/all_to_all | solution.py:402
  130.1 0.8 shard_map.131
  (32 shorter events, 0.4 us)
Async XLA Ops:
  2.0 1.0 copy-start
  3.7 9.2 %collective-permute-start.2 = (f32[1,16,128]{2,1,0:T(8,128)S(1)}, f32[1,16,128]{2,1,0:T(8,128)S(1)}, u32[]{:S(2)}, u32[]{:S(2)}) collective-permute-start(f32[1,16,128]{2,1,0:T(8,128)S(1)} %get-tuple-element.59), channel_id=1, source_target_pairs={{0,1},{1,0},{2,3},{3,2},{4,5},{5,4},{6,7},{7,6},{8,9},{9,8},{10,11... | collective-permute-start | bytes 24584 | tf_op jit(solution)/shard_map/ppermute | solution.py:342
  5.2 7.6 %collective-permute-start = (f32[1,4,64,128]{3,2,1,0:T(8,128)S(1)}, f32[1,4,64,128]{3,2,1,0:T(8,128)S(1)}, u32[]{:S(2)}, u32[]{:S(2)}) collective-permute-start(f32[1,4,64,128]{3,2,1,0:T(8,128)S(1)} %get-tuple-element.57), channel_id=1, source_target_pairs={{2,4},{6,8},{10,12},{14,0},{4,2},{8,6},{12,10},{0,14},{3,5},{7,9},... | collective-permute-start | bytes 393224 | tf_op jit(solution)/shard_map/ppermute | solution.py:340
  7.4 5.4 %collective-permute-start.1 = (f32[1,4,64,128]{3,2,1,0:T(8,128)S(1)}, f32[1,4,64,128]{3,2,1,0:T(8,128)S(1)}, u32[]{:S(2)}, u32[]{:S(2)}) collective-permute-start(f32[1,4,64,128]{3,2,1,0:T(8,128)S(1)} %get-tuple-element.58), channel_id=1, source_target_pairs={{0,2},{2,0},{4,6},{6,4},{8,10},{10,8},{12,14},{14,12},{1,3},{3,1},... | collective-permute-start | bytes 393224 | tf_op jit(solution)/shard_map/ppermute | solution.py:341
  10.8 1.0 copy-start.1
  11.8 0.9 copy-start.2
  14.4 7.1 %collective-permute-start.3 = (f32[2,4,64,128]{3,2,1,0:T(8,128)S(1)}, f32[2,4,64,128]{3,2,1,0:T(8,128)S(1)}, u32[]{:S(2)}, u32[]{:S(2)}) collective-permute-start(f32[2,4,64,128]{3,2,1,0:T(8,128)S(1)} %get-tuple-element.64), channel_id=1, source_target_pairs={{2,4},{6,8},{10,12},{14,0},{4,2},{8,6},{12,10},{0,14},{3,5},{7,9},... | collective-permute-start | bytes 786440 | tf_op jit(solution)/shard_map/ppermute | solution.py:340
  15.4 6.1 %collective-permute-start.4 = (f32[2,4,64,128]{3,2,1,0:T(8,128)S(1)}, f32[2,4,64,128]{3,2,1,0:T(8,128)S(1)}, u32[]{:S(2)}, u32[]{:S(2)}) collective-permute-start(f32[2,4,64,128]{3,2,1,0:T(8,128)S(1)} %get-tuple-element.65), channel_id=1, source_target_pairs={{0,2},{2,0},{4,6},{6,4},{8,10},{10,8},{12,14},{14,12},{1,3},{3,1},... | collective-permute-start | bytes 786440 | tf_op jit(solution)/shard_map/ppermute | solution.py:341
  15.7 4.2 %collective-permute-start.5 = (f32[2,16,128]{2,1,0:T(8,128)S(1)}, f32[2,16,128]{2,1,0:T(8,128)S(1)}, u32[]{:S(2)}, u32[]{:S(2)}) collective-permute-start(f32[2,16,128]{2,1,0:T(8,128)S(1)} %get-tuple-element.66), channel_id=1, source_target_pairs={{0,1},{1,0},{2,3},{3,2},{4,5},{5,4},{6,7},{7,6},{8,9},{9,8},{10,11... | collective-permute-start | bytes 49160 | tf_op jit(solution)/shard_map/ppermute | solution.py:342
  23.7 7.1 %collective-permute-start.6 = (f32[2,4,64,128]{3,2,1,0:T(8,128)S(1)}, f32[2,4,64,128]{3,2,1,0:T(8,128)S(1)}, u32[]{:S(2)}, u32[]{:S(2)}) collective-permute-start(f32[2,4,64,128]{3,2,1,0:T(8,128)S(1)} %get-tuple-element.70), channel_id=1, source_target_pairs={{2,4},{6,8},{10,12},{14,0},{4,2},{8,6},{12,10},{0,14},{3,5},{7,9},... | collective-permute-start | bytes 786440 | tf_op jit(solution)/shard_map/ppermute | solution.py:340
  24.7 6.1 %collective-permute-start.7 = (f32[2,4,64,128]{3,2,1,0:T(8,128)S(1)}, f32[2,4,64,128]{3,2,1,0:T(8,128)S(1)}, u32[]{:S(2)}, u32[]{:S(2)}) collective-permute-start(f32[2,4,64,128]{3,2,1,0:T(8,128)S(1)} %get-tuple-element.71), channel_id=1, source_target_pairs={{0,2},{2,0},{4,6},{6,4},{8,10},{10,8},{12,14},{14,12},{1,3},{3,1},... | collective-permute-start | bytes 786440 | tf_op jit(solution)/shard_map/ppermute | solution.py:341
  24.7 3.7 %collective-permute-start.8 = (f32[2,16,128]{2,1,0:T(8,128)S(1)}, f32[2,16,128]{2,1,0:T(8,128)S(1)}, u32[]{:S(2)}, u32[]{:S(2)}) collective-permute-start(f32[2,16,128]{2,1,0:T(8,128)S(1)} %get-tuple-element.72), channel_id=1, source_target_pairs={{0,1},{1,0},{2,3},{3,2},{4,5},{5,4},{6,7},{7,6},{8,9},{9,8},{10,11... | collective-permute-start | bytes 49160 | tf_op jit(solution)/shard_map/ppermute | solution.py:342
  33.0 7.3 %collective-permute-start.9 = (f32[2,4,64,128]{3,2,1,0:T(8,128)S(1)}, f32[2,4,64,128]{3,2,1,0:T(8,128)S(1)}, u32[]{:S(2)}, u32[]{:S(2)}) collective-permute-start(f32[2,4,64,128]{3,2,1,0:T(8,128)S(1)} %get-tuple-element.79), channel_id=1, source_target_pairs={{2,4},{6,8},{10,12},{14,0},{4,2},{8,6},{12,10},{0,14},{3,5},{7,9},... | collective-permute-start | bytes 786440 | tf_op jit(solution)/shard_map/ppermute | solution.py:340
  34.3 6.1 %collective-permute-start.10 = (f32[2,4,64,128]{3,2,1,0:T(8,128)S(1)}, f32[2,4,64,128]{3,2,1,0:T(8,128)S(1)}, u32[]{:S(2)}, u32[]{:S(2)}) collective-permute-start(f32[2,4,64,128]{3,2,1,0:T(8,128)S(1)} %get-tuple-element.80), channel_id=1, source_target_pairs={{0,2},{2,0},{4,6},{6,4},{8,10},{10,8},{12,14},{14,12},{1,3},{3,1},... | collective-permute-start | bytes 786440 | tf_op jit(solution)/shard_map/ppermute | solution.py:341
  34.3 3.7 %collective-permute-start.11 = (f32[2,16,128]{2,1,0:T(8,128)S(1)}, f32[2,16,128]{2,1,0:T(8,128)S(1)}, u32[]{:S(2)}, u32[]{:S(2)}) collective-permute-start(f32[2,16,128]{2,1,0:T(8,128)S(1)} %get-tuple-element.81), channel_id=1, source_target_pairs={{0,1},{1,0},{2,3},{3,2},{4,5},{5,4},{6,7},{7,6},{8,9},{9,8},{10,11... | collective-permute-start | bytes 49160 | tf_op jit(solution)/shard_map/ppermute | solution.py:342
  40.3 23.2 %copy-start.4 = (f32[4,8,128]{2,1,0:T(8,128)S(1)}, f32[4,8,128]{2,1,0:T(8,128)}, u32[]{:S(2)}) copy-start(f32[4,8,128]{2,1,0:T(8,128)} %param.13) | copy-start | bytes 49156
  78.9 6.0 %collective-permute-start.12 = (f32[1,4,64,128]{3,2,1,0:T(8,128)S(1)}, f32[1,4,64,128]{3,2,1,0:T(8,128)S(1)}, u32[]{:S(2)}, u32[]{:S(2)}) collective-permute-start(f32[1,4,64,128]{3,2,1,0:T(8,128)S(1)} %get-tuple-element.86), channel_id=1, source_target_pairs={{2,4},{6,8},{10,12},{14,0},{4,2},{8,6},{12,10},{0,14},{3,5},{7,9},... | collective-permute-start | bytes 393224 | tf_op jit(solution)/shard_map/ppermute | solution.py:340
  81.2 3.7 %collective-permute-start.13 = (f32[1,4,64,128]{3,2,1,0:T(8,128)S(1)}, f32[1,4,64,128]{3,2,1,0:T(8,128)S(1)}, u32[]{:S(2)}, u32[]{:S(2)}) collective-permute-start(f32[1,4,64,128]{3,2,1,0:T(8,128)S(1)} %get-tuple-element.87), channel_id=1, source_target_pairs={{0,2},{2,0},{4,6},{6,4},{8,10},{10,8},{12,14},{14,12},{1,3},{3,1},... | collective-permute-start | bytes 393224 | tf_op jit(solution)/shard_map/ppermute | solution.py:341
  81.2 3.7 %collective-permute-start.14 = (f32[1,16,128]{2,1,0:T(8,128)S(1)}, f32[1,16,128]{2,1,0:T(8,128)S(1)}, u32[]{:S(2)}, u32[]{:S(2)}) collective-permute-start(f32[1,16,128]{2,1,0:T(8,128)S(1)} %get-tuple-element.88), channel_id=1, source_target_pairs={{0,1},{1,0},{2,3},{3,2},{4,5},{5,4},{6,7},{7,6},{8,9},{9,8},{10,11... | collective-permute-start | bytes 24584 | tf_op jit(solution)/shard_map/ppermute | solution.py:342
  86.3 5.7 %collective-permute-start.15 = (f32[1,4,64,128]{3,2,1,0:T(8,128)S(1)}, f32[1,4,64,128]{3,2,1,0:T(8,128)S(1)}, u32[]{:S(2)}, u32[]{:S(2)}) collective-permute-start(f32[1,4,64,128]{3,2,1,0:T(8,128)S(1)} %get-tuple-element.90), channel_id=1, source_target_pairs={{2,4},{6,8},{10,12},{14,0},{4,2},{8,6},{12,10},{0,14},{3,5},{7,9},... | collective-permute-start | bytes 393224 | tf_op jit(solution)/shard_map/ppermute | solution.py:340
  88.3 3.7 %collective-permute-start.16 = (f32[1,4,64,128]{3,2,1,0:T(8,128)S(1)}, f32[1,4,64,128]{3,2,1,0:T(8,128)S(1)}, u32[]{:S(2)}, u32[]{:S(2)}) collective-permute-start(f32[1,4,64,128]{3,2,1,0:T(8,128)S(1)} %get-tuple-element.91), channel_id=1, source_target_pairs={{0,2},{2,0},{4,6},{6,4},{8,10},{10,8},{12,14},{14,12},{1,3},{3,1},... | collective-permute-start | bytes 393224 | tf_op jit(solution)/shard_map/ppermute | solution.py:341
  88.3 3.7 %collective-permute-start.17 = (f32[1,16,128]{2,1,0:T(8,128)S(1)}, f32[1,16,128]{2,1,0:T(8,128)S(1)}, u32[]{:S(2)}, u32[]{:S(2)}) collective-permute-start(f32[1,16,128]{2,1,0:T(8,128)S(1)} %get-tuple-element.92), channel_id=1, source_target_pairs={{0,1},{1,0},{2,3},{3,2},{4,5},{5,4},{6,7},{7,6},{8,9},{9,8},{10,11... | collective-permute-start | bytes 24584 | tf_op jit(solution)/shard_map/ppermute | solution.py:342
  93.4 7.6 %collective-permute-start.18 = (f32[1,4,64,128]{3,2,1,0:T(8,128)S(1)}, f32[1,4,64,128]{3,2,1,0:T(8,128)S(1)}, u32[]{:S(2)}, u32[]{:S(2)}) collective-permute-start(f32[1,4,64,128]{3,2,1,0:T(8,128)S(1)} %get-tuple-element.95), channel_id=1, source_target_pairs={{2,4},{6,8},{10,12},{14,0},{4,2},{8,6},{12,10},{0,14},{3,5},{7,9},... | collective-permute-start | bytes 393224 | tf_op jit(solution)/shard_map/ppermute | solution.py:340
  95.5 5.5 %collective-permute-start.19 = (f32[1,4,64,128]{3,2,1,0:T(8,128)S(1)}, f32[1,4,64,128]{3,2,1,0:T(8,128)S(1)}, u32[]{:S(2)}, u32[]{:S(2)}) collective-permute-start(f32[1,4,64,128]{3,2,1,0:T(8,128)S(1)} %get-tuple-element.96), channel_id=1, source_target_pairs={{0,2},{2,0},{4,6},{6,4},{8,10},{10,8},{12,14},{14,12},{1,3},{3,1},... | collective-permute-start | bytes 393224 | tf_op jit(solution)/shard_map/ppermute | solution.py:341
  97.0 4.0 %collective-permute-start.20 = (f32[1,16,128]{2,1,0:T(8,128)S(1)}, f32[1,16,128]{2,1,0:T(8,128)S(1)}, u32[]{:S(2)}, u32[]{:S(2)}) collective-permute-start(f32[1,16,128]{2,1,0:T(8,128)S(1)} %get-tuple-element.97), channel_id=1, source_target_pairs={{0,1},{1,0},{2,3},{3,2},{4,5},{5,4},{6,7},{7,6},{8,9},{9,8},{10,11... | collective-permute-start | bytes 24584 | tf_op jit(solution)/shard_map/ppermute | solution.py:342
  101.0 29.1 %copy-start.3 = (f32[1,4,2048]{2,1,0:T(4,128)S(1)}, f32[1,4,2048]{2,1,0:T(4,128)}, u32[]{:S(2)}) copy-start(f32[1,4,2048]{2,1,0:T(4,128)} %param.14) | copy-start | bytes 98308
  103.3 1.3 collective-permute-start.21

commit v4 on v3

--- a/solution.py
+++ b/solution.py
@@ -40,62 +40,87 @@
     return ((gy == 0) & (lane >= BY - 4)) | ((gy == 1) & (lane < 4))
 
 
-def far_edge(gy, lane):
-    return ((gy == 0) & (lane < 4)) | ((gy == 1) & (lane >= BY - 4))
-
-
-def send_edges(load, outer_ref, inner_ref, strip_ref, slot, scal):
+def send_edges(field, outer_ref, inner_ref, strip_ref, slot, scal):
     core, gy = scal[0], scal[1]
     keep = near_edge(gy, lanes(8))
     for i in range(4):
-        outer_ref[slot, i] = load(4 * core + i)
-        inner_ref[slot, i] = load(4 * (1 - core) + i)
+        outer_ref[slot, i] = field[4 * core + i]
+        inner_ref[slot, i] = field[4 * (1 - core) + i]
     for half in range(2):
-        packed = jnp.zeros((8, BY), F32)
+        sums = []
         for j in range(32):
-            index = half * 32 + j
-            plane = load(index // 8)[8 * (index % 8) : 8 * (index % 8) + 8]
-            packed = packed + pltpu.roll(jnp.where(keep, plane, 0.0), 4 * j, 1)
-        strip_ref[slot, 8 * half : 8 * half + 8] = packed
-
-
-def fill(padded, side, load, outer_ref, inner_ref, strip_ref, slot, scal):
+            x, z = 4 * half + j // 8, 8 * (j % 8)
+            turned = pltpu.roll(jnp.where(keep, field[x, z : z + 8], 0.0), 4 * j, 1)
+            if j < 4:
+                sums.append(turned)
+            else:
+                sums[j % 4] = sums[j % 4] + turned
+        strip_ref[slot, 8 * half : 8 * half + 8] = (sums[0] + sums[1]) + (sums[2] + sums[3])
+
+
+def interior(field, padded, part):
+    lane = lanes(NZ)
+    zero = jnp.zeros((8, BY), F32)
+    for x in range(BX):
+        padded[x, 0:8] = zero
+        padded[x, 72:80] = zero
+        padded[x, 8:72] = field[x]
+    for x in range(BX):
+        centre = field[x]
+        result = (3.0 * weights[0]) * centre
+        for k in range(1, 5):
+            pairs = padded[x, 8 + k : 72 + k] + padded[x, 8 - k : 72 - k]
+            if x + k < BX:
+                pairs = pairs + field[x + k]
+            if x - k >= 0:
+                pairs = pairs + field[x - k]
+            right = pltpu.roll(jnp.where(lane < k, 0.0, centre), BY - k, 1)
+            left = pltpu.roll(jnp.where(lane >= BY - k, 0.0, centre), k, 1)
+            result = result + weights[k] * (pairs + (right + left))
+        part[x] = result
+
+
+def interior_kernel(*refs):
+    count = (len(refs) - 1) // 2
+    for i in range(count):
+        interior(refs[i], refs[-1], refs[count + i])
+
+
+def receive(halo, outer_ref, inner_ref, strip_ref, slot, scal):
     core, gy = scal[0], scal[1]
-    keep = far_edge(gy, lanes(8))
-    zero = jnp.zeros((8, BY), F32)
-    for x in range(BX):
-        padded[4 + x, 0:8] = zero
-        padded[4 + x, 72:80] = zero
-        padded[4 + x, 8:72] = load(x)
     inside = ((scal[2] > 0) | (core == 1)) & ((scal[2] < 7 * BX) | (core == 0))
     for i in range(4):
-        padded[12 * core + i, 8:72] = jnp.where(inside, outer_ref[slot, i], 0.0)
-        padded[12 * (1 - core) + i, 8:72] = inner_ref[slot, i]
-    for half in range(2):
-        packed = strip_ref[slot, 8 * half : 8 * half + 8]
-        for j in range(32):
-            index = half * 32 + j
-            turned = pltpu.roll(packed, (BY - 4 * j) % BY, 1)
-            side[index // 8, 8 * (index % 8) : 8 * (index % 8) + 8] = jnp.where(keep, turned, 0.0)
-
-
-def lap(padded, side, x):
-    lane = lanes(NZ)
-    centre = padded[4 + x, 8:72]
-    other = side[x]
-    result = (3.0 * weights[0]) * centre
+        halo[4 * core + i] = jnp.where(inside, outer_ref[slot, i], 0.0)
+        halo[4 * (1 - core) + i] = inner_ref[slot, i]
+    packed = strip_ref[slot]
+    place = lanes(16) & 3
+    after, before = weights[4] * packed, weights[4] * packed
+    for m in range(1, 4):
+        after = after + weights[4 - m] * jnp.where(place >= m, pltpu.roll(packed, m, 1), 0.0)
+        before = before + weights[4 - m] * jnp.where(place < 4 - m, pltpu.roll(packed, BY - m, 1), 0.0)
+    return jnp.where(gy == 0, pltpu.roll(after, BY - 4, 1), pltpu.roll(before, 4, 1))
+
+
+def complete(part, halo, strips, x, scal):
+    keep = near_edge(scal[1], lanes(8))
+    pieces = []
+    for z in range(8):
+        j = 8 * (x % 4) + z
+        row = 8 * (x // 4)
+        turned = pltpu.roll(strips[row : row + 8], (BY - 4 * j) % BY, 1)
+        pieces.append(jnp.where(keep, turned, 0.0))
+    result = part[x] + jnp.concatenate(pieces, axis=0)
     for k in range(1, 5):
-        along_z = padded[4 + x, 8 + k : 72 + k] + padded[4 + x, 8 - k : 72 - k]
-        along_x = padded[4 + x + k, 8:72] + padded[4 + x - k, 8:72]
-        right = pltpu.roll(jnp.where(lane < k, other, centre), BY - k, 1)
-        left = pltpu.roll(jnp.where(lane >= BY - k, other, centre), k, 1)
-        result = result + weights[k] * ((along_z + along_x) + (right + left))
+        if x - k < 0:
+            result = result + weights[k] * halo[4 + x - k]
+        if x + k >= BX:
+            result = result + weights[k] * halo[x + k - 4]
     return result
 
 
 FIELD = ((BX, NZ, BY), F32)
-PADDED = pltpu.VMEM((16, 80, BY), F32)
-SIDE = pltpu.VMEM((BX, NZ, BY), F32)
+PADDED = pltpu.VMEM((BX, 80, BY), F32)
+HALO = pltpu.VMEM((BX, NZ, BY), F32)
 
 
 def edges(count):
@@ -105,7 +130,7 @@
 def first_kernel(scal, newer, newer_out, outer, inner, strip):
     for x in range(BX):
         newer_out[x] = newer[pl.ds(x, NZ, stride=8), :]
-    send_edges(lambda x: newer_out[x], outer, inner, strip, 0, scal)
+    send_edges(newer_out, outer, inner, strip, 0, scal)
 
 
 def two_pieces(values):
@@ -121,7 +146,7 @@
     return jnp.broadcast_to(row, (16, NREC)).astype(BF16)
 
 
-def inject(n, traces, pick_cell, pick_y, spread, inj, slot=0):
+def inject(n, traces, pick_cell, pick_y, spread, inj):
     value = traces[n : n + 1, :]
     coarse = value.astype(BF16).astype(F32)
     high, low = wide(coarse), wide(value - coarse)
@@ -138,12 +163,14 @@
     )
     for x in range(BX):
         part = both[NZ * x : NZ * x + NZ]
-        inj[slot, x] = part[:, :BY] + part[:, BY:]
-
-
-def inject_kernel(shot, pick_cell, pick_y, inj, spread):
-    for n in range(3):
-        inject(n, shot, pick_cell, pick_y, spread, inj, n)
+        inj[x] = part[:, :BY] + part[:, BY:]
+
+
+def make_inject(n):
+    def kernel(shot, pick_cell, pick_y, inj, spread):
+        inject(n, shot, pick_cell, pick_y, spread, inj)
+
+    return kernel
 
 
 def prepare_kernel(scal, shot, inj, pick_cell, pick_y, at_depth, spread):
@@ -186,35 +213,35 @@
         vel[x] = vel_in[pl.ds(x, NZ, stride=8), :]
 
 
-def forward1_kernel(scal, newer, older, vel, inj3, outer, inner, strip, acc, nxt, q, outer_o, inner_o, strip_o, padded, side):
-    fill(padded, side, lambda x: newer[x], outer, inner, strip, 0, scal)
-    for x in range(BX):
-        a = vel[x] * lap(padded, side, x)
+def forward1_kernel(scal, part, newer, older, vel, inj3, outer, inner, strip, acc, nxt, q, outer_o, inner_o, strip_o, halo):
+    strips = receive(halo, outer, inner, strip, 0, scal)
+    for x in range(BX):
+        a = vel[x] * complete(part, halo, strips, x, scal)
         acc[x] = a
         nxt[x] = (2.0 * newer[x] - older[x]) + a
-        q[x] = vel[x] * inj3[0, x]
-    send_edges(lambda x: nxt[x], outer_o, inner_o, strip_o, 0, scal)
-    send_edges(lambda x: q[x], outer_o, inner_o, strip_o, 1, scal)
+        q[x] = vel[x] * inj3[x]
+    send_edges(nxt, outer_o, inner_o, strip_o, 0, scal)
+    send_edges(q, outer_o, inner_o, strip_o, 1, scal)
 
 
 def make_forward(moment):
-    def kernel(scal, newer, older, vel, inj, inj3, q_in, *rest):
+    def kernel(scal, part, part_q, newer, older, vel, inj, inj3, *rest):
         if moment == 2:
             later, rest = rest[0], rest[1:]
-        outer, inner, strip, acc, nxt, p, q, outer_o, inner_o, strip_o, padded, side = rest
-        fill(padded, side, lambda x: newer[x], outer, inner, strip, 0, scal)
+        outer, inner, strip, acc, nxt, p, q, outer_o, inner_o, strip_o, halo, halo_q = rest
+        strips = receive(halo, outer, inner, strip, 0, scal)
         for x in range(BX):
-            a = vel[x] * lap(padded, side, x)
+            a = vel[x] * complete(part, halo, strips, x, scal)
             acc[x] = a
             nxt[x] = (2.0 * newer[x] - older[x]) + a
-        send_edges(lambda x: nxt[x], outer_o, inner_o, strip_o, 0, scal)
-        fill(padded, side, lambda x: q_in[x], outer, inner, strip, 1, scal)
+        send_edges(nxt, outer_o, inner_o, strip_o, 0, scal)
+        strips = receive(halo_q, outer, inner, strip, 1, scal)
         for x in range(BX):
-            before = 2.0 * inj3[0, x] if moment == 1 else 2.0 * later[x] - inj3[0, x]
-            value = (before + lap(padded, side, x)) + inj[3 - moment, x]
+            before = 2.0 * inj3[x] if moment == 1 else 2.0 * later[x] - inj3[x]
+            value = (before + complete(part_q, halo_q, strips, x, scal)) + inj[x]
             p[x] = value
             q[x] = vel[x] * value
-        send_edges(lambda x: q[x], outer_o, inner_o, strip_o, 1, scal)
+        send_edges(q, outer_o, inner_o, strip_o, 1, scal)
 
     return kernel
 
@@ -226,14 +253,14 @@
     return (column >= scal[5]) & (column < scal[5] + 192) & inside_x
 
 
-def last_kernel(scal, newer, vel, inj, inj3, q_in, latest, later, acc0, acc1, acc2, outer, inner, strip, acc3, grad, padded, side, padded2, side2):
-    fill(padded, side, lambda x: newer[x], outer, inner, strip, 0, scal)
-    fill(padded2, side2, lambda x: q_in[x], outer, inner, strip, 1, scal)
-    for x in range(BX):
-        a = vel[x] * lap(padded, side, x)
+def last_kernel(scal, part, part_q, vel, inj0, inj3, latest, later, acc0, acc1, acc2, outer, inner, strip, acc3, grad, halo, halo_q):
+    strips = receive(halo, outer, inner, strip, 0, scal)
+    strips_q = receive(halo_q, outer, inner, strip, 1, scal)
+    for x in range(BX):
+        a = vel[x] * complete(part, halo, strips, x, scal)
         acc3[x] = a
-        p0 = ((2.0 * later[x] - latest[x]) + lap(padded2, side2, x)) + inj[0, x]
-        total = ((a * inj3[0, x] + acc2[x] * latest[x]) + acc1[x] * later[x]) + acc0[x] * p0
+        p0 = ((2.0 * later[x] - latest[x]) + complete(part_q, halo_q, strips_q, x, scal)) + inj0[x]
+        total = ((a * inj3[x] + acc2[x] * latest[x]) + acc1[x] * later[x]) + acc0[x] * p0
         grad[pl.ds(x, NZ, stride=8), :] = jnp.where(window(scal, x), total, 0.0)
 
 
@@ -254,23 +281,23 @@
         s = jnp.where(window(scal, x), full[pl.ds(x, NZ, stride=8), :], 0.0)
         source[x] = s
         d[x] = s * acc0[x]
-    send_edges(lambda x: d[x], outer_o, inner_o, strip_o, 0, scal)
+    send_edges(d, outer_o, inner_o, strip_o, 0, scal)
 
 
 def make_born(moment, last):
-    def kernel(scal, now, before, source, acc, vel, outer, inner, strip, *rest):
+    def kernel(scal, part, now, before, source, acc, vel, outer, inner, strip, *rest):
         if last:
-            pick_cell, pick_y, s1, s2, s3, dot, block, padded, side, d, pieces = rest
+            pick_cell, pick_y, s1, s2, s3, dot, block, halo, d, pieces = rest
         else:
-            d, outer_o, inner_o, strip_o, padded, side = rest
-        fill(padded, side, lambda x: now[x], outer, inner, strip, 0, scal)
+            samples, d, outer_o, inner_o, strip_o, halo = rest
+        strips = receive(halo, outer, inner, strip, 0, scal)
         for x in range(BX):
             base = 2.0 * now[x]
             if moment > 1:
                 base = base - before[x]
-            d[x] = (base + vel[x] * lap(padded, side, x)) + source[x] * acc[x]
+            d[x] = (base + vel[x] * complete(part, halo, strips, x, scal)) + source[x] * acc[x]
         if not last:
-            send_edges(lambda x: d[x], outer_o, inner_o, strip_o, 0, scal)
+            send_edges(d, outer_o, inner_o, strip_o, 0, scal)
             return
         s4 = sampled(d, pieces, pick_cell, pick_y)
         energy = jnp.zeros((1, BY), F32)
@@ -354,24 +381,28 @@
     shot = jnp.concatenate([traces[0], code.astype(F32)], axis=0)
     inj3, pick_cell, pick_y = call(
         prepare_kernel,
-        [((1, BX, NZ, BY), F32), ((512, NREC), BF16), ((BY, NREC), BF16)],
+        [FIELD, ((512, NREC), BF16), ((BY, NREC), BF16)],
         [pltpu.VMEM((NZ, NREC), BF16), pltpu.VMEM((2 * BY, NREC), BF16)],
     )(scal, shot, smem=1)
+
+    def injection(n):
+        return call(make_inject(n), [FIELD], [pltpu.VMEM((2 * BY, NREC), BF16)], flops=1_000_000_000)(
+            shot, pick_cell, pick_y)[0]
+
+    one = call(interior_kernel, [FIELD], [PADDED])
+    two = call(interior_kernel, [FIELD] * 2, [PADDED])
     older, vel = call(planes_kernel, [FIELD, FIELD])(older_field.reshape(flat), velocity.reshape(flat))
-    acc0, u1, q, *e = call(forward1_kernel, [FIELD] * 3 + edges(2), [PADDED, SIDE])(
-        scal, newer, older, vel, inj3, *e, smem=1)
-    e = exchange(*e)
-    inj, = call(inject_kernel, [((3, BX, NZ, BY), F32)], [pltpu.VMEM((2 * BY, NREC), BF16)], flops=2_000_000_000)(
-        shot, pick_cell, pick_y)
-    acc1, u2, p2, q, *e = call(make_forward(1), [FIELD] * 4 + edges(2), [PADDED, SIDE])(
-        scal, u1, newer, vel, inj, inj3, q, *e, smem=1)
-    e = exchange(*e)
-    acc2, u3, p1, q, *e = call(
-        make_forward(2), [FIELD] * 4 + edges(2), [PADDED, SIDE])(
-        scal, u2, u1, vel, inj, inj3, q, p2, *e, smem=1)
-    e = exchange(*e)
-    acc3, grad = call(last_kernel, [FIELD, (flat, F32)], [PADDED, SIDE, PADDED, SIDE])(
-        scal, u3, vel, inj, inj3, q, p2, p1, acc0, acc1, acc2, *e, smem=1)
+    acc0, u1, q, *e = call(forward1_kernel, [FIELD] * 3 + edges(2), [HALO])(
+        scal, *one(newer), newer, older, vel, inj3, *e, smem=1)
+    e = exchange(*e)
+    acc1, u2, p2, q, *e = call(make_forward(1), [FIELD] * 4 + edges(2), [HALO] * 2)(
+        scal, *two(u1, q), u1, newer, vel, injection(2), inj3, *e, smem=1)
+    e = exchange(*e)
+    acc2, u3, p1, q, *e = call(make_forward(2), [FIELD] * 4 + edges(2), [HALO] * 2)(
+        scal, *two(u2, q), u2, u1, vel, injection(1), inj3, p2, *e, smem=1)
+    e = exchange(*e)
+    acc3, grad = call(last_kernel, [FIELD, (flat, F32)], [HALO] * 2)(
+        scal, *two(u3, q), vel, injection(0), inj3, p2, p1, acc0, acc1, acc2, *e, smem=1)
     parts = lax.all_to_all(grad.reshape(16, 4, BX, BY), "shot", 0, 0, tiled=True)
     scaled, copies, dot = call(
         gradient_kernel, [((32, BY), F32), (flat, F32), ((8, BY), F32)])(
@@ -382,18 +413,18 @@
     e = exchange(*e)
     sample = call(sample_kernel, [((1, NREC), F32)], [pltpu.VMEM((512, 2 * BY), BF16)], flops=600_000_000)
     s1, = sample(d1, pick_cell, pick_y)
-    d2, *e = call(make_born(1, False), [FIELD] + edges(1), [PADDED, SIDE])(
-        scal, d1, d1, source, acc1, vel, *e, smem=1)
+    d2, *e = call(make_born(1, False), [FIELD] + edges(1), [HALO])(
+        scal, *one(d1), d1, d1, source, acc1, vel, *e, s1, smem=1)
     e = exchange(*e)
     s2, = sample(d2, pick_cell, pick_y)
-    d3, *e = call(make_born(2, False), [FIELD] + edges(1), [PADDED, SIDE])(
-        scal, d2, d1, source, acc2, vel, *e, smem=1)
+    d3, *e = call(make_born(2, False), [FIELD] + edges(1), [HALO])(
+        scal, *one(d2), d2, d1, source, acc2, vel, *e, s2, smem=1)
     e = exchange(*e)
     s3, = sample(d3, pick_cell, pick_y)
     block, = call(
         make_born(3, True), [((72, BY), F32)],
-        [PADDED, SIDE, pltpu.VMEM((BX, NZ, BY), F32), pltpu.VMEM((512, 2 * BY), BF16)],
-    )(scal, d3, d2, source, acc3, vel, *e, pick_cell, pick_y, s1, s2, s3, dot, smem=1)
+        [HALO, pltpu.VMEM((BX, NZ, BY), F32), pltpu.VMEM((512, 2 * BY), BF16)],
+    )(scal, *one(d3), d3, d2, source, acc3, vel, *e, pick_cell, pick_y, s1, s2, s3, dot, smem=1)
     theirs = lax.ppermute(block, "gx", [(i, i ^ 1) for i in range(8)])
     payload, = call(pair_kernel, [((8, 72, BY), F32)])(block, theirs)
     same_core = [[2 * (2 * c + k) + g for c in range(4) for g in range(2)] for k in range(2)]

time: 131 us -> 126 us (0.962)
  starting transfers between devices: 16.4 us -> 11 us
    ppermute x7, waiting for transfers between devices: 15.9 us -> 8.42 us  [exchange(): lax.ppermute(strip, 'gy', [(0, 1), (1, 0)])]
    ppermute x7, waiting for transfers between devices: 6.25 us -> 12.6 us  [exchange(): lax.ppermute(outer, 'gx', across)]
    ppermute x7, starting transfers between devices: 11.9 us -> 5.77 us  [exchange(): lax.ppermute(outer, 'gx', across)]
    pallas_call x19 -> x28, Pallas kernels: 23.5 us -> 23.6 us  [run(): pl.pallas_call(kernel, out_shape=[jax.ShapeDtypeStruct(s, d) for s, d in...]
  transfers between devices with their start and end apart: 22 -> 22, of which waited for: 9 -> 13; matrix products, arithmetic and copies ran while one was open for 1% -> 1% of each run, Pallas kernels for 6% -> 11%
where the time goes in v4:
time: 126 us; the launch traced here: 125 us
  blocking collectives  61.6 us (49%)
  Pallas kernels  23.6 us (19%)
  waiting for transfers between devices  22.2 us (18%)
  starting transfers between devices  11 us (9%)
  local copies, waits for them, and re-layouts  2.94 us (2%)
  between operations  2.18 us (2%)
  other arithmetic  1.53 us (1%)
    pallas_call x28, Pallas kernels, run(): pl.pallas_call(kernel, out_shape=[jax.ShapeDtypeStruct(s, d) for s, d in...  23.6 us
    all_to_all x1, blocking collectives, on_device(): lax.all_to_all(grad.reshape(16, 4, BX, BY), 'shot', 0, 0, tiled=True)  21.8 us
    all_to_all x1, blocking collectives, on_device(): lax.all_to_all(copies.reshape(16, 4, BX, BY), 'shot', 0, 0, tiled=True)  15.1 us
    all_to_all x1, blocking collectives, on_device(): stats = lax.all_to_all(stats, 'shot', 0, 0, tiled=True)  13.8 us
    ppermute x7, waiting for transfers between devices, exchange(): lax.ppermute(outer, 'gx', across)  12.6 us
    all_to_all x1, blocking collectives, on_device(): lax.all_to_all(payload, ('gx', 'gy'), 0, 0, axis_index_groups=same_core,...  10.8 us
    ppermute x7, waiting for transfers between devices, exchange(): lax.ppermute(strip, 'gy', [(0, 1), (1, 0)])  8.42 us
    ppermute x7, starting transfers between devices, exchange(): lax.ppermute(outer, 'gx', across)  5.77 us
  transfers between devices with their start and end apart: 22, of which 13 were waited for; matrix products, arithmetic and copies ran while one was open for 1% of the time, Pallas kernels for 11%

profile of v4, /device:TPU:32, one launch (start us, length us, event | category | flops | bytes accessed | tf_op | source)
XLA Modules:
  0.0 125.1 jit_solution(17110253119501702932)
XLA Ops:
  2.0 1.0 copy-done
  3.0 0.7 shard_map.113
  3.7 2.5 %collective-permute-start = (f32[1,4,64,128]{3,2,1,0:T(8,128)S(1)}, f32[1,4,64,128]{3,2,1,0:T(8,128)S(1)}, u32[]{:S(2)}, u32[]{:S(2)}) collective-permute-start(f32[1,4,64,128]{3,2,1,0:T(8,128)S(1)} %get-tuple-element.63), channel_id=1, source_target_pairs={{2,4},{6,8},{10,12},{14,0},{4,2},{8,6},{12,10},{0,14},{3,5},{7,9},... | collective-permute-start | bytes 393224 | tf_op jit(solution)/shard_map/ppermute | solution.py:367
  6.2 1.5 %collective-permute-start.2 = (f32[1,16,128]{2,1,0:T(8,128)S(1)}, f32[1,16,128]{2,1,0:T(8,128)S(1)}, u32[]{:S(2)}, u32[]{:S(2)}) collective-permute-start(f32[1,16,128]{2,1,0:T(8,128)S(1)} %get-tuple-element.65), channel_id=1, source_target_pairs={{0,1},{1,0},{2,3},{3,2},{4,5},{5,4},{6,7},{7,6},{8,9},{9,8},{10,11... | collective-permute-start | bytes 24584 | tf_op jit(solution)/shard_map/ppermute | solution.py:369
  7.7 0.7 or_convert_fusion
  8.4 0.8 pad_maximum_fusion.shot
  9.2 1.9 %shard_map.116 = (f32[8,64,128]{2,1,0:T(8,128)S(1)}, bf16[512,2048]{1,0:T(8,128)(2,1)S(1)}, bf16[128,2048]{1,0:T(8,128)(2,1)S(1)}) custom-call(s32[6]{0:T(128)S(1)} %stack.19.scal, f32[5,2048]{1,0:T(8,128)S(1)} %pad_maximum_fusion.shot), custom_call_target="tpu_custom_call" | custom-call | flops 10000000 | bytes 2000000 | tf_op jit(solution)/shard_map/pallas_call | solution.py:20
  11.7 0.9 copy-done.1
  12.7 0.9 copy-done.2
  13.8 1.0 shard_map.117
  14.8 0.7 collective-permute-start.3
  16.3 0.9 shard_map.119.inj
  17.2 1.3 %shard_map.118 = (f32[8,64,128]{2,1,0:T(8,128)S(1)}, f32[8,64,128]{2,1,0:T(8,128)S(1)}) custom-call(f32[8,64,128]{2,1,0:T(8,128)S(1)} %get-tuple-element.66.refs_0_.newer.older, f32[8,64,128]{2,1,0:T(8,128)S(1)} %get-tuple-element.67.refs_1_), custom_call_target="tpu_custom_call" | custom-call | flops 10000000 | bytes 2000000 | tf_op jit(solution)/shard_map/pallas_call | solution.py:20
  18.5 1.1 collective-permute-done.5.rest_2_
  19.5 2.3 %collective-permute-done.3.rest_0_ = f32[2,4,64,128]{3,2,1,0:T(8,128)S(1)} collective-permute-done((f32[2,4,64,128]{3,2,1,0:T(8,128)S(1)}, f32[2,4,64,128]{3,2,1,0:T(8,128)S(1)}, u32[]{:S(2)}, u32[]{:S(2)}) %collective-permute-start.3) | collective-permute-done | bytes 262176 | tf_op jit(solution)/shard_map/ppermute | solution.py:367
  21.9 1.2 shard_map.120
  24.2 0.9 shard_map.122.inj
  25.1 1.2 shard_map.121
  26.3 1.1 collective-permute-done.8.rest_3_
  27.4 2.7 %collective-permute-done.6.rest_1_ = f32[2,4,64,128]{3,2,1,0:T(8,128)S(1)} collective-permute-done((f32[2,4,64,128]{3,2,1,0:T(8,128)S(1)}, f32[2,4,64,128]{3,2,1,0:T(8,128)S(1)}, u32[]{:S(2)}, u32[]{:S(2)}) %collective-permute-start.6) | collective-permute-done | bytes 262176 | tf_op jit(solution)/shard_map/ppermute | solution.py:367
  30.1 1.2 shard_map.123
  31.4 0.8 collective-permute-start.9
  32.8 0.9 shard_map.125.inj0
  33.7 1.2 shard_map.124
  34.9 1.1 collective-permute-done.11.strip
  36.0 2.7 %collective-permute-done.9.outer = f32[2,4,64,128]{3,2,1,0:T(8,128)S(1)} collective-permute-done((f32[2,4,64,128]{3,2,1,0:T(8,128)S(1)}, f32[2,4,64,128]{3,2,1,0:T(8,128)S(1)}, u32[]{:S(2)}, u32[]{:S(2)}) %collective-permute-start.9) | collective-permute-done | bytes 262176 | tf_op jit(solution)/shard_map/ppermute | solution.py:367
  38.7 1.1 shard_map.126
  39.8 21.8 %all_to_all.20 = f32[16,4,8,128]{3,2,1,0:T(8,128)S(1)} all-to-all(f32[16,4,8,128]{3,2,1,0:T(8,128)S(1)} %bitcast.20), channel_id=1, replica_groups=mesh['shot'=16,'gx'=8,'gy'=2] {'shot'}, dimensions={0} | all-to-all | bytes 524288 | tf_op jit(solution)/shard_map/all_to_all | solution.py:406
  61.7 15.1 %all_to_all.21 = f32[16,4,8,128]{3,2,1,0:T(8,128)S(1)} all-to-all(f32[16,4,8,128]{3,2,1,0:T(8,128)S(1)} %bitcast.21), channel_id=1, replica_groups=mesh['shot'=16,'gx'=8,'gy'=2] {'shot'}, dimensions={0} | all-to-all | bytes 524288 | tf_op jit(solution)/shard_map/all_to_all | solution.py:410
  76.8 0.7 shard_map.128
  78.3 0.8 shard_map.130.rest_0_.rest_2_
  79.1 0.7 shard_map.129.part
  79.8 1.7 %collective-permute-done.14.strip = f32[1,16,128]{2,1,0:T(8,128)S(1)} collective-permute-done((f32[1,16,128]{2,1,0:T(8,128)S(1)}, f32[1,16,128]{2,1,0:T(8,128)S(1)}, u32[]{:S(2)}, u32[]{:S(2)}) %collective-permute-start.14) | collective-permute-done | bytes 8224 | tf_op jit(solution)/shard_map/ppermute | solution.py:369
  81.5 1.7 %collective-permute-done.12.outer = f32[1,4,64,128]{3,2,1,0:T(8,128)S(1)} collective-permute-done((f32[1,4,64,128]{3,2,1,0:T(8,128)S(1)}, f32[1,4,64,128]{3,2,1,0:T(8,128)S(1)}, u32[]{:S(2)}, u32[]{:S(2)}) %collective-permute-start.12) | collective-permute-done | bytes 131104 | tf_op jit(solution)/shard_map/ppermute | solution.py:367
  83.2 1.0 shard_map.131
  85.0 0.8 shard_map.133.rest_0_.rest_3_
  86.5 1.8 %collective-permute-done.17.strip = f32[1,16,128]{2,1,0:T(8,128)S(1)} collective-permute-done((f32[1,16,128]{2,1,0:T(8,128)S(1)}, f32[1,16,128]{2,1,0:T(8,128)S(1)}, u32[]{:S(2)}, u32[]{:S(2)}) %collective-permute-start.17) | collective-permute-done | bytes 8224 | tf_op jit(solution)/shard_map/ppermute | solution.py:369
  88.2 1.7 %collective-permute-done.15.outer = f32[1,4,64,128]{3,2,1,0:T(8,128)S(1)} collective-permute-done((f32[1,4,64,128]{3,2,1,0:T(8,128)S(1)}, f32[1,4,64,128]{3,2,1,0:T(8,128)S(1)}, u32[]{:S(2)}, u32[]{:S(2)}) %collective-permute-start.15) | collective-permute-done | bytes 131104 | tf_op jit(solution)/shard_map/ppermute | solution.py:367
  89.9 1.0 shard_map.134
  91.3 0.7 collective-permute-start.20
  92.0 0.8 shard_map.136.rest_4_
  93.4 1.7 %collective-permute-done.20.strip = f32[1,16,128]{2,1,0:T(8,128)S(1)} collective-permute-done((f32[1,16,128]{2,1,0:T(8,128)S(1)}, f32[1,16,128]{2,1,0:T(8,128)S(1)}, u32[]{:S(2)}, u32[]{:S(2)}) %collective-permute-start.20) | collective-permute-done | bytes 8224 | tf_op jit(solution)/shard_map/ppermute | solution.py:369
  95.1 1.5 %collective-permute-done.18.outer = f32[1,4,64,128]{3,2,1,0:T(8,128)S(1)} collective-permute-done((f32[1,4,64,128]{3,2,1,0:T(8,128)S(1)}, f32[1,4,64,128]{3,2,1,0:T(8,128)S(1)}, u32[]{:S(2)}, u32[]{:S(2)}) %collective-permute-start.18) | collective-permute-done | bytes 131104 | tf_op jit(solution)/shard_map/ppermute | solution.py:367
  96.6 1.7 %shard_map.137.mine = f32[72,128]{1,0:T(8,128)S(1)} custom-call(s32[6]{0:T(128)S(1)} %stack.19.scal, f32[8,64,128]{2,1,0:T(8,128)S(1)} %shard_map.135.part, f32[8,64,128]{2,1,0:T(8,128)S(1)} %get-tuple-element.105.refs_0_.field.now, f32[8,64,128]{2,1,0:T(8,128)S(1)} %get-tuple-element.101.refs_0_.field.now.before, ...), custom_call_target="tpu_custom_call" | custom-call | flops 10000000 | bytes 2000000 | tf_op jit(solution)/shard_map/pallas_call | solution.py:20
  98.4 1.2 collective-permute-done.21.theirs
  99.6 10.8 %all_to_all.22.arrived = f32[8,72,128]{2,1,0:T(8,128)S(1)} all-to-all(f32[8,72,128]{2,1,0:T(8,128)S(1)} %shard_map.138), channel_id=1, replica_groups={{0,1,4,5,8,9,12,13},{2,3,6,7,10,11,14,15},{16,17,20,21,24,25,28,29},{18..., dimensions={0} | all-to-all | bytes 589824 | tf_op jit(solution)/shard_map/all_to_all | solution.py:431
  110.5 13.8 %all_to_all.23.stats = f32[16,8,128]{2,1,0:T(8,128)S(1)} all-to-all(f32[16,8,128]{2,1,0:T(8,128)S(1)} %get-tuple-element.111), channel_id=1, replica_groups=mesh['shot'=16,'gx'=8,'gy'=2] {'shot'}, dimensions={0} | all-to-all | bytes 131072 | tf_op jit(solution)/shard_map/all_to_all | solution.py:433
  124.2 0.8 shard_map.140
  (41 shorter events, 7.1 us)
Async XLA Ops:
  2.0 1.0 copy-start
  3.7 10.1 %collective-permute-start = (f32[1,4,64,128]{3,2,1,0:T(8,128)S(1)}, f32[1,4,64,128]{3,2,1,0:T(8,128)S(1)}, u32[]{:S(2)}, u32[]{:S(2)}) collective-permute-start(f32[1,4,64,128]{3,2,1,0:T(8,128)S(1)} %get-tuple-element.63), channel_id=1, source_target_pairs={{2,4},{6,8},{10,12},{14,0},{4,2},{8,6},{12,10},{0,14},{3,5},{7,9},... | collective-permute-start | bytes 393224 | tf_op jit(solution)/shard_map/ppermute | solution.py:367
  6.2 7.6 %collective-permute-start.1 = (f32[1,4,64,128]{3,2,1,0:T(8,128)S(1)}, f32[1,4,64,128]{3,2,1,0:T(8,128)S(1)}, u32[]{:S(2)}, u32[]{:S(2)}) collective-permute-start(f32[1,4,64,128]{3,2,1,0:T(8,128)S(1)} %get-tuple-element.64), channel_id=1, source_target_pairs={{0,2},{2,0},{4,6},{6,4},{8,10},{10,8},{12,14},{14,12},{1,3},{3,1},... | collective-permute-start | bytes 393224 | tf_op jit(solution)/shard_map/ppermute | solution.py:368
  6.2 7.5 %collective-permute-start.2 = (f32[1,16,128]{2,1,0:T(8,128)S(1)}, f32[1,16,128]{2,1,0:T(8,128)S(1)}, u32[]{:S(2)}, u32[]{:S(2)}) collective-permute-start(f32[1,16,128]{2,1,0:T(8,128)S(1)} %get-tuple-element.65), channel_id=1, source_target_pairs={{0,1},{1,0},{2,3},{3,2},{4,5},{5,4},{6,7},{7,6},{8,9},{9,8},{10,11... | collective-permute-start | bytes 24584 | tf_op jit(solution)/shard_map/ppermute | solution.py:369
  11.7 1.0 copy-start.1
  12.7 0.9 copy-start.2
  14.8 7.1 %collective-permute-start.3 = (f32[2,4,64,128]{3,2,1,0:T(8,128)S(1)}, f32[2,4,64,128]{3,2,1,0:T(8,128)S(1)}, u32[]{:S(2)}, u32[]{:S(2)}) collective-permute-start(f32[2,4,64,128]{3,2,1,0:T(8,128)S(1)} %get-tuple-element.72), channel_id=1, source_target_pairs={{2,4},{6,8},{10,12},{14,0},{4,2},{8,6},{12,10},{0,14},{3,5},{7,9},... | collective-permute-start | bytes 786440 | tf_op jit(solution)/shard_map/ppermute | solution.py:367
  15.4 6.4 %collective-permute-start.4 = (f32[2,4,64,128]{3,2,1,0:T(8,128)S(1)}, f32[2,4,64,128]{3,2,1,0:T(8,128)S(1)}, u32[]{:S(2)}, u32[]{:S(2)}) collective-permute-start(f32[2,4,64,128]{3,2,1,0:T(8,128)S(1)} %get-tuple-element.73), channel_id=1, source_target_pairs={{0,2},{2,0},{4,6},{6,4},{8,10},{10,8},{12,14},{14,12},{1,3},{3,1},... | collective-permute-start | bytes 786440 | tf_op jit(solution)/shard_map/ppermute | solution.py:368
  15.8 3.7 %collective-permute-start.5 = (f32[2,16,128]{2,1,0:T(8,128)S(1)}, f32[2,16,128]{2,1,0:T(8,128)S(1)}, u32[]{:S(2)}, u32[]{:S(2)}) collective-permute-start(f32[2,16,128]{2,1,0:T(8,128)S(1)} %get-tuple-element.74), channel_id=1, source_target_pairs={{0,1},{1,0},{2,3},{3,2},{4,5},{5,4},{6,7},{7,6},{8,9},{9,8},{10,11... | collective-permute-start | bytes 49160 | tf_op jit(solution)/shard_map/ppermute | solution.py:369
  23.0 7.1 %collective-permute-start.6 = (f32[2,4,64,128]{3,2,1,0:T(8,128)S(1)}, f32[2,4,64,128]{3,2,1,0:T(8,128)S(1)}, u32[]{:S(2)}, u32[]{:S(2)}) collective-permute-start(f32[2,4,64,128]{3,2,1,0:T(8,128)S(1)} %get-tuple-element.80), channel_id=1, source_target_pairs={{2,4},{6,8},{10,12},{14,0},{4,2},{8,6},{12,10},{0,14},{3,5},{7,9},... | collective-permute-start | bytes 786440 | tf_op jit(solution)/shard_map/ppermute | solution.py:367
  23.7 6.4 %collective-permute-start.7 = (f32[2,4,64,128]{3,2,1,0:T(8,128)S(1)}, f32[2,4,64,128]{3,2,1,0:T(8,128)S(1)}, u32[]{:S(2)}, u32[]{:S(2)}) collective-permute-start(f32[2,4,64,128]{3,2,1,0:T(8,128)S(1)} %get-tuple-element.81), channel_id=1, source_target_pairs={{0,2},{2,0},{4,6},{6,4},{8,10},{10,8},{12,14},{14,12},{1,3},{3,1},... | collective-permute-start | bytes 786440 | tf_op jit(solution)/shard_map/ppermute | solution.py:368
  23.7 3.7 %collective-permute-start.8 = (f32[2,16,128]{2,1,0:T(8,128)S(1)}, f32[2,16,128]{2,1,0:T(8,128)S(1)}, u32[]{:S(2)}, u32[]{:S(2)}) collective-permute-start(f32[2,16,128]{2,1,0:T(8,128)S(1)} %get-tuple-element.82), channel_id=1, source_target_pairs={{0,1},{1,0},{2,3},{3,2},{4,5},{5,4},{6,7},{7,6},{8,9},{9,8},{10,11... | collective-permute-start | bytes 49160 | tf_op jit(solution)/shard_map/ppermute | solution.py:369
  31.3 4.7 %collective-permute-start.10 = (f32[2,4,64,128]{3,2,1,0:T(8,128)S(1)}, f32[2,4,64,128]{3,2,1,0:T(8,128)S(1)}, u32[]{:S(2)}, u32[]{:S(2)}) collective-permute-start(f32[2,4,64,128]{3,2,1,0:T(8,128)S(1)} %get-tuple-element.92), channel_id=1, source_target_pairs={{0,2},{2,0},{4,6},{6,4},{8,10},{10,8},{12,14},{14,12},{1,3},{3,1},... | collective-permute-start | bytes 786440 | tf_op jit(solution)/shard_map/ppermute | solution.py:368
  31.4 7.3 %collective-permute-start.9 = (f32[2,4,64,128]{3,2,1,0:T(8,128)S(1)}, f32[2,4,64,128]{3,2,1,0:T(8,128)S(1)}, u32[]{:S(2)}, u32[]{:S(2)}) collective-permute-start(f32[2,4,64,128]{3,2,1,0:T(8,128)S(1)} %get-tuple-element.91), channel_id=1, source_target_pairs={{2,4},{6,8},{10,12},{14,0},{4,2},{8,6},{12,10},{0,14},{3,5},{7,9},... | collective-permute-start | bytes 786440 | tf_op jit(solution)/shard_map/ppermute | solution.py:367
  32.3 3.7 %collective-permute-start.11 = (f32[2,16,128]{2,1,0:T(8,128)S(1)}, f32[2,16,128]{2,1,0:T(8,128)S(1)}, u32[]{:S(2)}, u32[]{:S(2)}) collective-permute-start(f32[2,16,128]{2,1,0:T(8,128)S(1)} %get-tuple-element.93), channel_id=1, source_target_pairs={{0,1},{1,0},{2,3},{3,2},{4,5},{5,4},{6,7},{7,6},{8,9},{9,8},{10,11... | collective-permute-start | bytes 49160 | tf_op jit(solution)/shard_map/ppermute | solution.py:369
  33.7 27.9 %copy-start.4 = (f32[4,8,128]{2,1,0:T(8,128)S(1)}, f32[4,8,128]{2,1,0:T(8,128)}, u32[]{:S(2)}) copy-start(f32[4,8,128]{2,1,0:T(8,128)} %param.13) | copy-start | bytes 49156
  77.5 5.7 %collective-permute-start.12 = (f32[1,4,64,128]{3,2,1,0:T(8,128)S(1)}, f32[1,4,64,128]{3,2,1,0:T(8,128)S(1)}, u32[]{:S(2)}, u32[]{:S(2)}) collective-permute-start(f32[1,4,64,128]{3,2,1,0:T(8,128)S(1)} %get-tuple-element.98), channel_id=1, source_target_pairs={{2,4},{6,8},{10,12},{14,0},{4,2},{8,6},{12,10},{0,14},{3,5},{7,9},... | collective-permute-start | bytes 393224 | tf_op jit(solution)/shard_map/ppermute | solution.py:367
  77.9 5.3 %collective-permute-start.13 = (f32[1,4,64,128]{3,2,1,0:T(8,128)S(1)}, f32[1,4,64,128]{3,2,1,0:T(8,128)S(1)}, u32[]{:S(2)}, u32[]{:S(2)}) collective-permute-start(f32[1,4,64,128]{3,2,1,0:T(8,128)S(1)} %get-tuple-element.99), channel_id=1, source_target_pairs={{0,2},{2,0},{4,6},{6,4},{8,10},{10,8},{12,14},{14,12},{1,3},{3,1},... | collective-permute-start | bytes 393224 | tf_op jit(solution)/shard_map/ppermute | solution.py:368
  77.9 3.7 %collective-permute-start.14 = (f32[1,16,128]{2,1,0:T(8,128)S(1)}, f32[1,16,128]{2,1,0:T(8,128)S(1)}, u32[]{:S(2)}, u32[]{:S(2)}) collective-permute-start(f32[1,16,128]{2,1,0:T(8,128)S(1)} %get-tuple-element.100), channel_id=1, source_target_pairs={{0,1},{1,0},{2,3},{3,2},{4,5},{5,4},{6,7},{7,6},{8,9},{9,8},{10,11... | collective-permute-start | bytes 24584 | tf_op jit(solution)/shard_map/ppermute | solution.py:369
  84.2 5.7 %collective-permute-start.15 = (f32[1,4,64,128]{3,2,1,0:T(8,128)S(1)}, f32[1,4,64,128]{3,2,1,0:T(8,128)S(1)}, u32[]{:S(2)}, u32[]{:S(2)}) collective-permute-start(f32[1,4,64,128]{3,2,1,0:T(8,128)S(1)} %get-tuple-element.102), channel_id=1, source_target_pairs={{2,4},{6,8},{10,12},{14,0},{4,2},{8,6},{12,10},{0,14},{3,5},{7,9},... | collective-permute-start | bytes 393224 | tf_op jit(solution)/shard_map/ppermute | solution.py:367
  84.6 5.3 %collective-permute-start.16 = (f32[1,4,64,128]{3,2,1,0:T(8,128)S(1)}, f32[1,4,64,128]{3,2,1,0:T(8,128)S(1)}, u32[]{:S(2)}, u32[]{:S(2)}) collective-permute-start(f32[1,4,64,128]{3,2,1,0:T(8,128)S(1)} %get-tuple-element.103), channel_id=1, source_target_pairs={{0,2},{2,0},{4,6},{6,4},{8,10},{10,8},{12,14},{14,12},{1,3},{3,1},... | collective-permute-start | bytes 393224 | tf_op jit(solution)/shard_map/ppermute | solution.py:368
  84.6 3.7 %collective-permute-start.17 = (f32[1,16,128]{2,1,0:T(8,128)S(1)}, f32[1,16,128]{2,1,0:T(8,128)S(1)}, u32[]{:S(2)}, u32[]{:S(2)}) collective-permute-start(f32[1,16,128]{2,1,0:T(8,128)S(1)} %get-tuple-element.104), channel_id=1, source_target_pairs={{0,1},{1,0},{2,3},{3,2},{4,5},{5,4},{6,7},{7,6},{8,9},{9,8},{10,11... | collective-permute-start | bytes 24584 | tf_op jit(solution)/shard_map/ppermute | solution.py:369
  90.9 5.7 %collective-permute-start.18 = (f32[1,4,64,128]{3,2,1,0:T(8,128)S(1)}, f32[1,4,64,128]{3,2,1,0:T(8,128)S(1)}, u32[]{:S(2)}, u32[]{:S(2)}) collective-permute-start(f32[1,4,64,128]{3,2,1,0:T(8,128)S(1)} %get-tuple-element.107), channel_id=1, source_target_pairs={{2,4},{6,8},{10,12},{14,0},{4,2},{8,6},{12,10},{0,14},{3,5},{7,9},... | collective-permute-start | bytes 393224 | tf_op jit(solution)/shard_map/ppermute | solution.py:367
  91.3 5.3 %collective-permute-start.19 = (f32[1,4,64,128]{3,2,1,0:T(8,128)S(1)}, f32[1,4,64,128]{3,2,1,0:T(8,128)S(1)}, u32[]{:S(2)}, u32[]{:S(2)}) collective-permute-start(f32[1,4,64,128]{3,2,1,0:T(8,128)S(1)} %get-tuple-element.108), channel_id=1, source_target_pairs={{0,2},{2,0},{4,6},{6,4},{8,10},{10,8},{12,14},{14,12},{1,3},{3,1},... | collective-permute-start | bytes 393224 | tf_op jit(solution)/shard_map/ppermute | solution.py:368
  91.3 3.8 %collective-permute-start.20 = (f32[1,16,128]{2,1,0:T(8,128)S(1)}, f32[1,16,128]{2,1,0:T(8,128)S(1)}, u32[]{:S(2)}, u32[]{:S(2)}) collective-permute-start(f32[1,16,128]{2,1,0:T(8,128)S(1)} %get-tuple-element.109), channel_id=1, source_target_pairs={{0,1},{1,0},{2,3},{3,2},{4,5},{5,4},{6,7},{7,6},{8,9},{9,8},{10,11... | collective-permute-start | bytes 24584 | tf_op jit(solution)/shard_map/ppermute | solution.py:369
  96.6 27.6 %copy-start.3 = (f32[1,4,2048]{2,1,0:T(4,128)S(1)}, f32[1,4,2048]{2,1,0:T(4,128)}, u32[]{:S(2)}) copy-start(f32[1,4,2048]{2,1,0:T(4,128)} %param.14) | copy-start | bytes 98308
  98.3 1.3 %collective-permute-start.21 = (f32[72,128]{1,0:T(8,128)S(1)}, f32[72,128]{1,0:T(8,128)S(1)}, u32[]{:S(2)}, u32[]{:S(2)}) collective-permute-start(f32[72,128]{1,0:T(8,128)S(1)} %shard_map.137.mine), channel_id=1, source_target_pairs={{0,2},{2,0},{4,6},{6,4},{8,10},{10,8},{12,14},{14,12},{1,3},{3,1},... | collective-permute-start | bytes 110600 | tf_op jit(solution)/shard_map/ppermute | solution.py:428

commit v5 on v4

--- a/solution.py
+++ b/solution.py
@@ -40,22 +40,27 @@
     return ((gy == 0) & (lane >= BY - 4)) | ((gy == 1) & (lane < 4))
 
 
-def send_edges(field, outer_ref, inner_ref, strip_ref, slot, scal):
-    core, gy = scal[0], scal[1]
-    keep = near_edge(gy, lanes(8))
+def send_rows(field, outer_ref, inner_ref, slot, scal):
+    core = scal[0]
     for i in range(4):
         outer_ref[slot, i] = field[4 * core + i]
         inner_ref[slot, i] = field[4 * (1 - core) + i]
-    for half in range(2):
-        sums = []
-        for j in range(32):
-            x, z = 4 * half + j // 8, 8 * (j % 8)
-            turned = pltpu.roll(jnp.where(keep, field[x, z : z + 8], 0.0), 4 * j, 1)
-            if j < 4:
-                sums.append(turned)
-            else:
-                sums[j % 4] = sums[j % 4] + turned
-        strip_ref[slot, 8 * half : 8 * half + 8] = (sums[0] + sums[1]) + (sums[2] + sums[3])
+
+
+def pack_kernel(scal, *refs):
+    strip_ref = refs[-1]
+    keep = near_edge(scal[1], lanes(8))
+    for slot, field in enumerate(refs[:-1]):
+        for half in range(2):
+            sums = []
+            for j in range(32):
+                x, z = 4 * half + j // 8, 8 * (j % 8)
+                turned = pltpu.roll(jnp.where(keep, field[x, z : z + 8], 0.0), 4 * j, 1)
+                if j < 4:
+                    sums.append(turned)
+                else:
+                    sums[j % 4] = sums[j % 4] + turned
+            strip_ref[slot, 8 * half : 8 * half + 8] = (sums[0] + sums[1]) + (sums[2] + sums[3])
 
 
 def interior(field, padded, part):
@@ -124,13 +129,13 @@
 
 
 def edges(count):
-    return [((count, 4, NZ, BY), F32), ((count, 4, NZ, BY), F32), ((count, 16, BY), F32)]
-
-
-def first_kernel(scal, newer, newer_out, outer, inner, strip):
+    return [((count, 4, NZ, BY), F32), ((count, 4, NZ, BY), F32)]
+
+
+def first_kernel(scal, newer, newer_out, outer, inner):
     for x in range(BX):
         newer_out[x] = newer[pl.ds(x, NZ, stride=8), :]
-    send_edges(newer_out, outer, inner, strip, 0, scal)
+    send_rows(newer_out, outer, inner, 0, scal)
 
 
 def two_pieces(values):
@@ -213,35 +218,35 @@
         vel[x] = vel_in[pl.ds(x, NZ, stride=8), :]
 
 
-def forward1_kernel(scal, part, newer, older, vel, inj3, outer, inner, strip, acc, nxt, q, outer_o, inner_o, strip_o, halo):
+def forward1_kernel(scal, part, newer, older, vel, inj3, outer, inner, strip, acc, nxt, q, outer_o, inner_o, halo):
     strips = receive(halo, outer, inner, strip, 0, scal)
     for x in range(BX):
         a = vel[x] * complete(part, halo, strips, x, scal)
         acc[x] = a
         nxt[x] = (2.0 * newer[x] - older[x]) + a
         q[x] = vel[x] * inj3[x]
-    send_edges(nxt, outer_o, inner_o, strip_o, 0, scal)
-    send_edges(q, outer_o, inner_o, strip_o, 1, scal)
+    send_rows(nxt, outer_o, inner_o, 0, scal)
+    send_rows(q, outer_o, inner_o, 1, scal)
 
 
 def make_forward(moment):
     def kernel(scal, part, part_q, newer, older, vel, inj, inj3, *rest):
         if moment == 2:
             later, rest = rest[0], rest[1:]
-        outer, inner, strip, acc, nxt, p, q, outer_o, inner_o, strip_o, halo, halo_q = rest
+        outer, inner, strip, acc, nxt, p, q, outer_o, inner_o, halo, halo_q = rest
         strips = receive(halo, outer, inner, strip, 0, scal)
         for x in range(BX):
             a = vel[x] * complete(part, halo, strips, x, scal)
             acc[x] = a
             nxt[x] = (2.0 * newer[x] - older[x]) + a
-        send_edges(nxt, outer_o, inner_o, strip_o, 0, scal)
+        send_rows(nxt, outer_o, inner_o, 0, scal)
         strips = receive(halo_q, outer, inner, strip, 1, scal)
         for x in range(BX):
             before = 2.0 * inj3[x] if moment == 1 else 2.0 * later[x] - inj3[x]
             value = (before + complete(part_q, halo_q, strips, x, scal)) + inj[x]
             p[x] = value
             q[x] = vel[x] * value
-        send_edges(q, outer_o, inner_o, strip_o, 1, scal)
+        send_rows(q, outer_o, inner_o, 1, scal)
 
     return kernel
 
@@ -276,12 +281,12 @@
     dot[...] = (product[0:8] + product[8:16]) + (product[16:24] + product[24:32])
 
 
-def born1_kernel(scal, full, acc0, source, d, outer_o, inner_o, strip_o):
+def born1_kernel(scal, full, acc0, source, d, outer_o, inner_o):
     for x in range(BX):
         s = jnp.where(window(scal, x), full[pl.ds(x, NZ, stride=8), :], 0.0)
         source[x] = s
         d[x] = s * acc0[x]
-    send_edges(d, outer_o, inner_o, strip_o, 0, scal)
+    send_rows(d, outer_o, inner_o, 0, scal)
 
 
 def make_born(moment, last):
@@ -289,7 +294,7 @@
         if last:
             pick_cell, pick_y, s1, s2, s3, dot, block, halo, d, pieces = rest
         else:
-            samples, d, outer_o, inner_o, strip_o, halo = rest
+            samples, d, outer_o, inner_o, halo = rest
         strips = receive(halo, outer, inner, strip, 0, scal)
         for x in range(BX):
             base = 2.0 * now[x]
@@ -297,7 +302,7 @@
                 base = base - before[x]
             d[x] = (base + vel[x] * complete(part, halo, strips, x, scal)) + source[x] * acc[x]
         if not last:
-            send_edges(d, outer_o, inner_o, strip_o, 0, scal)
+            send_rows(d, outer_o, inner_o, 0, scal)
             return
         s4 = sampled(d, pieces, pick_cell, pick_y)
         energy = jnp.zeros((1, BY), F32)
@@ -359,10 +364,11 @@
             residual[n : n + 1, at] = traces[n : n + 1, at] - step * row
 
 
-def exchange(outer, inner, strip):
+def exchange(scal, outer, inner, *fields):
     chips = [(2 * i + 1, (2 * i + 2) % 8) for i in range(4)]
     across = chips + [(b, a) for a, b in chips]
     swap = [(i, i ^ 1) for i in range(8)]
+    strip, = call(pack_kernel, [((len(fields), 16, BY), F32)])(scal, *fields, smem=1)
     return (
         lax.ppermute(outer, "gx", across),
         lax.ppermute(inner, "gx", swap),
@@ -376,7 +382,7 @@
     gx, gy = lax.axis_index("gx"), lax.axis_index("gy")
     scal = jnp.stack([gx % 2, gy, gx * BX, gy * BY, aperture_x[0], aperture_y[0]]).astype(I32)
     newer, *e = call(first_kernel, [FIELD] + edges(1))(scal, newer_field.reshape(flat), smem=1)
-    e = exchange(*e)
+    e = exchange(scal, *e, newer)
     code = receiver_z | (receiver_x << 6) | (receiver_y << 12)
     shot = jnp.concatenate([traces[0], code.astype(F32)], axis=0)
     inj3, pick_cell, pick_y = call(
@@ -394,13 +400,13 @@
     older, vel = call(planes_kernel, [FIELD, FIELD])(older_field.reshape(flat), velocity.reshape(flat))
     acc0, u1, q, *e = call(forward1_kernel, [FIELD] * 3 + edges(2), [HALO])(
         scal, *one(newer), newer, older, vel, inj3, *e, smem=1)
-    e = exchange(*e)
+    e = exchange(scal, *e, u1, q)
     acc1, u2, p2, q, *e = call(make_forward(1), [FIELD] * 4 + edges(2), [HALO] * 2)(
         scal, *two(u1, q), u1, newer, vel, injection(2), inj3, *e, smem=1)
-    e = exchange(*e)
+    e = exchange(scal, *e, u2, q)
     acc2, u3, p1, q, *e = call(make_forward(2), [FIELD] * 4 + edges(2), [HALO] * 2)(
         scal, *two(u2, q), u2, u1, vel, injection(1), inj3, p2, *e, smem=1)
-    e = exchange(*e)
+    e = exchange(scal, *e, u3, q)
     acc3, grad = call(last_kernel, [FIELD, (flat, F32)], [HALO] * 2)(
         scal, *two(u3, q), vel, injection(0), inj3, p2, p1, acc0, acc1, acc2, *e, smem=1)
     parts = lax.all_to_all(grad.reshape(16, 4, BX, BY), "shot", 0, 0, tiled=True)
@@ -410,16 +416,16 @@
     full = lax.all_to_all(copies.reshape(16, 4, BX, BY), "shot", 0, 0, tiled=True)
     source, d1, *e = call(born1_kernel, [FIELD, FIELD] + edges(1))(
         scal, full.reshape(flat), acc0, smem=1)
-    e = exchange(*e)
+    e = exchange(scal, *e, d1)
     sample = call(sample_kernel, [((1, NREC), F32)], [pltpu.VMEM((512, 2 * BY), BF16)], flops=600_000_000)
     s1, = sample(d1, pick_cell, pick_y)
     d2, *e = call(make_born(1, False), [FIELD] + edges(1), [HALO])(
         scal, *one(d1), d1, d1, source, acc1, vel, *e, s1, smem=1)
-    e = exchange(*e)
+    e = exchange(scal, *e, d2)
     s2, = sample(d2, pick_cell, pick_y)
     d3, *e = call(make_born(2, False), [FIELD] + edges(1), [HALO])(
         scal, *one(d2), d2, d1, source, acc2, vel, *e, s2, smem=1)
-    e = exchange(*e)
+    e = exchange(scal, *e, d3)
     s3, = sample(d3, pick_cell, pick_y)
     block, = call(
         make_born(3, True), [((72, BY), F32)],

time: 126 us -> 127 us (level)
  waiting for transfers between devices: 22.2 us -> 15.2 us
  Pallas kernels: 23.6 us -> 27.8 us
  starting transfers between devices: 11 us -> 14.6 us
    ppermute x7, waiting for transfers between devices: 12.6 us -> 4.96 us  [exchange(): lax.ppermute(outer, 'gx', across)]
    pallas_call x28 -> x35, Pallas kernels: 23.6 us -> 27.8 us  [run(): pl.pallas_call(kernel, out_shape=[jax.ShapeDtypeStruct(s, d) for s, d in...]
    ppermute x7, starting transfers between devices: 5.77 us -> 8.26 us  [exchange(): lax.ppermute(outer, 'gx', across)]
  transfers between devices with their start and end apart: 22 -> 22, of which waited for: 13 -> 12; matrix products, arithmetic and copies ran while one was open for 1% -> 1% of each run, Pallas kernels for 11% -> 14%
where the time goes in v5:
time: 127 us
  blocking collectives  62.3 us (49%)
  Pallas kernels  27.8 us (22%)
  waiting for transfers between devices  15.2 us (12%)
  starting transfers between devices  14.6 us (11%)
  local copies, waits for them, and re-layouts  2.94 us (2%)
  between operations  2.25 us (2%)
  other arithmetic  1.53 us (1%)
    pallas_call x35, Pallas kernels, run(): pl.pallas_call(kernel, out_shape=[jax.ShapeDtypeStruct(s, d) for s, d in...  27.8 us
    all_to_all x1, blocking collectives, on_device(): lax.all_to_all(grad.reshape(16, 4, BX, BY), 'shot', 0, 0, tiled=True)  21.9 us
    all_to_all x1, blocking collectives, on_device(): lax.all_to_all(copies.reshape(16, 4, BX, BY), 'shot', 0, 0, tiled=True)  15.1 us
    all_to_all x1, blocking collectives, on_device(): stats = lax.all_to_all(stats, 'shot', 0, 0, tiled=True)  14.3 us
    all_to_all x1, blocking collectives, on_device(): lax.all_to_all(payload, ('gx', 'gy'), 0, 0, axis_index_groups=same_core,...  11 us
    ppermute x7, waiting for transfers between devices, exchange(): lax.ppermute(strip, 'gy', [(0, 1), (1, 0)])  8.98 us
    ppermute x7, starting transfers between devices, exchange(): lax.ppermute(outer, 'gx', across)  8.26 us
    ppermute x7, waiting for transfers between devices, exchange(): lax.ppermute(outer, 'gx', across)  4.96 us
  transfers between devices with their start and end apart: 22, of which 12 were waited for; matrix products, arithmetic and copies ran while one was open for 1% of the time, Pallas kernels for 14%

profile of v5, /device:TPU:32, one launch (start us, length us, event | category | flops | bytes accessed | tf_op | source)
XLA Modules:
  0.0 126.6 jit_solution(1887573099998279778)
XLA Ops:
  2.0 1.0 copy-done
  4.3 1.6 %collective-permute-start.2 = (f32[1,16,128]{2,1,0:T(8,128)S(1)}, f32[1,16,128]{2,1,0:T(8,128)S(1)}, u32[]{:S(2)}, u32[]{:S(2)}) collective-permute-start(f32[1,16,128]{2,1,0:T(8,128)S(1)} %shard_map.117), channel_id=1, source_target_pairs={{0,1},{1,0},{2,3},{3,2},{4,5},{5,4},{6,7},{7,6},{8,9},{9,8},{10,11... | collective-permute-start | bytes 24584 | tf_op jit(solution)/shard_map/ppermute | solution.py:375
  5.8 2.2 %collective-permute-start = (f32[1,4,64,128]{3,2,1,0:T(8,128)S(1)}, f32[1,4,64,128]{3,2,1,0:T(8,128)S(1)}, u32[]{:S(2)}, u32[]{:S(2)}) collective-permute-start(f32[1,4,64,128]{3,2,1,0:T(8,128)S(1)} %get-tuple-element.56), channel_id=1, source_target_pairs={{2,4},{6,8},{10,12},{14,0},{4,2},{8,6},{12,10},{0,14},{3,5},{7,9},... | collective-permute-start | bytes 393224 | tf_op jit(solution)/shard_map/ppermute | solution.py:373
  8.0 0.7 or_convert_fusion
  8.8 0.8 pad_maximum_fusion.shot
  10.2 1.9 %shard_map.116 = (f32[8,64,128]{2,1,0:T(8,128)S(1)}, bf16[512,2048]{1,0:T(8,128)(2,1)S(1)}, bf16[128,2048]{1,0:T(8,128)(2,1)S(1)}) custom-call(s32[6]{0:T(128)S(1)} %stack.19.scal, f32[5,2048]{1,0:T(8,128)S(1)} %pad_maximum_fusion.shot), custom_call_target="tpu_custom_call" | custom-call | flops 10000000 | bytes 2000000 | tf_op jit(solution)/shard_map/pallas_call | solution.py:20
  12.1 0.9 copy-done.1
  13.0 0.9 copy-done.2
  14.1 0.9 shard_map.118
  15.0 1.0 collective-permute-start.3
  16.3 0.7 shard_map.121
  17.7 0.9 shard_map.120.inj
  18.6 1.2 shard_map.119
  19.8 1.1 collective-permute-done.5.rest_2_
  20.9 1.2 collective-permute-done.3.rest_0_
  22.1 1.0 shard_map.122
  23.2 1.0 collective-permute-start.6
  24.2 0.7 shard_map.125
  25.6 0.9 shard_map.124.inj
  26.5 1.2 shard_map.123
  27.7 1.1 collective-permute-done.8.rest_3_
  28.8 1.5 %collective-permute-done.6.rest_1_ = f32[2,4,64,128]{3,2,1,0:T(8,128)S(1)} collective-permute-done((f32[2,4,64,128]{3,2,1,0:T(8,128)S(1)}, f32[2,4,64,128]{3,2,1,0:T(8,128)S(1)}, u32[]{:S(2)}, u32[]{:S(2)}) %collective-permute-start.6) | collective-permute-done | bytes 262176 | tf_op jit(solution)/shard_map/ppermute | solution.py:373
  30.3 1.1 shard_map.126
  31.5 1.2 collective-permute-start.9
  32.7 0.7 shard_map.129
  34.0 0.9 shard_map.128.inj0
  34.9 1.2 shard_map.127
  36.2 1.1 collective-permute-done.11.strip
  37.3 1.5 %collective-permute-done.9.outer = f32[2,4,64,128]{3,2,1,0:T(8,128)S(1)} collective-permute-done((f32[2,4,64,128]{3,2,1,0:T(8,128)S(1)}, f32[2,4,64,128]{3,2,1,0:T(8,128)S(1)}, u32[]{:S(2)}, u32[]{:S(2)}) %collective-permute-start.9) | collective-permute-done | bytes 262176 | tf_op jit(solution)/shard_map/ppermute | solution.py:373
  38.7 1.1 shard_map.130
  39.8 21.9 %all_to_all.20 = f32[16,4,8,128]{3,2,1,0:T(8,128)S(1)} all-to-all(f32[16,4,8,128]{3,2,1,0:T(8,128)S(1)} %bitcast.20), channel_id=1, replica_groups=mesh['shot'=16,'gx'=8,'gy'=2] {'shot'}, dimensions={0} | all-to-all | bytes 524288 | tf_op jit(solution)/shard_map/all_to_all | solution.py:412
  61.7 15.1 %all_to_all.21 = f32[16,4,8,128]{3,2,1,0:T(8,128)S(1)} all-to-all(f32[16,4,8,128]{3,2,1,0:T(8,128)S(1)} %bitcast.21), channel_id=1, replica_groups=mesh['shot'=16,'gx'=8,'gy'=2] {'shot'}, dimensions={0} | all-to-all | bytes 524288 | tf_op jit(solution)/shard_map/all_to_all | solution.py:416
  79.2 0.8 shard_map.135.rest_0_.rest_2_
  80.7 2.0 %collective-permute-done.14.strip = f32[1,16,128]{2,1,0:T(8,128)S(1)} collective-permute-done((f32[1,16,128]{2,1,0:T(8,128)S(1)}, f32[1,16,128]{2,1,0:T(8,128)S(1)}, u32[]{:S(2)}, u32[]{:S(2)}) %collective-permute-start.14) | collective-permute-done | bytes 8224 | tf_op jit(solution)/shard_map/ppermute | solution.py:375
  83.2 0.9 shard_map.136
  84.1 1.0 collective-permute-start.15
  86.3 0.8 shard_map.139.rest_0_.rest_3_
  87.7 1.8 %collective-permute-done.17.strip = f32[1,16,128]{2,1,0:T(8,128)S(1)} collective-permute-done((f32[1,16,128]{2,1,0:T(8,128)S(1)}, f32[1,16,128]{2,1,0:T(8,128)S(1)}, u32[]{:S(2)}, u32[]{:S(2)}) %collective-permute-start.17) | collective-permute-done | bytes 8224 | tf_op jit(solution)/shard_map/ppermute | solution.py:375
  89.8 0.9 shard_map.140
  90.7 1.0 collective-permute-start.18
  91.7 1.0 collective-permute-start.19
  94.0 0.8 shard_map.143.rest_4_
  95.4 2.0 %collective-permute-done.20.strip = f32[1,16,128]{2,1,0:T(8,128)S(1)} collective-permute-done((f32[1,16,128]{2,1,0:T(8,128)S(1)}, f32[1,16,128]{2,1,0:T(8,128)S(1)}, u32[]{:S(2)}, u32[]{:S(2)}) %collective-permute-start.20) | collective-permute-done | bytes 8224 | tf_op jit(solution)/shard_map/ppermute | solution.py:375
  97.4 1.7 %shard_map.144.mine = f32[72,128]{1,0:T(8,128)S(1)} custom-call(s32[6]{0:T(128)S(1)} %stack.19.scal, f32[8,64,128]{2,1,0:T(8,128)S(1)} %shard_map.141.part, f32[8,64,128]{2,1,0:T(8,128)S(1)} %get-tuple-element.92.refs_0_.field.now, f32[8,64,128]{2,1,0:T(8,128)S(1)} %get-tuple-element.89.refs_0_.field.now.before, f32[8,64,128]{2,1,0:T(8,128)S(1)} %get-tuple-element.86.source, ...), custom_call_target="tpu_custom_call" | custom-call | flops 10000000 | bytes 2000000 | tf_op jit(solution)/shard_map/pallas_call | solution.py:20
  99.2 1.2 collective-permute-done.21.theirs
  100.4 11.0 %all_to_all.22.arrived = f32[8,72,128]{2,1,0:T(8,128)S(1)} all-to-all(f32[8,72,128]{2,1,0:T(8,128)S(1)} %shard_map.145), channel_id=1, replica_groups={{0,1,4,5,8,9,12,13},{2,3,6,7,10,11,14,15},{16,17,20,21,24,25,28,29},{18..., dimensions={0} | all-to-all | bytes 589824 | tf_op jit(solution)/shard_map/all_to_all | solution.py:437
  111.4 14.3 %all_to_all.23.stats = f32[16,8,128]{2,1,0:T(8,128)S(1)} all-to-all(f32[16,8,128]{2,1,0:T(8,128)S(1)} %get-tuple-element.97), channel_id=1, replica_groups=mesh['shot'=16,'gx'=8,'gy'=2] {'shot'}, dimensions={0} | all-to-all | bytes 131072 | tf_op jit(solution)/shard_map/all_to_all | solution.py:439
  125.8 0.8 shard_map.147
  (48 shorter events, 12.1 us)
Async XLA Ops:
  2.0 1.0 copy-start
  4.3 9.8 %collective-permute-start.2 = (f32[1,16,128]{2,1,0:T(8,128)S(1)}, f32[1,16,128]{2,1,0:T(8,128)S(1)}, u32[]{:S(2)}, u32[]{:S(2)}) collective-permute-start(f32[1,16,128]{2,1,0:T(8,128)S(1)} %shard_map.117), channel_id=1, source_target_pairs={{0,1},{1,0},{2,3},{3,2},{4,5},{5,4},{6,7},{7,6},{8,9},{9,8},{10,11... | collective-permute-start | bytes 24584 | tf_op jit(solution)/shard_map/ppermute | solution.py:375
  5.8 8.2 %collective-permute-start = (f32[1,4,64,128]{3,2,1,0:T(8,128)S(1)}, f32[1,4,64,128]{3,2,1,0:T(8,128)S(1)}, u32[]{:S(2)}, u32[]{:S(2)}) collective-permute-start(f32[1,4,64,128]{3,2,1,0:T(8,128)S(1)} %get-tuple-element.56), channel_id=1, source_target_pairs={{2,4},{6,8},{10,12},{14,0},{4,2},{8,6},{12,10},{0,14},{3,5},{7,9},... | collective-permute-start | bytes 393224 | tf_op jit(solution)/shard_map/ppermute | solution.py:373
  8.0 6.1 %collective-permute-start.1 = (f32[1,4,64,128]{3,2,1,0:T(8,128)S(1)}, f32[1,4,64,128]{3,2,1,0:T(8,128)S(1)}, u32[]{:S(2)}, u32[]{:S(2)}) collective-permute-start(f32[1,4,64,128]{3,2,1,0:T(8,128)S(1)} %get-tuple-element.57), channel_id=1, source_target_pairs={{0,2},{2,0},{4,6},{6,4},{8,10},{10,8},{12,14},{14,12},{1,3},{3,1},... | collective-permute-start | bytes 393224 | tf_op jit(solution)/shard_map/ppermute | solution.py:374
  12.1 1.0 copy-start.1
  13.0 0.9 copy-start.2
  15.0 7.1 %collective-permute-start.3 = (f32[2,4,64,128]{3,2,1,0:T(8,128)S(1)}, f32[2,4,64,128]{3,2,1,0:T(8,128)S(1)}, u32[]{:S(2)}, u32[]{:S(2)}) collective-permute-start(f32[2,4,64,128]{3,2,1,0:T(8,128)S(1)} %get-tuple-element.64), channel_id=1, source_target_pairs={{2,4},{6,8},{10,12},{14,0},{4,2},{8,6},{12,10},{0,14},{3,5},{7,9},... | collective-permute-start | bytes 786440 | tf_op jit(solution)/shard_map/ppermute | solution.py:373
  16.1 6.1 %collective-permute-start.4 = (f32[2,4,64,128]{3,2,1,0:T(8,128)S(1)}, f32[2,4,64,128]{3,2,1,0:T(8,128)S(1)}, u32[]{:S(2)}, u32[]{:S(2)}) collective-permute-start(f32[2,4,64,128]{3,2,1,0:T(8,128)S(1)} %get-tuple-element.65), channel_id=1, source_target_pairs={{0,2},{2,0},{4,6},{6,4},{8,10},{10,8},{12,14},{14,12},{1,3},{3,1},... | collective-permute-start | bytes 786440 | tf_op jit(solution)/shard_map/ppermute | solution.py:374
  17.1 3.8 %collective-permute-start.5 = (f32[2,16,128]{2,1,0:T(8,128)S(1)}, f32[2,16,128]{2,1,0:T(8,128)S(1)}, u32[]{:S(2)}, u32[]{:S(2)}) collective-permute-start(f32[2,16,128]{2,1,0:T(8,128)S(1)} %shard_map.121), channel_id=1, source_target_pairs={{0,1},{1,0},{2,3},{3,2},{4,5},{5,4},{6,7},{7,6},{8,9},{9,8},{10,11... | collective-permute-start | bytes 49160 | tf_op jit(solution)/shard_map/ppermute | solution.py:375
  23.2 7.1 %collective-permute-start.6 = (f32[2,4,64,128]{3,2,1,0:T(8,128)S(1)}, f32[2,4,64,128]{3,2,1,0:T(8,128)S(1)}, u32[]{:S(2)}, u32[]{:S(2)}) collective-permute-start(f32[2,4,64,128]{3,2,1,0:T(8,128)S(1)} %get-tuple-element.71), channel_id=1, source_target_pairs={{2,4},{6,8},{10,12},{14,0},{4,2},{8,6},{12,10},{0,14},{3,5},{7,9},... | collective-permute-start | bytes 786440 | tf_op jit(solution)/shard_map/ppermute | solution.py:373
  24.2 6.0 %collective-permute-start.7 = (f32[2,4,64,128]{3,2,1,0:T(8,128)S(1)}, f32[2,4,64,128]{3,2,1,0:T(8,128)S(1)}, u32[]{:S(2)}, u32[]{:S(2)}) collective-permute-start(f32[2,4,64,128]{3,2,1,0:T(8,128)S(1)} %get-tuple-element.72), channel_id=1, source_target_pairs={{0,2},{2,0},{4,6},{6,4},{8,10},{10,8},{12,14},{14,12},{1,3},{3,1},... | collective-permute-start | bytes 786440 | tf_op jit(solution)/shard_map/ppermute | solution.py:374
  25.0 3.8 %collective-permute-start.8 = (f32[2,16,128]{2,1,0:T(8,128)S(1)}, f32[2,16,128]{2,1,0:T(8,128)S(1)}, u32[]{:S(2)}, u32[]{:S(2)}) collective-permute-start(f32[2,16,128]{2,1,0:T(8,128)S(1)} %shard_map.125), channel_id=1, source_target_pairs={{0,1},{1,0},{2,3},{3,2},{4,5},{5,4},{6,7},{7,6},{8,9},{9,8},{10,11... | collective-permute-start | bytes 49160 | tf_op jit(solution)/shard_map/ppermute | solution.py:375
  31.4 5.9 %collective-permute-start.10 = (f32[2,4,64,128]{3,2,1,0:T(8,128)S(1)}, f32[2,4,64,128]{3,2,1,0:T(8,128)S(1)}, u32[]{:S(2)}, u32[]{:S(2)}) collective-permute-start(f32[2,4,64,128]{3,2,1,0:T(8,128)S(1)} %get-tuple-element.82), channel_id=1, source_target_pairs={{0,2},{2,0},{4,6},{6,4},{8,10},{10,8},{12,14},{14,12},{1,3},{3,1},... | collective-permute-start | bytes 786440 | tf_op jit(solution)/shard_map/ppermute | solution.py:374
  31.5 7.3 %collective-permute-start.9 = (f32[2,4,64,128]{3,2,1,0:T(8,128)S(1)}, f32[2,4,64,128]{3,2,1,0:T(8,128)S(1)}, u32[]{:S(2)}, u32[]{:S(2)}) collective-permute-start(f32[2,4,64,128]{3,2,1,0:T(8,128)S(1)} %get-tuple-element.81), channel_id=1, source_target_pairs={{2,4},{6,8},{10,12},{14,0},{4,2},{8,6},{12,10},{0,14},{3,5},{7,9},... | collective-permute-start | bytes 786440 | tf_op jit(solution)/shard_map/ppermute | solution.py:373
  33.4 3.8 %collective-permute-start.11 = (f32[2,16,128]{2,1,0:T(8,128)S(1)}, f32[2,16,128]{2,1,0:T(8,128)S(1)}, u32[]{:S(2)}, u32[]{:S(2)}) collective-permute-start(f32[2,16,128]{2,1,0:T(8,128)S(1)} %shard_map.129), channel_id=1, source_target_pairs={{0,1},{1,0},{2,3},{3,2},{4,5},{5,4},{6,7},{7,6},{8,9},{9,8},{10,11... | collective-permute-start | bytes 49160 | tf_op jit(solution)/shard_map/ppermute | solution.py:375
  34.9 26.7 %copy-start.4 = (f32[4,8,128]{2,1,0:T(8,128)S(1)}, f32[4,8,128]{2,1,0:T(8,128)}, u32[]{:S(2)}) copy-start(f32[4,8,128]{2,1,0:T(8,128)} %param.13) | copy-start | bytes 49156
  77.5 5.7 %collective-permute-start.12 = (f32[1,4,64,128]{3,2,1,0:T(8,128)S(1)}, f32[1,4,64,128]{3,2,1,0:T(8,128)S(1)}, u32[]{:S(2)}, u32[]{:S(2)}) collective-permute-start(f32[1,4,64,128]{3,2,1,0:T(8,128)S(1)} %get-tuple-element.87), channel_id=1, source_target_pairs={{2,4},{6,8},{10,12},{14,0},{4,2},{8,6},{12,10},{0,14},{3,5},{7,9},... | collective-permute-start | bytes 393224 | tf_op jit(solution)/shard_map/ppermute | solution.py:373
  78.2 5.0 %collective-permute-start.13 = (f32[1,4,64,128]{3,2,1,0:T(8,128)S(1)}, f32[1,4,64,128]{3,2,1,0:T(8,128)S(1)}, u32[]{:S(2)}, u32[]{:S(2)}) collective-permute-start(f32[1,4,64,128]{3,2,1,0:T(8,128)S(1)} %get-tuple-element.88), channel_id=1, source_target_pairs={{0,2},{2,0},{4,6},{6,4},{8,10},{10,8},{12,14},{14,12},{1,3},{3,1},... | collective-permute-start | bytes 393224 | tf_op jit(solution)/shard_map/ppermute | solution.py:374
  78.9 3.7 %collective-permute-start.14 = (f32[1,16,128]{2,1,0:T(8,128)S(1)}, f32[1,16,128]{2,1,0:T(8,128)S(1)}, u32[]{:S(2)}, u32[]{:S(2)}) collective-permute-start(f32[1,16,128]{2,1,0:T(8,128)S(1)} %shard_map.134), channel_id=1, source_target_pairs={{0,1},{1,0},{2,3},{3,2},{4,5},{5,4},{6,7},{7,6},{8,9},{9,8},{10,11... | collective-permute-start | bytes 24584 | tf_op jit(solution)/shard_map/ppermute | solution.py:375
  84.1 5.7 %collective-permute-start.15 = (f32[1,4,64,128]{3,2,1,0:T(8,128)S(1)}, f32[1,4,64,128]{3,2,1,0:T(8,128)S(1)}, u32[]{:S(2)}, u32[]{:S(2)}) collective-permute-start(f32[1,4,64,128]{3,2,1,0:T(8,128)S(1)} %get-tuple-element.90), channel_id=1, source_target_pairs={{2,4},{6,8},{10,12},{14,0},{4,2},{8,6},{12,10},{0,14},{3,5},{7,9},... | collective-permute-start | bytes 393224 | tf_op jit(solution)/shard_map/ppermute | solution.py:373
  85.1 4.7 %collective-permute-start.16 = (f32[1,4,64,128]{3,2,1,0:T(8,128)S(1)}, f32[1,4,64,128]{3,2,1,0:T(8,128)S(1)}, u32[]{:S(2)}, u32[]{:S(2)}) collective-permute-start(f32[1,4,64,128]{3,2,1,0:T(8,128)S(1)} %get-tuple-element.91), channel_id=1, source_target_pairs={{0,2},{2,0},{4,6},{6,4},{8,10},{10,8},{12,14},{14,12},{1,3},{3,1},... | collective-permute-start | bytes 393224 | tf_op jit(solution)/shard_map/ppermute | solution.py:374
  85.8 3.7 %collective-permute-start.17 = (f32[1,16,128]{2,1,0:T(8,128)S(1)}, f32[1,16,128]{2,1,0:T(8,128)S(1)}, u32[]{:S(2)}, u32[]{:S(2)}) collective-permute-start(f32[1,16,128]{2,1,0:T(8,128)S(1)} %shard_map.138), channel_id=1, source_target_pairs={{0,1},{1,0},{2,3},{3,2},{4,5},{5,4},{6,7},{7,6},{8,9},{9,8},{10,11... | collective-permute-start | bytes 24584 | tf_op jit(solution)/shard_map/ppermute | solution.py:375
  90.7 6.7 %collective-permute-start.18 = (f32[1,4,64,128]{3,2,1,0:T(8,128)S(1)}, f32[1,4,64,128]{3,2,1,0:T(8,128)S(1)}, u32[]{:S(2)}, u32[]{:S(2)}) collective-permute-start(f32[1,4,64,128]{3,2,1,0:T(8,128)S(1)} %get-tuple-element.94), channel_id=1, source_target_pairs={{2,4},{6,8},{10,12},{14,0},{4,2},{8,6},{12,10},{0,14},{3,5},{7,9},... | collective-permute-start | bytes 393224 | tf_op jit(solution)/shard_map/ppermute | solution.py:373
  91.7 5.7 %collective-permute-start.19 = (f32[1,4,64,128]{3,2,1,0:T(8,128)S(1)}, f32[1,4,64,128]{3,2,1,0:T(8,128)S(1)}, u32[]{:S(2)}, u32[]{:S(2)}) collective-permute-start(f32[1,4,64,128]{3,2,1,0:T(8,128)S(1)} %get-tuple-element.95), channel_id=1, source_target_pairs={{0,2},{2,0},{4,6},{6,4},{8,10},{10,8},{12,14},{14,12},{1,3},{3,1},... | collective-permute-start | bytes 393224 | tf_op jit(solution)/shard_map/ppermute | solution.py:374
  93.4 4.0 %collective-permute-start.20 = (f32[1,16,128]{2,1,0:T(8,128)S(1)}, f32[1,16,128]{2,1,0:T(8,128)S(1)}, u32[]{:S(2)}, u32[]{:S(2)}) collective-permute-start(f32[1,16,128]{2,1,0:T(8,128)S(1)} %shard_map.142), channel_id=1, source_target_pairs={{0,1},{1,0},{2,3},{3,2},{4,5},{5,4},{6,7},{7,6},{8,9},{9,8},{10,11... | collective-permute-start | bytes 24584 | tf_op jit(solution)/shard_map/ppermute | solution.py:375
  97.4 28.4 %copy-start.3 = (f32[1,4,2048]{2,1,0:T(4,128)S(1)}, f32[1,4,2048]{2,1,0:T(4,128)}, u32[]{:S(2)}) copy-start(f32[1,4,2048]{2,1,0:T(4,128)} %param.14) | copy-start | bytes 98308
  99.1 1.3 %collective-permute-start.21 = (f32[72,128]{1,0:T(8,128)S(1)}, f32[72,128]{1,0:T(8,128)S(1)}, u32[]{:S(2)}, u32[]{:S(2)}) collective-permute-start(f32[72,128]{1,0:T(8,128)S(1)} %shard_map.144.mine), channel_id=1, source_target_pairs={{0,2},{2,0},{4,6},{6,4},{8,10},{10,8},{12,14},{14,12},{1,3},{3,1},... | collective-permute-start | bytes 110600 | tf_op jit(solution)/shard_map/ppermute | solution.py:434

commit v6 on v4

--- a/solution.py
+++ b/solution.py
@@ -10,6 +10,11 @@
 NREC = 2048
 F32, BF16, I32 = jnp.float32, jnp.bfloat16, jnp.int32
 weights = (-205.0 / 72.0, 8.0 / 5.0, -1.0 / 5.0, 8.0 / 315.0, -1.0 / 560.0)
+
+
+def position():
+    gx, gy = lax.axis_index("gx"), lax.axis_index("gy")
+    return gx & 1, gy, gx * BX, gy * BY
 
 
 def call(kernel, outs, scratch=(), limit=24, flops=10_000_000):
@@ -127,7 +132,8 @@
     return [((count, 4, NZ, BY), F32), ((count, 4, NZ, BY), F32), ((count, 16, BY), F32)]
 
 
-def first_kernel(scal, newer, newer_out, outer, inner, strip):
+def first_kernel(newer, newer_out, outer, inner, strip):
+    scal = position()
     for x in range(BX):
         newer_out[x] = newer[pl.ds(x, NZ, stride=8), :]
     send_edges(newer_out, outer, inner, strip, 0, scal)
@@ -173,7 +179,8 @@
     return kernel
 
 
-def prepare_kernel(scal, shot, inj, pick_cell, pick_y, at_depth, spread):
+def prepare_kernel(shot, inj, pick_cell, pick_y, at_depth, spread):
+    scal = position()
     code = shot[4:5, :].astype(I32)
     lat_x = ((code >> 6) & 63) - scal[2]
     lat_y = (code >> 12) - scal[3]
@@ -213,7 +220,8 @@
         vel[x] = vel_in[pl.ds(x, NZ, stride=8), :]
 
 
-def forward1_kernel(scal, part, newer, older, vel, inj3, outer, inner, strip, acc, nxt, q, outer_o, inner_o, strip_o, halo):
+def forward1_kernel(part, newer, older, vel, inj3, outer, inner, strip, acc, nxt, q, outer_o, inner_o, strip_o, halo):
+    scal = position()
     strips = receive(halo, outer, inner, strip, 0, scal)
     for x in range(BX):
         a = vel[x] * complete(part, halo, strips, x, scal)
@@ -225,7 +233,8 @@
 
 
 def make_forward(moment):
-    def kernel(scal, part, part_q, newer, older, vel, inj, inj3, *rest):
+    def kernel(part, part_q, newer, older, vel, inj, inj3, *rest):
+        scal = position()
         if moment == 2:
             later, rest = rest[0], rest[1:]
         outer, inner, strip, acc, nxt, p, q, outer_o, inner_o, strip_o, halo, halo_q = rest
@@ -246,14 +255,22 @@
     return kernel
 
 
-def window(scal, x):
-    column = lanes(NZ) + scal[3]
-    at_x = scal[2] + x
-    inside_x = (at_x >= scal[4]) & (at_x < scal[4] + 48)
-    return (column >= scal[5]) & (column < scal[5] + 192) & inside_x
-
-
-def last_kernel(scal, part, part_q, vel, inj0, inj3, latest, later, acc0, acc1, acc2, outer, inner, strip, acc3, grad, halo, halo_q):
+def window_kernel(aperture_x, aperture_y, after, mask):
+    _, _, first_x, first_y = position()
+    column = lanes(8) + first_y
+    inside_y = (column >= aperture_y[0]) & (column < aperture_y[0] + 192)
+    for x in range(BX):
+        inside_x = (first_x + x >= aperture_x[0]) & (first_x + x < aperture_x[0] + 48)
+        mask[x] = jnp.where(inside_y & inside_x, 1.0, 0.0)
+
+
+def masked(mask, x, values):
+    inside = jnp.broadcast_to(mask[x, 0:1], (NZ, BY)) > 0.5
+    return jnp.where(inside, values, 0.0)
+
+
+def last_kernel(mask, part, part_q, vel, inj0, inj3, latest, later, acc0, acc1, acc2, outer, inner, strip, acc3, grad, halo, halo_q):
+    scal = position()
     strips = receive(halo, outer, inner, strip, 0, scal)
     strips_q = receive(halo_q, outer, inner, strip, 1, scal)
     for x in range(BX):
@@ -261,7 +278,7 @@
         acc3[x] = a
         p0 = ((2.0 * later[x] - latest[x]) + complete(part_q, halo_q, strips_q, x, scal)) + inj0[x]
         total = ((a * inj3[x] + acc2[x] * latest[x]) + acc1[x] * later[x]) + acc0[x] * p0
-        grad[pl.ds(x, NZ, stride=8), :] = jnp.where(window(scal, x), total, 0.0)
+        grad[pl.ds(x, NZ, stride=8), :] = masked(mask, x, total)
 
 
 def gradient_kernel(parts, pre, scaled, copies, dot):
@@ -276,16 +293,18 @@
     dot[...] = (product[0:8] + product[8:16]) + (product[16:24] + product[24:32])
 
 
-def born1_kernel(scal, full, acc0, source, d, outer_o, inner_o, strip_o):
-    for x in range(BX):
-        s = jnp.where(window(scal, x), full[pl.ds(x, NZ, stride=8), :], 0.0)
+def born1_kernel(mask, full, acc0, source, d, outer_o, inner_o, strip_o):
+    scal = position()
+    for x in range(BX):
+        s = masked(mask, x, full[pl.ds(x, NZ, stride=8), :])
         source[x] = s
         d[x] = s * acc0[x]
     send_edges(d, outer_o, inner_o, strip_o, 0, scal)
 
 
 def make_born(moment, last):
-    def kernel(scal, part, now, before, source, acc, vel, outer, inner, strip, *rest):
+    def kernel(part, now, before, source, acc, vel, outer, inner, strip, *rest):
+        scal = position()
         if last:
             pick_cell, pick_y, s1, s2, s3, dot, block, halo, d, pieces = rest
         else:
@@ -373,9 +392,7 @@
 def on_device(older_field, newer_field, velocity, preconditioner, traces,
               receiver_z, receiver_x, receiver_y, aperture_x, aperture_y):
     flat = (NZ * BX, BY)
-    gx, gy = lax.axis_index("gx"), lax.axis_index("gy")
-    scal = jnp.stack([gx % 2, gy, gx * BX, gy * BY, aperture_x[0], aperture_y[0]]).astype(I32)
-    newer, *e = call(first_kernel, [FIELD] + edges(1))(scal, newer_field.reshape(flat), smem=1)
+    newer, *e = call(first_kernel, [FIELD] + edges(1))(newer_field.reshape(flat))
     e = exchange(*e)
     code = receiver_z | (receiver_x << 6) | (receiver_y << 12)
     shot = jnp.concatenate([traces[0], code.astype(F32)], axis=0)
@@ -383,7 +400,7 @@
         prepare_kernel,
         [FIELD, ((512, NREC), BF16), ((BY, NREC), BF16)],
         [pltpu.VMEM((NZ, NREC), BF16), pltpu.VMEM((2 * BY, NREC), BF16)],
-    )(scal, shot, smem=1)
+    )(shot)
 
     def injection(n):
         return call(make_inject(n), [FIELD], [pltpu.VMEM((2 * BY, NREC), BF16)], flops=1_000_000_000)(
@@ -393,38 +410,39 @@
     two = call(interior_kernel, [FIELD] * 2, [PADDED])
     older, vel = call(planes_kernel, [FIELD, FIELD])(older_field.reshape(flat), velocity.reshape(flat))
     acc0, u1, q, *e = call(forward1_kernel, [FIELD] * 3 + edges(2), [HALO])(
-        scal, *one(newer), newer, older, vel, inj3, *e, smem=1)
+        *one(newer), newer, older, vel, inj3, *e)
     e = exchange(*e)
     acc1, u2, p2, q, *e = call(make_forward(1), [FIELD] * 4 + edges(2), [HALO] * 2)(
-        scal, *two(u1, q), u1, newer, vel, injection(2), inj3, *e, smem=1)
+        *two(u1, q), u1, newer, vel, injection(2), inj3, *e)
     e = exchange(*e)
     acc2, u3, p1, q, *e = call(make_forward(2), [FIELD] * 4 + edges(2), [HALO] * 2)(
-        scal, *two(u2, q), u2, u1, vel, injection(1), inj3, p2, *e, smem=1)
-    e = exchange(*e)
+        *two(u2, q), u2, u1, vel, injection(1), inj3, p2, *e)
+    e = exchange(*e)
+    mask, = call(window_kernel, [((BX, 8, BY), F32)])(aperture_x, aperture_y, u2, smem=2)
     acc3, grad = call(last_kernel, [FIELD, (flat, F32)], [HALO] * 2)(
-        scal, *two(u3, q), vel, injection(0), inj3, p2, p1, acc0, acc1, acc2, *e, smem=1)
+        mask, *two(u3, q), vel, injection(0), inj3, p2, p1, acc0, acc1, acc2, *e)
     parts = lax.all_to_all(grad.reshape(16, 4, BX, BY), "shot", 0, 0, tiled=True)
     scaled, copies, dot = call(
         gradient_kernel, [((32, BY), F32), (flat, F32), ((8, BY), F32)])(
         parts.reshape(flat), preconditioner.reshape(32, BY))
     full = lax.all_to_all(copies.reshape(16, 4, BX, BY), "shot", 0, 0, tiled=True)
     source, d1, *e = call(born1_kernel, [FIELD, FIELD] + edges(1))(
-        scal, full.reshape(flat), acc0, smem=1)
+        mask, full.reshape(flat), acc0)
     e = exchange(*e)
     sample = call(sample_kernel, [((1, NREC), F32)], [pltpu.VMEM((512, 2 * BY), BF16)], flops=600_000_000)
     s1, = sample(d1, pick_cell, pick_y)
     d2, *e = call(make_born(1, False), [FIELD] + edges(1), [HALO])(
-        scal, *one(d1), d1, d1, source, acc1, vel, *e, s1, smem=1)
+        *one(d1), d1, d1, source, acc1, vel, *e, s1)
     e = exchange(*e)
     s2, = sample(d2, pick_cell, pick_y)
     d3, *e = call(make_born(2, False), [FIELD] + edges(1), [HALO])(
-        scal, *one(d2), d2, d1, source, acc2, vel, *e, s2, smem=1)
+        *one(d2), d2, d1, source, acc2, vel, *e, s2)
     e = exchange(*e)
     s3, = sample(d3, pick_cell, pick_y)
     block, = call(
         make_born(3, True), [((72, BY), F32)],
         [HALO, pltpu.VMEM((BX, NZ, BY), F32), pltpu.VMEM((512, 2 * BY), BF16)],
-    )(scal, *one(d3), d3, d2, source, acc3, vel, *e, pick_cell, pick_y, s1, s2, s3, dot, smem=1)
+    )(*one(d3), d3, d2, source, acc3, vel, *e, pick_cell, pick_y, s1, s2, s3, dot)
     theirs = lax.ppermute(block, "gx", [(i, i ^ 1) for i in range(8)])
     payload, = call(pair_kernel, [((8, 72, BY), F32)])(block, theirs)
     same_core = [[2 * (2 * c + k) + g for c in range(4) for g in range(2)] for k in range(2)]

time: 126 us -> 119 us (0.944)
  Pallas kernels: 23.6 us -> 18.3 us
    pallas_call x28 -> x29, Pallas kernels: 23.6 us -> 18.3 us  [run(): pl.pallas_call(kernel, out_shape=[jax.ShapeDtypeStruct(s, d) for s, d in...]
  transfers between devices with their start and end apart: 22 -> 22, of which waited for: 13 -> 12; matrix products, arithmetic and copies ran while one was open for 1% -> 1% of each run, Pallas kernels for 11% -> 11%
where the time goes in v6:
time: 119 us
  blocking collectives  61.6 us (52%)
  waiting for transfers between devices  21.1 us (18%)
  Pallas kernels  18.3 us (15%)
  starting transfers between devices  11 us (9%)
  local copies, waits for them, and re-layouts  2.85 us (2%)
  between operations  2.2 us (2%)
  other arithmetic  1.53 us (1%)
    all_to_all x1, blocking collectives, on_device(): lax.all_to_all(grad.reshape(16, 4, BX, BY), 'shot', 0, 0, tiled=True)  21.9 us
    pallas_call x29, Pallas kernels, run(): pl.pallas_call(kernel, out_shape=[jax.ShapeDtypeStruct(s, d) for s, d in...  18.3 us
    all_to_all x1, blocking collectives, on_device(): lax.all_to_all(copies.reshape(16, 4, BX, BY), 'shot', 0, 0, tiled=True)  15.1 us
    all_to_all x1, blocking collectives, on_device(): stats = lax.all_to_all(stats, 'shot', 0, 0, tiled=True)  13.8 us
    ppermute x7, waiting for transfers between devices, exchange(): lax.ppermute(outer, 'gx', across)  12.4 us
    all_to_all x1, blocking collectives, on_device(): lax.all_to_all(payload, ('gx', 'gy'), 0, 0, axis_index_groups=same_core,...  10.8 us
    ppermute x7, waiting for transfers between devices, exchange(): lax.ppermute(strip, 'gy', [(0, 1), (1, 0)])  7.49 us
    ppermute x7, starting transfers between devices, exchange(): lax.ppermute(outer, 'gx', across)  5.81 us
  transfers between devices with their start and end apart: 22, of which 12 were waited for; matrix products, arithmetic and copies ran while one was open for 1% of the time, Pallas kernels for 11%

profile of v6, /device:TPU:32, one launch (start us, length us, event | category | flops | bytes accessed | tf_op | source)
XLA Modules:
  0.0 118.5 jit_solution(13915074493503817036)
XLA Ops:
  0.6 0.9 copy-done
  1.8 2.5 %collective-permute-start = (f32[1,4,64,128]{3,2,1,0:T(8,128)S(1)}, f32[1,4,64,128]{3,2,1,0:T(8,128)S(1)}, u32[]{:S(2)}, u32[]{:S(2)}) collective-permute-start(f32[1,4,64,128]{3,2,1,0:T(8,128)S(1)} %get-tuple-element.63), channel_id=1, source_target_pairs={{2,4},{6,8},{10,12},{14,0},{4,2},{8,6},{12,10},{0,14},{3,5},{7,9},... | collective-permute-start | bytes 393224 | tf_op jit(solution)/shard_map/ppermute | solution.py:386
  4.3 1.5 %collective-permute-start.2 = (f32[1,16,128]{2,1,0:T(8,128)S(1)}, f32[1,16,128]{2,1,0:T(8,128)S(1)}, u32[]{:S(2)}, u32[]{:S(2)}) collective-permute-start(f32[1,16,128]{2,1,0:T(8,128)S(1)} %get-tuple-element.65), channel_id=1, source_target_pairs={{0,1},{1,0},{2,3},{3,2},{4,5},{5,4},{6,7},{7,6},{8,9},{9,8},{10,11... | collective-permute-start | bytes 24584 | tf_op jit(solution)/shard_map/ppermute | solution.py:388
  5.8 0.7 or_convert_fusion
  6.6 0.8 pad_maximum_fusion.shot
  7.3 1.3 %shard_map.116 = (f32[8,64,128]{2,1,0:T(8,128)S(1)}, bf16[512,2048]{1,0:T(8,128)(2,1)S(1)}, bf16[128,2048]{1,0:T(8,128)(2,1)S(1)}) custom-call(f32[5,2048]{1,0:T(8,128)S(1)} %pad_maximum_fusion.shot), custom_call_target="tpu_custom_call" | custom-call | flops 10000000 | bytes 2000000 | tf_op jit(solution)/shard_map/pallas_call | solution.py:25
  8.7 0.6 shard_map.114.part
  9.3 0.9 copy-done.1
  10.2 0.9 copy-done.2
  11.8 0.7 collective-permute-start.3
  12.8 0.5 collective-permute-start.5
  13.3 0.9 shard_map.119.inj
  14.2 1.2 %shard_map.118 = (f32[8,64,128]{2,1,0:T(8,128)S(1)}, f32[8,64,128]{2,1,0:T(8,128)S(1)}) custom-call(f32[8,64,128]{2,1,0:T(8,128)S(1)} %get-tuple-element.66.refs_0_.newer.older, f32[8,64,128]{2,1,0:T(8,128)S(1)} %get-tuple-element.67.refs_1_), custom_call_target="tpu_custom_call" | custom-call | flops 10000000 | bytes 2000000 | tf_op jit(solution)/shard_map/pallas_call | solution.py:25
  15.5 1.1 collective-permute-done.5.rest_2_
  16.5 2.3 %collective-permute-done.3.rest_0_ = f32[2,4,64,128]{3,2,1,0:T(8,128)S(1)} collective-permute-done((f32[2,4,64,128]{3,2,1,0:T(8,128)S(1)}, f32[2,4,64,128]{3,2,1,0:T(8,128)S(1)}, u32[]{:S(2)}, u32[]{:S(2)}) %collective-permute-start.3) | collective-permute-done | bytes 262176 | tf_op jit(solution)/shard_map/ppermute | solution.py:386
  18.9 0.7 shard_map.120
  19.6 0.7 collective-permute-start.6
  20.3 0.5 collective-permute-start.8
  20.8 0.9 shard_map.123.inj
  21.7 1.2 %shard_map.122 = (f32[8,64,128]{2,1,0:T(8,128)S(1)}, f32[8,64,128]{2,1,0:T(8,128)S(1)}) custom-call(f32[8,64,128]{2,1,0:T(8,128)S(1)} %get-tuple-element.75.after.refs_0_.newer, f32[8,64,128]{2,1,0:T(8,128)S(1)} %get-tuple-element.76.refs_1_), custom_call_target="tpu_custom_call" | custom-call | flops 10000000 | bytes 2000000 | tf_op jit(solution)/shard_map/pallas_call | solution.py:25
  22.9 1.1 collective-permute-done.8.rest_3_
  24.0 2.7 %collective-permute-done.6.rest_1_ = f32[2,4,64,128]{3,2,1,0:T(8,128)S(1)} collective-permute-done((f32[2,4,64,128]{3,2,1,0:T(8,128)S(1)}, f32[2,4,64,128]{3,2,1,0:T(8,128)S(1)}, u32[]{:S(2)}, u32[]{:S(2)}) %collective-permute-start.6) | collective-permute-done | bytes 262176 | tf_op jit(solution)/shard_map/ppermute | solution.py:386
  26.7 0.7 shard_map.124
  27.5 0.9 collective-permute-start.9
  28.4 0.5 collective-permute-start.11
  28.9 0.9 shard_map.126.inj0
  31.1 1.2 shard_map.125
  32.3 2.5 %collective-permute-done.9.outer = f32[2,4,64,128]{3,2,1,0:T(8,128)S(1)} collective-permute-done((f32[2,4,64,128]{3,2,1,0:T(8,128)S(1)}, f32[2,4,64,128]{3,2,1,0:T(8,128)S(1)}, u32[]{:S(2)}, u32[]{:S(2)}) %collective-permute-start.9) | collective-permute-done | bytes 262176 | tf_op jit(solution)/shard_map/ppermute | solution.py:386
  35.3 21.9 %all_to_all.20 = f32[16,4,8,128]{3,2,1,0:T(8,128)S(1)} all-to-all(f32[16,4,8,128]{3,2,1,0:T(8,128)S(1)} %bitcast.16), channel_id=1, replica_groups=mesh['shot'=16,'gx'=8,'gy'=2] {'shot'}, dimensions={0} | all-to-all | bytes 524288 | tf_op jit(solution)/shard_map/all_to_all | solution.py:424
  57.2 15.1 %all_to_all.21 = f32[16,4,8,128]{3,2,1,0:T(8,128)S(1)} all-to-all(f32[16,4,8,128]{3,2,1,0:T(8,128)S(1)} %bitcast.17), channel_id=1, replica_groups=mesh['shot'=16,'gx'=8,'gy'=2] {'shot'}, dimensions={0} | all-to-all | bytes 524288 | tf_op jit(solution)/shard_map/all_to_all | solution.py:428
  73.4 0.8 shard_map.131.rest_0_.rest_2_
  74.1 0.7 shard_map.130.part
  74.8 1.7 %collective-permute-done.14.strip = f32[1,16,128]{2,1,0:T(8,128)S(1)} collective-permute-done((f32[1,16,128]{2,1,0:T(8,128)S(1)}, f32[1,16,128]{2,1,0:T(8,128)S(1)}, u32[]{:S(2)}, u32[]{:S(2)}) %collective-permute-start.14) | collective-permute-done | bytes 8224 | tf_op jit(solution)/shard_map/ppermute | solution.py:388
  76.6 1.7 %collective-permute-done.12.outer = f32[1,4,64,128]{3,2,1,0:T(8,128)S(1)} collective-permute-done((f32[1,4,64,128]{3,2,1,0:T(8,128)S(1)}, f32[1,4,64,128]{3,2,1,0:T(8,128)S(1)}, u32[]{:S(2)}, u32[]{:S(2)}) %collective-permute-start.12) | collective-permute-done | bytes 131104 | tf_op jit(solution)/shard_map/ppermute | solution.py:386
  79.5 0.8 shard_map.134.rest_0_.rest_3_
  80.3 0.6 shard_map.133.part
  81.0 1.8 %collective-permute-done.17.strip = f32[1,16,128]{2,1,0:T(8,128)S(1)} collective-permute-done((f32[1,16,128]{2,1,0:T(8,128)S(1)}, f32[1,16,128]{2,1,0:T(8,128)S(1)}, u32[]{:S(2)}, u32[]{:S(2)}) %collective-permute-start.17) | collective-permute-done | bytes 8224 | tf_op jit(solution)/shard_map/ppermute | solution.py:388
  82.8 1.7 %collective-permute-done.15.outer = f32[1,4,64,128]{3,2,1,0:T(8,128)S(1)} collective-permute-done((f32[1,4,64,128]{3,2,1,0:T(8,128)S(1)}, f32[1,4,64,128]{3,2,1,0:T(8,128)S(1)}, u32[]{:S(2)}, u32[]{:S(2)}) %collective-permute-start.15) | collective-permute-done | bytes 131104 | tf_op jit(solution)/shard_map/ppermute | solution.py:386
  85.3 0.7 collective-permute-start.20
  86.0 0.8 shard_map.137.rest_4_
  86.8 0.6 shard_map.136.part
  87.4 1.7 %collective-permute-done.20.strip = f32[1,16,128]{2,1,0:T(8,128)S(1)} collective-permute-done((f32[1,16,128]{2,1,0:T(8,128)S(1)}, f32[1,16,128]{2,1,0:T(8,128)S(1)}, u32[]{:S(2)}, u32[]{:S(2)}) %collective-permute-start.20) | collective-permute-done | bytes 8224 | tf_op jit(solution)/shard_map/ppermute | solution.py:388
  89.1 1.5 %collective-permute-done.18.outer = f32[1,4,64,128]{3,2,1,0:T(8,128)S(1)} collective-permute-done((f32[1,4,64,128]{3,2,1,0:T(8,128)S(1)}, f32[1,4,64,128]{3,2,1,0:T(8,128)S(1)}, u32[]{:S(2)}, u32[]{:S(2)}) %collective-permute-start.18) | collective-permute-done | bytes 131104 | tf_op jit(solution)/shard_map/ppermute | solution.py:386
  90.6 1.1 shard_map.138.mine
  91.8 1.2 %collective-permute-done.21.theirs = f32[72,128]{1,0:T(8,128)S(1)} collective-permute-done((f32[72,128]{1,0:T(8,128)S(1)}, f32[72,128]{1,0:T(8,128)S(1)}, u32[]{:S(2)}, u32[]{:S(2)}) %collective-permute-start.21) | collective-permute-done | bytes 36896 | tf_op jit(solution)/shard_map/ppermute | solution.py:446
  93.1 10.8 %all_to_all.22.arrived = f32[8,72,128]{2,1,0:T(8,128)S(1)} all-to-all(f32[8,72,128]{2,1,0:T(8,128)S(1)} %shard_map.139), channel_id=1, replica_groups={{0,1,4,5,8,9,12,13},{2,3,6,7,10,11,14,15},{16,17,20,21,24,25,28,29},{18..., dimensions={0} | all-to-all | bytes 589824 | tf_op jit(solution)/shard_map/all_to_all | solution.py:449
  103.9 13.8 %all_to_all.23.stats = f32[16,8,128]{2,1,0:T(8,128)S(1)} all-to-all(f32[16,8,128]{2,1,0:T(8,128)S(1)} %get-tuple-element.111), channel_id=1, replica_groups=mesh['shot'=16,'gx'=8,'gy'=2] {'shot'}, dimensions={0} | all-to-all | bytes 131072 | tf_op jit(solution)/shard_map/all_to_all | solution.py:451
  117.7 0.8 shard_map.141
  (41 shorter events, 5.1 us)
Async XLA Ops:
  0.6 1.0 copy-start
  1.8 9.5 %collective-permute-start = (f32[1,4,64,128]{3,2,1,0:T(8,128)S(1)}, f32[1,4,64,128]{3,2,1,0:T(8,128)S(1)}, u32[]{:S(2)}, u32[]{:S(2)}) collective-permute-start(f32[1,4,64,128]{3,2,1,0:T(8,128)S(1)} %get-tuple-element.63), channel_id=1, source_target_pairs={{2,4},{6,8},{10,12},{14,0},{4,2},{8,6},{12,10},{0,14},{3,5},{7,9},... | collective-permute-start | bytes 393224 | tf_op jit(solution)/shard_map/ppermute | solution.py:386
  4.3 7.0 %collective-permute-start.1 = (f32[1,4,64,128]{3,2,1,0:T(8,128)S(1)}, f32[1,4,64,128]{3,2,1,0:T(8,128)S(1)}, u32[]{:S(2)}, u32[]{:S(2)}) collective-permute-start(f32[1,4,64,128]{3,2,1,0:T(8,128)S(1)} %get-tuple-element.64), channel_id=1, source_target_pairs={{0,2},{2,0},{4,6},{6,4},{8,10},{10,8},{12,14},{14,12},{1,3},{3,1},... | collective-permute-start | bytes 393224 | tf_op jit(solution)/shard_map/ppermute | solution.py:387
  4.3 7.0 %collective-permute-start.2 = (f32[1,16,128]{2,1,0:T(8,128)S(1)}, f32[1,16,128]{2,1,0:T(8,128)S(1)}, u32[]{:S(2)}, u32[]{:S(2)}) collective-permute-start(f32[1,16,128]{2,1,0:T(8,128)S(1)} %get-tuple-element.65), channel_id=1, source_target_pairs={{0,1},{1,0},{2,3},{3,2},{4,5},{5,4},{6,7},{7,6},{8,9},{9,8},{10,11... | collective-permute-start | bytes 24584 | tf_op jit(solution)/shard_map/ppermute | solution.py:388
  9.3 1.0 copy-start.1
  10.2 0.9 copy-start.2
  11.8 7.1 %collective-permute-start.3 = (f32[2,4,64,128]{3,2,1,0:T(8,128)S(1)}, f32[2,4,64,128]{3,2,1,0:T(8,128)S(1)}, u32[]{:S(2)}, u32[]{:S(2)}) collective-permute-start(f32[2,4,64,128]{3,2,1,0:T(8,128)S(1)} %get-tuple-element.72), channel_id=1, source_target_pairs={{2,4},{6,8},{10,12},{14,0},{4,2},{8,6},{12,10},{0,14},{3,5},{7,9},... | collective-permute-start | bytes 786440 | tf_op jit(solution)/shard_map/ppermute | solution.py:386
  12.5 6.4 %collective-permute-start.4 = (f32[2,4,64,128]{3,2,1,0:T(8,128)S(1)}, f32[2,4,64,128]{3,2,1,0:T(8,128)S(1)}, u32[]{:S(2)}, u32[]{:S(2)}) collective-permute-start(f32[2,4,64,128]{3,2,1,0:T(8,128)S(1)} %get-tuple-element.73), channel_id=1, source_target_pairs={{0,2},{2,0},{4,6},{6,4},{8,10},{10,8},{12,14},{14,12},{1,3},{3,1},... | collective-permute-start | bytes 786440 | tf_op jit(solution)/shard_map/ppermute | solution.py:387
  12.8 3.7 %collective-permute-start.5 = (f32[2,16,128]{2,1,0:T(8,128)S(1)}, f32[2,16,128]{2,1,0:T(8,128)S(1)}, u32[]{:S(2)}, u32[]{:S(2)}) collective-permute-start(f32[2,16,128]{2,1,0:T(8,128)S(1)} %get-tuple-element.74), channel_id=1, source_target_pairs={{0,1},{1,0},{2,3},{3,2},{4,5},{5,4},{6,7},{7,6},{8,9},{9,8},{10,11... | collective-permute-start | bytes 49160 | tf_op jit(solution)/shard_map/ppermute | solution.py:388
  19.6 7.1 %collective-permute-start.6 = (f32[2,4,64,128]{3,2,1,0:T(8,128)S(1)}, f32[2,4,64,128]{3,2,1,0:T(8,128)S(1)}, u32[]{:S(2)}, u32[]{:S(2)}) collective-permute-start(f32[2,4,64,128]{3,2,1,0:T(8,128)S(1)} %get-tuple-element.80), channel_id=1, source_target_pairs={{2,4},{6,8},{10,12},{14,0},{4,2},{8,6},{12,10},{0,14},{3,5},{7,9},... | collective-permute-start | bytes 786440 | tf_op jit(solution)/shard_map/ppermute | solution.py:386
  20.3 6.4 %collective-permute-start.7 = (f32[2,4,64,128]{3,2,1,0:T(8,128)S(1)}, f32[2,4,64,128]{3,2,1,0:T(8,128)S(1)}, u32[]{:S(2)}, u32[]{:S(2)}) collective-permute-start(f32[2,4,64,128]{3,2,1,0:T(8,128)S(1)} %get-tuple-element.81), channel_id=1, source_target_pairs={{0,2},{2,0},{4,6},{6,4},{8,10},{10,8},{12,14},{14,12},{1,3},{3,1},... | collective-permute-start | bytes 786440 | tf_op jit(solution)/shard_map/ppermute | solution.py:387
  20.3 3.7 %collective-permute-start.8 = (f32[2,16,128]{2,1,0:T(8,128)S(1)}, f32[2,16,128]{2,1,0:T(8,128)S(1)}, u32[]{:S(2)}, u32[]{:S(2)}) collective-permute-start(f32[2,16,128]{2,1,0:T(8,128)S(1)} %get-tuple-element.82), channel_id=1, source_target_pairs={{0,1},{1,0},{2,3},{3,2},{4,5},{5,4},{6,7},{7,6},{8,9},{9,8},{10,11... | collective-permute-start | bytes 49160 | tf_op jit(solution)/shard_map/ppermute | solution.py:388
  27.4 4.9 %collective-permute-start.10 = (f32[2,4,64,128]{3,2,1,0:T(8,128)S(1)}, f32[2,4,64,128]{3,2,1,0:T(8,128)S(1)}, u32[]{:S(2)}, u32[]{:S(2)}) collective-permute-start(f32[2,4,64,128]{3,2,1,0:T(8,128)S(1)} %get-tuple-element.92), channel_id=1, source_target_pairs={{0,2},{2,0},{4,6},{6,4},{8,10},{10,8},{12,14},{14,12},{1,3},{3,1},... | collective-permute-start | bytes 786440 | tf_op jit(solution)/shard_map/ppermute | solution.py:387
  27.5 7.3 %collective-permute-start.9 = (f32[2,4,64,128]{3,2,1,0:T(8,128)S(1)}, f32[2,4,64,128]{3,2,1,0:T(8,128)S(1)}, u32[]{:S(2)}, u32[]{:S(2)}) collective-permute-start(f32[2,4,64,128]{3,2,1,0:T(8,128)S(1)} %get-tuple-element.91), channel_id=1, source_target_pairs={{2,4},{6,8},{10,12},{14,0},{4,2},{8,6},{12,10},{0,14},{3,5},{7,9},... | collective-permute-start | bytes 786440 | tf_op jit(solution)/shard_map/ppermute | solution.py:386
  28.4 3.9 %collective-permute-start.11 = (f32[2,16,128]{2,1,0:T(8,128)S(1)}, f32[2,16,128]{2,1,0:T(8,128)S(1)}, u32[]{:S(2)}, u32[]{:S(2)}) collective-permute-start(f32[2,16,128]{2,1,0:T(8,128)S(1)} %get-tuple-element.93), channel_id=1, source_target_pairs={{0,1},{1,0},{2,3},{3,2},{4,5},{5,4},{6,7},{7,6},{8,9},{9,8},{10,11... | collective-permute-start | bytes 49160 | tf_op jit(solution)/shard_map/ppermute | solution.py:388
  31.1 26.1 %copy-start.4 = (f32[4,8,128]{2,1,0:T(8,128)S(1)}, f32[4,8,128]{2,1,0:T(8,128)}, u32[]{:S(2)}) copy-start(f32[4,8,128]{2,1,0:T(8,128)} %param.13) | copy-start | bytes 49156
  72.6 5.7 %collective-permute-start.12 = (f32[1,4,64,128]{3,2,1,0:T(8,128)S(1)}, f32[1,4,64,128]{3,2,1,0:T(8,128)S(1)}, u32[]{:S(2)}, u32[]{:S(2)}) collective-permute-start(f32[1,4,64,128]{3,2,1,0:T(8,128)S(1)} %get-tuple-element.98), channel_id=1, source_target_pairs={{2,4},{6,8},{10,12},{14,0},{4,2},{8,6},{12,10},{0,14},{3,5},{7,9},... | collective-permute-start | bytes 393224 | tf_op jit(solution)/shard_map/ppermute | solution.py:386
  72.9 5.3 %collective-permute-start.13 = (f32[1,4,64,128]{3,2,1,0:T(8,128)S(1)}, f32[1,4,64,128]{3,2,1,0:T(8,128)S(1)}, u32[]{:S(2)}, u32[]{:S(2)}) collective-permute-start(f32[1,4,64,128]{3,2,1,0:T(8,128)S(1)} %get-tuple-element.99), channel_id=1, source_target_pairs={{0,2},{2,0},{4,6},{6,4},{8,10},{10,8},{12,14},{14,12},{1,3},{3,1},... | collective-permute-start | bytes 393224 | tf_op jit(solution)/shard_map/ppermute | solution.py:387
  72.9 3.7 %collective-permute-start.14 = (f32[1,16,128]{2,1,0:T(8,128)S(1)}, f32[1,16,128]{2,1,0:T(8,128)S(1)}, u32[]{:S(2)}, u32[]{:S(2)}) collective-permute-start(f32[1,16,128]{2,1,0:T(8,128)S(1)} %get-tuple-element.100), channel_id=1, source_target_pairs={{0,1},{1,0},{2,3},{3,2},{4,5},{5,4},{6,7},{7,6},{8,9},{9,8},{10,11... | collective-permute-start | bytes 24584 | tf_op jit(solution)/shard_map/ppermute | solution.py:388
  78.7 5.7 %collective-permute-start.15 = (f32[1,4,64,128]{3,2,1,0:T(8,128)S(1)}, f32[1,4,64,128]{3,2,1,0:T(8,128)S(1)}, u32[]{:S(2)}, u32[]{:S(2)}) collective-permute-start(f32[1,4,64,128]{3,2,1,0:T(8,128)S(1)} %get-tuple-element.102), channel_id=1, source_target_pairs={{2,4},{6,8},{10,12},{14,0},{4,2},{8,6},{12,10},{0,14},{3,5},{7,9},... | collective-permute-start | bytes 393224 | tf_op jit(solution)/shard_map/ppermute | solution.py:386
  79.1 5.3 %collective-permute-start.16 = (f32[1,4,64,128]{3,2,1,0:T(8,128)S(1)}, f32[1,4,64,128]{3,2,1,0:T(8,128)S(1)}, u32[]{:S(2)}, u32[]{:S(2)}) collective-permute-start(f32[1,4,64,128]{3,2,1,0:T(8,128)S(1)} %get-tuple-element.103), channel_id=1, source_target_pairs={{0,2},{2,0},{4,6},{6,4},{8,10},{10,8},{12,14},{14,12},{1,3},{3,1},... | collective-permute-start | bytes 393224 | tf_op jit(solution)/shard_map/ppermute | solution.py:387
  79.1 3.7 %collective-permute-start.17 = (f32[1,16,128]{2,1,0:T(8,128)S(1)}, f32[1,16,128]{2,1,0:T(8,128)S(1)}, u32[]{:S(2)}, u32[]{:S(2)}) collective-permute-start(f32[1,16,128]{2,1,0:T(8,128)S(1)} %get-tuple-element.104), channel_id=1, source_target_pairs={{0,1},{1,0},{2,3},{3,2},{4,5},{5,4},{6,7},{7,6},{8,9},{9,8},{10,11... | collective-permute-start | bytes 24584 | tf_op jit(solution)/shard_map/ppermute | solution.py:388
  84.9 5.7 %collective-permute-start.18 = (f32[1,4,64,128]{3,2,1,0:T(8,128)S(1)}, f32[1,4,64,128]{3,2,1,0:T(8,128)S(1)}, u32[]{:S(2)}, u32[]{:S(2)}) collective-permute-start(f32[1,4,64,128]{3,2,1,0:T(8,128)S(1)} %get-tuple-element.107), channel_id=1, source_target_pairs={{2,4},{6,8},{10,12},{14,0},{4,2},{8,6},{12,10},{0,14},{3,5},{7,9},... | collective-permute-start | bytes 393224 | tf_op jit(solution)/shard_map/ppermute | solution.py:386
  85.3 5.3 %collective-permute-start.19 = (f32[1,4,64,128]{3,2,1,0:T(8,128)S(1)}, f32[1,4,64,128]{3,2,1,0:T(8,128)S(1)}, u32[]{:S(2)}, u32[]{:S(2)}) collective-permute-start(f32[1,4,64,128]{3,2,1,0:T(8,128)S(1)} %get-tuple-element.108), channel_id=1, source_target_pairs={{0,2},{2,0},{4,6},{6,4},{8,10},{10,8},{12,14},{14,12},{1,3},{3,1},... | collective-permute-start | bytes 393224 | tf_op jit(solution)/shard_map/ppermute | solution.py:387
  85.3 3.8 %collective-permute-start.20 = (f32[1,16,128]{2,1,0:T(8,128)S(1)}, f32[1,16,128]{2,1,0:T(8,128)S(1)}, u32[]{:S(2)}, u32[]{:S(2)}) collective-permute-start(f32[1,16,128]{2,1,0:T(8,128)S(1)} %get-tuple-element.109), channel_id=1, source_target_pairs={{0,1},{1,0},{2,3},{3,2},{4,5},{5,4},{6,7},{7,6},{8,9},{9,8},{10,11... | collective-permute-start | bytes 24584 | tf_op jit(solution)/shard_map/ppermute | solution.py:388
  90.6 27.1 %copy-start.3 = (f32[1,4,2048]{2,1,0:T(4,128)S(1)}, f32[1,4,2048]{2,1,0:T(4,128)}, u32[]{:S(2)}) copy-start(f32[1,4,2048]{2,1,0:T(4,128)} %param.14) | copy-start | bytes 98308
  91.7 1.3 %collective-permute-start.21 = (f32[72,128]{1,0:T(8,128)S(1)}, f32[72,128]{1,0:T(8,128)S(1)}, u32[]{:S(2)}, u32[]{:S(2)}) collective-permute-start(f32[72,128]{1,0:T(8,128)S(1)} %shard_map.138.mine), channel_id=1, source_target_pairs={{0,2},{2,0},{4,6},{6,4},{8,10},{10,8},{12,14},{14,12},{1,3},{3,1},... | collective-permute-start | bytes 110600 | tf_op jit(solution)/shard_map/ppermute | solution.py:446

commit v7 on v6

--- a/solution.py
+++ b/solution.py
@@ -214,10 +214,10 @@
     inject(3, shot, pick_cell, pick_y, spread, inj)
 
 
-def planes_kernel(older_in, vel_in, older, vel):
-    for x in range(BX):
-        older[x] = older_in[pl.ds(x, NZ, stride=8), :]
-        vel[x] = vel_in[pl.ds(x, NZ, stride=8), :]
+def planes_kernel(both, older, vel):
+    for x in range(BX):
+        older[x] = both[pl.ds(x, NZ, stride=8), :]
+        vel[x] = both[pl.ds(NZ * BX + x, NZ, stride=8), :]
 
 
 def forward1_kernel(part, newer, older, vel, inj3, outer, inner, strip, acc, nxt, q, outer_o, inner_o, strip_o, halo):
@@ -408,7 +408,8 @@
 
     one = call(interior_kernel, [FIELD], [PADDED])
     two = call(interior_kernel, [FIELD] * 2, [PADDED])
-    older, vel = call(planes_kernel, [FIELD, FIELD])(older_field.reshape(flat), velocity.reshape(flat))
+    both = jnp.concatenate([older_field.reshape(flat), velocity.reshape(flat)], axis=0)
+    older, vel = call(planes_kernel, [FIELD, FIELD])(both)
     acc0, u1, q, *e = call(forward1_kernel, [FIELD] * 3 + edges(2), [HALO])(
         *one(newer), newer, older, vel, inj3, *e)
     e = exchange(*e)

time: 119 us -> 118 us (level)
  local copies, waits for them, and re-layouts: 2.85 us -> 0.95 us
    unnamed x10 -> x6, local copies, waits for them, and re-layouts: 2.85 us -> 0.95 us
  transfers between devices with their start and end apart: 22 -> 22, of which waited for: 12 -> 12; matrix products, arithmetic and copies ran while one was open for 1% -> 2% of each run, Pallas kernels for 11% -> 11%
where the time goes in v7:
time: 118 us
  blocking collectives  61.8 us (52%)
  waiting for transfers between devices  21.8 us (18%)
  Pallas kernels  18.3 us (16%)
  starting transfers between devices  10.2 us (9%)
  other arithmetic  2.59 us (2%)
  between operations  2.21 us (2%)
    all_to_all x1, blocking collectives, on_device(): lax.all_to_all(grad.reshape(16, 4, BX, BY), 'shot', 0, 0, tiled=True)  22 us
    pallas_call x29, Pallas kernels, run(): pl.pallas_call(kernel, out_shape=[jax.ShapeDtypeStruct(s, d) for s, d in...  18.3 us
    all_to_all x1, blocking collectives, on_device(): lax.all_to_all(copies.reshape(16, 4, BX, BY), 'shot', 0, 0, tiled=True)  15.4 us
    all_to_all x1, blocking collectives, on_device(): stats = lax.all_to_all(stats, 'shot', 0, 0, tiled=True)  13.6 us
    ppermute x7, waiting for transfers between devices, exchange(): lax.ppermute(outer, 'gx', across)  12.5 us
    all_to_all x1, blocking collectives, on_device(): lax.all_to_all(payload, ('gx', 'gy'), 0, 0, axis_index_groups=same_core,...  10.8 us
    ppermute x7, waiting for transfers between devices, exchange(): lax.ppermute(strip, 'gy', [(0, 1), (1, 0)])  8.05 us
    ppermute x7, starting transfers between devices, exchange(): lax.ppermute(outer, 'gx', across)  5.19 us
  transfers between devices with their start and end apart: 22, of which 12 were waited for; matrix products, arithmetic and copies ran while one was open for 2% of the time, Pallas kernels for 11%

profile of v7, /device:TPU:32, one launch (start us, length us, event | category | flops | bytes accessed | tf_op | source)
XLA Modules:
  0.0 117.9 jit_solution(14584180728500248006)
XLA Ops:
  0.6 0.9 copy-done
  1.8 2.5 %collective-permute-start = (f32[1,4,64,128]{3,2,1,0:T(8,128)S(1)}, f32[1,4,64,128]{3,2,1,0:T(8,128)S(1)}, u32[]{:S(2)}, u32[]{:S(2)}) collective-permute-start(f32[1,4,64,128]{3,2,1,0:T(8,128)S(1)} %get-tuple-element.63), channel_id=1, source_target_pairs={{2,4},{6,8},{10,12},{14,0},{4,2},{8,6},{12,10},{0,14},{3,5},{7,9},... | collective-permute-start | bytes 393224 | tf_op jit(solution)/shard_map/ppermute | solution.py:386
  4.3 1.5 %collective-permute-start.2 = (f32[1,16,128]{2,1,0:T(8,128)S(1)}, f32[1,16,128]{2,1,0:T(8,128)S(1)}, u32[]{:S(2)}, u32[]{:S(2)}) collective-permute-start(f32[1,16,128]{2,1,0:T(8,128)S(1)} %get-tuple-element.65), channel_id=1, source_target_pairs={{0,1},{1,0},{2,3},{3,2},{4,5},{5,4},{6,7},{7,6},{8,9},{9,8},{10,11... | collective-permute-start | bytes 24584 | tf_op jit(solution)/shard_map/ppermute | solution.py:388
  5.8 0.7 or_convert_fusion
  6.6 0.8 pad_maximum_fusion.1.shot
  7.3 1.1 pad_maximum_fusion.both
  8.4 1.3 %shard_map.116 = (f32[8,64,128]{2,1,0:T(8,128)S(1)}, bf16[512,2048]{1,0:T(8,128)(2,1)S(1)}, bf16[128,2048]{1,0:T(8,128)(2,1)S(1)}) custom-call(f32[5,2048]{1,0:T(8,128)S(1)} %pad_maximum_fusion.1.shot), custom_call_target="tpu_custom_call" | custom-call | flops 10000000 | bytes 2000000 | tf_op jit(solution)/shard_map/pallas_call | solution.py:25
  9.8 0.6 shard_map.114.part
  11.0 0.7 collective-permute-start.3
  12.0 0.5 collective-permute-start.5
  12.5 0.9 shard_map.119.inj
  13.4 1.2 %shard_map.118 = (f32[8,64,128]{2,1,0:T(8,128)S(1)}, f32[8,64,128]{2,1,0:T(8,128)S(1)}) custom-call(f32[8,64,128]{2,1,0:T(8,128)S(1)} %get-tuple-element.66.refs_0_.newer.older, f32[8,64,128]{2,1,0:T(8,128)S(1)} %get-tuple-element.67.refs_1_), custom_call_target="tpu_custom_call" | custom-call | flops 10000000 | bytes 2000000 | tf_op jit(solution)/shard_map/pallas_call | solution.py:25
  14.6 1.1 collective-permute-done.5.rest_2_
  15.7 2.3 %collective-permute-done.3.rest_0_ = f32[2,4,64,128]{3,2,1,0:T(8,128)S(1)} collective-permute-done((f32[2,4,64,128]{3,2,1,0:T(8,128)S(1)}, f32[2,4,64,128]{3,2,1,0:T(8,128)S(1)}, u32[]{:S(2)}, u32[]{:S(2)}) %collective-permute-start.3) | collective-permute-done | bytes 262176 | tf_op jit(solution)/shard_map/ppermute | solution.py:386
  18.1 0.7 shard_map.120
  18.8 0.7 collective-permute-start.6
  19.5 0.5 collective-permute-start.8
  20.0 0.9 shard_map.123.inj
  20.9 1.2 %shard_map.122 = (f32[8,64,128]{2,1,0:T(8,128)S(1)}, f32[8,64,128]{2,1,0:T(8,128)S(1)}) custom-call(f32[8,64,128]{2,1,0:T(8,128)S(1)} %get-tuple-element.75.after.refs_0_.newer, f32[8,64,128]{2,1,0:T(8,128)S(1)} %get-tuple-element.76.refs_1_), custom_call_target="tpu_custom_call" | custom-call | flops 10000000 | bytes 2000000 | tf_op jit(solution)/shard_map/pallas_call | solution.py:25
  22.1 1.1 collective-permute-done.8.rest_3_
  23.2 2.7 %collective-permute-done.6.rest_1_ = f32[2,4,64,128]{3,2,1,0:T(8,128)S(1)} collective-permute-done((f32[2,4,64,128]{3,2,1,0:T(8,128)S(1)}, f32[2,4,64,128]{3,2,1,0:T(8,128)S(1)}, u32[]{:S(2)}, u32[]{:S(2)}) %collective-permute-start.6) | collective-permute-done | bytes 262176 | tf_op jit(solution)/shard_map/ppermute | solution.py:386
  25.9 0.7 shard_map.124
  26.9 0.7 collective-permute-start.9
  27.5 0.5 collective-permute-start.11
  28.1 0.9 shard_map.126.inj0
  30.3 1.2 shard_map.125
  31.5 2.5 %collective-permute-done.9.outer = f32[2,4,64,128]{3,2,1,0:T(8,128)S(1)} collective-permute-done((f32[2,4,64,128]{3,2,1,0:T(8,128)S(1)}, f32[2,4,64,128]{3,2,1,0:T(8,128)S(1)}, u32[]{:S(2)}, u32[]{:S(2)}) %collective-permute-start.9) | collective-permute-done | bytes 262176 | tf_op jit(solution)/shard_map/ppermute | solution.py:386
  34.0 0.5 shard_map.127
  34.5 22.0 %all_to_all.20 = f32[16,4,8,128]{3,2,1,0:T(8,128)S(1)} all-to-all(f32[16,4,8,128]{3,2,1,0:T(8,128)S(1)} %bitcast.14), channel_id=1, replica_groups=mesh['shot'=16,'gx'=8,'gy'=2] {'shot'}, dimensions={0} | all-to-all | bytes 524288 | tf_op jit(solution)/shard_map/all_to_all | solution.py:425
  56.5 15.4 %all_to_all.21 = f32[16,4,8,128]{3,2,1,0:T(8,128)S(1)} all-to-all(f32[16,4,8,128]{3,2,1,0:T(8,128)S(1)} %bitcast.15), channel_id=1, replica_groups=mesh['shot'=16,'gx'=8,'gy'=2] {'shot'}, dimensions={0} | all-to-all | bytes 524288 | tf_op jit(solution)/shard_map/all_to_all | solution.py:429
  72.6 0.8 shard_map.131.rest_0_.rest_2_
  73.4 0.7 shard_map.130.part
  74.1 2.0 %collective-permute-done.14.strip = f32[1,16,128]{2,1,0:T(8,128)S(1)} collective-permute-done((f32[1,16,128]{2,1,0:T(8,128)S(1)}, f32[1,16,128]{2,1,0:T(8,128)S(1)}, u32[]{:S(2)}, u32[]{:S(2)}) %collective-permute-start.14) | collective-permute-done | bytes 8224 | tf_op jit(solution)/shard_map/ppermute | solution.py:388
  76.1 1.8 %collective-permute-done.12.outer = f32[1,4,64,128]{3,2,1,0:T(8,128)S(1)} collective-permute-done((f32[1,4,64,128]{3,2,1,0:T(8,128)S(1)}, f32[1,4,64,128]{3,2,1,0:T(8,128)S(1)}, u32[]{:S(2)}, u32[]{:S(2)}) %collective-permute-start.12) | collective-permute-done | bytes 131104 | tf_op jit(solution)/shard_map/ppermute | solution.py:386
  79.0 0.8 shard_map.134.rest_0_.rest_3_
  79.8 0.6 shard_map.133.part
  80.4 1.9 %collective-permute-done.17.strip = f32[1,16,128]{2,1,0:T(8,128)S(1)} collective-permute-done((f32[1,16,128]{2,1,0:T(8,128)S(1)}, f32[1,16,128]{2,1,0:T(8,128)S(1)}, u32[]{:S(2)}, u32[]{:S(2)}) %collective-permute-start.17) | collective-permute-done | bytes 8224 | tf_op jit(solution)/shard_map/ppermute | solution.py:388
  82.3 1.8 %collective-permute-done.15.outer = f32[1,4,64,128]{3,2,1,0:T(8,128)S(1)} collective-permute-done((f32[1,4,64,128]{3,2,1,0:T(8,128)S(1)}, f32[1,4,64,128]{3,2,1,0:T(8,128)S(1)}, u32[]{:S(2)}, u32[]{:S(2)}) %collective-permute-start.15) | collective-permute-done | bytes 131104 | tf_op jit(solution)/shard_map/ppermute | solution.py:386
  84.0 0.5 shard_map.135
  85.2 0.8 shard_map.137.rest_4_
  86.0 0.6 shard_map.136.part
  86.6 2.0 %collective-permute-done.20.strip = f32[1,16,128]{2,1,0:T(8,128)S(1)} collective-permute-done((f32[1,16,128]{2,1,0:T(8,128)S(1)}, f32[1,16,128]{2,1,0:T(8,128)S(1)}, u32[]{:S(2)}, u32[]{:S(2)}) %collective-permute-start.20) | collective-permute-done | bytes 8224 | tf_op jit(solution)/shard_map/ppermute | solution.py:388
  88.7 1.5 %collective-permute-done.18.outer = f32[1,4,64,128]{3,2,1,0:T(8,128)S(1)} collective-permute-done((f32[1,4,64,128]{3,2,1,0:T(8,128)S(1)}, f32[1,4,64,128]{3,2,1,0:T(8,128)S(1)}, u32[]{:S(2)}, u32[]{:S(2)}) %collective-permute-start.18) | collective-permute-done | bytes 131104 | tf_op jit(solution)/shard_map/ppermute | solution.py:386
  90.2 1.1 shard_map.138.mine
  91.4 1.2 %collective-permute-done.21.theirs = f32[72,128]{1,0:T(8,128)S(1)} collective-permute-done((f32[72,128]{1,0:T(8,128)S(1)}, f32[72,128]{1,0:T(8,128)S(1)}, u32[]{:S(2)}, u32[]{:S(2)}) %collective-permute-start.21) | collective-permute-done | bytes 36896 | tf_op jit(solution)/shard_map/ppermute | solution.py:447
  92.6 10.8 %all_to_all.22.arrived = f32[8,72,128]{2,1,0:T(8,128)S(1)} all-to-all(f32[8,72,128]{2,1,0:T(8,128)S(1)} %shard_map.139), channel_id=1, replica_groups={{0,1,4,5,8,9,12,13},{2,3,6,7,10,11,14,15},{16,17,20,21,24,25,28,29},{18..., dimensions={0} | all-to-all | bytes 589824 | tf_op jit(solution)/shard_map/all_to_all | solution.py:450
  103.5 13.6 %all_to_all.23.stats = f32[16,8,128]{2,1,0:T(8,128)S(1)} all-to-all(f32[16,8,128]{2,1,0:T(8,128)S(1)} %get-tuple-element.111), channel_id=1, replica_groups=mesh['shot'=16,'gx'=8,'gy'=2] {'shot'}, dimensions={0} | all-to-all | bytes 131072 | tf_op jit(solution)/shard_map/all_to_all | solution.py:452
  117.1 0.8 shard_map.141
  (38 shorter events, 4.2 us)
Async XLA Ops:
  0.6 1.0 copy-start
  1.8 8.7 %collective-permute-start = (f32[1,4,64,128]{3,2,1,0:T(8,128)S(1)}, f32[1,4,64,128]{3,2,1,0:T(8,128)S(1)}, u32[]{:S(2)}, u32[]{:S(2)}) collective-permute-start(f32[1,4,64,128]{3,2,1,0:T(8,128)S(1)} %get-tuple-element.63), channel_id=1, source_target_pairs={{2,4},{6,8},{10,12},{14,0},{4,2},{8,6},{12,10},{0,14},{3,5},{7,9},... | collective-permute-start | bytes 393224 | tf_op jit(solution)/shard_map/ppermute | solution.py:386
  4.3 6.2 %collective-permute-start.1 = (f32[1,4,64,128]{3,2,1,0:T(8,128)S(1)}, f32[1,4,64,128]{3,2,1,0:T(8,128)S(1)}, u32[]{:S(2)}, u32[]{:S(2)}) collective-permute-start(f32[1,4,64,128]{3,2,1,0:T(8,128)S(1)} %get-tuple-element.64), channel_id=1, source_target_pairs={{0,2},{2,0},{4,6},{6,4},{8,10},{10,8},{12,14},{14,12},{1,3},{3,1},... | collective-permute-start | bytes 393224 | tf_op jit(solution)/shard_map/ppermute | solution.py:387
  4.3 6.1 %collective-permute-start.2 = (f32[1,16,128]{2,1,0:T(8,128)S(1)}, f32[1,16,128]{2,1,0:T(8,128)S(1)}, u32[]{:S(2)}, u32[]{:S(2)}) collective-permute-start(f32[1,16,128]{2,1,0:T(8,128)S(1)} %get-tuple-element.65), channel_id=1, source_target_pairs={{0,1},{1,0},{2,3},{3,2},{4,5},{5,4},{6,7},{7,6},{8,9},{9,8},{10,11... | collective-permute-start | bytes 24584 | tf_op jit(solution)/shard_map/ppermute | solution.py:388
  11.0 7.1 %collective-permute-start.3 = (f32[2,4,64,128]{3,2,1,0:T(8,128)S(1)}, f32[2,4,64,128]{3,2,1,0:T(8,128)S(1)}, u32[]{:S(2)}, u32[]{:S(2)}) collective-permute-start(f32[2,4,64,128]{3,2,1,0:T(8,128)S(1)} %get-tuple-element.72), channel_id=1, source_target_pairs={{2,4},{6,8},{10,12},{14,0},{4,2},{8,6},{12,10},{0,14},{3,5},{7,9},... | collective-permute-start | bytes 786440 | tf_op jit(solution)/shard_map/ppermute | solution.py:386
  11.6 6.4 %collective-permute-start.4 = (f32[2,4,64,128]{3,2,1,0:T(8,128)S(1)}, f32[2,4,64,128]{3,2,1,0:T(8,128)S(1)}, u32[]{:S(2)}, u32[]{:S(2)}) collective-permute-start(f32[2,4,64,128]{3,2,1,0:T(8,128)S(1)} %get-tuple-element.73), channel_id=1, source_target_pairs={{0,2},{2,0},{4,6},{6,4},{8,10},{10,8},{12,14},{14,12},{1,3},{3,1},... | collective-permute-start | bytes 786440 | tf_op jit(solution)/shard_map/ppermute | solution.py:387
  12.0 3.7 %collective-permute-start.5 = (f32[2,16,128]{2,1,0:T(8,128)S(1)}, f32[2,16,128]{2,1,0:T(8,128)S(1)}, u32[]{:S(2)}, u32[]{:S(2)}) collective-permute-start(f32[2,16,128]{2,1,0:T(8,128)S(1)} %get-tuple-element.74), channel_id=1, source_target_pairs={{0,1},{1,0},{2,3},{3,2},{4,5},{5,4},{6,7},{7,6},{8,9},{9,8},{10,11... | collective-permute-start | bytes 49160 | tf_op jit(solution)/shard_map/ppermute | solution.py:388
  18.8 7.1 %collective-permute-start.6 = (f32[2,4,64,128]{3,2,1,0:T(8,128)S(1)}, f32[2,4,64,128]{3,2,1,0:T(8,128)S(1)}, u32[]{:S(2)}, u32[]{:S(2)}) collective-permute-start(f32[2,4,64,128]{3,2,1,0:T(8,128)S(1)} %get-tuple-element.80), channel_id=1, source_target_pairs={{2,4},{6,8},{10,12},{14,0},{4,2},{8,6},{12,10},{0,14},{3,5},{7,9},... | collective-permute-start | bytes 786440 | tf_op jit(solution)/shard_map/ppermute | solution.py:386
  19.4 6.4 %collective-permute-start.7 = (f32[2,4,64,128]{3,2,1,0:T(8,128)S(1)}, f32[2,4,64,128]{3,2,1,0:T(8,128)S(1)}, u32[]{:S(2)}, u32[]{:S(2)}) collective-permute-start(f32[2,4,64,128]{3,2,1,0:T(8,128)S(1)} %get-tuple-element.81), channel_id=1, source_target_pairs={{0,2},{2,0},{4,6},{6,4},{8,10},{10,8},{12,14},{14,12},{1,3},{3,1},... | collective-permute-start | bytes 786440 | tf_op jit(solution)/shard_map/ppermute | solution.py:387
  19.5 3.7 %collective-permute-start.8 = (f32[2,16,128]{2,1,0:T(8,128)S(1)}, f32[2,16,128]{2,1,0:T(8,128)S(1)}, u32[]{:S(2)}, u32[]{:S(2)}) collective-permute-start(f32[2,16,128]{2,1,0:T(8,128)S(1)} %get-tuple-element.82), channel_id=1, source_target_pairs={{0,1},{1,0},{2,3},{3,2},{4,5},{5,4},{6,7},{7,6},{8,9},{9,8},{10,11... | collective-permute-start | bytes 49160 | tf_op jit(solution)/shard_map/ppermute | solution.py:388
  26.6 4.9 %collective-permute-start.10 = (f32[2,4,64,128]{3,2,1,0:T(8,128)S(1)}, f32[2,4,64,128]{3,2,1,0:T(8,128)S(1)}, u32[]{:S(2)}, u32[]{:S(2)}) collective-permute-start(f32[2,4,64,128]{3,2,1,0:T(8,128)S(1)} %get-tuple-element.92), channel_id=1, source_target_pairs={{0,2},{2,0},{4,6},{6,4},{8,10},{10,8},{12,14},{14,12},{1,3},{3,1},... | collective-permute-start | bytes 786440 | tf_op jit(solution)/shard_map/ppermute | solution.py:387
  26.9 7.1 %collective-permute-start.9 = (f32[2,4,64,128]{3,2,1,0:T(8,128)S(1)}, f32[2,4,64,128]{3,2,1,0:T(8,128)S(1)}, u32[]{:S(2)}, u32[]{:S(2)}) collective-permute-start(f32[2,4,64,128]{3,2,1,0:T(8,128)S(1)} %get-tuple-element.91), channel_id=1, source_target_pairs={{2,4},{6,8},{10,12},{14,0},{4,2},{8,6},{12,10},{0,14},{3,5},{7,9},... | collective-permute-start | bytes 786440 | tf_op jit(solution)/shard_map/ppermute | solution.py:386
  27.5 3.9 %collective-permute-start.11 = (f32[2,16,128]{2,1,0:T(8,128)S(1)}, f32[2,16,128]{2,1,0:T(8,128)S(1)}, u32[]{:S(2)}, u32[]{:S(2)}) collective-permute-start(f32[2,16,128]{2,1,0:T(8,128)S(1)} %get-tuple-element.93), channel_id=1, source_target_pairs={{0,1},{1,0},{2,3},{3,2},{4,5},{5,4},{6,7},{7,6},{8,9},{9,8},{10,11... | collective-permute-start | bytes 49160 | tf_op jit(solution)/shard_map/ppermute | solution.py:388
  30.3 26.2 %copy-start.2 = (f32[4,8,128]{2,1,0:T(8,128)S(1)}, f32[4,8,128]{2,1,0:T(8,128)}, u32[]{:S(2)}) copy-start(f32[4,8,128]{2,1,0:T(8,128)} %param.13) | copy-start | bytes 49156
  72.1 5.7 %collective-permute-start.12 = (f32[1,4,64,128]{3,2,1,0:T(8,128)S(1)}, f32[1,4,64,128]{3,2,1,0:T(8,128)S(1)}, u32[]{:S(2)}, u32[]{:S(2)}) collective-permute-start(f32[1,4,64,128]{3,2,1,0:T(8,128)S(1)} %get-tuple-element.98), channel_id=1, source_target_pairs={{2,4},{6,8},{10,12},{14,0},{4,2},{8,6},{12,10},{0,14},{3,5},{7,9},... | collective-permute-start | bytes 393224 | tf_op jit(solution)/shard_map/ppermute | solution.py:386
  72.3 5.5 %collective-permute-start.13 = (f32[1,4,64,128]{3,2,1,0:T(8,128)S(1)}, f32[1,4,64,128]{3,2,1,0:T(8,128)S(1)}, u32[]{:S(2)}, u32[]{:S(2)}) collective-permute-start(f32[1,4,64,128]{3,2,1,0:T(8,128)S(1)} %get-tuple-element.99), channel_id=1, source_target_pairs={{0,2},{2,0},{4,6},{6,4},{8,10},{10,8},{12,14},{14,12},{1,3},{3,1},... | collective-permute-start | bytes 393224 | tf_op jit(solution)/shard_map/ppermute | solution.py:387
  72.3 3.7 %collective-permute-start.14 = (f32[1,16,128]{2,1,0:T(8,128)S(1)}, f32[1,16,128]{2,1,0:T(8,128)S(1)}, u32[]{:S(2)}, u32[]{:S(2)}) collective-permute-start(f32[1,16,128]{2,1,0:T(8,128)S(1)} %get-tuple-element.100), channel_id=1, source_target_pairs={{0,1},{1,0},{2,3},{3,2},{4,5},{5,4},{6,7},{7,6},{8,9},{9,8},{10,11... | collective-permute-start | bytes 24584 | tf_op jit(solution)/shard_map/ppermute | solution.py:388
  78.3 5.7 %collective-permute-start.15 = (f32[1,4,64,128]{3,2,1,0:T(8,128)S(1)}, f32[1,4,64,128]{3,2,1,0:T(8,128)S(1)}, u32[]{:S(2)}, u32[]{:S(2)}) collective-permute-start(f32[1,4,64,128]{3,2,1,0:T(8,128)S(1)} %get-tuple-element.102), channel_id=1, source_target_pairs={{2,4},{6,8},{10,12},{14,0},{4,2},{8,6},{12,10},{0,14},{3,5},{7,9},... | collective-permute-start | bytes 393224 | tf_op jit(solution)/shard_map/ppermute | solution.py:386
  78.6 5.4 %collective-permute-start.16 = (f32[1,4,64,128]{3,2,1,0:T(8,128)S(1)}, f32[1,4,64,128]{3,2,1,0:T(8,128)S(1)}, u32[]{:S(2)}, u32[]{:S(2)}) collective-permute-start(f32[1,4,64,128]{3,2,1,0:T(8,128)S(1)} %get-tuple-element.103), channel_id=1, source_target_pairs={{0,2},{2,0},{4,6},{6,4},{8,10},{10,8},{12,14},{14,12},{1,3},{3,1},... | collective-permute-start | bytes 393224 | tf_op jit(solution)/shard_map/ppermute | solution.py:387
  78.6 3.7 %collective-permute-start.17 = (f32[1,16,128]{2,1,0:T(8,128)S(1)}, f32[1,16,128]{2,1,0:T(8,128)S(1)}, u32[]{:S(2)}, u32[]{:S(2)}) collective-permute-start(f32[1,16,128]{2,1,0:T(8,128)S(1)} %get-tuple-element.104), channel_id=1, source_target_pairs={{0,1},{1,0},{2,3},{3,2},{4,5},{5,4},{6,7},{7,6},{8,9},{9,8},{10,11... | collective-permute-start | bytes 24584 | tf_op jit(solution)/shard_map/ppermute | solution.py:388
  84.5 5.7 %collective-permute-start.18 = (f32[1,4,64,128]{3,2,1,0:T(8,128)S(1)}, f32[1,4,64,128]{3,2,1,0:T(8,128)S(1)}, u32[]{:S(2)}, u32[]{:S(2)}) collective-permute-start(f32[1,4,64,128]{3,2,1,0:T(8,128)S(1)} %get-tuple-element.107), channel_id=1, source_target_pairs={{2,4},{6,8},{10,12},{14,0},{4,2},{8,6},{12,10},{0,14},{3,5},{7,9},... | collective-permute-start | bytes 393224 | tf_op jit(solution)/shard_map/ppermute | solution.py:386
  84.8 5.4 %collective-permute-start.19 = (f32[1,4,64,128]{3,2,1,0:T(8,128)S(1)}, f32[1,4,64,128]{3,2,1,0:T(8,128)S(1)}, u32[]{:S(2)}, u32[]{:S(2)}) collective-permute-start(f32[1,4,64,128]{3,2,1,0:T(8,128)S(1)} %get-tuple-element.108), channel_id=1, source_target_pairs={{0,2},{2,0},{4,6},{6,4},{8,10},{10,8},{12,14},{14,12},{1,3},{3,1},... | collective-permute-start | bytes 393224 | tf_op jit(solution)/shard_map/ppermute | solution.py:387
  84.8 3.9 %collective-permute-start.20 = (f32[1,16,128]{2,1,0:T(8,128)S(1)}, f32[1,16,128]{2,1,0:T(8,128)S(1)}, u32[]{:S(2)}, u32[]{:S(2)}) collective-permute-start(f32[1,16,128]{2,1,0:T(8,128)S(1)} %get-tuple-element.109), channel_id=1, source_target_pairs={{0,1},{1,0},{2,3},{3,2},{4,5},{5,4},{6,7},{7,6},{8,9},{9,8},{10,11... | collective-permute-start | bytes 24584 | tf_op jit(solution)/shard_map/ppermute | solution.py:388
  90.2 26.9 %copy-start.1 = (f32[1,4,2048]{2,1,0:T(4,128)S(1)}, f32[1,4,2048]{2,1,0:T(4,128)}, u32[]{:S(2)}) copy-start(f32[1,4,2048]{2,1,0:T(4,128)} %param.14) | copy-start | bytes 98308
  91.3 1.3 %collective-permute-start.21 = (f32[72,128]{1,0:T(8,128)S(1)}, f32[72,128]{1,0:T(8,128)S(1)}, u32[]{:S(2)}, u32[]{:S(2)}) collective-permute-start(f32[72,128]{1,0:T(8,128)S(1)} %shard_map.138.mine), channel_id=1, source_target_pairs={{0,2},{2,0},{4,6},{6,4},{8,10},{10,8},{12,14},{14,12},{1,3},{3,1},... | collective-permute-start | bytes 110600 | tf_op jit(solution)/shard_map/ppermute | solution.py:447

commit v8 on v7

--- a/solution.py
+++ b/solution.py
@@ -394,8 +394,11 @@
     flat = (NZ * BX, BY)
     newer, *e = call(first_kernel, [FIELD] + edges(1))(newer_field.reshape(flat))
     e = exchange(*e)
-    code = receiver_z | (receiver_x << 6) | (receiver_y << 12)
-    shot = jnp.concatenate([traces[0], code.astype(F32)], axis=0)
+    def last_row(array):
+        return jnp.pad(array, ((STEPS, 0), (0, 0)))
+
+    code = last_row(receiver_z) | (last_row(receiver_x) << 6) | (last_row(receiver_y) << 12)
+    shot = jnp.pad(traces[0], ((0, 1), (0, 0))) + code.astype(F32)
     inj3, pick_cell, pick_y = call(
         prepare_kernel,
         [FIELD, ((512, NREC), BF16), ((BY, NREC), BF16)],

time: 118 us -> 118 us (level)
  starting transfers between devices: 10.2 us -> 11.5 us
  waiting for transfers between devices: 21.8 us -> 20.6 us
    ppermute x7, starting transfers between devices: 4.31 us -> 5.53 us  [exchange(): lax.ppermute(strip, 'gy', [(0, 1), (1, 0)])]
where the time goes in v8:
time: 118 us; the launch traced here: 117 us
  blocking collectives  62 us (53%)
  waiting for transfers between devices  20.6 us (17%)
  Pallas kernels  18.3 us (16%)
  starting transfers between devices  11.5 us (10%)
  between operations  2.21 us (2%)
  other arithmetic  1.91 us (2%)
    all_to_all x1, blocking collectives, on_device(): lax.all_to_all(grad.reshape(16, 4, BX, BY), 'shot', 0, 0, tiled=True)  22 us
    pallas_call x29, Pallas kernels, run(): pl.pallas_call(kernel, out_shape=[jax.ShapeDtypeStruct(s, d) for s, d in...  18.3 us
    all_to_all x1, blocking collectives, on_device(): lax.all_to_all(copies.reshape(16, 4, BX, BY), 'shot', 0, 0, tiled=True)  15.4 us
    all_to_all x1, blocking collectives, on_device(): stats = lax.all_to_all(stats, 'shot', 0, 0, tiled=True)  13.8 us
    ppermute x7, waiting for transfers between devices, exchange(): lax.ppermute(outer, 'gx', across)  12 us
    all_to_all x1, blocking collectives, on_device(): lax.all_to_all(payload, ('gx', 'gy'), 0, 0, axis_index_groups=same_core,...  10.8 us
    ppermute x7, waiting for transfers between devices, exchange(): lax.ppermute(strip, 'gy', [(0, 1), (1, 0)])  7.33 us
    ppermute x7, starting transfers between devices, exchange(): lax.ppermute(strip, 'gy', [(0, 1), (1, 0)])  5.53 us
  transfers between devices with their start and end apart: 22, of which 12 were waited for; matrix products, arithmetic and copies ran while one was open for 2% of the time, Pallas kernels for 11%

profile of v8, /device:TPU:32, one launch (start us, length us, event | category | flops | bytes accessed | tf_op | source)
XLA Modules:
  0.0 117.4 jit_solution(15216432372727855955)
XLA Ops:
  0.6 0.9 copy-done
  1.8 2.5 %collective-permute-start = (f32[1,4,64,128]{3,2,1,0:T(8,128)S(1)}, f32[1,4,64,128]{3,2,1,0:T(8,128)S(1)}, u32[]{:S(2)}, u32[]{:S(2)}) collective-permute-start(f32[1,4,64,128]{3,2,1,0:T(8,128)S(1)} %get-tuple-element.63), channel_id=1, source_target_pairs={{2,4},{6,8},{10,12},{14,0},{4,2},{8,6},{12,10},{0,14},{3,5},{7,9},... | collective-permute-start | bytes 393224 | tf_op jit(solution)/shard_map/ppermute | solution.py:386
  4.3 1.5 %collective-permute-start.2 = (f32[1,16,128]{2,1,0:T(8,128)S(1)}, f32[1,16,128]{2,1,0:T(8,128)S(1)}, u32[]{:S(2)}, u32[]{:S(2)}) collective-permute-start(f32[1,16,128]{2,1,0:T(8,128)S(1)} %get-tuple-element.65), channel_id=1, source_target_pairs={{0,1},{1,0},{2,3},{3,2},{4,5},{5,4},{6,7},{7,6},{8,9},{9,8},{10,11... | collective-permute-start | bytes 24584 | tf_op jit(solution)/shard_map/ppermute | solution.py:388
  5.8 0.8 convert_add_fusion.shot
  6.7 1.1 pad_maximum_fusion.both
  7.7 1.3 %shard_map.116 = (f32[8,64,128]{2,1,0:T(8,128)S(1)}, bf16[512,2048]{1,0:T(8,128)(2,1)S(1)}, bf16[128,2048]{1,0:T(8,128)(2,1)S(1)}) custom-call(f32[5,2048]{1,0:T(8,128)S(1)} %convert_add_fusion.shot), custom_call_target="tpu_custom_call" | custom-call | flops 10000000 | bytes 2000000 | tf_op jit(solution)/shard_map/pallas_call | solution.py:25
  9.1 0.6 shard_map.114.part
  10.3 0.7 collective-permute-start.3
  11.3 0.7 collective-permute-start.5
  12.0 0.9 shard_map.119.inj
  12.9 1.2 %shard_map.118 = (f32[8,64,128]{2,1,0:T(8,128)S(1)}, f32[8,64,128]{2,1,0:T(8,128)S(1)}) custom-call(f32[8,64,128]{2,1,0:T(8,128)S(1)} %get-tuple-element.66.refs_0_.newer.older, f32[8,64,128]{2,1,0:T(8,128)S(1)} %get-tuple-element.67.refs_1_), custom_call_target="tpu_custom_call" | custom-call | flops 10000000 | bytes 2000000 | tf_op jit(solution)/shard_map/pallas_call | solution.py:25
  14.1 1.0 collective-permute-done.5.rest_2_
  15.0 2.3 %collective-permute-done.3.rest_0_ = f32[2,4,64,128]{3,2,1,0:T(8,128)S(1)} collective-permute-done((f32[2,4,64,128]{3,2,1,0:T(8,128)S(1)}, f32[2,4,64,128]{3,2,1,0:T(8,128)S(1)}, u32[]{:S(2)}, u32[]{:S(2)}) %collective-permute-start.3) | collective-permute-done | bytes 262176 | tf_op jit(solution)/shard_map/ppermute | solution.py:386
  17.4 0.7 shard_map.120
  18.1 0.7 collective-permute-start.6
  18.8 1.0 collective-permute-start.8
  19.8 0.9 shard_map.123.inj
  20.7 1.2 %shard_map.122 = (f32[8,64,128]{2,1,0:T(8,128)S(1)}, f32[8,64,128]{2,1,0:T(8,128)S(1)}) custom-call(f32[8,64,128]{2,1,0:T(8,128)S(1)} %get-tuple-element.75.after.refs_0_.newer, f32[8,64,128]{2,1,0:T(8,128)S(1)} %get-tuple-element.76.refs_1_), custom_call_target="tpu_custom_call" | custom-call | flops 10000000 | bytes 2000000 | tf_op jit(solution)/shard_map/pallas_call | solution.py:25
  21.9 0.6 collective-permute-done.8.rest_3_
  22.5 2.7 %collective-permute-done.6.rest_1_ = f32[2,4,64,128]{3,2,1,0:T(8,128)S(1)} collective-permute-done((f32[2,4,64,128]{3,2,1,0:T(8,128)S(1)}, f32[2,4,64,128]{3,2,1,0:T(8,128)S(1)}, u32[]{:S(2)}, u32[]{:S(2)}) %collective-permute-start.6) | collective-permute-done | bytes 262176 | tf_op jit(solution)/shard_map/ppermute | solution.py:386
  25.2 0.7 shard_map.124
  26.2 0.7 collective-permute-start.9
  26.8 1.0 collective-permute-start.11
  27.9 0.9 shard_map.126.inj0
  30.1 1.2 shard_map.125
  31.3 2.0 %collective-permute-done.9.outer = f32[2,4,64,128]{3,2,1,0:T(8,128)S(1)} collective-permute-done((f32[2,4,64,128]{3,2,1,0:T(8,128)S(1)}, f32[2,4,64,128]{3,2,1,0:T(8,128)S(1)}, u32[]{:S(2)}, u32[]{:S(2)}) %collective-permute-start.9) | collective-permute-done | bytes 262176 | tf_op jit(solution)/shard_map/ppermute | solution.py:386
  33.3 0.5 shard_map.127
  33.8 22.0 %all_to_all.20 = f32[16,4,8,128]{3,2,1,0:T(8,128)S(1)} all-to-all(f32[16,4,8,128]{3,2,1,0:T(8,128)S(1)} %bitcast.14), channel_id=1, replica_groups=mesh['shot'=16,'gx'=8,'gy'=2] {'shot'}, dimensions={0} | all-to-all | bytes 524288 | tf_op jit(solution)/shard_map/all_to_all | solution.py:428
  55.8 15.4 %all_to_all.21 = f32[16,4,8,128]{3,2,1,0:T(8,128)S(1)} all-to-all(f32[16,4,8,128]{3,2,1,0:T(8,128)S(1)} %bitcast.15), channel_id=1, replica_groups=mesh['shot'=16,'gx'=8,'gy'=2] {'shot'}, dimensions={0} | all-to-all | bytes 524288 | tf_op jit(solution)/shard_map/all_to_all | solution.py:432
  72.0 0.8 shard_map.131.rest_0_.rest_2_
  72.8 0.7 shard_map.130.part
  73.5 1.9 %collective-permute-done.14.strip = f32[1,16,128]{2,1,0:T(8,128)S(1)} collective-permute-done((f32[1,16,128]{2,1,0:T(8,128)S(1)}, f32[1,16,128]{2,1,0:T(8,128)S(1)}, u32[]{:S(2)}, u32[]{:S(2)}) %collective-permute-start.14) | collective-permute-done | bytes 8224 | tf_op jit(solution)/shard_map/ppermute | solution.py:388
  75.4 1.8 %collective-permute-done.12.outer = f32[1,4,64,128]{3,2,1,0:T(8,128)S(1)} collective-permute-done((f32[1,4,64,128]{3,2,1,0:T(8,128)S(1)}, f32[1,4,64,128]{3,2,1,0:T(8,128)S(1)}, u32[]{:S(2)}, u32[]{:S(2)}) %collective-permute-start.12) | collective-permute-done | bytes 131104 | tf_op jit(solution)/shard_map/ppermute | solution.py:386
  77.1 0.5 shard_map.132
  78.3 0.8 shard_map.134.rest_0_.rest_3_
  79.1 0.6 shard_map.133.part
  79.7 1.9 %collective-permute-done.17.strip = f32[1,16,128]{2,1,0:T(8,128)S(1)} collective-permute-done((f32[1,16,128]{2,1,0:T(8,128)S(1)}, f32[1,16,128]{2,1,0:T(8,128)S(1)}, u32[]{:S(2)}, u32[]{:S(2)}) %collective-permute-start.17) | collective-permute-done | bytes 8224 | tf_op jit(solution)/shard_map/ppermute | solution.py:388
  81.6 1.8 %collective-permute-done.15.outer = f32[1,4,64,128]{3,2,1,0:T(8,128)S(1)} collective-permute-done((f32[1,4,64,128]{3,2,1,0:T(8,128)S(1)}, f32[1,4,64,128]{3,2,1,0:T(8,128)S(1)}, u32[]{:S(2)}, u32[]{:S(2)}) %collective-permute-start.15) | collective-permute-done | bytes 131104 | tf_op jit(solution)/shard_map/ppermute | solution.py:386
  83.3 0.5 shard_map.135
  84.6 0.8 shard_map.137.rest_4_
  85.3 0.6 shard_map.136.part
  86.0 2.0 %collective-permute-done.20.strip = f32[1,16,128]{2,1,0:T(8,128)S(1)} collective-permute-done((f32[1,16,128]{2,1,0:T(8,128)S(1)}, f32[1,16,128]{2,1,0:T(8,128)S(1)}, u32[]{:S(2)}, u32[]{:S(2)}) %collective-permute-start.20) | collective-permute-done | bytes 8224 | tf_op jit(solution)/shard_map/ppermute | solution.py:388
  88.0 1.5 %collective-permute-done.18.outer = f32[1,4,64,128]{3,2,1,0:T(8,128)S(1)} collective-permute-done((f32[1,4,64,128]{3,2,1,0:T(8,128)S(1)}, f32[1,4,64,128]{3,2,1,0:T(8,128)S(1)}, u32[]{:S(2)}, u32[]{:S(2)}) %collective-permute-start.18) | collective-permute-done | bytes 131104 | tf_op jit(solution)/shard_map/ppermute | solution.py:386
  89.5 1.1 shard_map.138.mine
  90.7 1.2 %collective-permute-done.21.theirs = f32[72,128]{1,0:T(8,128)S(1)} collective-permute-done((f32[72,128]{1,0:T(8,128)S(1)}, f32[72,128]{1,0:T(8,128)S(1)}, u32[]{:S(2)}, u32[]{:S(2)}) %collective-permute-start.21) | collective-permute-done | bytes 36896 | tf_op jit(solution)/shard_map/ppermute | solution.py:450
  92.0 10.8 %all_to_all.22.arrived = f32[8,72,128]{2,1,0:T(8,128)S(1)} all-to-all(f32[8,72,128]{2,1,0:T(8,128)S(1)} %shard_map.139), channel_id=1, replica_groups={{0,1,4,5,8,9,12,13},{2,3,6,7,10,11,14,15},{16,17,20,21,24,25,28,29},{18..., dimensions={0} | all-to-all | bytes 589824 | tf_op jit(solution)/shard_map/all_to_all | solution.py:453
  102.8 13.8 %all_to_all.23.stats = f32[16,8,128]{2,1,0:T(8,128)S(1)} all-to-all(f32[16,8,128]{2,1,0:T(8,128)S(1)} %get-tuple-element.111), channel_id=1, replica_groups=mesh['shot'=16,'gx'=8,'gy'=2] {'shot'}, dimensions={0} | all-to-all | bytes 131072 | tf_op jit(solution)/shard_map/all_to_all | solution.py:455
  116.6 0.8 shard_map.141
  (37 shorter events, 3.8 us)
Async XLA Ops:
  0.6 1.0 copy-start
  1.8 8.0 %collective-permute-start = (f32[1,4,64,128]{3,2,1,0:T(8,128)S(1)}, f32[1,4,64,128]{3,2,1,0:T(8,128)S(1)}, u32[]{:S(2)}, u32[]{:S(2)}) collective-permute-start(f32[1,4,64,128]{3,2,1,0:T(8,128)S(1)} %get-tuple-element.63), channel_id=1, source_target_pairs={{2,4},{6,8},{10,12},{14,0},{4,2},{8,6},{12,10},{0,14},{3,5},{7,9},... | collective-permute-start | bytes 393224 | tf_op jit(solution)/shard_map/ppermute | solution.py:386
  4.3 5.5 %collective-permute-start.1 = (f32[1,4,64,128]{3,2,1,0:T(8,128)S(1)}, f32[1,4,64,128]{3,2,1,0:T(8,128)S(1)}, u32[]{:S(2)}, u32[]{:S(2)}) collective-permute-start(f32[1,4,64,128]{3,2,1,0:T(8,128)S(1)} %get-tuple-element.64), channel_id=1, source_target_pairs={{0,2},{2,0},{4,6},{6,4},{8,10},{10,8},{12,14},{14,12},{1,3},{3,1},... | collective-permute-start | bytes 393224 | tf_op jit(solution)/shard_map/ppermute | solution.py:387
  4.3 5.5 %collective-permute-start.2 = (f32[1,16,128]{2,1,0:T(8,128)S(1)}, f32[1,16,128]{2,1,0:T(8,128)S(1)}, u32[]{:S(2)}, u32[]{:S(2)}) collective-permute-start(f32[1,16,128]{2,1,0:T(8,128)S(1)} %get-tuple-element.65), channel_id=1, source_target_pairs={{0,1},{1,0},{2,3},{3,2},{4,5},{5,4},{6,7},{7,6},{8,9},{9,8},{10,11... | collective-permute-start | bytes 24584 | tf_op jit(solution)/shard_map/ppermute | solution.py:388
  10.3 7.1 %collective-permute-start.3 = (f32[2,4,64,128]{3,2,1,0:T(8,128)S(1)}, f32[2,4,64,128]{3,2,1,0:T(8,128)S(1)}, u32[]{:S(2)}, u32[]{:S(2)}) collective-permute-start(f32[2,4,64,128]{3,2,1,0:T(8,128)S(1)} %get-tuple-element.72), channel_id=1, source_target_pairs={{2,4},{6,8},{10,12},{14,0},{4,2},{8,6},{12,10},{0,14},{3,5},{7,9},... | collective-permute-start | bytes 786440 | tf_op jit(solution)/shard_map/ppermute | solution.py:386
  10.9 6.4 %collective-permute-start.4 = (f32[2,4,64,128]{3,2,1,0:T(8,128)S(1)}, f32[2,4,64,128]{3,2,1,0:T(8,128)S(1)}, u32[]{:S(2)}, u32[]{:S(2)}) collective-permute-start(f32[2,4,64,128]{3,2,1,0:T(8,128)S(1)} %get-tuple-element.73), channel_id=1, source_target_pairs={{0,2},{2,0},{4,6},{6,4},{8,10},{10,8},{12,14},{14,12},{1,3},{3,1},... | collective-permute-start | bytes 786440 | tf_op jit(solution)/shard_map/ppermute | solution.py:387
  11.3 3.7 %collective-permute-start.5 = (f32[2,16,128]{2,1,0:T(8,128)S(1)}, f32[2,16,128]{2,1,0:T(8,128)S(1)}, u32[]{:S(2)}, u32[]{:S(2)}) collective-permute-start(f32[2,16,128]{2,1,0:T(8,128)S(1)} %get-tuple-element.74), channel_id=1, source_target_pairs={{0,1},{1,0},{2,3},{3,2},{4,5},{5,4},{6,7},{7,6},{8,9},{9,8},{10,11... | collective-permute-start | bytes 49160 | tf_op jit(solution)/shard_map/ppermute | solution.py:388
  18.1 7.1 %collective-permute-start.6 = (f32[2,4,64,128]{3,2,1,0:T(8,128)S(1)}, f32[2,4,64,128]{3,2,1,0:T(8,128)S(1)}, u32[]{:S(2)}, u32[]{:S(2)}) collective-permute-start(f32[2,4,64,128]{3,2,1,0:T(8,128)S(1)} %get-tuple-element.80), channel_id=1, source_target_pairs={{2,4},{6,8},{10,12},{14,0},{4,2},{8,6},{12,10},{0,14},{3,5},{7,9},... | collective-permute-start | bytes 786440 | tf_op jit(solution)/shard_map/ppermute | solution.py:386
  18.8 6.4 %collective-permute-start.7 = (f32[2,4,64,128]{3,2,1,0:T(8,128)S(1)}, f32[2,4,64,128]{3,2,1,0:T(8,128)S(1)}, u32[]{:S(2)}, u32[]{:S(2)}) collective-permute-start(f32[2,4,64,128]{3,2,1,0:T(8,128)S(1)} %get-tuple-element.81), channel_id=1, source_target_pairs={{0,2},{2,0},{4,6},{6,4},{8,10},{10,8},{12,14},{14,12},{1,3},{3,1},... | collective-permute-start | bytes 786440 | tf_op jit(solution)/shard_map/ppermute | solution.py:387
  18.8 3.7 %collective-permute-start.8 = (f32[2,16,128]{2,1,0:T(8,128)S(1)}, f32[2,16,128]{2,1,0:T(8,128)S(1)}, u32[]{:S(2)}, u32[]{:S(2)}) collective-permute-start(f32[2,16,128]{2,1,0:T(8,128)S(1)} %get-tuple-element.82), channel_id=1, source_target_pairs={{0,1},{1,0},{2,3},{3,2},{4,5},{5,4},{6,7},{7,6},{8,9},{9,8},{10,11... | collective-permute-start | bytes 49160 | tf_op jit(solution)/shard_map/ppermute | solution.py:388
  25.9 5.4 %collective-permute-start.10 = (f32[2,4,64,128]{3,2,1,0:T(8,128)S(1)}, f32[2,4,64,128]{3,2,1,0:T(8,128)S(1)}, u32[]{:S(2)}, u32[]{:S(2)}) collective-permute-start(f32[2,4,64,128]{3,2,1,0:T(8,128)S(1)} %get-tuple-element.92), channel_id=1, source_target_pairs={{0,2},{2,0},{4,6},{6,4},{8,10},{10,8},{12,14},{14,12},{1,3},{3,1},... | collective-permute-start | bytes 786440 | tf_op jit(solution)/shard_map/ppermute | solution.py:387
  26.2 7.1 %collective-permute-start.9 = (f32[2,4,64,128]{3,2,1,0:T(8,128)S(1)}, f32[2,4,64,128]{3,2,1,0:T(8,128)S(1)}, u32[]{:S(2)}, u32[]{:S(2)}) collective-permute-start(f32[2,4,64,128]{3,2,1,0:T(8,128)S(1)} %get-tuple-element.91), channel_id=1, source_target_pairs={{2,4},{6,8},{10,12},{14,0},{4,2},{8,6},{12,10},{0,14},{3,5},{7,9},... | collective-permute-start | bytes 786440 | tf_op jit(solution)/shard_map/ppermute | solution.py:386
  26.8 4.4 %collective-permute-start.11 = (f32[2,16,128]{2,1,0:T(8,128)S(1)}, f32[2,16,128]{2,1,0:T(8,128)S(1)}, u32[]{:S(2)}, u32[]{:S(2)}) collective-permute-start(f32[2,16,128]{2,1,0:T(8,128)S(1)} %get-tuple-element.93), channel_id=1, source_target_pairs={{0,1},{1,0},{2,3},{3,2},{4,5},{5,4},{6,7},{7,6},{8,9},{9,8},{10,11... | collective-permute-start | bytes 49160 | tf_op jit(solution)/shard_map/ppermute | solution.py:388
  30.1 25.7 %copy-start.2 = (f32[4,8,128]{2,1,0:T(8,128)S(1)}, f32[4,8,128]{2,1,0:T(8,128)}, u32[]{:S(2)}) copy-start(f32[4,8,128]{2,1,0:T(8,128)} %param.13) | copy-start | bytes 49156
  71.5 5.7 %collective-permute-start.12 = (f32[1,4,64,128]{3,2,1,0:T(8,128)S(1)}, f32[1,4,64,128]{3,2,1,0:T(8,128)S(1)}, u32[]{:S(2)}, u32[]{:S(2)}) collective-permute-start(f32[1,4,64,128]{3,2,1,0:T(8,128)S(1)} %get-tuple-element.98), channel_id=1, source_target_pairs={{2,4},{6,8},{10,12},{14,0},{4,2},{8,6},{12,10},{0,14},{3,5},{7,9},... | collective-permute-start | bytes 393224 | tf_op jit(solution)/shard_map/ppermute | solution.py:386
  71.6 5.5 %collective-permute-start.13 = (f32[1,4,64,128]{3,2,1,0:T(8,128)S(1)}, f32[1,4,64,128]{3,2,1,0:T(8,128)S(1)}, u32[]{:S(2)}, u32[]{:S(2)}) collective-permute-start(f32[1,4,64,128]{3,2,1,0:T(8,128)S(1)} %get-tuple-element.99), channel_id=1, source_target_pairs={{0,2},{2,0},{4,6},{6,4},{8,10},{10,8},{12,14},{14,12},{1,3},{3,1},... | collective-permute-start | bytes 393224 | tf_op jit(solution)/shard_map/ppermute | solution.py:387
  71.7 3.7 %collective-permute-start.14 = (f32[1,16,128]{2,1,0:T(8,128)S(1)}, f32[1,16,128]{2,1,0:T(8,128)S(1)}, u32[]{:S(2)}, u32[]{:S(2)}) collective-permute-start(f32[1,16,128]{2,1,0:T(8,128)S(1)} %get-tuple-element.100), channel_id=1, source_target_pairs={{0,1},{1,0},{2,3},{3,2},{4,5},{5,4},{6,7},{7,6},{8,9},{9,8},{10,11... | collective-permute-start | bytes 24584 | tf_op jit(solution)/shard_map/ppermute | solution.py:388
  77.6 5.7 %collective-permute-start.15 = (f32[1,4,64,128]{3,2,1,0:T(8,128)S(1)}, f32[1,4,64,128]{3,2,1,0:T(8,128)S(1)}, u32[]{:S(2)}, u32[]{:S(2)}) collective-permute-start(f32[1,4,64,128]{3,2,1,0:T(8,128)S(1)} %get-tuple-element.102), channel_id=1, source_target_pairs={{2,4},{6,8},{10,12},{14,0},{4,2},{8,6},{12,10},{0,14},{3,5},{7,9},... | collective-permute-start | bytes 393224 | tf_op jit(solution)/shard_map/ppermute | solution.py:386
  77.9 5.4 %collective-permute-start.16 = (f32[1,4,64,128]{3,2,1,0:T(8,128)S(1)}, f32[1,4,64,128]{3,2,1,0:T(8,128)S(1)}, u32[]{:S(2)}, u32[]{:S(2)}) collective-permute-start(f32[1,4,64,128]{3,2,1,0:T(8,128)S(1)} %get-tuple-element.103), channel_id=1, source_target_pairs={{0,2},{2,0},{4,6},{6,4},{8,10},{10,8},{12,14},{14,12},{1,3},{3,1},... | collective-permute-start | bytes 393224 | tf_op jit(solution)/shard_map/ppermute | solution.py:387
  77.9 3.7 %collective-permute-start.17 = (f32[1,16,128]{2,1,0:T(8,128)S(1)}, f32[1,16,128]{2,1,0:T(8,128)S(1)}, u32[]{:S(2)}, u32[]{:S(2)}) collective-permute-start(f32[1,16,128]{2,1,0:T(8,128)S(1)} %get-tuple-element.104), channel_id=1, source_target_pairs={{0,1},{1,0},{2,3},{3,2},{4,5},{5,4},{6,7},{7,6},{8,9},{9,8},{10,11... | collective-permute-start | bytes 24584 | tf_op jit(solution)/shard_map/ppermute | solution.py:388
  83.8 5.7 %collective-permute-start.18 = (f32[1,4,64,128]{3,2,1,0:T(8,128)S(1)}, f32[1,4,64,128]{3,2,1,0:T(8,128)S(1)}, u32[]{:S(2)}, u32[]{:S(2)}) collective-permute-start(f32[1,4,64,128]{3,2,1,0:T(8,128)S(1)} %get-tuple-element.107), channel_id=1, source_target_pairs={{2,4},{6,8},{10,12},{14,0},{4,2},{8,6},{12,10},{0,14},{3,5},{7,9},... | collective-permute-start | bytes 393224 | tf_op jit(solution)/shard_map/ppermute | solution.py:386
  84.1 5.4 %collective-permute-start.19 = (f32[1,4,64,128]{3,2,1,0:T(8,128)S(1)}, f32[1,4,64,128]{3,2,1,0:T(8,128)S(1)}, u32[]{:S(2)}, u32[]{:S(2)}) collective-permute-start(f32[1,4,64,128]{3,2,1,0:T(8,128)S(1)} %get-tuple-element.108), channel_id=1, source_target_pairs={{0,2},{2,0},{4,6},{6,4},{8,10},{10,8},{12,14},{14,12},{1,3},{3,1},... | collective-permute-start | bytes 393224 | tf_op jit(solution)/shard_map/ppermute | solution.py:387
  84.1 3.9 %collective-permute-start.20 = (f32[1,16,128]{2,1,0:T(8,128)S(1)}, f32[1,16,128]{2,1,0:T(8,128)S(1)}, u32[]{:S(2)}, u32[]{:S(2)}) collective-permute-start(f32[1,16,128]{2,1,0:T(8,128)S(1)} %get-tuple-element.109), channel_id=1, source_target_pairs={{0,1},{1,0},{2,3},{3,2},{4,5},{5,4},{6,7},{7,6},{8,9},{9,8},{10,11... | collective-permute-start | bytes 24584 | tf_op jit(solution)/shard_map/ppermute | solution.py:388
  89.5 27.1 %copy-start.1 = (f32[1,4,2048]{2,1,0:T(4,128)S(1)}, f32[1,4,2048]{2,1,0:T(4,128)}, u32[]{:S(2)}) copy-start(f32[1,4,2048]{2,1,0:T(4,128)} %param.14) | copy-start | bytes 98308
  90.6 1.3 %collective-permute-start.21 = (f32[72,128]{1,0:T(8,128)S(1)}, f32[72,128]{1,0:T(8,128)S(1)}, u32[]{:S(2)}, u32[]{:S(2)}) collective-permute-start(f32[72,128]{1,0:T(8,128)S(1)} %shard_map.138.mine), channel_id=1, source_target_pairs={{0,2},{2,0},{4,6},{6,4},{8,10},{10,8},{12,14},{14,12},{1,3},{3,1},... | collective-permute-start | bytes 110600 | tf_op jit(solution)/shard_map/ppermute | solution.py:450

commit v9 on v8

--- a/solution.py
+++ b/solution.py
@@ -46,11 +46,15 @@
 
 
 def send_edges(field, outer_ref, inner_ref, strip_ref, slot, scal):
-    core, gy = scal[0], scal[1]
-    keep = near_edge(gy, lanes(8))
+    core = scal[0]
     for i in range(4):
         outer_ref[slot, i] = field[4 * core + i]
         inner_ref[slot, i] = field[4 * (1 - core) + i]
+    pack(field, strip_ref, slot, scal)
+
+
+def pack(field, strip_ref, slot, scal):
+    keep = near_edge(scal[1], lanes(8))
     for half in range(2):
         sums = []
         for j in range(32):
@@ -95,8 +99,9 @@
     core, gy = scal[0], scal[1]
     inside = ((scal[2] > 0) | (core == 1)) & ((scal[2] < 7 * BX) | (core == 0))
     for i in range(4):
-        halo[4 * core + i] = jnp.where(inside, outer_ref[slot, i], 0.0)
-        halo[4 * (1 - core) + i] = inner_ref[slot, i]
+        outer, inner = outer_ref[slot, i], inner_ref[slot, i]
+        halo[4 * core + i] = jnp.where(inside, outer, 0.0)
+        halo[4 * (1 - core) + i] = inner
     packed = strip_ref[slot]
     place = lanes(16) & 3
     after, before = weights[4] * packed, weights[4] * packed
@@ -132,11 +137,11 @@
     return [((count, 4, NZ, BY), F32), ((count, 4, NZ, BY), F32), ((count, 16, BY), F32)]
 
 
-def first_kernel(newer, newer_out, outer, inner, strip):
-    scal = position()
-    for x in range(BX):
-        newer_out[x] = newer[pl.ds(x, NZ, stride=8), :]
-    send_edges(newer_out, outer, inner, strip, 0, scal)
+def first_kernel(fields, newer, older, vel, outer, inner, strip):
+    for i, out in enumerate((newer, older, vel)):
+        for x in range(BX):
+            out[x] = fields[pl.ds(NZ * BX * i + x, NZ, stride=8), :]
+    send_edges(newer, outer, inner, strip, 0, position())
 
 
 def two_pieces(values):
@@ -212,12 +217,6 @@
 
     lax.fori_loop(0, 8, columns, 0)
     inject(3, shot, pick_cell, pick_y, spread, inj)
-
-
-def planes_kernel(both, older, vel):
-    for x in range(BX):
-        older[x] = both[pl.ds(x, NZ, stride=8), :]
-        vel[x] = both[pl.ds(NZ * BX + x, NZ, stride=8), :]
 
 
 def forward1_kernel(part, newer, older, vel, inj3, outer, inner, strip, acc, nxt, q, outer_o, inner_o, strip_o, halo):
@@ -392,7 +391,9 @@
 def on_device(older_field, newer_field, velocity, preconditioner, traces,
               receiver_z, receiver_x, receiver_y, aperture_x, aperture_y):
     flat = (NZ * BX, BY)
-    newer, *e = call(first_kernel, [FIELD] + edges(1))(newer_field.reshape(flat))
+    block = newer_field.reshape(flat)
+    fields = jnp.concatenate([block, older_field.reshape(flat), velocity.reshape(flat)], axis=0)
+    newer, older, vel, *e = call(first_kernel, [FIELD] * 3 + edges(1))(fields)
     e = exchange(*e)
     def last_row(array):
         return jnp.pad(array, ((STEPS, 0), (0, 0)))
@@ -411,8 +412,6 @@
 
     one = call(interior_kernel, [FIELD], [PADDED])
     two = call(interior_kernel, [FIELD] * 2, [PADDED])
-    both = jnp.concatenate([older_field.reshape(flat), velocity.reshape(flat)], axis=0)
-    older, vel = call(planes_kernel, [FIELD, FIELD])(both)
     acc0, u1, q, *e = call(forward1_kernel, [FIELD] * 3 + edges(2), [HALO])(
         *one(newer), newer, older, vel, inj3, *e)
     e = exchange(*e)
@@ -454,7 +453,7 @@
     predicted, stats = call(collect_kernel, [((64, BY), F32), ((16, 8, BY), F32)])(arrived)
     stats = lax.all_to_all(stats, "shot", 0, 0, tiled=True)
     image, residual = call(finish_kernel, [((32, BY), F32), ((4, NREC), F32)])(
-        stats, predicted, scaled, traces[0])
+        stats, predicted, scaled, shot)
     return image.reshape(4, BX, BY), residual[None]
 
 

time: 118 us -> 118 us (level)
  starting transfers between devices: 11.5 us -> 22 us
  waiting for transfers between devices: 20.6 us -> 10.3 us
  blocking collectives: 62 us -> 63.6 us
    ppermute x7, starting transfers between devices: 5.19 us -> 14 us  [exchange(): lax.ppermute(outer, 'gx', across)]
    ppermute x7, waiting for transfers between devices: 12 us -> 3.69 us  [exchange(): lax.ppermute(outer, 'gx', across)]
    ppermute x7, starting transfers between devices: 5.53 us -> 7.74 us  [exchange(): lax.ppermute(strip, 'gy', [(0, 1), (1, 0)])]
    ppermute x7, waiting for transfers between devices: 7.33 us -> 5.36 us  [exchange(): lax.ppermute(strip, 'gy', [(0, 1), (1, 0)])]
    all_to_all x1, blocking collectives: 13.8 us -> 15.2 us  [on_device(): stats = lax.all_to_all(stats, 'shot', 0, 0, tiled=True)]
    pallas_call x29 -> x28, Pallas kernels: 18.3 us -> 18.2 us  [run(): pl.pallas_call(kernel, out_shape=[jax.ShapeDtypeStruct(s, d) for s, d in...]
  transfers between devices with their start and end apart: 22 -> 22, of which waited for: 12 -> 13; matrix products, arithmetic and copies ran while one was open for 2% -> 0% of each run, Pallas kernels for 11% -> 11%
where the time goes in v9:
time: 118 us
  blocking collectives  63.6 us (54%)
  starting transfers between devices  22 us (19%)
  Pallas kernels  18.2 us (15%)
  waiting for transfers between devices  10.3 us (9%)
  between operations  2.21 us (2%)
  other arithmetic  1.22 us (1%)
    all_to_all x1, blocking collectives, on_device(): lax.all_to_all(grad.reshape(16, 4, BX, BY), 'shot', 0, 0, tiled=True)  22.1 us
    pallas_call x28, Pallas kernels, run(): pl.pallas_call(kernel, out_shape=[jax.ShapeDtypeStruct(s, d) for s, d in...  18.2 us
    all_to_all x1, blocking collectives, on_device(): stats = lax.all_to_all(stats, 'shot', 0, 0, tiled=True)  15.2 us
    all_to_all x1, blocking collectives, on_device(): lax.all_to_all(copies.reshape(16, 4, BX, BY), 'shot', 0, 0, tiled=True)  15.1 us
    ppermute x7, starting transfers between devices, exchange(): lax.ppermute(outer, 'gx', across)  14 us
    all_to_all x1, blocking collectives, on_device(): lax.all_to_all(payload, ('gx', 'gy'), 0, 0, axis_index_groups=same_core,...  11.1 us
    ppermute x7, starting transfers between devices, exchange(): lax.ppermute(strip, 'gy', [(0, 1), (1, 0)])  7.74 us
    ppermute x7, waiting for transfers between devices, exchange(): lax.ppermute(strip, 'gy', [(0, 1), (1, 0)])  5.36 us
  transfers between devices with their start and end apart: 22, of which 13 were waited for; matrix products, arithmetic and copies ran while one was open for 0% of the time, Pallas kernels for 11%

profile of v9, /device:TPU:32, one launch (start us, length us, event | category | flops | bytes accessed | tf_op | source)
XLA Modules:
  0.0 117.5 jit_solution(10646452669206805550)
XLA Ops:
  0.7 1.2 %pad_maximum_fusion.fields = f32[1536,128]{1,0:T(8,128)S(1)} fusion(f32[512,128]{1,0:T(8,128)} %bitcast.16, f32[512,128]{1,0:T(8,128)} %bitcast.17, f32[512,128]{1,0:T(8,128)} %bitcast.18), kind=kLoop, calls=%fused_computation | loop fusion | flops 393216 | bytes 1572864 | tf_op jit(solution)/shard_map/concatenate | solution.py:395
  2.1 2.5 %collective-permute-start = (f32[1,4,64,128]{3,2,1,0:T(8,128)S(1)}, f32[1,4,64,128]{3,2,1,0:T(8,128)S(1)}, u32[]{:S(2)}, u32[]{:S(2)}) collective-permute-start(f32[1,4,64,128]{3,2,1,0:T(8,128)S(1)} %get-tuple-element.63), channel_id=1, source_target_pairs={{2,4},{6,8},{10,12},{14,0},{4,2},{8,6},{12,10},{0,14},{3,5},{7,9},... | collective-permute-start | bytes 393224 | tf_op jit(solution)/shard_map/ppermute | solution.py:385
  4.6 1.5 %collective-permute-start.2 = (f32[1,16,128]{2,1,0:T(8,128)S(1)}, f32[1,16,128]{2,1,0:T(8,128)S(1)}, u32[]{:S(2)}, u32[]{:S(2)}) collective-permute-start(f32[1,16,128]{2,1,0:T(8,128)S(1)} %get-tuple-element.65), channel_id=1, source_target_pairs={{0,1},{1,0},{2,3},{3,2},{4,5},{5,4},{6,7},{7,6},{8,9},{9,8},{10,11... | collective-permute-start | bytes 24584 | tf_op jit(solution)/shard_map/ppermute | solution.py:387
  6.2 1.3 %shard_map.115 = (f32[8,64,128]{2,1,0:T(8,128)S(1)}, bf16[512,2048]{1,0:T(8,128)(2,1)S(1)}, bf16[128,2048]{1,0:T(8,128)(2,1)S(1)}) custom-call(f32[5,2048]{1,0:T(8,128)S(1)} %convert_add_fusion.shot.traces), custom_call_target="tpu_custom_call" | custom-call | flops 10000000 | bytes 2000000 | tf_op jit(solution)/shard_map/pallas_call | solution.py:25
  7.5 0.6 shard_map.114.part
  8.3 0.5 shard_map.116
  8.8 2.0 %collective-permute-start.3 = (f32[2,4,64,128]{3,2,1,0:T(8,128)S(1)}, f32[2,4,64,128]{3,2,1,0:T(8,128)S(1)}, u32[]{:S(2)}, u32[]{:S(2)}) collective-permute-start(f32[2,4,64,128]{3,2,1,0:T(8,128)S(1)} %get-tuple-element.72), channel_id=1, source_target_pairs={{2,4},{6,8},{10,12},{14,0},{4,2},{8,6},{12,10},{0,14},{3,5},{7,9},... | collective-permute-start | bytes 786440 | tf_op jit(solution)/shard_map/ppermute | solution.py:385
  10.8 1.5 %collective-permute-start.5 = (f32[2,16,128]{2,1,0:T(8,128)S(1)}, f32[2,16,128]{2,1,0:T(8,128)S(1)}, u32[]{:S(2)}, u32[]{:S(2)}) collective-permute-start(f32[2,16,128]{2,1,0:T(8,128)S(1)} %get-tuple-element.74), channel_id=1, source_target_pairs={{0,1},{1,0},{2,3},{3,2},{4,5},{5,4},{6,7},{7,6},{8,9},{9,8},{10,11... | collective-permute-start | bytes 49160 | tf_op jit(solution)/shard_map/ppermute | solution.py:387
  12.3 0.9 shard_map.118.inj
  13.2 1.2 %shard_map.117 = (f32[8,64,128]{2,1,0:T(8,128)S(1)}, f32[8,64,128]{2,1,0:T(8,128)S(1)}) custom-call(f32[8,64,128]{2,1,0:T(8,128)S(1)} %get-tuple-element.66.refs_0_.newer.older, f32[8,64,128]{2,1,0:T(8,128)S(1)} %get-tuple-element.67.refs_1_), custom_call_target="tpu_custom_call" | custom-call | flops 10000000 | bytes 2000000 | tf_op jit(solution)/shard_map/pallas_call | solution.py:25
  14.5 1.3 %collective-permute-done.3.rest_0_ = f32[2,4,64,128]{3,2,1,0:T(8,128)S(1)} collective-permute-done((f32[2,4,64,128]{3,2,1,0:T(8,128)S(1)}, f32[2,4,64,128]{3,2,1,0:T(8,128)S(1)}, u32[]{:S(2)}, u32[]{:S(2)}) %collective-permute-start.3) | collective-permute-done | bytes 262176 | tf_op jit(solution)/shard_map/ppermute | solution.py:385
  15.9 0.7 shard_map.119
  16.6 2.0 %collective-permute-start.6 = (f32[2,4,64,128]{3,2,1,0:T(8,128)S(1)}, f32[2,4,64,128]{3,2,1,0:T(8,128)S(1)}, u32[]{:S(2)}, u32[]{:S(2)}) collective-permute-start(f32[2,4,64,128]{3,2,1,0:T(8,128)S(1)} %get-tuple-element.80), channel_id=1, source_target_pairs={{2,4},{6,8},{10,12},{14,0},{4,2},{8,6},{12,10},{0,14},{3,5},{7,9},... | collective-permute-start | bytes 786440 | tf_op jit(solution)/shard_map/ppermute | solution.py:385
  18.6 1.5 %collective-permute-start.8 = (f32[2,16,128]{2,1,0:T(8,128)S(1)}, f32[2,16,128]{2,1,0:T(8,128)S(1)}, u32[]{:S(2)}, u32[]{:S(2)}) collective-permute-start(f32[2,16,128]{2,1,0:T(8,128)S(1)} %get-tuple-element.82), channel_id=1, source_target_pairs={{0,1},{1,0},{2,3},{3,2},{4,5},{5,4},{6,7},{7,6},{8,9},{9,8},{10,11... | collective-permute-start | bytes 49160 | tf_op jit(solution)/shard_map/ppermute | solution.py:387
  20.1 0.9 shard_map.122.inj
  21.0 1.2 %shard_map.121 = (f32[8,64,128]{2,1,0:T(8,128)S(1)}, f32[8,64,128]{2,1,0:T(8,128)S(1)}) custom-call(f32[8,64,128]{2,1,0:T(8,128)S(1)} %get-tuple-element.75.after.refs_0_.newer, f32[8,64,128]{2,1,0:T(8,128)S(1)} %get-tuple-element.76.refs_1_), custom_call_target="tpu_custom_call" | custom-call | flops 10000000 | bytes 2000000 | tf_op jit(solution)/shard_map/pallas_call | solution.py:25
  22.3 1.3 %collective-permute-done.6.rest_1_ = f32[2,4,64,128]{3,2,1,0:T(8,128)S(1)} collective-permute-done((f32[2,4,64,128]{3,2,1,0:T(8,128)S(1)}, f32[2,4,64,128]{3,2,1,0:T(8,128)S(1)}, u32[]{:S(2)}, u32[]{:S(2)}) %collective-permute-start.6) | collective-permute-done | bytes 262176 | tf_op jit(solution)/shard_map/ppermute | solution.py:385
  23.7 0.7 shard_map.123
  24.5 2.2 %collective-permute-start.9 = (f32[2,4,64,128]{3,2,1,0:T(8,128)S(1)}, f32[2,4,64,128]{3,2,1,0:T(8,128)S(1)}, u32[]{:S(2)}, u32[]{:S(2)}) collective-permute-start(f32[2,4,64,128]{3,2,1,0:T(8,128)S(1)} %get-tuple-element.91), channel_id=1, source_target_pairs={{2,4},{6,8},{10,12},{14,0},{4,2},{8,6},{12,10},{0,14},{3,5},{7,9},... | collective-permute-start | bytes 786440 | tf_op jit(solution)/shard_map/ppermute | solution.py:385
  26.7 1.5 %collective-permute-start.11 = (f32[2,16,128]{2,1,0:T(8,128)S(1)}, f32[2,16,128]{2,1,0:T(8,128)S(1)}, u32[]{:S(2)}, u32[]{:S(2)}) collective-permute-start(f32[2,16,128]{2,1,0:T(8,128)S(1)} %get-tuple-element.93), channel_id=1, source_target_pairs={{0,1},{1,0},{2,3},{3,2},{4,5},{5,4},{6,7},{7,6},{8,9},{9,8},{10,11... | collective-permute-start | bytes 49160 | tf_op jit(solution)/shard_map/ppermute | solution.py:387
  28.2 0.9 shard_map.125.inj0
  30.4 1.2 shard_map.124
  31.7 0.5 shard_map.126
  32.3 22.1 %all_to_all.20 = f32[16,4,8,128]{3,2,1,0:T(8,128)S(1)} all-to-all(f32[16,4,8,128]{3,2,1,0:T(8,128)S(1)} %bitcast.13), channel_id=1, replica_groups=mesh['shot'=16,'gx'=8,'gy'=2] {'shot'}, dimensions={0} | all-to-all | bytes 524288 | tf_op jit(solution)/shard_map/all_to_all | solution.py:427
  54.5 15.1 %all_to_all.21 = f32[16,4,8,128]{3,2,1,0:T(8,128)S(1)} all-to-all(f32[16,4,8,128]{3,2,1,0:T(8,128)S(1)} %bitcast.14), channel_id=1, replica_groups=mesh['shot'=16,'gx'=8,'gy'=2] {'shot'}, dimensions={0} | all-to-all | bytes 524288 | tf_op jit(solution)/shard_map/all_to_all | solution.py:431
  69.8 1.7 %collective-permute-start.12 = (f32[1,4,64,128]{3,2,1,0:T(8,128)S(1)}, f32[1,4,64,128]{3,2,1,0:T(8,128)S(1)}, u32[]{:S(2)}, u32[]{:S(2)}) collective-permute-start(f32[1,4,64,128]{3,2,1,0:T(8,128)S(1)} %get-tuple-element.98), channel_id=1, source_target_pairs={{2,4},{6,8},{10,12},{14,0},{4,2},{8,6},{12,10},{0,14},{3,5},{7,9},... | collective-permute-start | bytes 393224 | tf_op jit(solution)/shard_map/ppermute | solution.py:385
  71.6 0.6 collective-permute-start.14
  72.1 0.8 shard_map.130.rest_0_.rest_2_
  72.9 0.7 shard_map.129.part
  73.6 1.6 %collective-permute-done.14.strip = f32[1,16,128]{2,1,0:T(8,128)S(1)} collective-permute-done((f32[1,16,128]{2,1,0:T(8,128)S(1)}, f32[1,16,128]{2,1,0:T(8,128)S(1)}, u32[]{:S(2)}, u32[]{:S(2)}) %collective-permute-start.14) | collective-permute-done | bytes 8224 | tf_op jit(solution)/shard_map/ppermute | solution.py:387
  75.2 0.3 collective-permute-done.12.outer
  75.5 0.5 shard_map.131
  76.0 1.7 %collective-permute-start.15 = (f32[1,4,64,128]{3,2,1,0:T(8,128)S(1)}, f32[1,4,64,128]{3,2,1,0:T(8,128)S(1)}, u32[]{:S(2)}, u32[]{:S(2)}) collective-permute-start(f32[1,4,64,128]{3,2,1,0:T(8,128)S(1)} %get-tuple-element.102), channel_id=1, source_target_pairs={{2,4},{6,8},{10,12},{14,0},{4,2},{8,6},{12,10},{0,14},{3,5},{7,9},... | collective-permute-start | bytes 393224 | tf_op jit(solution)/shard_map/ppermute | solution.py:385
  77.7 0.6 collective-permute-start.17
  78.3 0.8 shard_map.133.rest_0_.rest_3_
  79.1 0.6 shard_map.132.part
  79.7 1.7 %collective-permute-done.17.strip = f32[1,16,128]{2,1,0:T(8,128)S(1)} collective-permute-done((f32[1,16,128]{2,1,0:T(8,128)S(1)}, f32[1,16,128]{2,1,0:T(8,128)S(1)}, u32[]{:S(2)}, u32[]{:S(2)}) %collective-permute-start.17) | collective-permute-done | bytes 8224 | tf_op jit(solution)/shard_map/ppermute | solution.py:387
  81.7 0.5 shard_map.134
  82.2 1.7 %collective-permute-start.18 = (f32[1,4,64,128]{3,2,1,0:T(8,128)S(1)}, f32[1,4,64,128]{3,2,1,0:T(8,128)S(1)}, u32[]{:S(2)}, u32[]{:S(2)}) collective-permute-start(f32[1,4,64,128]{3,2,1,0:T(8,128)S(1)} %get-tuple-element.107), channel_id=1, source_target_pairs={{2,4},{6,8},{10,12},{14,0},{4,2},{8,6},{12,10},{0,14},{3,5},{7,9},... | collective-permute-start | bytes 393224 | tf_op jit(solution)/shard_map/ppermute | solution.py:385
  83.9 0.6 collective-permute-start.20
  84.5 0.8 shard_map.136.rest_4_
  85.3 0.6 shard_map.135.part
  85.9 1.7 %collective-permute-done.20.strip = f32[1,16,128]{2,1,0:T(8,128)S(1)} collective-permute-done((f32[1,16,128]{2,1,0:T(8,128)S(1)}, f32[1,16,128]{2,1,0:T(8,128)S(1)}, u32[]{:S(2)}, u32[]{:S(2)}) %collective-permute-start.20) | collective-permute-done | bytes 8224 | tf_op jit(solution)/shard_map/ppermute | solution.py:387
  87.9 1.1 shard_map.137.mine
  89.1 1.2 %collective-permute-done.21.theirs = f32[72,128]{1,0:T(8,128)S(1)} collective-permute-done((f32[72,128]{1,0:T(8,128)S(1)}, f32[72,128]{1,0:T(8,128)S(1)}, u32[]{:S(2)}, u32[]{:S(2)}) %collective-permute-start.21) | collective-permute-done | bytes 36896 | tf_op jit(solution)/shard_map/ppermute | solution.py:449
  90.3 11.1 %all_to_all.22.arrived = f32[8,72,128]{2,1,0:T(8,128)S(1)} all-to-all(f32[8,72,128]{2,1,0:T(8,128)S(1)} %shard_map.138), channel_id=1, replica_groups={{0,1,4,5,8,9,12,13},{2,3,6,7,10,11,14,15},{16,17,20,21,24,25,28,29},{18..., dimensions={0} | all-to-all | bytes 589824 | tf_op jit(solution)/shard_map/all_to_all | solution.py:452
  101.5 15.2 %all_to_all.23.stats = f32[16,8,128]{2,1,0:T(8,128)S(1)} all-to-all(f32[16,8,128]{2,1,0:T(8,128)S(1)} %get-tuple-element.111), channel_id=1, replica_groups=mesh['shot'=16,'gx'=8,'gy'=2] {'shot'}, dimensions={0} | all-to-all | bytes 131072 | tf_op jit(solution)/shard_map/all_to_all | solution.py:454
  116.7 0.8 shard_map.140
  (40 shorter events, 2.0 us)
Async XLA Ops:
  0.6 5.5 %copy-start.1 = (f32[1,4,2048]{2,1,0:T(4,128)S(1)}, f32[1,4,2048]{2,1,0:T(4,128)}, u32[]{:S(2)}) copy-start(f32[1,4,2048]{2,1,0:T(4,128)} %param.14) | copy-start | bytes 98308
  0.6 5.5 %copy-start.4 = (s32[1,2048]{1,0:T(1,128)S(1)}, s32[1,2048]{1,0:T(1,128)}, u32[]{:S(2)}) copy-start(s32[1,2048]{1,0:T(1,128)} %param.15) | copy-start | bytes 24580
  0.7 5.5 %copy-start.3 = (s32[1,2048]{1,0:T(1,128)S(1)}, s32[1,2048]{1,0:T(1,128)}, u32[]{:S(2)}) copy-start(s32[1,2048]{1,0:T(1,128)} %param.16) | copy-start | bytes 24580
  0.7 5.5 %copy-start.2 = (s32[1,2048]{1,0:T(1,128)S(1)}, s32[1,2048]{1,0:T(1,128)}, u32[]{:S(2)}) copy-start(s32[1,2048]{1,0:T(1,128)} %param.17) | copy-start | bytes 24580
  2.1 6.2 %collective-permute-start = (f32[1,4,64,128]{3,2,1,0:T(8,128)S(1)}, f32[1,4,64,128]{3,2,1,0:T(8,128)S(1)}, u32[]{:S(2)}, u32[]{:S(2)}) collective-permute-start(f32[1,4,64,128]{3,2,1,0:T(8,128)S(1)} %get-tuple-element.63), channel_id=1, source_target_pairs={{2,4},{6,8},{10,12},{14,0},{4,2},{8,6},{12,10},{0,14},{3,5},{7,9},... | collective-permute-start | bytes 393224 | tf_op jit(solution)/shard_map/ppermute | solution.py:385
  4.6 3.7 %collective-permute-start.1 = (f32[1,4,64,128]{3,2,1,0:T(8,128)S(1)}, f32[1,4,64,128]{3,2,1,0:T(8,128)S(1)}, u32[]{:S(2)}, u32[]{:S(2)}) collective-permute-start(f32[1,4,64,128]{3,2,1,0:T(8,128)S(1)} %get-tuple-element.64), channel_id=1, source_target_pairs={{0,2},{2,0},{4,6},{6,4},{8,10},{10,8},{12,14},{14,12},{1,3},{3,1},... | collective-permute-start | bytes 393224 | tf_op jit(solution)/shard_map/ppermute | solution.py:386
  4.6 3.7 %collective-permute-start.2 = (f32[1,16,128]{2,1,0:T(8,128)S(1)}, f32[1,16,128]{2,1,0:T(8,128)S(1)}, u32[]{:S(2)}, u32[]{:S(2)}) collective-permute-start(f32[1,16,128]{2,1,0:T(8,128)S(1)} %get-tuple-element.65), channel_id=1, source_target_pairs={{0,1},{1,0},{2,3},{3,2},{4,5},{5,4},{6,7},{7,6},{8,9},{9,8},{10,11... | collective-permute-start | bytes 24584 | tf_op jit(solution)/shard_map/ppermute | solution.py:387
  8.8 7.1 %collective-permute-start.3 = (f32[2,4,64,128]{3,2,1,0:T(8,128)S(1)}, f32[2,4,64,128]{3,2,1,0:T(8,128)S(1)}, u32[]{:S(2)}, u32[]{:S(2)}) collective-permute-start(f32[2,4,64,128]{3,2,1,0:T(8,128)S(1)} %get-tuple-element.72), channel_id=1, source_target_pairs={{2,4},{6,8},{10,12},{14,0},{4,2},{8,6},{12,10},{0,14},{3,5},{7,9},... | collective-permute-start | bytes 786440 | tf_op jit(solution)/shard_map/ppermute | solution.py:385
  10.8 5.1 %collective-permute-start.4 = (f32[2,4,64,128]{3,2,1,0:T(8,128)S(1)}, f32[2,4,64,128]{3,2,1,0:T(8,128)S(1)}, u32[]{:S(2)}, u32[]{:S(2)}) collective-permute-start(f32[2,4,64,128]{3,2,1,0:T(8,128)S(1)} %get-tuple-element.73), channel_id=1, source_target_pairs={{0,2},{2,0},{4,6},{6,4},{8,10},{10,8},{12,14},{14,12},{1,3},{3,1},... | collective-permute-start | bytes 786440 | tf_op jit(solution)/shard_map/ppermute | solution.py:386
  10.8 3.7 %collective-permute-start.5 = (f32[2,16,128]{2,1,0:T(8,128)S(1)}, f32[2,16,128]{2,1,0:T(8,128)S(1)}, u32[]{:S(2)}, u32[]{:S(2)}) collective-permute-start(f32[2,16,128]{2,1,0:T(8,128)S(1)} %get-tuple-element.74), channel_id=1, source_target_pairs={{0,1},{1,0},{2,3},{3,2},{4,5},{5,4},{6,7},{7,6},{8,9},{9,8},{10,11... | collective-permute-start | bytes 49160 | tf_op jit(solution)/shard_map/ppermute | solution.py:387
  16.6 7.1 %collective-permute-start.6 = (f32[2,4,64,128]{3,2,1,0:T(8,128)S(1)}, f32[2,4,64,128]{3,2,1,0:T(8,128)S(1)}, u32[]{:S(2)}, u32[]{:S(2)}) collective-permute-start(f32[2,4,64,128]{3,2,1,0:T(8,128)S(1)} %get-tuple-element.80), channel_id=1, source_target_pairs={{2,4},{6,8},{10,12},{14,0},{4,2},{8,6},{12,10},{0,14},{3,5},{7,9},... | collective-permute-start | bytes 786440 | tf_op jit(solution)/shard_map/ppermute | solution.py:385
  18.6 5.1 %collective-permute-start.7 = (f32[2,4,64,128]{3,2,1,0:T(8,128)S(1)}, f32[2,4,64,128]{3,2,1,0:T(8,128)S(1)}, u32[]{:S(2)}, u32[]{:S(2)}) collective-permute-start(f32[2,4,64,128]{3,2,1,0:T(8,128)S(1)} %get-tuple-element.81), channel_id=1, source_target_pairs={{0,2},{2,0},{4,6},{6,4},{8,10},{10,8},{12,14},{14,12},{1,3},{3,1},... | collective-permute-start | bytes 786440 | tf_op jit(solution)/shard_map/ppermute | solution.py:386
  18.6 3.7 %collective-permute-start.8 = (f32[2,16,128]{2,1,0:T(8,128)S(1)}, f32[2,16,128]{2,1,0:T(8,128)S(1)}, u32[]{:S(2)}, u32[]{:S(2)}) collective-permute-start(f32[2,16,128]{2,1,0:T(8,128)S(1)} %get-tuple-element.82), channel_id=1, source_target_pairs={{0,1},{1,0},{2,3},{3,2},{4,5},{5,4},{6,7},{7,6},{8,9},{9,8},{10,11... | collective-permute-start | bytes 49160 | tf_op jit(solution)/shard_map/ppermute | solution.py:387
  24.4 7.2 %collective-permute-start.10 = (f32[2,4,64,128]{3,2,1,0:T(8,128)S(1)}, f32[2,4,64,128]{3,2,1,0:T(8,128)S(1)}, u32[]{:S(2)}, u32[]{:S(2)}) collective-permute-start(f32[2,4,64,128]{3,2,1,0:T(8,128)S(1)} %get-tuple-element.92), channel_id=1, source_target_pairs={{0,2},{2,0},{4,6},{6,4},{8,10},{10,8},{12,14},{14,12},{1,3},{3,1},... | collective-permute-start | bytes 786440 | tf_op jit(solution)/shard_map/ppermute | solution.py:386
  24.5 7.3 %collective-permute-start.9 = (f32[2,4,64,128]{3,2,1,0:T(8,128)S(1)}, f32[2,4,64,128]{3,2,1,0:T(8,128)S(1)}, u32[]{:S(2)}, u32[]{:S(2)}) collective-permute-start(f32[2,4,64,128]{3,2,1,0:T(8,128)S(1)} %get-tuple-element.91), channel_id=1, source_target_pairs={{2,4},{6,8},{10,12},{14,0},{4,2},{8,6},{12,10},{0,14},{3,5},{7,9},... | collective-permute-start | bytes 786440 | tf_op jit(solution)/shard_map/ppermute | solution.py:385
  26.7 4.9 %collective-permute-start.11 = (f32[2,16,128]{2,1,0:T(8,128)S(1)}, f32[2,16,128]{2,1,0:T(8,128)S(1)}, u32[]{:S(2)}, u32[]{:S(2)}) collective-permute-start(f32[2,16,128]{2,1,0:T(8,128)S(1)} %get-tuple-element.93), channel_id=1, source_target_pairs={{0,1},{1,0},{2,3},{3,2},{4,5},{5,4},{6,7},{7,6},{8,9},{9,8},{10,11... | collective-permute-start | bytes 49160 | tf_op jit(solution)/shard_map/ppermute | solution.py:387
  30.4 24.0 %copy-start = (f32[4,8,128]{2,1,0:T(8,128)S(1)}, f32[4,8,128]{2,1,0:T(8,128)}, u32[]{:S(2)}) copy-start(f32[4,8,128]{2,1,0:T(8,128)} %param.13) | copy-start | bytes 49156
  69.8 5.7 %collective-permute-start.12 = (f32[1,4,64,128]{3,2,1,0:T(8,128)S(1)}, f32[1,4,64,128]{3,2,1,0:T(8,128)S(1)}, u32[]{:S(2)}, u32[]{:S(2)}) collective-permute-start(f32[1,4,64,128]{3,2,1,0:T(8,128)S(1)} %get-tuple-element.98), channel_id=1, source_target_pairs={{2,4},{6,8},{10,12},{14,0},{4,2},{8,6},{12,10},{0,14},{3,5},{7,9},... | collective-permute-start | bytes 393224 | tf_op jit(solution)/shard_map/ppermute | solution.py:385
  71.5 4.0 %collective-permute-start.13 = (f32[1,4,64,128]{3,2,1,0:T(8,128)S(1)}, f32[1,4,64,128]{3,2,1,0:T(8,128)S(1)}, u32[]{:S(2)}, u32[]{:S(2)}) collective-permute-start(f32[1,4,64,128]{3,2,1,0:T(8,128)S(1)} %get-tuple-element.99), channel_id=1, source_target_pairs={{0,2},{2,0},{4,6},{6,4},{8,10},{10,8},{12,14},{14,12},{1,3},{3,1},... | collective-permute-start | bytes 393224 | tf_op jit(solution)/shard_map/ppermute | solution.py:386
  71.6 3.7 %collective-permute-start.14 = (f32[1,16,128]{2,1,0:T(8,128)S(1)}, f32[1,16,128]{2,1,0:T(8,128)S(1)}, u32[]{:S(2)}, u32[]{:S(2)}) collective-permute-start(f32[1,16,128]{2,1,0:T(8,128)S(1)} %get-tuple-element.100), channel_id=1, source_target_pairs={{0,1},{1,0},{2,3},{3,2},{4,5},{5,4},{6,7},{7,6},{8,9},{9,8},{10,11... | collective-permute-start | bytes 24584 | tf_op jit(solution)/shard_map/ppermute | solution.py:387
  76.0 5.7 %collective-permute-start.15 = (f32[1,4,64,128]{3,2,1,0:T(8,128)S(1)}, f32[1,4,64,128]{3,2,1,0:T(8,128)S(1)}, u32[]{:S(2)}, u32[]{:S(2)}) collective-permute-start(f32[1,4,64,128]{3,2,1,0:T(8,128)S(1)} %get-tuple-element.102), channel_id=1, source_target_pairs={{2,4},{6,8},{10,12},{14,0},{4,2},{8,6},{12,10},{0,14},{3,5},{7,9},... | collective-permute-start | bytes 393224 | tf_op jit(solution)/shard_map/ppermute | solution.py:385
  77.7 4.0 %collective-permute-start.16 = (f32[1,4,64,128]{3,2,1,0:T(8,128)S(1)}, f32[1,4,64,128]{3,2,1,0:T(8,128)S(1)}, u32[]{:S(2)}, u32[]{:S(2)}) collective-permute-start(f32[1,4,64,128]{3,2,1,0:T(8,128)S(1)} %get-tuple-element.103), channel_id=1, source_target_pairs={{0,2},{2,0},{4,6},{6,4},{8,10},{10,8},{12,14},{14,12},{1,3},{3,1},... | collective-permute-start | bytes 393224 | tf_op jit(solution)/shard_map/ppermute | solution.py:386
  77.7 3.7 %collective-permute-start.17 = (f32[1,16,128]{2,1,0:T(8,128)S(1)}, f32[1,16,128]{2,1,0:T(8,128)S(1)}, u32[]{:S(2)}, u32[]{:S(2)}) collective-permute-start(f32[1,16,128]{2,1,0:T(8,128)S(1)} %get-tuple-element.104), channel_id=1, source_target_pairs={{0,1},{1,0},{2,3},{3,2},{4,5},{5,4},{6,7},{7,6},{8,9},{9,8},{10,11... | collective-permute-start | bytes 24584 | tf_op jit(solution)/shard_map/ppermute | solution.py:387
  82.2 5.7 %collective-permute-start.18 = (f32[1,4,64,128]{3,2,1,0:T(8,128)S(1)}, f32[1,4,64,128]{3,2,1,0:T(8,128)S(1)}, u32[]{:S(2)}, u32[]{:S(2)}) collective-permute-start(f32[1,4,64,128]{3,2,1,0:T(8,128)S(1)} %get-tuple-element.107), channel_id=1, source_target_pairs={{2,4},{6,8},{10,12},{14,0},{4,2},{8,6},{12,10},{0,14},{3,5},{7,9},... | collective-permute-start | bytes 393224 | tf_op jit(solution)/shard_map/ppermute | solution.py:385
  83.9 4.0 %collective-permute-start.19 = (f32[1,4,64,128]{3,2,1,0:T(8,128)S(1)}, f32[1,4,64,128]{3,2,1,0:T(8,128)S(1)}, u32[]{:S(2)}, u32[]{:S(2)}) collective-permute-start(f32[1,4,64,128]{3,2,1,0:T(8,128)S(1)} %get-tuple-element.108), channel_id=1, source_target_pairs={{0,2},{2,0},{4,6},{6,4},{8,10},{10,8},{12,14},{14,12},{1,3},{3,1},... | collective-permute-start | bytes 393224 | tf_op jit(solution)/shard_map/ppermute | solution.py:386
  83.9 3.7 %collective-permute-start.20 = (f32[1,16,128]{2,1,0:T(8,128)S(1)}, f32[1,16,128]{2,1,0:T(8,128)S(1)}, u32[]{:S(2)}, u32[]{:S(2)}) collective-permute-start(f32[1,16,128]{2,1,0:T(8,128)S(1)} %get-tuple-element.109), channel_id=1, source_target_pairs={{0,1},{1,0},{2,3},{3,2},{4,5},{5,4},{6,7},{7,6},{8,9},{9,8},{10,11... | collective-permute-start | bytes 24584 | tf_op jit(solution)/shard_map/ppermute | solution.py:387
  89.0 1.3 %collective-permute-start.21 = (f32[72,128]{1,0:T(8,128)S(1)}, f32[72,128]{1,0:T(8,128)S(1)}, u32[]{:S(2)}, u32[]{:S(2)}) collective-permute-start(f32[72,128]{1,0:T(8,128)S(1)} %shard_map.137.mine), channel_id=1, source_target_pairs={{0,2},{2,0},{4,6},{6,4},{8,10},{10,8},{12,14},{14,12},{1,3},{3,1},... | collective-permute-start | bytes 110600 | tf_op jit(solution)/shard_map/ppermute | solution.py:449

commit v10 on v8

--- a/solution.py
+++ b/solution.py
@@ -349,21 +349,26 @@
 
 
 def pair_kernel(mine, theirs, copies):
-    total = mine[...] + theirs[...]
+    own = pl.ds(pl.multiple_of(32 * position()[0], 8), 32)
+    samples = mine[own, :] + theirs[own, :]
+    sums = mine[64:72] + theirs[64:72]
     for i in range(8):
-        copies[i] = total
-
-
-def collect_kernel(arrived, predicted, copies):
+        copies[i, 0:32] = samples
+        copies[i, 32:40] = sums
+
+
+def collect_kernel(arrived, half, copies):
     total = arrived[0]
     for i in range(1, 8):
         total = total + arrived[i]
-    predicted[...] = total[0:64]
+    half[...] = total[0:32]
     for i in range(16):
-        copies[i] = total[64:72]
-
-
-def finish_kernel(stats, predicted, scaled, traces, image, residual):
+        copies[i] = total[32:40]
+
+
+def finish_kernel(stats, half, other, scaled, traces, image, residual):
+    core = position()[0]
+    predicted = (jnp.where(core == 0, half[...], other[...]), jnp.where(core == 0, other[...], half[...]))
     total = stats[0]
     for i in range(1, 16):
         total = total + stats[i]
@@ -374,7 +379,8 @@
     for n in range(STEPS):
         for j in range(16):
             at = pl.ds(BY * j, BY)
-            row = predicted[16 * n + j : 16 * n + j + 1, :]
+            number = 16 * (n % 2) + j
+            row = predicted[n // 2][number : number + 1]
             residual[n : n + 1, at] = traces[n : n + 1, at] - step * row
 
 
@@ -447,14 +453,16 @@
         make_born(3, True), [((72, BY), F32)],
         [HALO, pltpu.VMEM((BX, NZ, BY), F32), pltpu.VMEM((512, 2 * BY), BF16)],
     )(*one(d3), d3, d2, source, acc3, vel, *e, pick_cell, pick_y, s1, s2, s3, dot)
-    theirs = lax.ppermute(block, "gx", [(i, i ^ 1) for i in range(8)])
-    payload, = call(pair_kernel, [((8, 72, BY), F32)])(block, theirs)
+    swap = [(i, i ^ 1) for i in range(8)]
+    theirs = lax.ppermute(block, "gx", swap)
+    payload, = call(pair_kernel, [((8, 40, BY), F32)])(block, theirs)
     same_core = [[2 * (2 * c + k) + g for c in range(4) for g in range(2)] for k in range(2)]
     arrived = lax.all_to_all(payload, ("gx", "gy"), 0, 0, axis_index_groups=same_core, tiled=True)
-    predicted, stats = call(collect_kernel, [((64, BY), F32), ((16, 8, BY), F32)])(arrived)
+    half, stats = call(collect_kernel, [((32, BY), F32), ((16, 8, BY), F32)])(arrived)
+    other = lax.ppermute(half, "gx", swap)
     stats = lax.all_to_all(stats, "shot", 0, 0, tiled=True)
     image, residual = call(finish_kernel, [((32, BY), F32), ((4, NREC), F32)])(
-        stats, predicted, scaled, traces[0])
+        stats, half, other, scaled, traces[0])
     return image.reshape(4, BX, BY), residual[None]
 
 

time: 118 us -> 117 us (level)
  blocking collectives: 62 us -> 46.7 us
  waiting for transfers between devices: 20.6 us -> 29.7 us
  starting transfers between devices: 11.5 us -> 16.3 us
    all_to_all x1 -> x0, blocking collectives: 13.8 us -> none  [on_device(): stats = lax.all_to_all(stats, 'shot', 0, 0, tiled=True)]
    all_to_all x0 -> x1, waiting for transfers between devices: none -> 7.93 us  [on_device(): stats = lax.all_to_all(stats, 'shot', 0, 0, tiled=True)]
    all_to_all x0 -> x1, starting transfers between devices: none -> 4.86 us  [on_device(): stats = lax.all_to_all(stats, 'shot', 0, 0, tiled=True)]
    all_to_all x1, blocking collectives: 10.8 us -> 9.31 us  [on_device(): lax.all_to_all(payload, ('gx', 'gy'), 0, 0, axis_index_groups=same_core,...]
    ppermute x1 -> x2, waiting for transfers between devices: 1.2 us -> 2.38 us  [the longest x1 1.2 us: on_device(): theirs = lax.ppermute(block, 'gx', swap)]
  transfers between devices with their start and end apart: 22 -> 24, of which waited for: 12 -> 14; matrix products, arithmetic and copies ran while one was open for 2% -> 2% of each run, Pallas kernels for 11% -> 11%
where the time goes in v10:
time: 117 us
  blocking collectives  46.7 us (40%)
  waiting for transfers between devices  29.7 us (25%)
  Pallas kernels  18.9 us (16%)
  starting transfers between devices  16.3 us (14%)
  between operations  2.21 us (2%)
  other arithmetic  1.91 us (2%)
    all_to_all x1, blocking collectives, on_device(): lax.all_to_all(grad.reshape(16, 4, BX, BY), 'shot', 0, 0, tiled=True)  22 us
    pallas_call x29, Pallas kernels, run(): pl.pallas_call(kernel, out_shape=[jax.ShapeDtypeStruct(s, d) for s, d in...  18.9 us
    all_to_all x1, blocking collectives, on_device(): lax.all_to_all(copies.reshape(16, 4, BX, BY), 'shot', 0, 0, tiled=True)  15.4 us
    ppermute x7, waiting for transfers between devices, exchange(): lax.ppermute(outer, 'gx', across)  12 us
    all_to_all x1, blocking collectives, on_device(): lax.all_to_all(payload, ('gx', 'gy'), 0, 0, axis_index_groups=same_core,...  9.31 us
    all_to_all x1, waiting for transfers between devices, on_device(): stats = lax.all_to_all(stats, 'shot', 0, 0, tiled=True)  7.93 us
    ppermute x7, waiting for transfers between devices, exchange(): lax.ppermute(strip, 'gy', [(0, 1), (1, 0)])  7.33 us
    ppermute x7, starting transfers between devices, exchange(): lax.ppermute(strip, 'gy', [(0, 1), (1, 0)])  5.53 us
  transfers between devices with their start and end apart: 24, of which 14 were waited for; matrix products, arithmetic and copies ran while one was open for 2% of the time, Pallas kernels for 11%

profile of v10, /device:TPU:32, one launch (start us, length us, event | category | flops | bytes accessed | tf_op | source)
XLA Modules:
  0.0 116.7 jit_solution(2832704387032343768)
XLA Ops:
  0.6 0.9 copy-done
  1.8 2.5 %collective-permute-start = (f32[1,4,64,128]{3,2,1,0:T(8,128)S(1)}, f32[1,4,64,128]{3,2,1,0:T(8,128)S(1)}, u32[]{:S(2)}, u32[]{:S(2)}) collective-permute-start(f32[1,4,64,128]{3,2,1,0:T(8,128)S(1)} %get-tuple-element.63), channel_id=1, source_target_pairs={{2,4},{6,8},{10,12},{14,0},{4,2},{8,6},{12,10},{0,14},{3,5},{7,9},... | collective-permute-start | bytes 393224 | tf_op jit(solution)/shard_map/ppermute | solution.py:392
  4.3 1.5 %collective-permute-start.2 = (f32[1,16,128]{2,1,0:T(8,128)S(1)}, f32[1,16,128]{2,1,0:T(8,128)S(1)}, u32[]{:S(2)}, u32[]{:S(2)}) collective-permute-start(f32[1,16,128]{2,1,0:T(8,128)S(1)} %get-tuple-element.65), channel_id=1, source_target_pairs={{0,1},{1,0},{2,3},{3,2},{4,5},{5,4},{6,7},{7,6},{8,9},{9,8},{10,11... | collective-permute-start | bytes 24584 | tf_op jit(solution)/shard_map/ppermute | solution.py:394
  5.8 0.8 convert_add_fusion.shot
  6.7 1.1 pad_maximum_fusion.both
  7.7 1.3 %shard_map.116 = (f32[8,64,128]{2,1,0:T(8,128)S(1)}, bf16[512,2048]{1,0:T(8,128)(2,1)S(1)}, bf16[128,2048]{1,0:T(8,128)(2,1)S(1)}) custom-call(f32[5,2048]{1,0:T(8,128)S(1)} %convert_add_fusion.shot), custom_call_target="tpu_custom_call" | custom-call | flops 10000000 | bytes 2000000 | tf_op jit(solution)/shard_map/pallas_call | solution.py:25
  9.1 0.6 shard_map.114.part
  10.3 0.7 collective-permute-start.3
  11.3 0.7 collective-permute-start.5
  12.0 0.9 shard_map.119.inj
  12.9 1.2 %shard_map.118 = (f32[8,64,128]{2,1,0:T(8,128)S(1)}, f32[8,64,128]{2,1,0:T(8,128)S(1)}) custom-call(f32[8,64,128]{2,1,0:T(8,128)S(1)} %get-tuple-element.66.refs_0_.newer.older, f32[8,64,128]{2,1,0:T(8,128)S(1)} %get-tuple-element.67.refs_1_), custom_call_target="tpu_custom_call" | custom-call | flops 10000000 | bytes 2000000 | tf_op jit(solution)/shard_map/pallas_call | solution.py:25
  14.1 1.0 collective-permute-done.5.rest_2_
  15.0 2.3 %collective-permute-done.3.rest_0_ = f32[2,4,64,128]{3,2,1,0:T(8,128)S(1)} collective-permute-done((f32[2,4,64,128]{3,2,1,0:T(8,128)S(1)}, f32[2,4,64,128]{3,2,1,0:T(8,128)S(1)}, u32[]{:S(2)}, u32[]{:S(2)}) %collective-permute-start.3) | collective-permute-done | bytes 262176 | tf_op jit(solution)/shard_map/ppermute | solution.py:392
  17.4 0.7 shard_map.120
  18.1 0.7 collective-permute-start.6
  18.8 1.0 collective-permute-start.8
  19.8 0.9 shard_map.123.inj
  20.7 1.2 %shard_map.122 = (f32[8,64,128]{2,1,0:T(8,128)S(1)}, f32[8,64,128]{2,1,0:T(8,128)S(1)}) custom-call(f32[8,64,128]{2,1,0:T(8,128)S(1)} %get-tuple-element.75.after.refs_0_.newer, f32[8,64,128]{2,1,0:T(8,128)S(1)} %get-tuple-element.76.refs_1_), custom_call_target="tpu_custom_call" | custom-call | flops 10000000 | bytes 2000000 | tf_op jit(solution)/shard_map/pallas_call | solution.py:25
  21.9 0.6 collective-permute-done.8.rest_3_
  22.5 2.7 %collective-permute-done.6.rest_1_ = f32[2,4,64,128]{3,2,1,0:T(8,128)S(1)} collective-permute-done((f32[2,4,64,128]{3,2,1,0:T(8,128)S(1)}, f32[2,4,64,128]{3,2,1,0:T(8,128)S(1)}, u32[]{:S(2)}, u32[]{:S(2)}) %collective-permute-start.6) | collective-permute-done | bytes 262176 | tf_op jit(solution)/shard_map/ppermute | solution.py:392
  25.2 0.7 shard_map.124
  26.2 0.7 collective-permute-start.9
  26.8 1.0 collective-permute-start.11
  27.9 0.9 shard_map.126.inj0
  30.1 1.2 shard_map.125
  31.3 2.0 %collective-permute-done.9.outer = f32[2,4,64,128]{3,2,1,0:T(8,128)S(1)} collective-permute-done((f32[2,4,64,128]{3,2,1,0:T(8,128)S(1)}, f32[2,4,64,128]{3,2,1,0:T(8,128)S(1)}, u32[]{:S(2)}, u32[]{:S(2)}) %collective-permute-start.9) | collective-permute-done | bytes 262176 | tf_op jit(solution)/shard_map/ppermute | solution.py:392
  33.8 22.0 %all_to_all.20 = f32[16,4,8,128]{3,2,1,0:T(8,128)S(1)} all-to-all(f32[16,4,8,128]{3,2,1,0:T(8,128)S(1)} %bitcast.14), channel_id=1, replica_groups=mesh['shot'=16,'gx'=8,'gy'=2] {'shot'}, dimensions={0} | all-to-all | bytes 524288 | tf_op jit(solution)/shard_map/all_to_all | solution.py:434
  55.8 15.4 %all_to_all.21 = f32[16,4,8,128]{3,2,1,0:T(8,128)S(1)} all-to-all(f32[16,4,8,128]{3,2,1,0:T(8,128)S(1)} %bitcast.15), channel_id=1, replica_groups=mesh['shot'=16,'gx'=8,'gy'=2] {'shot'}, dimensions={0} | all-to-all | bytes 524288 | tf_op jit(solution)/shard_map/all_to_all | solution.py:438
  72.0 0.8 shard_map.131.rest_0_.rest_2_
  72.8 0.7 shard_map.130.part
  73.5 1.9 %collective-permute-done.14.strip = f32[1,16,128]{2,1,0:T(8,128)S(1)} collective-permute-done((f32[1,16,128]{2,1,0:T(8,128)S(1)}, f32[1,16,128]{2,1,0:T(8,128)S(1)}, u32[]{:S(2)}, u32[]{:S(2)}) %collective-permute-start.14) | collective-permute-done | bytes 8224 | tf_op jit(solution)/shard_map/ppermute | solution.py:394
  75.4 1.8 %collective-permute-done.12.outer = f32[1,4,64,128]{3,2,1,0:T(8,128)S(1)} collective-permute-done((f32[1,4,64,128]{3,2,1,0:T(8,128)S(1)}, f32[1,4,64,128]{3,2,1,0:T(8,128)S(1)}, u32[]{:S(2)}, u32[]{:S(2)}) %collective-permute-start.12) | collective-permute-done | bytes 131104 | tf_op jit(solution)/shard_map/ppermute | solution.py:392
  78.3 0.8 shard_map.134.rest_0_.rest_3_
  79.1 0.6 shard_map.133.part
  79.7 1.9 %collective-permute-done.17.strip = f32[1,16,128]{2,1,0:T(8,128)S(1)} collective-permute-done((f32[1,16,128]{2,1,0:T(8,128)S(1)}, f32[1,16,128]{2,1,0:T(8,128)S(1)}, u32[]{:S(2)}, u32[]{:S(2)}) %collective-permute-start.17) | collective-permute-done | bytes 8224 | tf_op jit(solution)/shard_map/ppermute | solution.py:394
  81.6 1.8 %collective-permute-done.15.outer = f32[1,4,64,128]{3,2,1,0:T(8,128)S(1)} collective-permute-done((f32[1,4,64,128]{3,2,1,0:T(8,128)S(1)}, f32[1,4,64,128]{3,2,1,0:T(8,128)S(1)}, u32[]{:S(2)}, u32[]{:S(2)}) %collective-permute-start.15) | collective-permute-done | bytes 131104 | tf_op jit(solution)/shard_map/ppermute | solution.py:392
  84.6 0.8 shard_map.137.rest_4_
  85.3 0.6 shard_map.136.part
  86.0 2.0 %collective-permute-done.20.strip = f32[1,16,128]{2,1,0:T(8,128)S(1)} collective-permute-done((f32[1,16,128]{2,1,0:T(8,128)S(1)}, f32[1,16,128]{2,1,0:T(8,128)S(1)}, u32[]{:S(2)}, u32[]{:S(2)}) %collective-permute-start.20) | collective-permute-done | bytes 8224 | tf_op jit(solution)/shard_map/ppermute | solution.py:394
  88.0 1.5 %collective-permute-done.18.outer = f32[1,4,64,128]{3,2,1,0:T(8,128)S(1)} collective-permute-done((f32[1,4,64,128]{3,2,1,0:T(8,128)S(1)}, f32[1,4,64,128]{3,2,1,0:T(8,128)S(1)}, u32[]{:S(2)}, u32[]{:S(2)}) %collective-permute-start.18) | collective-permute-done | bytes 131104 | tf_op jit(solution)/shard_map/ppermute | solution.py:392
  89.5 1.1 shard_map.138.mine
  90.7 1.2 %collective-permute-done.21.theirs = f32[72,128]{1,0:T(8,128)S(1)} collective-permute-done((f32[72,128]{1,0:T(8,128)S(1)}, f32[72,128]{1,0:T(8,128)S(1)}, u32[]{:S(2)}, u32[]{:S(2)}) %collective-permute-start.21) | collective-permute-done | bytes 36896 | tf_op jit(solution)/shard_map/ppermute | solution.py:457
  92.0 9.3 %all_to_all.22.arrived = f32[8,40,128]{2,1,0:T(8,128)S(1)} all-to-all(f32[8,40,128]{2,1,0:T(8,128)S(1)} %shard_map.139), channel_id=1, replica_groups={{0,1,4,5,8,9,12,13},{2,3,6,7,10,11,14,15},{16,17,20,21,24,25,28,29},{18..., dimensions={0} | all-to-all | bytes 327680 | tf_op jit(solution)/shard_map/all_to_all | solution.py:460
  101.3 0.6 shard_map.140
  101.9 4.9 %all-to-all-start.3 = ((f32[16,8,128]{2,1,0:T(8,128)}), f32[16,8,128]{2,1,0:T(8,128)S(1)}, u32[]{:S(2)}, u32[]{:S(2)}) async-start(f32[16,8,128]{2,1,0:T(8,128)} %get-tuple-element.111), calls=%async_computation.3 | async-start | bytes 131072 | tf_op jit(solution)/shard_map/all_to_all | solution.py:463
  106.8 1.2 %collective-permute-done.22.other = f32[32,128]{1,0:T(8,128)S(1)} collective-permute-done((f32[32,128]{1,0:T(8,128)S(1)}, f32[32,128]{1,0:T(8,128)S(1)}, u32[]{:S(2)}, u32[]{:S(2)}) %collective-permute-start.22) | collective-permute-done | bytes 16416 | tf_op jit(solution)/shard_map/ppermute | solution.py:462
  107.9 7.9 %all-to-all-done.3.stats = f32[16,8,128]{2,1,0:T(8,128)S(1)} async-done(((f32[16,8,128]{2,1,0:T(8,128)}), f32[16,8,128]{2,1,0:T(8,128)S(1)}, u32[]{:S(2)}, u32[]{:S(2)}) %all-to-all-start.3) | async-done | bytes 65568 | tf_op jit(solution)/shard_map/all_to_all | solution.py:463
  115.9 0.8 shard_map.141
  (40 shorter events, 5.3 us)
Async XLA Ops:
  0.6 1.0 copy-start
  1.8 8.0 %collective-permute-start = (f32[1,4,64,128]{3,2,1,0:T(8,128)S(1)}, f32[1,4,64,128]{3,2,1,0:T(8,128)S(1)}, u32[]{:S(2)}, u32[]{:S(2)}) collective-permute-start(f32[1,4,64,128]{3,2,1,0:T(8,128)S(1)} %get-tuple-element.63), channel_id=1, source_target_pairs={{2,4},{6,8},{10,12},{14,0},{4,2},{8,6},{12,10},{0,14},{3,5},{7,9},... | collective-permute-start | bytes 393224 | tf_op jit(solution)/shard_map/ppermute | solution.py:392
  4.3 5.5 %collective-permute-start.1 = (f32[1,4,64,128]{3,2,1,0:T(8,128)S(1)}, f32[1,4,64,128]{3,2,1,0:T(8,128)S(1)}, u32[]{:S(2)}, u32[]{:S(2)}) collective-permute-start(f32[1,4,64,128]{3,2,1,0:T(8,128)S(1)} %get-tuple-element.64), channel_id=1, source_target_pairs={{0,2},{2,0},{4,6},{6,4},{8,10},{10,8},{12,14},{14,12},{1,3},{3,1},... | collective-permute-start | bytes 393224 | tf_op jit(solution)/shard_map/ppermute | solution.py:393
  4.3 5.5 %collective-permute-start.2 = (f32[1,16,128]{2,1,0:T(8,128)S(1)}, f32[1,16,128]{2,1,0:T(8,128)S(1)}, u32[]{:S(2)}, u32[]{:S(2)}) collective-permute-start(f32[1,16,128]{2,1,0:T(8,128)S(1)} %get-tuple-element.65), channel_id=1, source_target_pairs={{0,1},{1,0},{2,3},{3,2},{4,5},{5,4},{6,7},{7,6},{8,9},{9,8},{10,11... | collective-permute-start | bytes 24584 | tf_op jit(solution)/shard_map/ppermute | solution.py:394
  10.3 7.1 %collective-permute-start.3 = (f32[2,4,64,128]{3,2,1,0:T(8,128)S(1)}, f32[2,4,64,128]{3,2,1,0:T(8,128)S(1)}, u32[]{:S(2)}, u32[]{:S(2)}) collective-permute-start(f32[2,4,64,128]{3,2,1,0:T(8,128)S(1)} %get-tuple-element.72), channel_id=1, source_target_pairs={{2,4},{6,8},{10,12},{14,0},{4,2},{8,6},{12,10},{0,14},{3,5},{7,9},... | collective-permute-start | bytes 786440 | tf_op jit(solution)/shard_map/ppermute | solution.py:392
  10.9 6.4 %collective-permute-start.4 = (f32[2,4,64,128]{3,2,1,0:T(8,128)S(1)}, f32[2,4,64,128]{3,2,1,0:T(8,128)S(1)}, u32[]{:S(2)}, u32[]{:S(2)}) collective-permute-start(f32[2,4,64,128]{3,2,1,0:T(8,128)S(1)} %get-tuple-element.73), channel_id=1, source_target_pairs={{0,2},{2,0},{4,6},{6,4},{8,10},{10,8},{12,14},{14,12},{1,3},{3,1},... | collective-permute-start | bytes 786440 | tf_op jit(solution)/shard_map/ppermute | solution.py:393
  11.3 3.7 %collective-permute-start.5 = (f32[2,16,128]{2,1,0:T(8,128)S(1)}, f32[2,16,128]{2,1,0:T(8,128)S(1)}, u32[]{:S(2)}, u32[]{:S(2)}) collective-permute-start(f32[2,16,128]{2,1,0:T(8,128)S(1)} %get-tuple-element.74), channel_id=1, source_target_pairs={{0,1},{1,0},{2,3},{3,2},{4,5},{5,4},{6,7},{7,6},{8,9},{9,8},{10,11... | collective-permute-start | bytes 49160 | tf_op jit(solution)/shard_map/ppermute | solution.py:394
  18.1 7.1 %collective-permute-start.6 = (f32[2,4,64,128]{3,2,1,0:T(8,128)S(1)}, f32[2,4,64,128]{3,2,1,0:T(8,128)S(1)}, u32[]{:S(2)}, u32[]{:S(2)}) collective-permute-start(f32[2,4,64,128]{3,2,1,0:T(8,128)S(1)} %get-tuple-element.80), channel_id=1, source_target_pairs={{2,4},{6,8},{10,12},{14,0},{4,2},{8,6},{12,10},{0,14},{3,5},{7,9},... | collective-permute-start | bytes 786440 | tf_op jit(solution)/shard_map/ppermute | solution.py:392
  18.8 6.4 %collective-permute-start.7 = (f32[2,4,64,128]{3,2,1,0:T(8,128)S(1)}, f32[2,4,64,128]{3,2,1,0:T(8,128)S(1)}, u32[]{:S(2)}, u32[]{:S(2)}) collective-permute-start(f32[2,4,64,128]{3,2,1,0:T(8,128)S(1)} %get-tuple-element.81), channel_id=1, source_target_pairs={{0,2},{2,0},{4,6},{6,4},{8,10},{10,8},{12,14},{14,12},{1,3},{3,1},... | collective-permute-start | bytes 786440 | tf_op jit(solution)/shard_map/ppermute | solution.py:393
  18.8 3.7 %collective-permute-start.8 = (f32[2,16,128]{2,1,0:T(8,128)S(1)}, f32[2,16,128]{2,1,0:T(8,128)S(1)}, u32[]{:S(2)}, u32[]{:S(2)}) collective-permute-start(f32[2,16,128]{2,1,0:T(8,128)S(1)} %get-tuple-element.82), channel_id=1, source_target_pairs={{0,1},{1,0},{2,3},{3,2},{4,5},{5,4},{6,7},{7,6},{8,9},{9,8},{10,11... | collective-permute-start | bytes 49160 | tf_op jit(solution)/shard_map/ppermute | solution.py:394
  25.9 5.4 %collective-permute-start.10 = (f32[2,4,64,128]{3,2,1,0:T(8,128)S(1)}, f32[2,4,64,128]{3,2,1,0:T(8,128)S(1)}, u32[]{:S(2)}, u32[]{:S(2)}) collective-permute-start(f32[2,4,64,128]{3,2,1,0:T(8,128)S(1)} %get-tuple-element.92), channel_id=1, source_target_pairs={{0,2},{2,0},{4,6},{6,4},{8,10},{10,8},{12,14},{14,12},{1,3},{3,1},... | collective-permute-start | bytes 786440 | tf_op jit(solution)/shard_map/ppermute | solution.py:393
  26.2 7.1 %collective-permute-start.9 = (f32[2,4,64,128]{3,2,1,0:T(8,128)S(1)}, f32[2,4,64,128]{3,2,1,0:T(8,128)S(1)}, u32[]{:S(2)}, u32[]{:S(2)}) collective-permute-start(f32[2,4,64,128]{3,2,1,0:T(8,128)S(1)} %get-tuple-element.91), channel_id=1, source_target_pairs={{2,4},{6,8},{10,12},{14,0},{4,2},{8,6},{12,10},{0,14},{3,5},{7,9},... | collective-permute-start | bytes 786440 | tf_op jit(solution)/shard_map/ppermute | solution.py:392
  26.8 4.4 %collective-permute-start.11 = (f32[2,16,128]{2,1,0:T(8,128)S(1)}, f32[2,16,128]{2,1,0:T(8,128)S(1)}, u32[]{:S(2)}, u32[]{:S(2)}) collective-permute-start(f32[2,16,128]{2,1,0:T(8,128)S(1)} %get-tuple-element.93), channel_id=1, source_target_pairs={{0,1},{1,0},{2,3},{3,2},{4,5},{5,4},{6,7},{7,6},{8,9},{9,8},{10,11... | collective-permute-start | bytes 49160 | tf_op jit(solution)/shard_map/ppermute | solution.py:394
  30.1 25.7 %copy-start.2 = (f32[4,8,128]{2,1,0:T(8,128)S(1)}, f32[4,8,128]{2,1,0:T(8,128)}, u32[]{:S(2)}) copy-start(f32[4,8,128]{2,1,0:T(8,128)} %param.13) | copy-start | bytes 49156
  71.5 5.7 %collective-permute-start.12 = (f32[1,4,64,128]{3,2,1,0:T(8,128)S(1)}, f32[1,4,64,128]{3,2,1,0:T(8,128)S(1)}, u32[]{:S(2)}, u32[]{:S(2)}) collective-permute-start(f32[1,4,64,128]{3,2,1,0:T(8,128)S(1)} %get-tuple-element.98), channel_id=1, source_target_pairs={{2,4},{6,8},{10,12},{14,0},{4,2},{8,6},{12,10},{0,14},{3,5},{7,9},... | collective-permute-start | bytes 393224 | tf_op jit(solution)/shard_map/ppermute | solution.py:392
  71.6 5.5 %collective-permute-start.13 = (f32[1,4,64,128]{3,2,1,0:T(8,128)S(1)}, f32[1,4,64,128]{3,2,1,0:T(8,128)S(1)}, u32[]{:S(2)}, u32[]{:S(2)}) collective-permute-start(f32[1,4,64,128]{3,2,1,0:T(8,128)S(1)} %get-tuple-element.99), channel_id=1, source_target_pairs={{0,2},{2,0},{4,6},{6,4},{8,10},{10,8},{12,14},{14,12},{1,3},{3,1},... | collective-permute-start | bytes 393224 | tf_op jit(solution)/shard_map/ppermute | solution.py:393
  71.7 3.7 %collective-permute-start.14 = (f32[1,16,128]{2,1,0:T(8,128)S(1)}, f32[1,16,128]{2,1,0:T(8,128)S(1)}, u32[]{:S(2)}, u32[]{:S(2)}) collective-permute-start(f32[1,16,128]{2,1,0:T(8,128)S(1)} %get-tuple-element.100), channel_id=1, source_target_pairs={{0,1},{1,0},{2,3},{3,2},{4,5},{5,4},{6,7},{7,6},{8,9},{9,8},{10,11... | collective-permute-start | bytes 24584 | tf_op jit(solution)/shard_map/ppermute | solution.py:394
  77.6 5.7 %collective-permute-start.15 = (f32[1,4,64,128]{3,2,1,0:T(8,128)S(1)}, f32[1,4,64,128]{3,2,1,0:T(8,128)S(1)}, u32[]{:S(2)}, u32[]{:S(2)}) collective-permute-start(f32[1,4,64,128]{3,2,1,0:T(8,128)S(1)} %get-tuple-element.102), channel_id=1, source_target_pairs={{2,4},{6,8},{10,12},{14,0},{4,2},{8,6},{12,10},{0,14},{3,5},{7,9},... | collective-permute-start | bytes 393224 | tf_op jit(solution)/shard_map/ppermute | solution.py:392
  77.9 5.4 %collective-permute-start.16 = (f32[1,4,64,128]{3,2,1,0:T(8,128)S(1)}, f32[1,4,64,128]{3,2,1,0:T(8,128)S(1)}, u32[]{:S(2)}, u32[]{:S(2)}) collective-permute-start(f32[1,4,64,128]{3,2,1,0:T(8,128)S(1)} %get-tuple-element.103), channel_id=1, source_target_pairs={{0,2},{2,0},{4,6},{6,4},{8,10},{10,8},{12,14},{14,12},{1,3},{3,1},... | collective-permute-start | bytes 393224 | tf_op jit(solution)/shard_map/ppermute | solution.py:393
  77.9 3.7 %collective-permute-start.17 = (f32[1,16,128]{2,1,0:T(8,128)S(1)}, f32[1,16,128]{2,1,0:T(8,128)S(1)}, u32[]{:S(2)}, u32[]{:S(2)}) collective-permute-start(f32[1,16,128]{2,1,0:T(8,128)S(1)} %get-tuple-element.104), channel_id=1, source_target_pairs={{0,1},{1,0},{2,3},{3,2},{4,5},{5,4},{6,7},{7,6},{8,9},{9,8},{10,11... | collective-permute-start | bytes 24584 | tf_op jit(solution)/shard_map/ppermute | solution.py:394
  83.8 5.7 %collective-permute-start.18 = (f32[1,4,64,128]{3,2,1,0:T(8,128)S(1)}, f32[1,4,64,128]{3,2,1,0:T(8,128)S(1)}, u32[]{:S(2)}, u32[]{:S(2)}) collective-permute-start(f32[1,4,64,128]{3,2,1,0:T(8,128)S(1)} %get-tuple-element.107), channel_id=1, source_target_pairs={{2,4},{6,8},{10,12},{14,0},{4,2},{8,6},{12,10},{0,14},{3,5},{7,9},... | collective-permute-start | bytes 393224 | tf_op jit(solution)/shard_map/ppermute | solution.py:392
  84.1 5.4 %collective-permute-start.19 = (f32[1,4,64,128]{3,2,1,0:T(8,128)S(1)}, f32[1,4,64,128]{3,2,1,0:T(8,128)S(1)}, u32[]{:S(2)}, u32[]{:S(2)}) collective-permute-start(f32[1,4,64,128]{3,2,1,0:T(8,128)S(1)} %get-tuple-element.108), channel_id=1, source_target_pairs={{0,2},{2,0},{4,6},{6,4},{8,10},{10,8},{12,14},{14,12},{1,3},{3,1},... | collective-permute-start | bytes 393224 | tf_op jit(solution)/shard_map/ppermute | solution.py:393
  84.1 3.9 %collective-permute-start.20 = (f32[1,16,128]{2,1,0:T(8,128)S(1)}, f32[1,16,128]{2,1,0:T(8,128)S(1)}, u32[]{:S(2)}, u32[]{:S(2)}) collective-permute-start(f32[1,16,128]{2,1,0:T(8,128)S(1)} %get-tuple-element.109), channel_id=1, source_target_pairs={{0,1},{1,0},{2,3},{3,2},{4,5},{5,4},{6,7},{7,6},{8,9},{9,8},{10,11... | collective-permute-start | bytes 24584 | tf_op jit(solution)/shard_map/ppermute | solution.py:394
  89.5 26.3 %copy-start.1 = (f32[1,4,2048]{2,1,0:T(4,128)S(1)}, f32[1,4,2048]{2,1,0:T(4,128)}, u32[]{:S(2)}) copy-start(f32[1,4,2048]{2,1,0:T(4,128)} %param.14) | copy-start | bytes 98308
  90.6 1.3 %collective-permute-start.21 = (f32[72,128]{1,0:T(8,128)S(1)}, f32[72,128]{1,0:T(8,128)S(1)}, u32[]{:S(2)}, u32[]{:S(2)}) collective-permute-start(f32[72,128]{1,0:T(8,128)S(1)} %shard_map.138.mine), channel_id=1, source_target_pairs={{0,2},{2,0},{4,6},{6,4},{8,10},{10,8},{12,14},{14,12},{1,3},{3,1},... | collective-permute-start | bytes 110600 | tf_op jit(solution)/shard_map/ppermute | solution.py:457
  101.9 14.0 %all-to-all-start.3 = ((f32[16,8,128]{2,1,0:T(8,128)}), f32[16,8,128]{2,1,0:T(8,128)S(1)}, u32[]{:S(2)}, u32[]{:S(2)}) async-start(f32[16,8,128]{2,1,0:T(8,128)} %get-tuple-element.111), calls=%async_computation.3 | async-start | bytes 131072 | tf_op jit(solution)/shard_map/all_to_all | solution.py:463
  106.8 1.2 %collective-permute-start.22 = (f32[32,128]{1,0:T(8,128)S(1)}, f32[32,128]{1,0:T(8,128)S(1)}, u32[]{:S(2)}, u32[]{:S(2)}) collective-permute-start(f32[32,128]{1,0:T(8,128)S(1)} %get-tuple-element.112.half), channel_id=1, source_target_pairs={{0,2},{2,0},{4,6},{6,4},{8,10},{10,8},{12,14},{14,12},{1,3},{3,1},... | collective-permute-start | bytes 49160 | tf_op jit(solution)/shard_map/ppermute | solution.py:462

commit v11 on v10

--- a/solution.py
+++ b/solution.py
@@ -357,13 +357,19 @@
         copies[i, 32:40] = sums
 
 
-def collect_kernel(arrived, half, copies):
-    total = arrived[0]
+def half_kernel(arrived, half):
+    total = arrived[0, 0:32]
     for i in range(1, 8):
-        total = total + arrived[i]
-    half[...] = total[0:32]
+        total = total + arrived[i, 0:32]
+    half[...] = total
+
+
+def collect_kernel(arrived, copies):
+    total = arrived[0, 32:40]
+    for i in range(1, 8):
+        total = total + arrived[i, 32:40]
     for i in range(16):
-        copies[i] = total[32:40]
+        copies[i] = total
 
 
 def finish_kernel(stats, half, other, scaled, traces, image, residual):
@@ -458,7 +464,8 @@
     payload, = call(pair_kernel, [((8, 40, BY), F32)])(block, theirs)
     same_core = [[2 * (2 * c + k) + g for c in range(4) for g in range(2)] for k in range(2)]
     arrived = lax.all_to_all(payload, ("gx", "gy"), 0, 0, axis_index_groups=same_core, tiled=True)
-    half, stats = call(collect_kernel, [((32, BY), F32), ((16, 8, BY), F32)])(arrived)
+    stats, = call(collect_kernel, [((16, 8, BY), F32)])(arrived)
+    half, = call(half_kernel, [((32, BY), F32)])(arrived)
     other = lax.ppermute(half, "gx", swap)
     stats = lax.all_to_all(stats, "shot", 0, 0, tiled=True)
     image, residual = call(finish_kernel, [((32, BY), F32), ((4, NREC), F32)])(

time: 117 us -> 117 us (level)
    pallas_call x29 -> x30, Pallas kernels: 18.9 us -> 18.9 us  [run(): pl.pallas_call(kernel, out_shape=[jax.ShapeDtypeStruct(s, d) for s, d in...]
where the time goes in v11:
time: 117 us
  blocking collectives  46.7 us (40%)
  waiting for transfers between devices  29.6 us (25%)
  Pallas kernels  18.9 us (16%)
  starting transfers between devices  16.4 us (14%)
  between operations  2.21 us (2%)
  other arithmetic  1.91 us (2%)
    all_to_all x1, blocking collectives, on_device(): lax.all_to_all(grad.reshape(16, 4, BX, BY), 'shot', 0, 0, tiled=True)  22 us
    pallas_call x30, Pallas kernels, run(): pl.pallas_call(kernel, out_shape=[jax.ShapeDtypeStruct(s, d) for s, d in...  18.9 us
    all_to_all x1, blocking collectives, on_device(): lax.all_to_all(copies.reshape(16, 4, BX, BY), 'shot', 0, 0, tiled=True)  15.4 us
    ppermute x7, waiting for transfers between devices, exchange(): lax.ppermute(outer, 'gx', across)  12 us
    all_to_all x1, blocking collectives, on_device(): lax.all_to_all(payload, ('gx', 'gy'), 0, 0, axis_index_groups=same_core,...  9.31 us
    all_to_all x1, waiting for transfers between devices, on_device(): stats = lax.all_to_all(stats, 'shot', 0, 0, tiled=True)  7.83 us
    ppermute x7, waiting for transfers between devices, exchange(): lax.ppermute(strip, 'gy', [(0, 1), (1, 0)])  7.33 us
    ppermute x7, starting transfers between devices, exchange(): lax.ppermute(strip, 'gy', [(0, 1), (1, 0)])  5.53 us
  transfers between devices with their start and end apart: 24, of which 14 were waited for; matrix products, arithmetic and copies ran while one was open for 2% of the time, Pallas kernels for 11%

profile of v11, /device:TPU:32, one launch (start us, length us, event | category | flops | bytes accessed | tf_op | source)
XLA Modules:
  0.0 116.7 jit_solution(11312019827996963792)
XLA Ops:
  0.6 0.9 copy-done
  1.8 2.5 %collective-permute-start = (f32[1,4,64,128]{3,2,1,0:T(8,128)S(1)}, f32[1,4,64,128]{3,2,1,0:T(8,128)S(1)}, u32[]{:S(2)}, u32[]{:S(2)}) collective-permute-start(f32[1,4,64,128]{3,2,1,0:T(8,128)S(1)} %get-tuple-element.61), channel_id=1, source_target_pairs={{2,4},{6,8},{10,12},{14,0},{4,2},{8,6},{12,10},{0,14},{3,5},{7,9},... | collective-permute-start | bytes 393224 | tf_op jit(solution)/shard_map/ppermute | solution.py:398
  4.3 1.5 %collective-permute-start.2 = (f32[1,16,128]{2,1,0:T(8,128)S(1)}, f32[1,16,128]{2,1,0:T(8,128)S(1)}, u32[]{:S(2)}, u32[]{:S(2)}) collective-permute-start(f32[1,16,128]{2,1,0:T(8,128)S(1)} %get-tuple-element.63), channel_id=1, source_target_pairs={{0,1},{1,0},{2,3},{3,2},{4,5},{5,4},{6,7},{7,6},{8,9},{9,8},{10,11... | collective-permute-start | bytes 24584 | tf_op jit(solution)/shard_map/ppermute | solution.py:400
  5.8 0.8 convert_add_fusion.shot
  6.7 1.1 pad_maximum_fusion.both
  7.7 1.3 %shard_map.116 = (f32[8,64,128]{2,1,0:T(8,128)S(1)}, bf16[512,2048]{1,0:T(8,128)(2,1)S(1)}, bf16[128,2048]{1,0:T(8,128)(2,1)S(1)}) custom-call(f32[5,2048]{1,0:T(8,128)S(1)} %convert_add_fusion.shot), custom_call_target="tpu_custom_call" | custom-call | flops 10000000 | bytes 2000000 | tf_op jit(solution)/shard_map/pallas_call | solution.py:25
  9.1 0.6 shard_map.114.part
  10.3 0.7 collective-permute-start.3
  11.3 0.7 collective-permute-start.5
  12.0 0.9 shard_map.119.inj
  12.9 1.2 %shard_map.118 = (f32[8,64,128]{2,1,0:T(8,128)S(1)}, f32[8,64,128]{2,1,0:T(8,128)S(1)}) custom-call(f32[8,64,128]{2,1,0:T(8,128)S(1)} %get-tuple-element.64.refs_0_.newer.older, f32[8,64,128]{2,1,0:T(8,128)S(1)} %get-tuple-element.65.refs_1_), custom_call_target="tpu_custom_call" | custom-call | flops 10000000 | bytes 2000000 | tf_op jit(solution)/shard_map/pallas_call | solution.py:25
  14.1 1.0 collective-permute-done.5.rest_2_
  15.0 2.3 %collective-permute-done.3.rest_0_ = f32[2,4,64,128]{3,2,1,0:T(8,128)S(1)} collective-permute-done((f32[2,4,64,128]{3,2,1,0:T(8,128)S(1)}, f32[2,4,64,128]{3,2,1,0:T(8,128)S(1)}, u32[]{:S(2)}, u32[]{:S(2)}) %collective-permute-start.3) | collective-permute-done | bytes 262176 | tf_op jit(solution)/shard_map/ppermute | solution.py:398
  17.4 0.7 shard_map.120
  18.1 0.7 collective-permute-start.6
  18.8 1.0 collective-permute-start.8
  19.8 0.9 shard_map.123.inj
  20.7 1.2 %shard_map.122 = (f32[8,64,128]{2,1,0:T(8,128)S(1)}, f32[8,64,128]{2,1,0:T(8,128)S(1)}) custom-call(f32[8,64,128]{2,1,0:T(8,128)S(1)} %get-tuple-element.73.after.refs_0_.newer, f32[8,64,128]{2,1,0:T(8,128)S(1)} %get-tuple-element.74.refs_1_), custom_call_target="tpu_custom_call" | custom-call | flops 10000000 | bytes 2000000 | tf_op jit(solution)/shard_map/pallas_call | solution.py:25
  21.9 0.6 collective-permute-done.8.rest_3_
  22.5 2.7 %collective-permute-done.6.rest_1_ = f32[2,4,64,128]{3,2,1,0:T(8,128)S(1)} collective-permute-done((f32[2,4,64,128]{3,2,1,0:T(8,128)S(1)}, f32[2,4,64,128]{3,2,1,0:T(8,128)S(1)}, u32[]{:S(2)}, u32[]{:S(2)}) %collective-permute-start.6) | collective-permute-done | bytes 262176 | tf_op jit(solution)/shard_map/ppermute | solution.py:398
  25.2 0.7 shard_map.124
  26.2 0.7 collective-permute-start.9
  26.8 1.0 collective-permute-start.11
  27.9 0.9 shard_map.126.inj0
  30.1 1.2 shard_map.125
  31.3 2.0 %collective-permute-done.9.outer = f32[2,4,64,128]{3,2,1,0:T(8,128)S(1)} collective-permute-done((f32[2,4,64,128]{3,2,1,0:T(8,128)S(1)}, f32[2,4,64,128]{3,2,1,0:T(8,128)S(1)}, u32[]{:S(2)}, u32[]{:S(2)}) %collective-permute-start.9) | collective-permute-done | bytes 262176 | tf_op jit(solution)/shard_map/ppermute | solution.py:398
  33.8 22.0 %all_to_all.20 = f32[16,4,8,128]{3,2,1,0:T(8,128)S(1)} all-to-all(f32[16,4,8,128]{3,2,1,0:T(8,128)S(1)} %bitcast.14), channel_id=1, replica_groups=mesh['shot'=16,'gx'=8,'gy'=2] {'shot'}, dimensions={0} | all-to-all | bytes 524288 | tf_op jit(solution)/shard_map/all_to_all | solution.py:440
  55.8 15.4 %all_to_all.21 = f32[16,4,8,128]{3,2,1,0:T(8,128)S(1)} all-to-all(f32[16,4,8,128]{3,2,1,0:T(8,128)S(1)} %bitcast.15), channel_id=1, replica_groups=mesh['shot'=16,'gx'=8,'gy'=2] {'shot'}, dimensions={0} | all-to-all | bytes 524288 | tf_op jit(solution)/shard_map/all_to_all | solution.py:444
  72.0 0.8 shard_map.131.rest_0_.rest_2_
  72.8 0.7 shard_map.130.part
  73.5 1.9 %collective-permute-done.14.strip = f32[1,16,128]{2,1,0:T(8,128)S(1)} collective-permute-done((f32[1,16,128]{2,1,0:T(8,128)S(1)}, f32[1,16,128]{2,1,0:T(8,128)S(1)}, u32[]{:S(2)}, u32[]{:S(2)}) %collective-permute-start.14) | collective-permute-done | bytes 8224 | tf_op jit(solution)/shard_map/ppermute | solution.py:400
  75.4 1.8 %collective-permute-done.12.outer = f32[1,4,64,128]{3,2,1,0:T(8,128)S(1)} collective-permute-done((f32[1,4,64,128]{3,2,1,0:T(8,128)S(1)}, f32[1,4,64,128]{3,2,1,0:T(8,128)S(1)}, u32[]{:S(2)}, u32[]{:S(2)}) %collective-permute-start.12) | collective-permute-done | bytes 131104 | tf_op jit(solution)/shard_map/ppermute | solution.py:398
  78.3 0.8 shard_map.134.rest_0_.rest_3_
  79.1 0.6 shard_map.133.part
  79.7 1.9 %collective-permute-done.17.strip = f32[1,16,128]{2,1,0:T(8,128)S(1)} collective-permute-done((f32[1,16,128]{2,1,0:T(8,128)S(1)}, f32[1,16,128]{2,1,0:T(8,128)S(1)}, u32[]{:S(2)}, u32[]{:S(2)}) %collective-permute-start.17) | collective-permute-done | bytes 8224 | tf_op jit(solution)/shard_map/ppermute | solution.py:400
  81.6 1.8 %collective-permute-done.15.outer = f32[1,4,64,128]{3,2,1,0:T(8,128)S(1)} collective-permute-done((f32[1,4,64,128]{3,2,1,0:T(8,128)S(1)}, f32[1,4,64,128]{3,2,1,0:T(8,128)S(1)}, u32[]{:S(2)}, u32[]{:S(2)}) %collective-permute-start.15) | collective-permute-done | bytes 131104 | tf_op jit(solution)/shard_map/ppermute | solution.py:398
  84.6 0.8 shard_map.137.rest_4_
  85.3 0.6 shard_map.136.part
  86.0 2.0 %collective-permute-done.20.strip = f32[1,16,128]{2,1,0:T(8,128)S(1)} collective-permute-done((f32[1,16,128]{2,1,0:T(8,128)S(1)}, f32[1,16,128]{2,1,0:T(8,128)S(1)}, u32[]{:S(2)}, u32[]{:S(2)}) %collective-permute-start.20) | collective-permute-done | bytes 8224 | tf_op jit(solution)/shard_map/ppermute | solution.py:400
  88.0 1.5 %collective-permute-done.18.outer = f32[1,4,64,128]{3,2,1,0:T(8,128)S(1)} collective-permute-done((f32[1,4,64,128]{3,2,1,0:T(8,128)S(1)}, f32[1,4,64,128]{3,2,1,0:T(8,128)S(1)}, u32[]{:S(2)}, u32[]{:S(2)}) %collective-permute-start.18) | collective-permute-done | bytes 131104 | tf_op jit(solution)/shard_map/ppermute | solution.py:398
  89.5 1.1 shard_map.138.mine
  90.7 1.2 %collective-permute-done.21.theirs = f32[72,128]{1,0:T(8,128)S(1)} collective-permute-done((f32[72,128]{1,0:T(8,128)S(1)}, f32[72,128]{1,0:T(8,128)S(1)}, u32[]{:S(2)}, u32[]{:S(2)}) %collective-permute-start.21) | collective-permute-done | bytes 36896 | tf_op jit(solution)/shard_map/ppermute | solution.py:463
  92.0 9.3 %all_to_all.22.arrived = f32[8,40,128]{2,1,0:T(8,128)S(1)} all-to-all(f32[8,40,128]{2,1,0:T(8,128)S(1)} %shard_map.139), channel_id=1, replica_groups={{0,1,4,5,8,9,12,13},{2,3,6,7,10,11,14,15},{16,17,20,21,24,25,28,29},{18..., dimensions={0} | all-to-all | bytes 327680 | tf_op jit(solution)/shard_map/all_to_all | solution.py:466
  101.3 0.6 shard_map.140
  101.9 4.9 %all-to-all-start.3 = ((f32[16,8,128]{2,1,0:T(8,128)}), f32[16,8,128]{2,1,0:T(8,128)S(1)}, u32[]{:S(2)}, u32[]{:S(2)}) async-start(f32[16,8,128]{2,1,0:T(8,128)} %shard_map.140), calls=%async_computation.3 | async-start | bytes 131072 | tf_op jit(solution)/shard_map/all_to_all | solution.py:470
  106.9 1.2 %collective-permute-done.22.other = f32[32,128]{1,0:T(8,128)S(1)} collective-permute-done((f32[32,128]{1,0:T(8,128)S(1)}, f32[32,128]{1,0:T(8,128)S(1)}, u32[]{:S(2)}, u32[]{:S(2)}) %collective-permute-start.22) | collective-permute-done | bytes 16416 | tf_op jit(solution)/shard_map/ppermute | solution.py:469
  108.1 7.8 %all-to-all-done.3.stats = f32[16,8,128]{2,1,0:T(8,128)S(1)} async-done(((f32[16,8,128]{2,1,0:T(8,128)}), f32[16,8,128]{2,1,0:T(8,128)S(1)}, u32[]{:S(2)}, u32[]{:S(2)}) %all-to-all-start.3) | async-done | bytes 65568 | tf_op jit(solution)/shard_map/all_to_all | solution.py:470
  115.9 0.8 shard_map.142
  (41 shorter events, 5.4 us)
Async XLA Ops:
  0.6 1.0 copy-start
  1.8 8.0 %collective-permute-start = (f32[1,4,64,128]{3,2,1,0:T(8,128)S(1)}, f32[1,4,64,128]{3,2,1,0:T(8,128)S(1)}, u32[]{:S(2)}, u32[]{:S(2)}) collective-permute-start(f32[1,4,64,128]{3,2,1,0:T(8,128)S(1)} %get-tuple-element.61), channel_id=1, source_target_pairs={{2,4},{6,8},{10,12},{14,0},{4,2},{8,6},{12,10},{0,14},{3,5},{7,9},... | collective-permute-start | bytes 393224 | tf_op jit(solution)/shard_map/ppermute | solution.py:398
  4.3 5.5 %collective-permute-start.1 = (f32[1,4,64,128]{3,2,1,0:T(8,128)S(1)}, f32[1,4,64,128]{3,2,1,0:T(8,128)S(1)}, u32[]{:S(2)}, u32[]{:S(2)}) collective-permute-start(f32[1,4,64,128]{3,2,1,0:T(8,128)S(1)} %get-tuple-element.62), channel_id=1, source_target_pairs={{0,2},{2,0},{4,6},{6,4},{8,10},{10,8},{12,14},{14,12},{1,3},{3,1},... | collective-permute-start | bytes 393224 | tf_op jit(solution)/shard_map/ppermute | solution.py:399
  4.3 5.5 %collective-permute-start.2 = (f32[1,16,128]{2,1,0:T(8,128)S(1)}, f32[1,16,128]{2,1,0:T(8,128)S(1)}, u32[]{:S(2)}, u32[]{:S(2)}) collective-permute-start(f32[1,16,128]{2,1,0:T(8,128)S(1)} %get-tuple-element.63), channel_id=1, source_target_pairs={{0,1},{1,0},{2,3},{3,2},{4,5},{5,4},{6,7},{7,6},{8,9},{9,8},{10,11... | collective-permute-start | bytes 24584 | tf_op jit(solution)/shard_map/ppermute | solution.py:400
  10.3 7.1 %collective-permute-start.3 = (f32[2,4,64,128]{3,2,1,0:T(8,128)S(1)}, f32[2,4,64,128]{3,2,1,0:T(8,128)S(1)}, u32[]{:S(2)}, u32[]{:S(2)}) collective-permute-start(f32[2,4,64,128]{3,2,1,0:T(8,128)S(1)} %get-tuple-element.70), channel_id=1, source_target_pairs={{2,4},{6,8},{10,12},{14,0},{4,2},{8,6},{12,10},{0,14},{3,5},{7,9},... | collective-permute-start | bytes 786440 | tf_op jit(solution)/shard_map/ppermute | solution.py:398
  10.9 6.4 %collective-permute-start.4 = (f32[2,4,64,128]{3,2,1,0:T(8,128)S(1)}, f32[2,4,64,128]{3,2,1,0:T(8,128)S(1)}, u32[]{:S(2)}, u32[]{:S(2)}) collective-permute-start(f32[2,4,64,128]{3,2,1,0:T(8,128)S(1)} %get-tuple-element.71), channel_id=1, source_target_pairs={{0,2},{2,0},{4,6},{6,4},{8,10},{10,8},{12,14},{14,12},{1,3},{3,1},... | collective-permute-start | bytes 786440 | tf_op jit(solution)/shard_map/ppermute | solution.py:399
  11.3 3.7 %collective-permute-start.5 = (f32[2,16,128]{2,1,0:T(8,128)S(1)}, f32[2,16,128]{2,1,0:T(8,128)S(1)}, u32[]{:S(2)}, u32[]{:S(2)}) collective-permute-start(f32[2,16,128]{2,1,0:T(8,128)S(1)} %get-tuple-element.72), channel_id=1, source_target_pairs={{0,1},{1,0},{2,3},{3,2},{4,5},{5,4},{6,7},{7,6},{8,9},{9,8},{10,11... | collective-permute-start | bytes 49160 | tf_op jit(solution)/shard_map/ppermute | solution.py:400
  18.1 7.1 %collective-permute-start.6 = (f32[2,4,64,128]{3,2,1,0:T(8,128)S(1)}, f32[2,4,64,128]{3,2,1,0:T(8,128)S(1)}, u32[]{:S(2)}, u32[]{:S(2)}) collective-permute-start(f32[2,4,64,128]{3,2,1,0:T(8,128)S(1)} %get-tuple-element.78), channel_id=1, source_target_pairs={{2,4},{6,8},{10,12},{14,0},{4,2},{8,6},{12,10},{0,14},{3,5},{7,9},... | collective-permute-start | bytes 786440 | tf_op jit(solution)/shard_map/ppermute | solution.py:398
  18.8 6.4 %collective-permute-start.7 = (f32[2,4,64,128]{3,2,1,0:T(8,128)S(1)}, f32[2,4,64,128]{3,2,1,0:T(8,128)S(1)}, u32[]{:S(2)}, u32[]{:S(2)}) collective-permute-start(f32[2,4,64,128]{3,2,1,0:T(8,128)S(1)} %get-tuple-element.79), channel_id=1, source_target_pairs={{0,2},{2,0},{4,6},{6,4},{8,10},{10,8},{12,14},{14,12},{1,3},{3,1},... | collective-permute-start | bytes 786440 | tf_op jit(solution)/shard_map/ppermute | solution.py:399
  18.8 3.7 %collective-permute-start.8 = (f32[2,16,128]{2,1,0:T(8,128)S(1)}, f32[2,16,128]{2,1,0:T(8,128)S(1)}, u32[]{:S(2)}, u32[]{:S(2)}) collective-permute-start(f32[2,16,128]{2,1,0:T(8,128)S(1)} %get-tuple-element.80), channel_id=1, source_target_pairs={{0,1},{1,0},{2,3},{3,2},{4,5},{5,4},{6,7},{7,6},{8,9},{9,8},{10,11... | collective-permute-start | bytes 49160 | tf_op jit(solution)/shard_map/ppermute | solution.py:400
  25.9 5.4 %collective-permute-start.10 = (f32[2,4,64,128]{3,2,1,0:T(8,128)S(1)}, f32[2,4,64,128]{3,2,1,0:T(8,128)S(1)}, u32[]{:S(2)}, u32[]{:S(2)}) collective-permute-start(f32[2,4,64,128]{3,2,1,0:T(8,128)S(1)} %get-tuple-element.90), channel_id=1, source_target_pairs={{0,2},{2,0},{4,6},{6,4},{8,10},{10,8},{12,14},{14,12},{1,3},{3,1},... | collective-permute-start | bytes 786440 | tf_op jit(solution)/shard_map/ppermute | solution.py:399
  26.2 7.1 %collective-permute-start.9 = (f32[2,4,64,128]{3,2,1,0:T(8,128)S(1)}, f32[2,4,64,128]{3,2,1,0:T(8,128)S(1)}, u32[]{:S(2)}, u32[]{:S(2)}) collective-permute-start(f32[2,4,64,128]{3,2,1,0:T(8,128)S(1)} %get-tuple-element.89), channel_id=1, source_target_pairs={{2,4},{6,8},{10,12},{14,0},{4,2},{8,6},{12,10},{0,14},{3,5},{7,9},... | collective-permute-start | bytes 786440 | tf_op jit(solution)/shard_map/ppermute | solution.py:398
  26.8 4.4 %collective-permute-start.11 = (f32[2,16,128]{2,1,0:T(8,128)S(1)}, f32[2,16,128]{2,1,0:T(8,128)S(1)}, u32[]{:S(2)}, u32[]{:S(2)}) collective-permute-start(f32[2,16,128]{2,1,0:T(8,128)S(1)} %get-tuple-element.91), channel_id=1, source_target_pairs={{0,1},{1,0},{2,3},{3,2},{4,5},{5,4},{6,7},{7,6},{8,9},{9,8},{10,11... | collective-permute-start | bytes 49160 | tf_op jit(solution)/shard_map/ppermute | solution.py:400
  30.1 25.7 %copy-start.2 = (f32[4,8,128]{2,1,0:T(8,128)S(1)}, f32[4,8,128]{2,1,0:T(8,128)}, u32[]{:S(2)}) copy-start(f32[4,8,128]{2,1,0:T(8,128)} %param.13) | copy-start | bytes 49156
  71.5 5.7 %collective-permute-start.12 = (f32[1,4,64,128]{3,2,1,0:T(8,128)S(1)}, f32[1,4,64,128]{3,2,1,0:T(8,128)S(1)}, u32[]{:S(2)}, u32[]{:S(2)}) collective-permute-start(f32[1,4,64,128]{3,2,1,0:T(8,128)S(1)} %get-tuple-element.96), channel_id=1, source_target_pairs={{2,4},{6,8},{10,12},{14,0},{4,2},{8,6},{12,10},{0,14},{3,5},{7,9},... | collective-permute-start | bytes 393224 | tf_op jit(solution)/shard_map/ppermute | solution.py:398
  71.6 5.5 %collective-permute-start.13 = (f32[1,4,64,128]{3,2,1,0:T(8,128)S(1)}, f32[1,4,64,128]{3,2,1,0:T(8,128)S(1)}, u32[]{:S(2)}, u32[]{:S(2)}) collective-permute-start(f32[1,4,64,128]{3,2,1,0:T(8,128)S(1)} %get-tuple-element.97), channel_id=1, source_target_pairs={{0,2},{2,0},{4,6},{6,4},{8,10},{10,8},{12,14},{14,12},{1,3},{3,1},... | collective-permute-start | bytes 393224 | tf_op jit(solution)/shard_map/ppermute | solution.py:399
  71.7 3.7 %collective-permute-start.14 = (f32[1,16,128]{2,1,0:T(8,128)S(1)}, f32[1,16,128]{2,1,0:T(8,128)S(1)}, u32[]{:S(2)}, u32[]{:S(2)}) collective-permute-start(f32[1,16,128]{2,1,0:T(8,128)S(1)} %get-tuple-element.98), channel_id=1, source_target_pairs={{0,1},{1,0},{2,3},{3,2},{4,5},{5,4},{6,7},{7,6},{8,9},{9,8},{10,11... | collective-permute-start | bytes 24584 | tf_op jit(solution)/shard_map/ppermute | solution.py:400
  77.6 5.7 %collective-permute-start.15 = (f32[1,4,64,128]{3,2,1,0:T(8,128)S(1)}, f32[1,4,64,128]{3,2,1,0:T(8,128)S(1)}, u32[]{:S(2)}, u32[]{:S(2)}) collective-permute-start(f32[1,4,64,128]{3,2,1,0:T(8,128)S(1)} %get-tuple-element.100), channel_id=1, source_target_pairs={{2,4},{6,8},{10,12},{14,0},{4,2},{8,6},{12,10},{0,14},{3,5},{7,9},... | collective-permute-start | bytes 393224 | tf_op jit(solution)/shard_map/ppermute | solution.py:398
  77.9 5.4 %collective-permute-start.16 = (f32[1,4,64,128]{3,2,1,0:T(8,128)S(1)}, f32[1,4,64,128]{3,2,1,0:T(8,128)S(1)}, u32[]{:S(2)}, u32[]{:S(2)}) collective-permute-start(f32[1,4,64,128]{3,2,1,0:T(8,128)S(1)} %get-tuple-element.101), channel_id=1, source_target_pairs={{0,2},{2,0},{4,6},{6,4},{8,10},{10,8},{12,14},{14,12},{1,3},{3,1},... | collective-permute-start | bytes 393224 | tf_op jit(solution)/shard_map/ppermute | solution.py:399
  77.9 3.7 %collective-permute-start.17 = (f32[1,16,128]{2,1,0:T(8,128)S(1)}, f32[1,16,128]{2,1,0:T(8,128)S(1)}, u32[]{:S(2)}, u32[]{:S(2)}) collective-permute-start(f32[1,16,128]{2,1,0:T(8,128)S(1)} %get-tuple-element.102), channel_id=1, source_target_pairs={{0,1},{1,0},{2,3},{3,2},{4,5},{5,4},{6,7},{7,6},{8,9},{9,8},{10,11... | collective-permute-start | bytes 24584 | tf_op jit(solution)/shard_map/ppermute | solution.py:400
  83.8 5.7 %collective-permute-start.18 = (f32[1,4,64,128]{3,2,1,0:T(8,128)S(1)}, f32[1,4,64,128]{3,2,1,0:T(8,128)S(1)}, u32[]{:S(2)}, u32[]{:S(2)}) collective-permute-start(f32[1,4,64,128]{3,2,1,0:T(8,128)S(1)} %get-tuple-element.105), channel_id=1, source_target_pairs={{2,4},{6,8},{10,12},{14,0},{4,2},{8,6},{12,10},{0,14},{3,5},{7,9},... | collective-permute-start | bytes 393224 | tf_op jit(solution)/shard_map/ppermute | solution.py:398
  84.1 5.4 %collective-permute-start.19 = (f32[1,4,64,128]{3,2,1,0:T(8,128)S(1)}, f32[1,4,64,128]{3,2,1,0:T(8,128)S(1)}, u32[]{:S(2)}, u32[]{:S(2)}) collective-permute-start(f32[1,4,64,128]{3,2,1,0:T(8,128)S(1)} %get-tuple-element.106), channel_id=1, source_target_pairs={{0,2},{2,0},{4,6},{6,4},{8,10},{10,8},{12,14},{14,12},{1,3},{3,1},... | collective-permute-start | bytes 393224 | tf_op jit(solution)/shard_map/ppermute | solution.py:399
  84.1 3.9 %collective-permute-start.20 = (f32[1,16,128]{2,1,0:T(8,128)S(1)}, f32[1,16,128]{2,1,0:T(8,128)S(1)}, u32[]{:S(2)}, u32[]{:S(2)}) collective-permute-start(f32[1,16,128]{2,1,0:T(8,128)S(1)} %get-tuple-element.107), channel_id=1, source_target_pairs={{0,1},{1,0},{2,3},{3,2},{4,5},{5,4},{6,7},{7,6},{8,9},{9,8},{10,11... | collective-permute-start | bytes 24584 | tf_op jit(solution)/shard_map/ppermute | solution.py:400
  89.5 26.4 %copy-start.1 = (f32[1,4,2048]{2,1,0:T(4,128)S(1)}, f32[1,4,2048]{2,1,0:T(4,128)}, u32[]{:S(2)}) copy-start(f32[1,4,2048]{2,1,0:T(4,128)} %param.14) | copy-start | bytes 98308
  90.6 1.3 %collective-permute-start.21 = (f32[72,128]{1,0:T(8,128)S(1)}, f32[72,128]{1,0:T(8,128)S(1)}, u32[]{:S(2)}, u32[]{:S(2)}) collective-permute-start(f32[72,128]{1,0:T(8,128)S(1)} %shard_map.138.mine), channel_id=1, source_target_pairs={{0,2},{2,0},{4,6},{6,4},{8,10},{10,8},{12,14},{14,12},{1,3},{3,1},... | collective-permute-start | bytes 110600 | tf_op jit(solution)/shard_map/ppermute | solution.py:463
  101.9 14.0 %all-to-all-start.3 = ((f32[16,8,128]{2,1,0:T(8,128)}), f32[16,8,128]{2,1,0:T(8,128)S(1)}, u32[]{:S(2)}, u32[]{:S(2)}) async-start(f32[16,8,128]{2,1,0:T(8,128)} %shard_map.140), calls=%async_computation.3 | async-start | bytes 131072 | tf_op jit(solution)/shard_map/all_to_all | solution.py:470
  106.8 1.3 %collective-permute-start.22 = (f32[32,128]{1,0:T(8,128)S(1)}, f32[32,128]{1,0:T(8,128)S(1)}, u32[]{:S(2)}, u32[]{:S(2)}) collective-permute-start(f32[32,128]{1,0:T(8,128)S(1)} %shard_map.141.half), channel_id=1, source_target_pairs={{0,2},{2,0},{4,6},{6,4},{8,10},{10,8},{12,14},{14,12},{1,3},{3,1},... | collective-permute-start | bytes 49160 | tf_op jit(solution)/shard_map/ppermute | solution.py:469

commit v12 on v9

--- a/solution.py
+++ b/solution.py
@@ -348,21 +348,26 @@
 
 
 def pair_kernel(mine, theirs, copies):
-    total = mine[...] + theirs[...]
+    own = pl.ds(pl.multiple_of(32 * position()[0], 8), 32)
+    samples = mine[own, :] + theirs[own, :]
+    sums = mine[64:72] + theirs[64:72]
     for i in range(8):
-        copies[i] = total
-
-
-def collect_kernel(arrived, predicted, copies):
+        copies[i, 0:32] = samples
+        copies[i, 32:40] = sums
+
+
+def collect_kernel(arrived, half, copies):
     total = arrived[0]
     for i in range(1, 8):
         total = total + arrived[i]
-    predicted[...] = total[0:64]
+    half[...] = total[0:32]
     for i in range(16):
-        copies[i] = total[64:72]
-
-
-def finish_kernel(stats, predicted, scaled, traces, image, residual):
+        copies[i] = total[32:40]
+
+
+def finish_kernel(stats, half, other, scaled, traces, image, residual):
+    core = position()[0]
+    predicted = (jnp.where(core == 0, half[...], other[...]), jnp.where(core == 0, other[...], half[...]))
     total = stats[0]
     for i in range(1, 16):
         total = total + stats[i]
@@ -373,7 +378,8 @@
     for n in range(STEPS):
         for j in range(16):
             at = pl.ds(BY * j, BY)
-            row = predicted[16 * n + j : 16 * n + j + 1, :]
+            number = 16 * (n % 2) + j
+            row = predicted[n // 2][number : number + 1]
             residual[n : n + 1, at] = traces[n : n + 1, at] - step * row
 
 
@@ -446,14 +452,16 @@
         make_born(3, True), [((72, BY), F32)],
         [HALO, pltpu.VMEM((BX, NZ, BY), F32), pltpu.VMEM((512, 2 * BY), BF16)],
     )(*one(d3), d3, d2, source, acc3, vel, *e, pick_cell, pick_y, s1, s2, s3, dot)
-    theirs = lax.ppermute(block, "gx", [(i, i ^ 1) for i in range(8)])
-    payload, = call(pair_kernel, [((8, 72, BY), F32)])(block, theirs)
+    swap = [(i, i ^ 1) for i in range(8)]
+    theirs = lax.ppermute(block, "gx", swap)
+    payload, = call(pair_kernel, [((8, 40, BY), F32)])(block, theirs)
     same_core = [[2 * (2 * c + k) + g for c in range(4) for g in range(2)] for k in range(2)]
     arrived = lax.all_to_all(payload, ("gx", "gy"), 0, 0, axis_index_groups=same_core, tiled=True)
-    predicted, stats = call(collect_kernel, [((64, BY), F32), ((16, 8, BY), F32)])(arrived)
+    half, stats = call(collect_kernel, [((32, BY), F32), ((16, 8, BY), F32)])(arrived)
+    other = lax.ppermute(half, "gx", swap)
     stats = lax.all_to_all(stats, "shot", 0, 0, tiled=True)
     image, residual = call(finish_kernel, [((32, BY), F32), ((4, NREC), F32)])(
-        stats, predicted, scaled, shot)
+        stats, half, other, scaled, shot)
     return image.reshape(4, BX, BY), residual[None]
 
 

time: 118 us -> 117 us (level)
  blocking collectives: 63.6 us -> 46.9 us
  waiting for transfers between devices: 10.3 us -> 19.4 us
  starting transfers between devices: 22 us -> 28.2 us
    all_to_all x1 -> x0, blocking collectives: 15.2 us -> none  [on_device(): stats = lax.all_to_all(stats, 'shot', 0, 0, tiled=True)]
    all_to_all x0 -> x1, waiting for transfers between devices: none -> 7.93 us  [on_device(): stats = lax.all_to_all(stats, 'shot', 0, 0, tiled=True)]
    all_to_all x0 -> x1, starting transfers between devices: none -> 6.27 us  [on_device(): stats = lax.all_to_all(stats, 'shot', 0, 0, tiled=True)]
    all_to_all x1, blocking collectives: 11.1 us -> 9.64 us  [on_device(): lax.all_to_all(payload, ('gx', 'gy'), 0, 0, axis_index_groups=same_core,...]
    ppermute x1 -> x2, waiting for transfers between devices: 1.2 us -> 2.38 us  [the longest x1 1.2 us: on_device(): theirs = lax.ppermute(block, 'gx', swap)]
  transfers between devices with their start and end apart: 22 -> 24, of which waited for: 13 -> 15; matrix products, arithmetic and copies ran while one was open for 0% -> 0% of each run, Pallas kernels for 11% -> 11%
where the time goes in v12:
time: 117 us
  blocking collectives  46.9 us (40%)
  starting transfers between devices  28.2 us (24%)
  waiting for transfers between devices  19.4 us (17%)
  Pallas kernels  18.8 us (16%)
  between operations  2.21 us (2%)
  other arithmetic  1.22 us (1%)
    all_to_all x1, blocking collectives, on_device(): lax.all_to_all(grad.reshape(16, 4, BX, BY), 'shot', 0, 0, tiled=True)  22.1 us
    pallas_call x28, Pallas kernels, run(): pl.pallas_call(kernel, out_shape=[jax.ShapeDtypeStruct(s, d) for s, d in...  18.8 us
    all_to_all x1, blocking collectives, on_device(): lax.all_to_all(copies.reshape(16, 4, BX, BY), 'shot', 0, 0, tiled=True)  15.1 us
    ppermute x7, starting transfers between devices, exchange(): lax.ppermute(outer, 'gx', across)  14 us
    all_to_all x1, blocking collectives, on_device(): lax.all_to_all(payload, ('gx', 'gy'), 0, 0, axis_index_groups=same_core,...  9.64 us
    all_to_all x1, waiting for transfers between devices, on_device(): stats = lax.all_to_all(stats, 'shot', 0, 0, tiled=True)  7.93 us
    ppermute x7, starting transfers between devices, exchange(): lax.ppermute(strip, 'gy', [(0, 1), (1, 0)])  7.74 us
    all_to_all x1, starting transfers between devices, on_device(): stats = lax.all_to_all(stats, 'shot', 0, 0, tiled=True)  6.27 us
  transfers between devices with their start and end apart: 24, of which 15 were waited for; matrix products, arithmetic and copies ran while one was open for 0% of the time, Pallas kernels for 11%

profile of v12, /device:TPU:32, one launch (start us, length us, event | category | flops | bytes accessed | tf_op | source)
XLA Modules:
  0.0 116.8 jit_solution(1389531259395448555)
XLA Ops:
  0.7 1.2 %pad_maximum_fusion.fields = f32[1536,128]{1,0:T(8,128)S(1)} fusion(f32[512,128]{1,0:T(8,128)} %bitcast.16, f32[512,128]{1,0:T(8,128)} %bitcast.17, f32[512,128]{1,0:T(8,128)} %bitcast.18), kind=kLoop, calls=%fused_computation | loop fusion | flops 393216 | bytes 1572864 | tf_op jit(solution)/shard_map/concatenate | solution.py:401
  2.1 2.5 %collective-permute-start = (f32[1,4,64,128]{3,2,1,0:T(8,128)S(1)}, f32[1,4,64,128]{3,2,1,0:T(8,128)S(1)}, u32[]{:S(2)}, u32[]{:S(2)}) collective-permute-start(f32[1,4,64,128]{3,2,1,0:T(8,128)S(1)} %get-tuple-element.63), channel_id=1, source_target_pairs={{2,4},{6,8},{10,12},{14,0},{4,2},{8,6},{12,10},{0,14},{3,5},{7,9},... | collective-permute-start | bytes 393224 | tf_op jit(solution)/shard_map/ppermute | solution.py:391
  4.6 1.5 %collective-permute-start.2 = (f32[1,16,128]{2,1,0:T(8,128)S(1)}, f32[1,16,128]{2,1,0:T(8,128)S(1)}, u32[]{:S(2)}, u32[]{:S(2)}) collective-permute-start(f32[1,16,128]{2,1,0:T(8,128)S(1)} %get-tuple-element.65), channel_id=1, source_target_pairs={{0,1},{1,0},{2,3},{3,2},{4,5},{5,4},{6,7},{7,6},{8,9},{9,8},{10,11... | collective-permute-start | bytes 24584 | tf_op jit(solution)/shard_map/ppermute | solution.py:393
  6.2 1.3 %shard_map.115 = (f32[8,64,128]{2,1,0:T(8,128)S(1)}, bf16[512,2048]{1,0:T(8,128)(2,1)S(1)}, bf16[128,2048]{1,0:T(8,128)(2,1)S(1)}) custom-call(f32[5,2048]{1,0:T(8,128)S(1)} %convert_add_fusion.shot.traces), custom_call_target="tpu_custom_call" | custom-call | flops 10000000 | bytes 2000000 | tf_op jit(solution)/shard_map/pallas_call | solution.py:25
  7.5 0.6 shard_map.114.part
  8.8 2.0 %collective-permute-start.3 = (f32[2,4,64,128]{3,2,1,0:T(8,128)S(1)}, f32[2,4,64,128]{3,2,1,0:T(8,128)S(1)}, u32[]{:S(2)}, u32[]{:S(2)}) collective-permute-start(f32[2,4,64,128]{3,2,1,0:T(8,128)S(1)} %get-tuple-element.72), channel_id=1, source_target_pairs={{2,4},{6,8},{10,12},{14,0},{4,2},{8,6},{12,10},{0,14},{3,5},{7,9},... | collective-permute-start | bytes 786440 | tf_op jit(solution)/shard_map/ppermute | solution.py:391
  10.8 1.5 %collective-permute-start.5 = (f32[2,16,128]{2,1,0:T(8,128)S(1)}, f32[2,16,128]{2,1,0:T(8,128)S(1)}, u32[]{:S(2)}, u32[]{:S(2)}) collective-permute-start(f32[2,16,128]{2,1,0:T(8,128)S(1)} %get-tuple-element.74), channel_id=1, source_target_pairs={{0,1},{1,0},{2,3},{3,2},{4,5},{5,4},{6,7},{7,6},{8,9},{9,8},{10,11... | collective-permute-start | bytes 49160 | tf_op jit(solution)/shard_map/ppermute | solution.py:393
  12.3 0.9 shard_map.118.inj
  13.2 1.2 %shard_map.117 = (f32[8,64,128]{2,1,0:T(8,128)S(1)}, f32[8,64,128]{2,1,0:T(8,128)S(1)}) custom-call(f32[8,64,128]{2,1,0:T(8,128)S(1)} %get-tuple-element.66.refs_0_.newer.older, f32[8,64,128]{2,1,0:T(8,128)S(1)} %get-tuple-element.67.refs_1_), custom_call_target="tpu_custom_call" | custom-call | flops 10000000 | bytes 2000000 | tf_op jit(solution)/shard_map/pallas_call | solution.py:25
  14.5 1.3 %collective-permute-done.3.rest_0_ = f32[2,4,64,128]{3,2,1,0:T(8,128)S(1)} collective-permute-done((f32[2,4,64,128]{3,2,1,0:T(8,128)S(1)}, f32[2,4,64,128]{3,2,1,0:T(8,128)S(1)}, u32[]{:S(2)}, u32[]{:S(2)}) %collective-permute-start.3) | collective-permute-done | bytes 262176 | tf_op jit(solution)/shard_map/ppermute | solution.py:391
  15.9 0.7 shard_map.119
  16.6 2.0 %collective-permute-start.6 = (f32[2,4,64,128]{3,2,1,0:T(8,128)S(1)}, f32[2,4,64,128]{3,2,1,0:T(8,128)S(1)}, u32[]{:S(2)}, u32[]{:S(2)}) collective-permute-start(f32[2,4,64,128]{3,2,1,0:T(8,128)S(1)} %get-tuple-element.80), channel_id=1, source_target_pairs={{2,4},{6,8},{10,12},{14,0},{4,2},{8,6},{12,10},{0,14},{3,5},{7,9},... | collective-permute-start | bytes 786440 | tf_op jit(solution)/shard_map/ppermute | solution.py:391
  18.6 1.5 %collective-permute-start.8 = (f32[2,16,128]{2,1,0:T(8,128)S(1)}, f32[2,16,128]{2,1,0:T(8,128)S(1)}, u32[]{:S(2)}, u32[]{:S(2)}) collective-permute-start(f32[2,16,128]{2,1,0:T(8,128)S(1)} %get-tuple-element.82), channel_id=1, source_target_pairs={{0,1},{1,0},{2,3},{3,2},{4,5},{5,4},{6,7},{7,6},{8,9},{9,8},{10,11... | collective-permute-start | bytes 49160 | tf_op jit(solution)/shard_map/ppermute | solution.py:393
  20.1 0.9 shard_map.122.inj
  21.0 1.2 %shard_map.121 = (f32[8,64,128]{2,1,0:T(8,128)S(1)}, f32[8,64,128]{2,1,0:T(8,128)S(1)}) custom-call(f32[8,64,128]{2,1,0:T(8,128)S(1)} %get-tuple-element.75.after.refs_0_.newer, f32[8,64,128]{2,1,0:T(8,128)S(1)} %get-tuple-element.76.refs_1_), custom_call_target="tpu_custom_call" | custom-call | flops 10000000 | bytes 2000000 | tf_op jit(solution)/shard_map/pallas_call | solution.py:25
  22.3 1.3 %collective-permute-done.6.rest_1_ = f32[2,4,64,128]{3,2,1,0:T(8,128)S(1)} collective-permute-done((f32[2,4,64,128]{3,2,1,0:T(8,128)S(1)}, f32[2,4,64,128]{3,2,1,0:T(8,128)S(1)}, u32[]{:S(2)}, u32[]{:S(2)}) %collective-permute-start.6) | collective-permute-done | bytes 262176 | tf_op jit(solution)/shard_map/ppermute | solution.py:391
  23.7 0.7 shard_map.123
  24.5 2.2 %collective-permute-start.9 = (f32[2,4,64,128]{3,2,1,0:T(8,128)S(1)}, f32[2,4,64,128]{3,2,1,0:T(8,128)S(1)}, u32[]{:S(2)}, u32[]{:S(2)}) collective-permute-start(f32[2,4,64,128]{3,2,1,0:T(8,128)S(1)} %get-tuple-element.91), channel_id=1, source_target_pairs={{2,4},{6,8},{10,12},{14,0},{4,2},{8,6},{12,10},{0,14},{3,5},{7,9},... | collective-permute-start | bytes 786440 | tf_op jit(solution)/shard_map/ppermute | solution.py:391
  26.7 1.5 %collective-permute-start.11 = (f32[2,16,128]{2,1,0:T(8,128)S(1)}, f32[2,16,128]{2,1,0:T(8,128)S(1)}, u32[]{:S(2)}, u32[]{:S(2)}) collective-permute-start(f32[2,16,128]{2,1,0:T(8,128)S(1)} %get-tuple-element.93), channel_id=1, source_target_pairs={{0,1},{1,0},{2,3},{3,2},{4,5},{5,4},{6,7},{7,6},{8,9},{9,8},{10,11... | collective-permute-start | bytes 49160 | tf_op jit(solution)/shard_map/ppermute | solution.py:393
  28.2 0.9 shard_map.125.inj0
  30.4 1.2 shard_map.124
  31.7 0.5 shard_map.126
  32.3 22.1 %all_to_all.20 = f32[16,4,8,128]{3,2,1,0:T(8,128)S(1)} all-to-all(f32[16,4,8,128]{3,2,1,0:T(8,128)S(1)} %bitcast.13), channel_id=1, replica_groups=mesh['shot'=16,'gx'=8,'gy'=2] {'shot'}, dimensions={0} | all-to-all | bytes 524288 | tf_op jit(solution)/shard_map/all_to_all | solution.py:433
  54.5 15.1 %all_to_all.21 = f32[16,4,8,128]{3,2,1,0:T(8,128)S(1)} all-to-all(f32[16,4,8,128]{3,2,1,0:T(8,128)S(1)} %bitcast.14), channel_id=1, replica_groups=mesh['shot'=16,'gx'=8,'gy'=2] {'shot'}, dimensions={0} | all-to-all | bytes 524288 | tf_op jit(solution)/shard_map/all_to_all | solution.py:437
  69.8 1.7 %collective-permute-start.12 = (f32[1,4,64,128]{3,2,1,0:T(8,128)S(1)}, f32[1,4,64,128]{3,2,1,0:T(8,128)S(1)}, u32[]{:S(2)}, u32[]{:S(2)}) collective-permute-start(f32[1,4,64,128]{3,2,1,0:T(8,128)S(1)} %get-tuple-element.98), channel_id=1, source_target_pairs={{2,4},{6,8},{10,12},{14,0},{4,2},{8,6},{12,10},{0,14},{3,5},{7,9},... | collective-permute-start | bytes 393224 | tf_op jit(solution)/shard_map/ppermute | solution.py:391
  71.6 0.6 collective-permute-start.14
  72.1 0.8 shard_map.130.rest_0_.rest_2_
  72.9 0.7 shard_map.129.part
  73.6 1.6 %collective-permute-done.14.strip = f32[1,16,128]{2,1,0:T(8,128)S(1)} collective-permute-done((f32[1,16,128]{2,1,0:T(8,128)S(1)}, f32[1,16,128]{2,1,0:T(8,128)S(1)}, u32[]{:S(2)}, u32[]{:S(2)}) %collective-permute-start.14) | collective-permute-done | bytes 8224 | tf_op jit(solution)/shard_map/ppermute | solution.py:393
  76.0 1.7 %collective-permute-start.15 = (f32[1,4,64,128]{3,2,1,0:T(8,128)S(1)}, f32[1,4,64,128]{3,2,1,0:T(8,128)S(1)}, u32[]{:S(2)}, u32[]{:S(2)}) collective-permute-start(f32[1,4,64,128]{3,2,1,0:T(8,128)S(1)} %get-tuple-element.102), channel_id=1, source_target_pairs={{2,4},{6,8},{10,12},{14,0},{4,2},{8,6},{12,10},{0,14},{3,5},{7,9},... | collective-permute-start | bytes 393224 | tf_op jit(solution)/shard_map/ppermute | solution.py:391
  77.7 0.6 collective-permute-start.17
  78.3 0.8 shard_map.133.rest_0_.rest_3_
  79.1 0.6 shard_map.132.part
  79.7 1.7 %collective-permute-done.17.strip = f32[1,16,128]{2,1,0:T(8,128)S(1)} collective-permute-done((f32[1,16,128]{2,1,0:T(8,128)S(1)}, f32[1,16,128]{2,1,0:T(8,128)S(1)}, u32[]{:S(2)}, u32[]{:S(2)}) %collective-permute-start.17) | collective-permute-done | bytes 8224 | tf_op jit(solution)/shard_map/ppermute | solution.py:393
  81.7 0.5 shard_map.134
  82.2 1.7 %collective-permute-start.18 = (f32[1,4,64,128]{3,2,1,0:T(8,128)S(1)}, f32[1,4,64,128]{3,2,1,0:T(8,128)S(1)}, u32[]{:S(2)}, u32[]{:S(2)}) collective-permute-start(f32[1,4,64,128]{3,2,1,0:T(8,128)S(1)} %get-tuple-element.107), channel_id=1, source_target_pairs={{2,4},{6,8},{10,12},{14,0},{4,2},{8,6},{12,10},{0,14},{3,5},{7,9},... | collective-permute-start | bytes 393224 | tf_op jit(solution)/shard_map/ppermute | solution.py:391
  83.9 0.6 collective-permute-start.20
  84.5 0.8 shard_map.136.rest_4_
  85.3 0.6 shard_map.135.part
  85.9 1.7 %collective-permute-done.20.strip = f32[1,16,128]{2,1,0:T(8,128)S(1)} collective-permute-done((f32[1,16,128]{2,1,0:T(8,128)S(1)}, f32[1,16,128]{2,1,0:T(8,128)S(1)}, u32[]{:S(2)}, u32[]{:S(2)}) %collective-permute-start.20) | collective-permute-done | bytes 8224 | tf_op jit(solution)/shard_map/ppermute | solution.py:393
  87.9 1.1 shard_map.137.mine
  89.1 1.2 %collective-permute-done.21.theirs = f32[72,128]{1,0:T(8,128)S(1)} collective-permute-done((f32[72,128]{1,0:T(8,128)S(1)}, f32[72,128]{1,0:T(8,128)S(1)}, u32[]{:S(2)}, u32[]{:S(2)}) %collective-permute-start.21) | collective-permute-done | bytes 36896 | tf_op jit(solution)/shard_map/ppermute | solution.py:456
  90.3 9.6 %all_to_all.22.arrived = f32[8,40,128]{2,1,0:T(8,128)S(1)} all-to-all(f32[8,40,128]{2,1,0:T(8,128)S(1)} %shard_map.138), channel_id=1, replica_groups={{0,1,4,5,8,9,12,13},{2,3,6,7,10,11,14,15},{16,17,20,21,24,25,28,29},{18..., dimensions={0} | all-to-all | bytes 327680 | tf_op jit(solution)/shard_map/all_to_all | solution.py:459
  100.0 0.6 shard_map.139
  100.6 6.3 %all-to-all-start.3 = ((f32[16,8,128]{2,1,0:T(8,128)}), f32[16,8,128]{2,1,0:T(8,128)S(1)}, u32[]{:S(2)}, u32[]{:S(2)}) async-start(f32[16,8,128]{2,1,0:T(8,128)} %get-tuple-element.111), calls=%async_computation.3 | async-start | bytes 131072 | tf_op jit(solution)/shard_map/all_to_all | solution.py:462
  106.9 1.2 %collective-permute-done.22.other = f32[32,128]{1,0:T(8,128)S(1)} collective-permute-done((f32[32,128]{1,0:T(8,128)S(1)}, f32[32,128]{1,0:T(8,128)S(1)}, u32[]{:S(2)}, u32[]{:S(2)}) %collective-permute-start.22) | collective-permute-done | bytes 16416 | tf_op jit(solution)/shard_map/ppermute | solution.py:461
  108.0 7.9 %all-to-all-done.3.stats = f32[16,8,128]{2,1,0:T(8,128)S(1)} async-done(((f32[16,8,128]{2,1,0:T(8,128)}), f32[16,8,128]{2,1,0:T(8,128)S(1)}, u32[]{:S(2)}, u32[]{:S(2)}) %all-to-all-start.3) | async-done | bytes 65568 | tf_op jit(solution)/shard_map/all_to_all | solution.py:462
  116.0 0.8 shard_map.140
  (43 shorter events, 3.2 us)
Async XLA Ops:
  0.6 5.5 %copy-start.1 = (f32[1,4,2048]{2,1,0:T(4,128)S(1)}, f32[1,4,2048]{2,1,0:T(4,128)}, u32[]{:S(2)}) copy-start(f32[1,4,2048]{2,1,0:T(4,128)} %param.14) | copy-start | bytes 98308
  0.6 5.5 %copy-start.4 = (s32[1,2048]{1,0:T(1,128)S(1)}, s32[1,2048]{1,0:T(1,128)}, u32[]{:S(2)}) copy-start(s32[1,2048]{1,0:T(1,128)} %param.15) | copy-start | bytes 24580
  0.7 5.5 %copy-start.3 = (s32[1,2048]{1,0:T(1,128)S(1)}, s32[1,2048]{1,0:T(1,128)}, u32[]{:S(2)}) copy-start(s32[1,2048]{1,0:T(1,128)} %param.16) | copy-start | bytes 24580
  0.7 5.5 %copy-start.2 = (s32[1,2048]{1,0:T(1,128)S(1)}, s32[1,2048]{1,0:T(1,128)}, u32[]{:S(2)}) copy-start(s32[1,2048]{1,0:T(1,128)} %param.17) | copy-start | bytes 24580
  2.1 6.2 %collective-permute-start = (f32[1,4,64,128]{3,2,1,0:T(8,128)S(1)}, f32[1,4,64,128]{3,2,1,0:T(8,128)S(1)}, u32[]{:S(2)}, u32[]{:S(2)}) collective-permute-start(f32[1,4,64,128]{3,2,1,0:T(8,128)S(1)} %get-tuple-element.63), channel_id=1, source_target_pairs={{2,4},{6,8},{10,12},{14,0},{4,2},{8,6},{12,10},{0,14},{3,5},{7,9},... | collective-permute-start | bytes 393224 | tf_op jit(solution)/shard_map/ppermute | solution.py:391
  4.6 3.7 %collective-permute-start.1 = (f32[1,4,64,128]{3,2,1,0:T(8,128)S(1)}, f32[1,4,64,128]{3,2,1,0:T(8,128)S(1)}, u32[]{:S(2)}, u32[]{:S(2)}) collective-permute-start(f32[1,4,64,128]{3,2,1,0:T(8,128)S(1)} %get-tuple-element.64), channel_id=1, source_target_pairs={{0,2},{2,0},{4,6},{6,4},{8,10},{10,8},{12,14},{14,12},{1,3},{3,1},... | collective-permute-start | bytes 393224 | tf_op jit(solution)/shard_map/ppermute | solution.py:392
  4.6 3.7 %collective-permute-start.2 = (f32[1,16,128]{2,1,0:T(8,128)S(1)}, f32[1,16,128]{2,1,0:T(8,128)S(1)}, u32[]{:S(2)}, u32[]{:S(2)}) collective-permute-start(f32[1,16,128]{2,1,0:T(8,128)S(1)} %get-tuple-element.65), channel_id=1, source_target_pairs={{0,1},{1,0},{2,3},{3,2},{4,5},{5,4},{6,7},{7,6},{8,9},{9,8},{10,11... | collective-permute-start | bytes 24584 | tf_op jit(solution)/shard_map/ppermute | solution.py:393
  8.8 7.1 %collective-permute-start.3 = (f32[2,4,64,128]{3,2,1,0:T(8,128)S(1)}, f32[2,4,64,128]{3,2,1,0:T(8,128)S(1)}, u32[]{:S(2)}, u32[]{:S(2)}) collective-permute-start(f32[2,4,64,128]{3,2,1,0:T(8,128)S(1)} %get-tuple-element.72), channel_id=1, source_target_pairs={{2,4},{6,8},{10,12},{14,0},{4,2},{8,6},{12,10},{0,14},{3,5},{7,9},... | collective-permute-start | bytes 786440 | tf_op jit(solution)/shard_map/ppermute | solution.py:391
  10.8 5.1 %collective-permute-start.4 = (f32[2,4,64,128]{3,2,1,0:T(8,128)S(1)}, f32[2,4,64,128]{3,2,1,0:T(8,128)S(1)}, u32[]{:S(2)}, u32[]{:S(2)}) collective-permute-start(f32[2,4,64,128]{3,2,1,0:T(8,128)S(1)} %get-tuple-element.73), channel_id=1, source_target_pairs={{0,2},{2,0},{4,6},{6,4},{8,10},{10,8},{12,14},{14,12},{1,3},{3,1},... | collective-permute-start | bytes 786440 | tf_op jit(solution)/shard_map/ppermute | solution.py:392
  10.8 3.7 %collective-permute-start.5 = (f32[2,16,128]{2,1,0:T(8,128)S(1)}, f32[2,16,128]{2,1,0:T(8,128)S(1)}, u32[]{:S(2)}, u32[]{:S(2)}) collective-permute-start(f32[2,16,128]{2,1,0:T(8,128)S(1)} %get-tuple-element.74), channel_id=1, source_target_pairs={{0,1},{1,0},{2,3},{3,2},{4,5},{5,4},{6,7},{7,6},{8,9},{9,8},{10,11... | collective-permute-start | bytes 49160 | tf_op jit(solution)/shard_map/ppermute | solution.py:393
  16.6 7.1 %collective-permute-start.6 = (f32[2,4,64,128]{3,2,1,0:T(8,128)S(1)}, f32[2,4,64,128]{3,2,1,0:T(8,128)S(1)}, u32[]{:S(2)}, u32[]{:S(2)}) collective-permute-start(f32[2,4,64,128]{3,2,1,0:T(8,128)S(1)} %get-tuple-element.80), channel_id=1, source_target_pairs={{2,4},{6,8},{10,12},{14,0},{4,2},{8,6},{12,10},{0,14},{3,5},{7,9},... | collective-permute-start | bytes 786440 | tf_op jit(solution)/shard_map/ppermute | solution.py:391
  18.6 5.1 %collective-permute-start.7 = (f32[2,4,64,128]{3,2,1,0:T(8,128)S(1)}, f32[2,4,64,128]{3,2,1,0:T(8,128)S(1)}, u32[]{:S(2)}, u32[]{:S(2)}) collective-permute-start(f32[2,4,64,128]{3,2,1,0:T(8,128)S(1)} %get-tuple-element.81), channel_id=1, source_target_pairs={{0,2},{2,0},{4,6},{6,4},{8,10},{10,8},{12,14},{14,12},{1,3},{3,1},... | collective-permute-start | bytes 786440 | tf_op jit(solution)/shard_map/ppermute | solution.py:392
  18.6 3.7 %collective-permute-start.8 = (f32[2,16,128]{2,1,0:T(8,128)S(1)}, f32[2,16,128]{2,1,0:T(8,128)S(1)}, u32[]{:S(2)}, u32[]{:S(2)}) collective-permute-start(f32[2,16,128]{2,1,0:T(8,128)S(1)} %get-tuple-element.82), channel_id=1, source_target_pairs={{0,1},{1,0},{2,3},{3,2},{4,5},{5,4},{6,7},{7,6},{8,9},{9,8},{10,11... | collective-permute-start | bytes 49160 | tf_op jit(solution)/shard_map/ppermute | solution.py:393
  24.4 7.2 %collective-permute-start.10 = (f32[2,4,64,128]{3,2,1,0:T(8,128)S(1)}, f32[2,4,64,128]{3,2,1,0:T(8,128)S(1)}, u32[]{:S(2)}, u32[]{:S(2)}) collective-permute-start(f32[2,4,64,128]{3,2,1,0:T(8,128)S(1)} %get-tuple-element.92), channel_id=1, source_target_pairs={{0,2},{2,0},{4,6},{6,4},{8,10},{10,8},{12,14},{14,12},{1,3},{3,1},... | collective-permute-start | bytes 786440 | tf_op jit(solution)/shard_map/ppermute | solution.py:392
  24.5 7.3 %collective-permute-start.9 = (f32[2,4,64,128]{3,2,1,0:T(8,128)S(1)}, f32[2,4,64,128]{3,2,1,0:T(8,128)S(1)}, u32[]{:S(2)}, u32[]{:S(2)}) collective-permute-start(f32[2,4,64,128]{3,2,1,0:T(8,128)S(1)} %get-tuple-element.91), channel_id=1, source_target_pairs={{2,4},{6,8},{10,12},{14,0},{4,2},{8,6},{12,10},{0,14},{3,5},{7,9},... | collective-permute-start | bytes 786440 | tf_op jit(solution)/shard_map/ppermute | solution.py:391
  26.7 4.9 %collective-permute-start.11 = (f32[2,16,128]{2,1,0:T(8,128)S(1)}, f32[2,16,128]{2,1,0:T(8,128)S(1)}, u32[]{:S(2)}, u32[]{:S(2)}) collective-permute-start(f32[2,16,128]{2,1,0:T(8,128)S(1)} %get-tuple-element.93), channel_id=1, source_target_pairs={{0,1},{1,0},{2,3},{3,2},{4,5},{5,4},{6,7},{7,6},{8,9},{9,8},{10,11... | collective-permute-start | bytes 49160 | tf_op jit(solution)/shard_map/ppermute | solution.py:393
  30.4 24.0 %copy-start = (f32[4,8,128]{2,1,0:T(8,128)S(1)}, f32[4,8,128]{2,1,0:T(8,128)}, u32[]{:S(2)}) copy-start(f32[4,8,128]{2,1,0:T(8,128)} %param.13) | copy-start | bytes 49156
  69.8 5.7 %collective-permute-start.12 = (f32[1,4,64,128]{3,2,1,0:T(8,128)S(1)}, f32[1,4,64,128]{3,2,1,0:T(8,128)S(1)}, u32[]{:S(2)}, u32[]{:S(2)}) collective-permute-start(f32[1,4,64,128]{3,2,1,0:T(8,128)S(1)} %get-tuple-element.98), channel_id=1, source_target_pairs={{2,4},{6,8},{10,12},{14,0},{4,2},{8,6},{12,10},{0,14},{3,5},{7,9},... | collective-permute-start | bytes 393224 | tf_op jit(solution)/shard_map/ppermute | solution.py:391
  71.5 4.0 %collective-permute-start.13 = (f32[1,4,64,128]{3,2,1,0:T(8,128)S(1)}, f32[1,4,64,128]{3,2,1,0:T(8,128)S(1)}, u32[]{:S(2)}, u32[]{:S(2)}) collective-permute-start(f32[1,4,64,128]{3,2,1,0:T(8,128)S(1)} %get-tuple-element.99), channel_id=1, source_target_pairs={{0,2},{2,0},{4,6},{6,4},{8,10},{10,8},{12,14},{14,12},{1,3},{3,1},... | collective-permute-start | bytes 393224 | tf_op jit(solution)/shard_map/ppermute | solution.py:392
  71.6 3.7 %collective-permute-start.14 = (f32[1,16,128]{2,1,0:T(8,128)S(1)}, f32[1,16,128]{2,1,0:T(8,128)S(1)}, u32[]{:S(2)}, u32[]{:S(2)}) collective-permute-start(f32[1,16,128]{2,1,0:T(8,128)S(1)} %get-tuple-element.100), channel_id=1, source_target_pairs={{0,1},{1,0},{2,3},{3,2},{4,5},{5,4},{6,7},{7,6},{8,9},{9,8},{10,11... | collective-permute-start | bytes 24584 | tf_op jit(solution)/shard_map/ppermute | solution.py:393
  76.0 5.7 %collective-permute-start.15 = (f32[1,4,64,128]{3,2,1,0:T(8,128)S(1)}, f32[1,4,64,128]{3,2,1,0:T(8,128)S(1)}, u32[]{:S(2)}, u32[]{:S(2)}) collective-permute-start(f32[1,4,64,128]{3,2,1,0:T(8,128)S(1)} %get-tuple-element.102), channel_id=1, source_target_pairs={{2,4},{6,8},{10,12},{14,0},{4,2},{8,6},{12,10},{0,14},{3,5},{7,9},... | collective-permute-start | bytes 393224 | tf_op jit(solution)/shard_map/ppermute | solution.py:391
  77.7 4.0 %collective-permute-start.16 = (f32[1,4,64,128]{3,2,1,0:T(8,128)S(1)}, f32[1,4,64,128]{3,2,1,0:T(8,128)S(1)}, u32[]{:S(2)}, u32[]{:S(2)}) collective-permute-start(f32[1,4,64,128]{3,2,1,0:T(8,128)S(1)} %get-tuple-element.103), channel_id=1, source_target_pairs={{0,2},{2,0},{4,6},{6,4},{8,10},{10,8},{12,14},{14,12},{1,3},{3,1},... | collective-permute-start | bytes 393224 | tf_op jit(solution)/shard_map/ppermute | solution.py:392
  77.7 3.7 %collective-permute-start.17 = (f32[1,16,128]{2,1,0:T(8,128)S(1)}, f32[1,16,128]{2,1,0:T(8,128)S(1)}, u32[]{:S(2)}, u32[]{:S(2)}) collective-permute-start(f32[1,16,128]{2,1,0:T(8,128)S(1)} %get-tuple-element.104), channel_id=1, source_target_pairs={{0,1},{1,0},{2,3},{3,2},{4,5},{5,4},{6,7},{7,6},{8,9},{9,8},{10,11... | collective-permute-start | bytes 24584 | tf_op jit(solution)/shard_map/ppermute | solution.py:393
  82.2 5.7 %collective-permute-start.18 = (f32[1,4,64,128]{3,2,1,0:T(8,128)S(1)}, f32[1,4,64,128]{3,2,1,0:T(8,128)S(1)}, u32[]{:S(2)}, u32[]{:S(2)}) collective-permute-start(f32[1,4,64,128]{3,2,1,0:T(8,128)S(1)} %get-tuple-element.107), channel_id=1, source_target_pairs={{2,4},{6,8},{10,12},{14,0},{4,2},{8,6},{12,10},{0,14},{3,5},{7,9},... | collective-permute-start | bytes 393224 | tf_op jit(solution)/shard_map/ppermute | solution.py:391
  83.9 4.0 %collective-permute-start.19 = (f32[1,4,64,128]{3,2,1,0:T(8,128)S(1)}, f32[1,4,64,128]{3,2,1,0:T(8,128)S(1)}, u32[]{:S(2)}, u32[]{:S(2)}) collective-permute-start(f32[1,4,64,128]{3,2,1,0:T(8,128)S(1)} %get-tuple-element.108), channel_id=1, source_target_pairs={{0,2},{2,0},{4,6},{6,4},{8,10},{10,8},{12,14},{14,12},{1,3},{3,1},... | collective-permute-start | bytes 393224 | tf_op jit(solution)/shard_map/ppermute | solution.py:392
  83.9 3.7 %collective-permute-start.20 = (f32[1,16,128]{2,1,0:T(8,128)S(1)}, f32[1,16,128]{2,1,0:T(8,128)S(1)}, u32[]{:S(2)}, u32[]{:S(2)}) collective-permute-start(f32[1,16,128]{2,1,0:T(8,128)S(1)} %get-tuple-element.109), channel_id=1, source_target_pairs={{0,1},{1,0},{2,3},{3,2},{4,5},{5,4},{6,7},{7,6},{8,9},{9,8},{10,11... | collective-permute-start | bytes 24584 | tf_op jit(solution)/shard_map/ppermute | solution.py:393
  89.0 1.3 %collective-permute-start.21 = (f32[72,128]{1,0:T(8,128)S(1)}, f32[72,128]{1,0:T(8,128)S(1)}, u32[]{:S(2)}, u32[]{:S(2)}) collective-permute-start(f32[72,128]{1,0:T(8,128)S(1)} %shard_map.137.mine), channel_id=1, source_target_pairs={{0,2},{2,0},{4,6},{6,4},{8,10},{10,8},{12,14},{14,12},{1,3},{3,1},... | collective-permute-start | bytes 110600 | tf_op jit(solution)/shard_map/ppermute | solution.py:456
  100.6 15.4 %all-to-all-start.3 = ((f32[16,8,128]{2,1,0:T(8,128)}), f32[16,8,128]{2,1,0:T(8,128)S(1)}, u32[]{:S(2)}, u32[]{:S(2)}) async-start(f32[16,8,128]{2,1,0:T(8,128)} %get-tuple-element.111), calls=%async_computation.3 | async-start | bytes 131072 | tf_op jit(solution)/shard_map/all_to_all | solution.py:462
  106.9 1.2 %collective-permute-start.22 = (f32[32,128]{1,0:T(8,128)S(1)}, f32[32,128]{1,0:T(8,128)S(1)}, u32[]{:S(2)}, u32[]{:S(2)}) collective-permute-start(f32[32,128]{1,0:T(8,128)S(1)} %get-tuple-element.112.half), channel_id=1, source_target_pairs={{0,2},{2,0},{4,6},{6,4},{8,10},{10,8},{12,14},{14,12},{1,3},{3,1},... | collective-permute-start | bytes 49160 | tf_op jit(solution)/shard_map/ppermute | solution.py:461
